TPU v7x, 32 devices: a whole 2x2x4 slice. The times are simulated.
32 devices in a mesh: groups: 2 (over y), sector: 4 (over z), op: 2 (over x), rep: 2 (over core).
Axes of the slice: x: 2, y: 2, z: 4, core: 2. Of those that a mesh axis runs over, the one named last changes fastest.
Arguments:
- wavefunction: bfloat16 [32, 256, 256], P(('groups', 'sector')), parts along dimension 0, may hold values from -6 to 6
- left_ops: bfloat16 [128, 256, 256], P(('groups', 'op'), 'rep'), parts along dimension 0, may hold values from -0.375 to 0.375
- right_ops: bfloat16 [128, 256, 256], P(('groups', 'op')), parts along dimension 0, may hold values from -0.375 to 0.375
- site_coef: float32 [128, 16], P(('groups', 'op'), 'sector'), parts along dimension 0, may hold values from -4 to 4
- coupled: int32 [128, 16], P(('groups', 'op'), 'sector'), parts along dimension 0, may hold values from 0 to 1, as said below
- sector_shift: int32 [128], P(('groups', 'op')), parts along dimension 0, may hold values from 0 to 15
Outputs:
- sigma: float32 [32, 256, 256], P(('groups', 'sector'), 'rep', 'op'), parts along dimension 0
There are 2 independent parts, one for each index of `groups`. A program takes and returns all parts, laid end to end along the dimension named above; each array names one. Nothing has to cross between parts.
Inputs may be any that keep to these rules, and one draw needn't show every extreme that they name: coupled holds only 0 and 1; the share of coupled terms differs from sector to sector.
All inputs are finite; a program needn't handle non-finite values.
Results may differ from a plain program's by a relative error of at most 0.0029.
Values may be sent and summed in bfloat16 or wider, within the bound.
No kernel may reach another device: no remote copies, remote signals or barrier semaphores. Data moves between devices by JAX's collectives and lax.ppermute only.
A program may use at most 64 MiB of HBM per device.

v0:
```python
import jax
import jax.numpy as jnp
from jax import lax
from jax.sharding import PartitionSpec as P


def per_device(wavefunction, left_ops, right_ops, site_coef, coupled, sector_shift):
    sec_dev = wavefunction.shape[0]
    width = wavefunction.shape[1]
    k_dev = left_ops.shape[0]
    half_rows = left_ops.shape[1]
    total_sectors = sec_dev * lax.axis_size("sector")
    base_sector = lax.axis_index("sector") * sec_dev
    zero_sigma = jnp.zeros((sec_dev, half_rows, width), jnp.float32)
    term_block = 8
    block_count = k_dev // term_block
    local_ids = jnp.arange(sec_dev, dtype=jnp.int32)
    sources = (base_sector + local_ids[None, :] + sector_shift[:, None]) % total_sectors
    live_coef = jnp.where(coupled > 0, site_coef, 0.0)
    left_blocks = left_ops.reshape(block_count, term_block, half_rows, width)
    right_blocks = right_ops.reshape(block_count, term_block, width, width)
    everything = lax.all_gather(wavefunction, "sector", axis=0, tiled=True)
    count = everything.shape[0]
    inside = (sources >= 0) & (sources < 0 + count)
    weights = jnp.where(inside, live_coef, 0.0)
    positions = jnp.clip(sources - 0, 0, count - 1)
    weights = weights.reshape(block_count, term_block, sec_dev)
    positions = positions.reshape(block_count, term_block, sec_dev)

    def one_block(total, pieces):
        left_part, right_part, place, weight = pieces
        source_blocks = jnp.take(everything, place, axis=0)
        mixed = jnp.einsum(
            "kij,ksjl->ksil", left_part, source_blocks, preferred_element_type=jnp.float32
        ).astype(jnp.bfloat16)
        product = jnp.einsum(
            "ksil,kml->ksim", mixed, right_part, preferred_element_type=jnp.float32
        )
        return (total + jnp.sum(weight[:, :, None, None] * product, axis=0), None)

    result, unused = lax.scan(
        one_block, zero_sigma, (left_blocks, right_blocks, positions, weights)
    )
    summed = lax.psum(result, "op")
    columns = width // lax.axis_size("op")
    return lax.dynamic_slice_in_dim(summed, lax.axis_index("op") * columns, columns, 2)


def solution(mesh):
    placed = (
        P(("groups", "sector"), None, None),
        P(("groups", "op"), "rep", None),
        P(("groups", "op"), None, None),
        P(("groups", "op"), "sector"),
        P(("groups", "op"), "sector"),
        P(("groups", "op")),
    )
    return jax.shard_map(
        per_device,
        mesh=mesh,
        in_specs=placed,
        out_specs=P(("groups", "sector"), "rep", "op"),
        check_vma=False,
    )
```

profile of v0, /device:TPU:0, one launch (start us, length us, event | category | flops | bytes accessed | tf_op | source)
XLA Modules:
  0.0 158.2 jit_solution(12605947227906350444)
XLA Ops:
  6.5 0.7 all-gather.2.cloned.1.call-update
  7.3 0.7 add.81
  8.1 0.8 select_select_fusion
  8.8 0.1 reshape.62
  9.0 48.6 %all-gather.2.cloned.1.call-done = bf16[16,256,256]{2,1,0:T(8,128)(2,1)} async-done(((bf16[4,256,256]{2,1,0:T(8,128)(2,1)}), bf16[16,256,256]{2,1,0:T(8,128)(2,1)}) %all-gather.2.cloned.1.call-update) | async-done | bytes 2097168 | tf_op jit(solution)/shard_map/all_gather | solution.py:22
  57.6 63.8 %while.11 = (s32[]{:T(128)}, f32[4,128,256]{2,1,0:T(8,128)S(1)}, f32[4,8,4]{1,0,2:T(4,128)S(1)}, s32[4,8,4]{1,2,0:T(4,128)S(1)}, bf16[16,256,256]{2,1,0:T(8,128)...) while((s32[]{:T(128)}, f32[4,128,256]{2,1,0:T(8,128)S(1)}, ...), condition=%wide.region_2.3_spmd.clone, body=%wide.region_0.2_spmd.clone.sunk | while | flops 1079117056 | bytes 24648688 | solution.py:41
  57.6 0.1 copy.30
  57.8 4.3 %gather_fusion = bf16[32,256,256]{2,1,0:T(8,128)(2,1)} fusion(bf16[16,256,256]{2,1,0:T(8,128)(2,1)} %get-tuple-element.167, s32[1024]{0:T(1024)S(1)} %pad_clamp_fusion.2), kind=kCustom, calls=%fused_computation.clone.clone.1 | custom fusion | bytes 8388736 | tf_op jit(solution)/shard_map/while/body/eval_jaxpr/jit(_take)/gather | solution.py:32
  62.1 6.5 %copy.31 = bf16[8,4,256,256]{2,3,1,0:T(8,128)(2,1)} copy(bf16[8,4,256,256]{3,2,1,0:T(8,128)(2,1)} %bitcast.46) | data formatting | bytes 8388608 | tf_op jit(solution)/shard_map/while/body/eval_jaxpr/jit(_take)/gather | solution.py:32
  68.6 0.1 copy.32
  68.7 0.1 copy.29
  68.8 4.6 %multiply_reduce_fusion.2 = f32[4,128,256]{2,1,0:T(8,128)S(1)} fusion(f32[8,4]{1,0:T(8,128)S(1)} %copy.29, bf16[8,4,256,256]{2,3,1,0:T(8,128)(2,1)} %copy.31, pred[8,4]{1,0:T(8,128)(4,1)S(1)} %copy.32, bf16[4,8,256,256]{3,2,1,0:T(8,128)(2,1)} %get-tuple-element.169, s32[]{:T(128)} %get-tuple-element.154, bf16[4,8,128,256]{3,2,1,0:T(8,128)(2,1)} %get-tuple-element.168), kind=kOutput, calls=%fused_computation.1.clone.1 | convolution fusion | flops 1078853632 | bytes 6292640 | tf_op jit(solution)/shard_map/while/body/eval_jaxpr/ksil,kml->ksim/dot_general | solution.py:36
  73.4 0.2 select_add_fusion.2
  73.7 4.3 %gather_fusion = bf16[32,256,256]{2,1,0:T(8,128)(2,1)} fusion(bf16[16,256,256]{2,1,0:T(8,128)(2,1)} %get-tuple-element.167, s32[1024]{0:T(1024)S(1)} %pad_clamp_fusion.2), kind=kCustom, calls=%fused_computation.clone.clone.1 | custom fusion | bytes 8388736 | tf_op jit(solution)/shard_map/while/body/eval_jaxpr/jit(_take)/gather | solution.py:32
  78.1 6.5 %copy.31 = bf16[8,4,256,256]{2,3,1,0:T(8,128)(2,1)} copy(bf16[8,4,256,256]{3,2,1,0:T(8,128)(2,1)} %bitcast.46) | data formatting | bytes 8388608 | tf_op jit(solution)/shard_map/while/body/eval_jaxpr/jit(_take)/gather | solution.py:32
  84.6 0.1 copy.32
  84.8 4.6 %multiply_reduce_fusion.2 = f32[4,128,256]{2,1,0:T(8,128)S(1)} fusion(f32[8,4]{1,0:T(8,128)S(1)} %copy.29, bf16[8,4,256,256]{2,3,1,0:T(8,128)(2,1)} %copy.31, pred[8,4]{1,0:T(8,128)(4,1)S(1)} %copy.32, bf16[4,8,256,256]{3,2,1,0:T(8,128)(2,1)} %get-tuple-element.169, s32[]{:T(128)} %get-tuple-element.154, bf16[4,8,128,256]{3,2,1,0:T(8,128)(2,1)} %get-tuple-element.168), kind=kOutput, calls=%fused_computation.1.clone.1 | convolution fusion | flops 1078853632 | bytes 6292640 | tf_op jit(solution)/shard_map/while/body/eval_jaxpr/ksil,kml->ksim/dot_general | solution.py:36
  89.3 0.2 select_add_fusion.2
  89.7 4.3 %gather_fusion = bf16[32,256,256]{2,1,0:T(8,128)(2,1)} fusion(bf16[16,256,256]{2,1,0:T(8,128)(2,1)} %get-tuple-element.167, s32[1024]{0:T(1024)S(1)} %pad_clamp_fusion.2), kind=kCustom, calls=%fused_computation.clone.clone.1 | custom fusion | bytes 8388736 | tf_op jit(solution)/shard_map/while/body/eval_jaxpr/jit(_take)/gather | solution.py:32
  94.0 6.5 %copy.31 = bf16[8,4,256,256]{2,3,1,0:T(8,128)(2,1)} copy(bf16[8,4,256,256]{3,2,1,0:T(8,128)(2,1)} %bitcast.46) | data formatting | bytes 8388608 | tf_op jit(solution)/shard_map/while/body/eval_jaxpr/jit(_take)/gather | solution.py:32
  100.5 0.1 copy.32
  100.7 4.6 %multiply_reduce_fusion.2 = f32[4,128,256]{2,1,0:T(8,128)S(1)} fusion(f32[8,4]{1,0:T(8,128)S(1)} %copy.29, bf16[8,4,256,256]{2,3,1,0:T(8,128)(2,1)} %copy.31, pred[8,4]{1,0:T(8,128)(4,1)S(1)} %copy.32, bf16[4,8,256,256]{3,2,1,0:T(8,128)(2,1)} %get-tuple-element.169, s32[]{:T(128)} %get-tuple-element.154, bf16[4,8,128,256]{3,2,1,0:T(8,128)(2,1)} %get-tuple-element.168), kind=kOutput, calls=%fused_computation.1.clone.1 | convolution fusion | flops 1078853632 | bytes 6292640 | tf_op jit(solution)/shard_map/while/body/eval_jaxpr/ksil,kml->ksim/dot_general | solution.py:36
  105.3 0.2 select_add_fusion.2
  105.7 4.3 %gather_fusion = bf16[32,256,256]{2,1,0:T(8,128)(2,1)} fusion(bf16[16,256,256]{2,1,0:T(8,128)(2,1)} %get-tuple-element.167, s32[1024]{0:T(1024)S(1)} %pad_clamp_fusion.2), kind=kCustom, calls=%fused_computation.clone.clone.1 | custom fusion | bytes 8388736 | tf_op jit(solution)/shard_map/while/body/eval_jaxpr/jit(_take)/gather | solution.py:32
  110.0 6.5 %copy.31 = bf16[8,4,256,256]{2,3,1,0:T(8,128)(2,1)} copy(bf16[8,4,256,256]{3,2,1,0:T(8,128)(2,1)} %bitcast.46) | data formatting | bytes 8388608 | tf_op jit(solution)/shard_map/while/body/eval_jaxpr/jit(_take)/gather | solution.py:32
  116.5 0.1 copy.32
  116.6 0.1 copy.29
  116.7 4.6 %multiply_reduce_fusion.2 = f32[4,128,256]{2,1,0:T(8,128)S(1)} fusion(f32[8,4]{1,0:T(8,128)S(1)} %copy.29, bf16[8,4,256,256]{2,3,1,0:T(8,128)(2,1)} %copy.31, pred[8,4]{1,0:T(8,128)(4,1)S(1)} %copy.32, bf16[4,8,256,256]{3,2,1,0:T(8,128)(2,1)} %get-tuple-element.169, s32[]{:T(128)} %get-tuple-element.154, bf16[4,8,128,256]{3,2,1,0:T(8,128)(2,1)} %get-tuple-element.168), kind=kOutput, calls=%fused_computation.1.clone.1 | convolution fusion | flops 1078853632 | bytes 6292640 | tf_op jit(solution)/shard_map/while/body/eval_jaxpr/ksil,kml->ksim/dot_general | solution.py:36
  121.3 0.2 select_add_fusion.2
  121.4 0.8 copy-done
  122.2 27.5 %all-reduce.2.cloned.1.call-done = f32[4,128,256]{2,1,0:T(8,128)} async-done(((f32[4,128,256]{2,1,0:T(8,128)}), f32[4,128,256]{2,1,0:T(8,128)}) %all-reduce.2.cloned.1.call-update) | async-done | bytes 524304 | tf_op jit(solution)/shard_map/psum | solution.py:44
  149.7 1.7 %constant_dynamic-slice_fusion.1 = f32[4,128,128]{2,1,0:T(8,128)} fusion(f32[4,128,256]{2,1,0:T(8,128)} %all-reduce.2.cloned.1.call-done, s32[]{:T(128)S(6)} %select_n.44), kind=kLoop, calls=%fused_computation.35 | loop fusion | bytes 524292 | tf_op jit(solution)/shard_map/dynamic_slice | solution.py:46
  (32 shorter events, 1.0 us)
Async XLA Ops:
  6.5 51.1 %all-gather.2.cloned.1.call-start = ((), (), s32[]{:S(2)}) async-start(), calls=%async_computation | async-start | bytes 2621440 | tf_op jit(solution)/shard_map/all_gather | solution.py:22
  7.3 142.5 %all-reduce.2.cloned.1.call-start = ((), (), s32[]{:S(2)}) async-start(), calls=%async_computation.1 | async-start | bytes 1048576 | tf_op jit(solution)/shard_map/psum | solution.py:44
  121.4 0.8 copy-start
Sparse Core Ops, SparseCore 0:
  8.9 48.6 all-gather.1
  122.4 27.2 all-reduce.1
where the time goes:
time: 159 us; the launch traced here: 158 us
  waiting for transfers between devices  76.8 us (48%)
  local copies, waits for them, and re-layouts  48 us (30%)
  matrix products  18.2 us (11%)
  between operations  13.4 us (8%)
    all_gather x1, waiting for transfers between devices, per_device(): everything = lax.all_gather(wavefunction, 'sector', axis=0, tiled=True)  48.6 us
    gather x8, local copies, waits for them, and re-layouts, one_block(): source_blocks = jnp.take(everything, place, axis=0)  43.3 us
    psum x1, waiting for transfers between devices, per_device(): summed = lax.psum(result, 'op')  27.5 us
    dot_general x4, matrix products, one_block(): jnp.einsum('ksil,kml->ksim', mixed, right_part, preferred_element_type=jn...  18.2 us
  transfers between devices with their start and end apart: 2, of which 2 were waited for; matrix products, arithmetic and copies ran while one was open for 1% of the time, Pallas kernels for 0%

commit v1 on v0

v1 whole, which is shorter than its diff:
```python
import functools

import jax
import jax.numpy as jnp
from jax import lax
from jax.experimental import pallas as pl
from jax.experimental.pallas import tpu as pltpu
from jax.sharding import PartitionSpec as P

TERMS_A_STEP = 4


def sigma_kernel(counts, split, place_ref, weight_ref, side_ref, *refs):
    pieces = refs[: len(counts)]
    left_ref, right_ref = refs[len(counts) : len(counts) + 2]
    outs = refs[len(counts) + 2 : -3]
    blocks, total, sems = refs[-3:]
    step = pl.program_id(0)
    terms = left_ref.shape[0]
    sectors, rows, width = total.shape

    @pl.when(step == 0)
    def _():
        copies = []
        at = 0
        for number, count in enumerate(counts):
            copy = pltpu.make_async_copy(
                pieces[number], blocks.at[pl.ds(at, count)], sems.at[number]
            )
            copy.start()
            copies.append(copy)
            at += count
        total[...] = jnp.zeros_like(total)
        for copy in copies:
            copy.wait()

    for t in range(terms):
        k = step * terms + t
        left = left_ref[t]
        mixed = [
            jnp.dot(
                left, blocks[place_ref[k, s]], preferred_element_type=jnp.float32
            ).astype(jnp.bfloat16)
            for s in range(sectors)
        ]
        product = lax.dot_general(
            jnp.concatenate(mixed, axis=0),
            right_ref[t],
            (((1,), (1,)), ((), ())),
            preferred_element_type=jnp.float32,
        )
        for s in range(sectors):
            total[s] += weight_ref[k, s] * product[s * rows : (s + 1) * rows]

    @pl.when(step == pl.num_programs(0) - 1)
    def _():
        if not split:
            outs[0][...] = total[...]
        else:
            first = side_ref[0] == 0
            half = width // 2
            low, high = total[:, :, :half], total[:, :, half:]
            outs[0][...] = jnp.where(first, low, high)
            outs[1][...] = jnp.where(first, high, low).astype(jnp.bfloat16)


def all_terms(pieces, place, weight, side, left_ops, right_ops, split):
    k_dev, half_rows, width = left_ops.shape
    sec_dev = place.shape[1]
    counts = tuple(piece.shape[0] for piece in pieces)
    terms = TERMS_A_STEP
    if split:
        shape = (sec_dev, half_rows, width // 2)
        outs = [jax.ShapeDtypeStruct(shape, jnp.float32), jax.ShapeDtypeStruct(shape, jnp.bfloat16)]
    else:
        outs = [jax.ShapeDtypeStruct((sec_dev, half_rows, width), jnp.float32)]
    return pl.pallas_call(
        functools.partial(sigma_kernel, counts, split),
        grid=(k_dev // terms,),
        out_shape=outs,
        in_specs=[pl.BlockSpec(memory_space=pltpu.SMEM)] * 3
        + [pl.BlockSpec(memory_space=pl.ANY)] * len(pieces)
        + [
            pl.BlockSpec((terms, half_rows, width), lambda i: (i, 0, 0)),
            pl.BlockSpec((terms, width, width), lambda i: (i, 0, 0)),
        ],
        out_specs=[pl.BlockSpec(out.shape, lambda i: (0, 0, 0)) for out in outs],
        scratch_shapes=[
            pltpu.VMEM((sum(counts), width, width), jnp.bfloat16),
            pltpu.VMEM((sec_dev, half_rows, width), jnp.float32),
            pltpu.SemaphoreType.DMA((len(counts),)),
        ],
        compiler_params=pltpu.CompilerParams(vmem_limit_bytes=40 * 1024 * 1024),
        cost_estimate=pl.CostEstimate(
            flops=k_dev * sec_dev * 4 * half_rows * width * width,
            bytes_accessed=2 * (left_ops.size + right_ops.size + sum(counts) * width * width),
            transcendentals=0,
        ),
    )(place, weight, side, *pieces, left_ops, right_ops)


def shift_by(value, axis, distance):
    size = lax.axis_size(axis)
    return lax.ppermute(value, axis, [(i, (i + distance) % size) for i in range(size)])


def per_device(wavefunction, left_ops, right_ops, site_coef, coupled, sector_shift):
    sec_dev, width = wavefunction.shape[:2]
    devices = lax.axis_size("sector")
    total_sectors = sec_dev * devices
    me, op, rep = lax.axis_index("sector"), lax.axis_index("op"), lax.axis_index("rep")
    local_ids = jnp.arange(sec_dev, dtype=jnp.int32)
    source = (me * sec_dev + local_ids[None, :] + sector_shift[:, None]) % total_sectors
    weight = jnp.where(coupled > 0, site_coef, 0.0)
    side = jnp.reshape(op, (1,)).astype(jnp.int32)
    four = lax.axis_size("op") == 2 and lax.axis_size("rep") == 2

    if four and sec_dev == 4 and devices <= 4:
        own = lax.dynamic_slice_in_dim(wavefunction, op * 2 + rep, 1, 0)
        pieces = [wavefunction]
        for distance in range(1, devices):
            straight = shift_by(own, "sector", distance)
            across = shift_by(straight, "op", 1)
            beside = shift_by(straight, "rep", 1)
            diagonal = shift_by(across, "rep", 1)
            pieces += [straight, beside, across, diagonal]
        origin, block = source // sec_dev, source % sec_dev
        distance = (me - origin) % devices
        relative = block ^ (op * 2 + rep)
        place = jnp.where(distance == 0, block, distance * sec_dev + relative)
    else:
        pieces = [lax.all_gather(wavefunction, "sector", axis=0, tiled=True)]
        place = source

    if lax.axis_size("op") == 2:
        mine, theirs = all_terms(pieces, place, weight, side, left_ops, right_ops, True)
        return mine + shift_by(theirs, "op", 1).astype(jnp.float32)
    (total,) = all_terms(pieces, place, weight, side, left_ops, right_ops, False)
    return lax.psum_scatter(total, "op", scatter_dimension=2, tiled=True)


def solution(mesh):
    placed = (
        P(("groups", "sector"), None, None),
        P(("groups", "op"), "rep", None),
        P(("groups", "op"), None, None),
        P(("groups", "op"), "sector"),
        P(("groups", "op"), "sector"),
        P(("groups", "op")),
    )
    return jax.shard_map(
        per_device,
        mesh=mesh,
        in_specs=placed,
        out_specs=P(("groups", "sector"), "rep", "op"),
        check_vma=False,
    )
```

time: 159 us -> 48.7 us (0.31)
  waiting for transfers between devices: 76.8 us -> 16.7 us
  local copies, waits for them, and re-layouts: 48 us -> 6.6 us
  matrix products: 18.2 us -> 0 us
  between operations: 13.4 us -> 0.08 us
  starting transfers between devices: 0.04 us -> 11.8 us
  Pallas kernels: 0 us -> 11.1 us
    all_gather x1 -> x0, waiting for transfers between devices: 48.6 us -> none  [per_device(): everything = lax.all_gather(wavefunction, 'sector', axis=0, tiled=True)]
    gather x8 -> x0, local copies, waits for them, and re-layouts: 43.3 us -> none  [one_block(): source_blocks = jnp.take(everything, place, axis=0)]
    psum x1 -> x0, waiting for transfers between devices: 27.5 us -> none  [per_device(): summed = lax.psum(result, 'op')]
    dot_general x4 -> x0, matrix products: 18.2 us -> none  [one_block(): jnp.einsum('ksil,kml->ksim', mixed, right_part, preferred_element_type=jn...]
    ppermute x0 -> x13, waiting for transfers between devices: none -> 16.7 us  [shift_by(): lax.ppermute(value, axis, [(i, (i + distance) % size) for i in range(size)])]
    ppermute x0 -> x13, starting transfers between devices: none -> 11.8 us  [shift_by(): lax.ppermute(value, axis, [(i, (i + distance) % size) for i in range(size)])]
    pallas_call x0 -> x1, Pallas kernels: none -> 11.1 us  [all_terms(): pl.pallas_call(functools.partial(sigma_kernel, counts, split), grid=(k_de...]
    unnamed x2 -> x7, local copies, waits for them, and re-layouts: 0.79 us -> 5.58 us
  transfers between devices with their start and end apart: 2 -> 13, of which waited for: 2 -> 6; matrix products, arithmetic and copies ran while one was open for 1% -> 5% of each run, Pallas kernels for 0% -> 0%
where the time goes in v1:
time: 48.7 us; the launch traced here: 48.4 us
  waiting for transfers between devices  16.7 us (34%)
  starting transfers between devices  11.8 us (24%)
  Pallas kernels  11.1 us (23%)
  local copies, waits for them, and re-layouts  6.6 us (14%)
  other arithmetic  2.18 us (4%)
    ppermute x13, waiting for transfers between devices, shift_by(): lax.ppermute(value, axis, [(i, (i + distance) % size) for i in range(size)])  16.7 us
    ppermute x13, starting transfers between devices, shift_by(): lax.ppermute(value, axis, [(i, (i + distance) % size) for i in range(size)])  11.8 us
    pallas_call x1, Pallas kernels, all_terms(): pl.pallas_call(functools.partial(sigma_kernel, counts, split), grid=(k_de...  11.1 us
    unnamed x7, local copies, waits for them, and re-layouts  5.58 us
  transfers between devices with their start and end apart: 13, of which 6 were waited for; matrix products, arithmetic and copies ran while one was open for 5% of the time, Pallas kernels for 0%

profile of v1, /device:TPU:0, one launch (start us, length us, event | category | flops | bytes accessed | tf_op | source)
XLA Modules:
  0.0 48.4 jit_solution(8800184196666644024)
XLA Ops:
  0.0 0.9 %constant_dynamic-slice_fusion = bf16[1,256,256]{2,1,0:T(8,128)(2,1)S(1)} fusion(bf16[4,256,256]{2,1,0:T(8,128)(2,1)} %refs_0_.1, s32[]{:T(128)S(6)} %select_n.36), kind=kLoop, calls=%fused_computation.23 | loop fusion | bytes 262148 | tf_op jit(solution)/shard_map/dynamic_slice | solution.py:119
  0.9 5.1 %collective-permute-start.8 = (bf16[1,256,256]{2,1,0:T(8,128)(2,1)S(1)}, bf16[1,256,256]{2,1,0:T(8,128)(2,1)S(1)}, u32[]{:S(2)}, u32[]{:S(2)}) collective-permute-start(bf16[1,256,256]{2,1,0:T(8,128)(2,1)S(1)} %constant_dynamic-slice_fusion), channel_id=1, source_target_pairs={{0,12},{4,0},{8,4},{12,8},{1,13},{5,1},{9,5},{13,9},{2,14},{6,2},{... | collective-permute-start | bytes 393224 | tf_op jit(solution)/shard_map/ppermute | solution.py:104
  6.0 1.0 %collective-permute-start = (bf16[1,256,256]{2,1,0:T(8,128)(2,1)S(1)}, bf16[1,256,256]{2,1,0:T(8,128)(2,1)S(1)}, u32[]{:S(2)}, u32[]{:S(2)}) collective-permute-start(bf16[1,256,256]{2,1,0:T(8,128)(2,1)S(1)} %constant_dynamic-slice_fusion), channel_id=1, source_target_pairs={{0,4},{4,8},{8,12},{12,0},{1,5},{5,9},{9,13},{13,1},{2,6},{6,10},{... | collective-permute-start | bytes 393224 | tf_op jit(solution)/shard_map/ppermute | solution.py:104
  7.0 0.7 %broadcast_compare_fusion = pred[32,4]{0,1:T(4,128)(4,1)S(1)} fusion(s32[32,4]{0,1:T(4,128)} %param.10), kind=kLoop, calls=%fused_computation.21 | loop fusion | flops 128 | bytes 640 | tf_op jit(solution)/shard_map/gt | solution.py:114
  7.7 0.1 copy.8
  7.8 0.8 %copy.9 = f32[32,4]{1,0:T(8,128)S(1)} copy(f32[32,4]{0,1:T(4,128)} %param.9) | data formatting | bytes 1024 | tf_op args[3]
  8.6 1.3 %collective-permute-done.8.refs_9_ = bf16[1,256,256]{2,1,0:T(8,128)(2,1)S(1)} collective-permute-done((bf16[1,256,256]{2,1,0:T(8,128)(2,1)S(1)}, bf16[1,256,256]{2,1,0:T(8,128)(2,1)S(1)}, u32[]{:S(2)}, u32[]{:S(2)}) %collective-permute-start.8) | collective-permute-done | bytes 131104 | tf_op jit(solution)/shard_map/ppermute | solution.py:104
  9.9 1.5 %collective-permute-start.10 = (bf16[1,256,256]{2,1,0:T(8,128)(2,1)S(1)}, bf16[1,256,256]{2,1,0:T(8,128)(2,1)S(1)}, u32[]{:S(2)}, u32[]{:S(2)}) collective-permute-start(bf16[1,256,256]{2,1,0:T(8,128)(2,1)S(1)} %collective-permute-done.8.refs_9_), channel_id=1, source_target_pairs={{0,2},{2,0},{1,3},{3,1},{4,6},{6,4},{5,7},{7,5},{8,10},{10,8},{9,1... | collective-permute-start | bytes 393224 | tf_op jit(solution)/shard_map/ppermute | solution.py:104
  11.4 0.0 collective-permute-start.9
  11.4 5.8 %collective-permute-done.4.refs_5_ = bf16[1,256,256]{2,1,0:T(8,128)(2,1)S(1)} collective-permute-done((bf16[1,256,256]{2,1,0:T(8,128)(2,1)S(1)}, bf16[1,256,256]{2,1,0:T(8,128)(2,1)S(1)}, u32[]{:S(2)}, u32[]{:S(2)}) %collective-permute-start.4) | collective-permute-done | bytes 131104 | tf_op jit(solution)/shard_map/ppermute | solution.py:104
  17.2 1.5 %collective-permute-start.6 = (bf16[1,256,256]{2,1,0:T(8,128)(2,1)S(1)}, bf16[1,256,256]{2,1,0:T(8,128)(2,1)S(1)}, u32[]{:S(2)}, u32[]{:S(2)}) collective-permute-start(bf16[1,256,256]{2,1,0:T(8,128)(2,1)S(1)} %collective-permute-done.4.refs_5_), channel_id=1, source_target_pairs={{0,2},{2,0},{1,3},{3,1},{4,6},{6,4},{5,7},{7,5},{8,10},{10,8},{9,1... | collective-permute-start | bytes 393224 | tf_op jit(solution)/shard_map/ppermute | solution.py:104
  18.7 0.0 collective-permute-done.refs_1_
  18.7 0.5 %collective-permute-start.2 = (bf16[1,256,256]{2,1,0:T(8,128)(2,1)S(1)}, bf16[1,256,256]{2,1,0:T(8,128)(2,1)S(1)}, u32[]{:S(2)}, u32[]{:S(2)}) collective-permute-start(bf16[1,256,256]{2,1,0:T(8,128)(2,1)S(1)} %collective-permute-done.refs_1_), channel_id=1, source_target_pairs={{0,2},{2,0},{1,3},{3,1},{4,6},{6,4},{5,7},{7,5},{8,10},{10,8},{9,1... | collective-permute-start | bytes 393224 | tf_op jit(solution)/shard_map/ppermute | solution.py:104
  19.3 0.0 collective-permute-start.5
  19.3 0.0 collective-permute-done.10.refs_11_
  19.3 0.5 %collective-permute-start.1 = (bf16[1,256,256]{2,1,0:T(8,128)(2,1)S(1)}, bf16[1,256,256]{2,1,0:T(8,128)(2,1)S(1)}, u32[]{:S(2)}, u32[]{:S(2)}) collective-permute-start(bf16[1,256,256]{2,1,0:T(8,128)(2,1)S(1)} %collective-permute-done.refs_1_), channel_id=1, source_target_pairs={{0,1},{1,0},{2,3},{3,2},{4,5},{5,4},{6,7},{7,6},{8,9},{9,8},{10,11... | collective-permute-start | bytes 393224 | tf_op jit(solution)/shard_map/ppermute | solution.py:104
  19.8 0.0 collective-permute-done.9.refs_10_
  19.8 0.1 collective-permute-start.11
  19.9 3.5 %collective-permute-done.6.refs_7_ = bf16[1,256,256]{2,1,0:T(8,128)(2,1)S(1)} collective-permute-done((bf16[1,256,256]{2,1,0:T(8,128)(2,1)S(1)}, bf16[1,256,256]{2,1,0:T(8,128)(2,1)S(1)}, u32[]{:S(2)}, u32[]{:S(2)}) %collective-permute-start.6) | collective-permute-done | bytes 131104 | tf_op jit(solution)/shard_map/ppermute | solution.py:104
  23.4 0.0 collective-permute-start.7
  23.4 1.4 %collective-permute-done.2.refs_3_ = bf16[1,256,256]{2,1,0:T(8,128)(2,1)S(1)} collective-permute-done((bf16[1,256,256]{2,1,0:T(8,128)(2,1)S(1)}, bf16[1,256,256]{2,1,0:T(8,128)(2,1)S(1)}, u32[]{:S(2)}, u32[]{:S(2)}) %collective-permute-start.2) | collective-permute-done | bytes 131104 | tf_op jit(solution)/shard_map/ppermute | solution.py:104
  24.8 0.8 %add_select_fusion.5.place_ref = s32[32,4]{1,0:T(8,128)S(1)} fusion(s32[]{:T(128)S(6)} %add.60, s32[32]{0:T(128)} %param.11, s32[4]{0:T(128)S(1)} %iota_add_fusion, s32[]{:T(128)S(6)} %axis_index.33), kind=kLoop, calls=%fused_computation.17 | loop fusion | flops 6144 | bytes 664 | tf_op jit(solution)/shard_map/jit(_where)/select_n | solution.py:130
  25.6 0.0 collective-permute-done.5.refs_6_
  25.6 0.0 collective-permute-done.1.refs_2_
  25.6 0.5 %collective-permute-done.3.refs_4_ = bf16[1,256,256]{2,1,0:T(8,128)(2,1)S(1)} collective-permute-done((bf16[1,256,256]{2,1,0:T(8,128)(2,1)S(1)}, bf16[1,256,256]{2,1,0:T(8,128)(2,1)S(1)}, u32[]{:S(2)}, u32[]{:S(2)}) %collective-permute-start.3) | collective-permute-done | bytes 131104 | tf_op jit(solution)/shard_map/ppermute | solution.py:104
  26.1 1.0 %copy-done = bf16[4,256,256]{2,1,0:T(8,128)(2,1)S(1)} copy-done((bf16[4,256,256]{2,1,0:T(8,128)(2,1)S(1)}, bf16[4,256,256]{2,1,0:T(8,128)(2,1)}, u32[]{:S(2)}) %copy-start) | copy-done | bytes 524312
  27.2 2.2 %copy-done.1 = bf16[32,256,256]{2,1,0:T(8,128)(2,1)S(1)} copy-done((bf16[32,256,256]{2,1,0:T(8,128)(2,1)S(1)}, bf16[32,256,256]{2,1,0:T(8,128)(2,1)}, u32[]{:S(2)}) %copy-start.1) | copy-done | bytes 4194328
  29.4 1.6 %copy-done.2 = bf16[32,128,256]{2,1,0:T(8,128)(2,1)S(1)} copy-done((bf16[32,128,256]{2,1,0:T(8,128)(2,1)S(1)}, bf16[32,128,256]{2,1,0:T(8,128)(2,1)}, u32[]{:S(2)}) %copy-start.2) | copy-done | bytes 2097176
  31.0 11.1 %shard_map.64 = (f32[4,128,128]{2,1,0:T(8,128)S(1)}, bf16[4,128,128]{2,1,0:T(8,128)(2,1)S(1)}) custom-call(s32[32,4]{1,0:T(8,128)S(1)} %add_select_fusion.5.place_ref, f32[32,4]{1,0:T(8,128)S(1)} %broadcast_select_fusion.weight_ref, s32[1]{0:T(128)} %bitcast.side_ref, bf16[4,256,256]{2,1,0:T(8,128)(2,1)S(1)} %copy-done, ...), custom_call_target="tpu_custom_call" | custom-call | flops 4294967296 | bytes 8388608 | tf_op jit(solution)/shard_map/pallas_call | solution.py:77
  42.1 1.6 %collective-permute-start.12 = (bf16[4,128,128]{2,1,0:T(8,128)(2,1)S(1)}, bf16[4,128,128]{2,1,0:T(8,128)(2,1)S(1)}, u32[]{:S(2)}, u32[]{:S(2)}) collective-permute-start(bf16[4,128,128]{2,1,0:T(8,128)(2,1)S(1)} %get-tuple-element.8), channel_id=1, source_target_pairs={{0,2},{2,0},{1,3},{3,1},{4,6},{6,4},{5,7},{7,5},{8,10},{10,8},{9,1... | collective-permute-start | bytes 393224 | tf_op jit(solution)/shard_map/ppermute | solution.py:104
  43.7 4.1 %collective-permute-done.12 = bf16[4,128,128]{2,1,0:T(8,128)(2,1)S(1)} collective-permute-done((bf16[4,128,128]{2,1,0:T(8,128)(2,1)S(1)}, bf16[4,128,128]{2,1,0:T(8,128)(2,1)S(1)}, u32[]{:S(2)}, u32[]{:S(2)}) %collective-permute-start.12) | collective-permute-done | bytes 131104 | tf_op jit(solution)/shard_map/ppermute | solution.py:104
  47.7 0.7 %convert_add_fusion = f32[4,128,128]{2,1,0:T(8,128)} fusion(f32[4,128,128]{2,1,0:T(8,128)S(1)} %get-tuple-element.7, bf16[4,128,128]{2,1,0:T(8,128)(2,1)S(1)} %collective-permute-done.12), kind=kLoop, calls=%fused_computation | loop fusion | flops 131072 | bytes 655360 | tf_op jit(solution)/shard_map/add | solution.py:137
  (9 shorter events, 0.0 us)
Async XLA Ops:
  0.9 9.0 %collective-permute-start.8 = (bf16[1,256,256]{2,1,0:T(8,128)(2,1)S(1)}, bf16[1,256,256]{2,1,0:T(8,128)(2,1)S(1)}, u32[]{:S(2)}, u32[]{:S(2)}) collective-permute-start(bf16[1,256,256]{2,1,0:T(8,128)(2,1)S(1)} %constant_dynamic-slice_fusion), channel_id=1, source_target_pairs={{0,12},{4,0},{8,4},{12,8},{1,13},{5,1},{9,5},{13,9},{2,14},{6,2},{... | collective-permute-start | bytes 393224 | tf_op jit(solution)/shard_map/ppermute | solution.py:104
  6.0 11.2 %collective-permute-start.4 = (bf16[1,256,256]{2,1,0:T(8,128)(2,1)S(1)}, bf16[1,256,256]{2,1,0:T(8,128)(2,1)S(1)}, u32[]{:S(2)}, u32[]{:S(2)}) collective-permute-start(bf16[1,256,256]{2,1,0:T(8,128)(2,1)S(1)} %constant_dynamic-slice_fusion), channel_id=1, source_target_pairs={{0,8},{4,12},{8,0},{12,4},{1,9},{5,13},{9,1},{13,5},{2,10},{6,14},... | collective-permute-start | bytes 393224 | tf_op jit(solution)/shard_map/ppermute | solution.py:104
  6.0 12.7 %collective-permute-start = (bf16[1,256,256]{2,1,0:T(8,128)(2,1)S(1)}, bf16[1,256,256]{2,1,0:T(8,128)(2,1)S(1)}, u32[]{:S(2)}, u32[]{:S(2)}) collective-permute-start(bf16[1,256,256]{2,1,0:T(8,128)(2,1)S(1)} %constant_dynamic-slice_fusion), channel_id=1, source_target_pairs={{0,4},{4,8},{8,12},{12,0},{1,5},{5,9},{9,13},{13,1},{2,6},{6,10},{... | collective-permute-start | bytes 393224 | tf_op jit(solution)/shard_map/ppermute | solution.py:104
  9.9 9.3 %collective-permute-start.10 = (bf16[1,256,256]{2,1,0:T(8,128)(2,1)S(1)}, bf16[1,256,256]{2,1,0:T(8,128)(2,1)S(1)}, u32[]{:S(2)}, u32[]{:S(2)}) collective-permute-start(bf16[1,256,256]{2,1,0:T(8,128)(2,1)S(1)} %collective-permute-done.8.refs_9_), channel_id=1, source_target_pairs={{0,2},{2,0},{1,3},{3,1},{4,6},{6,4},{5,7},{7,5},{8,10},{10,8},{9,1... | collective-permute-start | bytes 393224 | tf_op jit(solution)/shard_map/ppermute | solution.py:104
  11.4 8.4 %collective-permute-start.9 = (bf16[1,256,256]{2,1,0:T(8,128)(2,1)S(1)}, bf16[1,256,256]{2,1,0:T(8,128)(2,1)S(1)}, u32[]{:S(2)}, u32[]{:S(2)}) collective-permute-start(bf16[1,256,256]{2,1,0:T(8,128)(2,1)S(1)} %collective-permute-done.8.refs_9_), channel_id=1, source_target_pairs={{0,1},{1,0},{2,3},{3,2},{4,5},{5,4},{6,7},{7,6},{8,9},{9,8},{10,11... | collective-permute-start | bytes 393224 | tf_op jit(solution)/shard_map/ppermute | solution.py:104
  17.2 6.2 %collective-permute-start.6 = (bf16[1,256,256]{2,1,0:T(8,128)(2,1)S(1)}, bf16[1,256,256]{2,1,0:T(8,128)(2,1)S(1)}, u32[]{:S(2)}, u32[]{:S(2)}) collective-permute-start(bf16[1,256,256]{2,1,0:T(8,128)(2,1)S(1)} %collective-permute-done.4.refs_5_), channel_id=1, source_target_pairs={{0,2},{2,0},{1,3},{3,1},{4,6},{6,4},{5,7},{7,5},{8,10},{10,8},{9,1... | collective-permute-start | bytes 393224 | tf_op jit(solution)/shard_map/ppermute | solution.py:104
  18.7 6.1 %collective-permute-start.2 = (bf16[1,256,256]{2,1,0:T(8,128)(2,1)S(1)}, bf16[1,256,256]{2,1,0:T(8,128)(2,1)S(1)}, u32[]{:S(2)}, u32[]{:S(2)}) collective-permute-start(bf16[1,256,256]{2,1,0:T(8,128)(2,1)S(1)} %collective-permute-done.refs_1_), channel_id=1, source_target_pairs={{0,2},{2,0},{1,3},{3,1},{4,6},{6,4},{5,7},{7,5},{8,10},{10,8},{9,1... | collective-permute-start | bytes 393224 | tf_op jit(solution)/shard_map/ppermute | solution.py:104
  19.3 6.3 %collective-permute-start.5 = (bf16[1,256,256]{2,1,0:T(8,128)(2,1)S(1)}, bf16[1,256,256]{2,1,0:T(8,128)(2,1)S(1)}, u32[]{:S(2)}, u32[]{:S(2)}) collective-permute-start(bf16[1,256,256]{2,1,0:T(8,128)(2,1)S(1)} %collective-permute-done.4.refs_5_), channel_id=1, source_target_pairs={{0,1},{1,0},{2,3},{3,2},{4,5},{5,4},{6,7},{7,6},{8,9},{9,8},{10,11... | collective-permute-start | bytes 393224 | tf_op jit(solution)/shard_map/ppermute | solution.py:104
  19.3 6.3 %collective-permute-start.1 = (bf16[1,256,256]{2,1,0:T(8,128)(2,1)S(1)}, bf16[1,256,256]{2,1,0:T(8,128)(2,1)S(1)}, u32[]{:S(2)}, u32[]{:S(2)}) collective-permute-start(bf16[1,256,256]{2,1,0:T(8,128)(2,1)S(1)} %collective-permute-done.refs_1_), channel_id=1, source_target_pairs={{0,1},{1,0},{2,3},{3,2},{4,5},{5,4},{6,7},{7,6},{8,9},{9,8},{10,11... | collective-permute-start | bytes 393224 | tf_op jit(solution)/shard_map/ppermute | solution.py:104
  19.8 5.8 %collective-permute-start.11 = (bf16[1,256,256]{2,1,0:T(8,128)(2,1)S(1)}, bf16[1,256,256]{2,1,0:T(8,128)(2,1)S(1)}, u32[]{:S(2)}, u32[]{:S(2)}) collective-permute-start(bf16[1,256,256]{2,1,0:T(8,128)(2,1)S(1)} %collective-permute-done.10.refs_11_), channel_id=1, source_target_pairs={{0,1},{1,0},{2,3},{3,2},{4,5},{5,4},{6,7},{7,6},{8,9},{9,8},{10,11... | collective-permute-start | bytes 393224 | tf_op jit(solution)/shard_map/ppermute | solution.py:104
  23.4 2.2 %collective-permute-start.7 = (bf16[1,256,256]{2,1,0:T(8,128)(2,1)S(1)}, bf16[1,256,256]{2,1,0:T(8,128)(2,1)S(1)}, u32[]{:S(2)}, u32[]{:S(2)}) collective-permute-start(bf16[1,256,256]{2,1,0:T(8,128)(2,1)S(1)} %collective-permute-done.6.refs_7_), channel_id=1, source_target_pairs={{0,1},{1,0},{2,3},{3,2},{4,5},{5,4},{6,7},{7,6},{8,9},{9,8},{10,11... | collective-permute-start | bytes 393224 | tf_op jit(solution)/shard_map/ppermute | solution.py:104
  24.8 1.3 %collective-permute-start.3 = (bf16[1,256,256]{2,1,0:T(8,128)(2,1)S(1)}, bf16[1,256,256]{2,1,0:T(8,128)(2,1)S(1)}, u32[]{:S(2)}, u32[]{:S(2)}) collective-permute-start(bf16[1,256,256]{2,1,0:T(8,128)(2,1)S(1)} %collective-permute-done.2.refs_3_), channel_id=1, source_target_pairs={{0,1},{1,0},{2,3},{3,2},{4,5},{5,4},{6,7},{7,6},{8,9},{9,8},{10,11... | collective-permute-start | bytes 393224 | tf_op jit(solution)/shard_map/ppermute | solution.py:104
  26.1 1.0 %copy-start = (bf16[4,256,256]{2,1,0:T(8,128)(2,1)S(1)}, bf16[4,256,256]{2,1,0:T(8,128)(2,1)}, u32[]{:S(2)}) copy-start(bf16[4,256,256]{2,1,0:T(8,128)(2,1)} %refs_0_.1) | copy-start | bytes 1572868
  27.2 2.2 %copy-start.1 = (bf16[32,256,256]{2,1,0:T(8,128)(2,1)S(1)}, bf16[32,256,256]{2,1,0:T(8,128)(2,1)}, u32[]{:S(2)}) copy-start(bf16[32,256,256]{2,1,0:T(8,128)(2,1)} %refs_14_.1) | copy-start | bytes 12582916
  29.4 1.6 %copy-start.2 = (bf16[32,128,256]{2,1,0:T(8,128)(2,1)S(1)}, bf16[32,128,256]{2,1,0:T(8,128)(2,1)}, u32[]{:S(2)}) copy-start(bf16[32,128,256]{2,1,0:T(8,128)(2,1)} %refs_13_.1) | copy-start | bytes 6291460
  42.1 5.6 %collective-permute-start.12 = (bf16[4,128,128]{2,1,0:T(8,128)(2,1)S(1)}, bf16[4,128,128]{2,1,0:T(8,128)(2,1)S(1)}, u32[]{:S(2)}, u32[]{:S(2)}) collective-permute-start(bf16[4,128,128]{2,1,0:T(8,128)(2,1)S(1)} %get-tuple-element.8), channel_id=1, source_target_pairs={{0,2},{2,0},{1,3},{3,1},{4,6},{6,4},{5,7},{7,5},{8,10},{10,8},{9,1... | collective-permute-start | bytes 393224 | tf_op jit(solution)/shard_map/ppermute | solution.py:104

commit v2 on v0

v2 whole, which is shorter than its diff:
```python
import functools

import jax
import jax.numpy as jnp
from jax import lax
from jax.experimental import pallas as pl
from jax.experimental.pallas import tpu as pltpu
from jax.sharding import PartitionSpec as P

MIX_TERMS = 8
SUM_TERMS = 4
VMEM_BYTES = 24 * 1024 * 1024


def mix_kernel(left_ref, wave_ref, mixed_ref):
    terms, rows, width = left_ref.shape
    left = left_ref[...].reshape(terms * rows, width)
    for s in range(wave_ref.shape[0]):
        product = jnp.dot(left, wave_ref[s], preferred_element_type=jnp.float32)
        mixed_ref[:, s] = product.astype(jnp.bfloat16).reshape(terms, rows, width)


def mix(left_ops, wavefunction):
    k_dev, rows, width = left_ops.shape
    sec_dev = wavefunction.shape[0]
    return pl.pallas_call(
        mix_kernel,
        grid=(k_dev // MIX_TERMS,),
        out_shape=jax.ShapeDtypeStruct((k_dev, sec_dev, rows, width), jnp.bfloat16),
        in_specs=[
            pl.BlockSpec((MIX_TERMS, rows, width), lambda i: (i, 0, 0)),
            pl.BlockSpec(wavefunction.shape, lambda i: (0, 0, 0)),
        ],
        out_specs=pl.BlockSpec((MIX_TERMS, sec_dev, rows, width), lambda i: (i, 0, 0, 0)),
        compiler_params=pltpu.CompilerParams(vmem_limit_bytes=VMEM_BYTES),
        cost_estimate=pl.CostEstimate(
            flops=2 * k_dev * sec_dev * rows * width * width,
            bytes_accessed=2 * k_dev * rows * width * (1 + sec_dev),
            transcendentals=0,
        ),
    )(left_ops, wavefunction)


def sum_kernel(split, shift_ref, coef_ref, base_ref, side_ref, mixed_ref, right_ref, *refs):
    outs, total = refs[:-1], refs[-1]
    step = pl.program_id(0)
    terms, sec_dev, rows, width = mixed_ref.shape
    targets = total.shape[0]

    @pl.when(step == 0)
    def _():
        total[...] = jnp.zeros_like(total)

    for t in range(terms):
        k = step * terms + t
        product = lax.dot_general(
            mixed_ref[t].reshape(sec_dev * rows, width),
            right_ref[t],
            (((1,), (1,)), ((), ())),
            preferred_element_type=jnp.float32,
        )
        for s in range(sec_dev):
            target = lax.rem(base_ref[0] + s + targets - shift_ref[k], targets)
            total[target] += coef_ref[k, target] * product[s * rows : (s + 1) * rows]

    @pl.when(step == pl.num_programs(0) - 1)
    def _():
        if not split:
            outs[0][...] = total[...]
        else:
            groups = len(outs) // 2
            first = side_ref[0] == 0
            half = width // 2
            for g in range(groups):
                low = total[g * sec_dev : (g + 1) * sec_dev, :, :half]
                high = total[g * sec_dev : (g + 1) * sec_dev, :, half:]
                outs[g][...] = jnp.where(first, low, high)
                outs[groups + g][...] = jnp.where(first, high, low).astype(jnp.bfloat16)


def summed(shift, coef, base, side, mixed, right_ops, split):
    k_dev, sec_dev, rows, width = mixed.shape
    targets = coef.shape[1]
    if split:
        shape = (sec_dev, rows, width // 2)
        groups = targets // sec_dev
        outs = [jax.ShapeDtypeStruct(shape, jnp.float32)] * groups
        outs += [jax.ShapeDtypeStruct(shape, jnp.bfloat16)] * groups
    else:
        outs = [jax.ShapeDtypeStruct((targets, rows, width), jnp.float32)]
    return pl.pallas_call(
        functools.partial(sum_kernel, split),
        grid=(k_dev // SUM_TERMS,),
        out_shape=outs,
        in_specs=[pl.BlockSpec(memory_space=pltpu.SMEM)] * 4
        + [
            pl.BlockSpec((SUM_TERMS, sec_dev, rows, width), lambda i: (i, 0, 0, 0)),
            pl.BlockSpec((SUM_TERMS, width, width), lambda i: (i, 0, 0)),
        ],
        out_specs=[pl.BlockSpec(out.shape, lambda i: (0, 0, 0)) for out in outs],
        scratch_shapes=[pltpu.VMEM((targets, rows, width), jnp.float32)],
        compiler_params=pltpu.CompilerParams(
            vmem_limit_bytes=VMEM_BYTES + 3 * targets * rows * width * 4
        ),
        cost_estimate=pl.CostEstimate(
            flops=2 * k_dev * sec_dev * rows * width * width,
            bytes_accessed=2 * (mixed.size + right_ops.size),
            transcendentals=0,
        ),
    )(shift, coef, base, side, mixed, right_ops)


def shift_by(value, axis, distance):
    size = lax.axis_size(axis)
    return lax.ppermute(value, axis, [(i, (i + distance) % size) for i in range(size)])


def per_device(wavefunction, left_ops, right_ops, site_coef, coupled, sector_shift):
    sec_dev = wavefunction.shape[0]
    devices = lax.axis_size("sector")
    live = jnp.where(coupled > 0, site_coef, 0.0)
    shift = lax.rem(sector_shift, sec_dev * devices)
    side = jnp.reshape(lax.axis_index("op"), (1,)).astype(jnp.int32)
    me = lax.axis_index("sector")

    if lax.axis_size("op") == 2 and devices <= 4:
        coefs = [live] + [shift_by(live, "sector", -g) for g in range(1, devices)]
        mixed = mix(left_ops, wavefunction)
        coef = jnp.concatenate(coefs, axis=1)
        base = jnp.zeros((1,), jnp.int32)
        parts = summed(shift, coef, base, side, mixed, right_ops, True)
        mine, theirs = parts[:devices], parts[devices:]
        order = sorted(range(devices), key=lambda g: (g == 0, abs(2 * g - devices)))
        crossed = {g: shift_by(theirs[g], "op", 1) for g in order}
        sigma = mine[0] + crossed[0].astype(jnp.float32)
        for g in order[:-1]:
            both = (mine[g] + crossed[g].astype(jnp.float32)).astype(jnp.bfloat16)
            sigma = sigma + shift_by(both, "sector", g).astype(jnp.float32)
        return sigma

    coef = lax.all_gather(live, "sector", axis=1, tiled=True)
    mixed = mix(left_ops, wavefunction)
    base = jnp.reshape(me * sec_dev, (1,)).astype(jnp.int32)
    (total,) = summed(shift, coef, base, side, mixed, right_ops, False)
    total = lax.psum_scatter(total, "op", scatter_dimension=2, tiled=True)
    return lax.psum_scatter(total, "sector", scatter_dimension=0, tiled=True)


def solution(mesh):
    placed = (
        P(("groups", "sector"), None, None),
        P(("groups", "op"), "rep", None),
        P(("groups", "op"), None, None),
        P(("groups", "op"), "sector"),
        P(("groups", "op"), "sector"),
        P(("groups", "op")),
    )
    return jax.shard_map(
        per_device,
        mesh=mesh,
        in_specs=placed,
        out_specs=P(("groups", "sector"), "rep", "op"),
        check_vma=False,
    )
```

time: 159 us -> 49.7 us (0.31)
  waiting for transfers between devices: 76.8 us -> 11.7 us
  local copies, waits for them, and re-layouts: 48 us -> 12.3 us
  matrix products: 18.2 us -> 0 us
  starting transfers between devices: 0.04 us -> 14.7 us
  between operations: 13.4 us -> 0.06 us
  Pallas kernels: 0 us -> 8.3 us
    all_gather x1 -> x0, waiting for transfers between devices: 48.6 us -> none  [per_device(): everything = lax.all_gather(wavefunction, 'sector', axis=0, tiled=True)]
    gather x8 -> x0, local copies, waits for them, and re-layouts: 43.3 us -> none  [one_block(): source_blocks = jnp.take(everything, place, axis=0)]
    psum x1 -> x0, waiting for transfers between devices: 27.5 us -> none  [per_device(): summed = lax.psum(result, 'op')]
    dot_general x4 -> x0, matrix products: 18.2 us -> none  [one_block(): jnp.einsum('ksil,kml->ksim', mixed, right_part, preferred_element_type=jn...]
    ppermute x0 -> x10, starting transfers between devices: none -> 14.7 us  [shift_by(): lax.ppermute(value, axis, [(i, (i + distance) % size) for i in range(size)])]
    ppermute x0 -> x10, waiting for transfers between devices: none -> 11.7 us  [shift_by(): lax.ppermute(value, axis, [(i, (i + distance) % size) for i in range(size)])]
    unnamed x2 -> x11, local copies, waits for them, and re-layouts: 0.79 us -> 12.2 us
    pallas_call x0 -> x2, Pallas kernels: none -> 8.3 us  [the longest x1 5.44 us: summed(): pl.pallas_call(functools.partial(sum_kernel, split), grid=(k_dev // SUM_T...]
  transfers between devices with their start and end apart: 2 -> 10, of which waited for: 2 -> 6; matrix products, arithmetic and copies ran while one was open for 1% -> 2% of each run, Pallas kernels for 0% -> 6%
where the time goes in v2:
time: 49.7 us; the launch traced here: 49.3 us
  starting transfers between devices  14.7 us (30%)
  local copies, waits for them, and re-layouts  12.3 us (25%)
  waiting for transfers between devices  11.7 us (24%)
  Pallas kernels  8.3 us (17%)
  other arithmetic  2.33 us (5%)
    ppermute x10, starting transfers between devices, shift_by(): lax.ppermute(value, axis, [(i, (i + distance) % size) for i in range(size)])  14.7 us
    unnamed x11, local copies, waits for them, and re-layouts  12.2 us
    ppermute x10, waiting for transfers between devices, shift_by(): lax.ppermute(value, axis, [(i, (i + distance) % size) for i in range(size)])  11.7 us
    pallas_call x1, Pallas kernels, summed(): pl.pallas_call(functools.partial(sum_kernel, split), grid=(k_dev // SUM_T...  5.44 us
    pallas_call x1, Pallas kernels, mix(): pl.pallas_call(mix_kernel, grid=(k_dev // MIX_TERMS,), out_shape=jax.Shap...  2.87 us
  transfers between devices with their start and end apart: 10, of which 6 were waited for; matrix products, arithmetic and copies ran while one was open for 2% of the time, Pallas kernels for 6%

profile of v2, /device:TPU:0, one launch (start us, length us, event | category | flops | bytes accessed | tf_op | source)
XLA Modules:
  0.0 49.3 jit_solution(5836116644669637827)
XLA Ops:
  0.0 0.7 %broadcast_compare_fusion = pred[32,4]{0,1:T(4,128)(4,1)S(1)} fusion(s32[32,4]{0,1:T(4,128)} %param.10), kind=kLoop, calls=%fused_computation.8 | loop fusion | flops 128 | bytes 640 | tf_op jit(solution)/shard_map/gt | solution.py:121
  0.7 0.1 copy.10
  0.8 0.8 %copy.11 = f32[32,4]{1,0:T(8,128)S(1)} copy(f32[32,4]{0,1:T(4,128)} %param.9) | data formatting | bytes 1024 | tf_op args[3]
  1.6 3.0 %collective-permute-start.2 = (f32[32,4]{1,0:T(8,128)S(1)}, f32[32,4]{1,0:T(8,128)S(1)}, u32[]{:S(2)}, u32[]{:S(2)}) collective-permute-start(f32[32,4]{1,0:T(8,128)S(1)} %broadcast_select_fusion), channel_id=1, source_target_pairs={{0,4},{4,8},{8,12},{12,0},{1,5},{5,9},{9,13},{13,1},{2,6},{6,10},{... | collective-permute-start | bytes 1544 | tf_op jit(solution)/shard_map/ppermute | solution.py:115
  4.6 2.6 %collective-permute-start.1 = (f32[32,4]{1,0:T(8,128)S(1)}, f32[32,4]{1,0:T(8,128)S(1)}, u32[]{:S(2)}, u32[]{:S(2)}) collective-permute-start(f32[32,4]{1,0:T(8,128)S(1)} %broadcast_select_fusion), channel_id=1, source_target_pairs={{0,8},{4,12},{8,0},{12,4},{1,9},{5,13},{9,1},{13,5},{2,10},{6,14},... | collective-permute-start | bytes 1544 | tf_op jit(solution)/shard_map/ppermute | solution.py:115
  7.2 1.3 %collective-permute-start = (f32[32,4]{1,0:T(8,128)S(1)}, f32[32,4]{1,0:T(8,128)S(1)}, u32[]{:S(2)}, u32[]{:S(2)}) collective-permute-start(f32[32,4]{1,0:T(8,128)S(1)} %broadcast_select_fusion), channel_id=1, source_target_pairs={{0,12},{4,0},{8,4},{12,8},{1,13},{5,1},{9,5},{13,9},{2,14},{6,2},{... | collective-permute-start | bytes 1544 | tf_op jit(solution)/shard_map/ppermute | solution.py:115
  8.6 0.7 %compare_select_fusion.shift_ref = s32[32]{0:T(128)S(1)} fusion(s32[32]{0:T(128)} %param.11), kind=kLoop, calls=%fused_computation.6 | loop fusion | flops 192 | bytes 256 | tf_op jit(solution)/shard_map/rem | solution.py:122
  9.2 1.6 %copy-done.3 = bf16[32,128,256]{2,1,0:T(8,128)(2,1)S(1)} copy-done((bf16[32,128,256]{2,1,0:T(8,128)(2,1)S(1)}, bf16[32,128,256]{2,1,0:T(8,128)(2,1)}, u32[]{:S(2)}) %copy-start.3) | copy-done | bytes 2097176
  10.8 1.0 %copy-done.4 = bf16[4,256,256]{2,1,0:T(8,128)(2,1)S(1)} copy-done((bf16[4,256,256]{2,1,0:T(8,128)(2,1)S(1)}, bf16[4,256,256]{2,1,0:T(8,128)(2,1)}, u32[]{:S(2)}) %copy-start.4) | copy-done | bytes 524312
  11.8 2.9 %shard_map.64.mixed_ref = bf16[32,4,128,256]{3,2,1,0:T(8,128)(2,1)S(1)} custom-call(bf16[32,128,256]{2,1,0:T(8,128)(2,1)S(1)} %copy-done.3, bf16[4,256,256]{2,1,0:T(8,128)(2,1)S(1)} %copy-done.4), custom_call_target="tpu_custom_call" | custom-call | flops 2147483648 | bytes 10485760 | tf_op jit(solution)/shard_map/pallas_call | solution.py:26
  14.7 3.2 %copy-done = bf16[32,4,128,256]{3,2,1,0:T(8,128)(2,1)} copy-done((bf16[32,4,128,256]{3,2,1,0:T(8,128)(2,1)}, bf16[32,4,128,256]{3,2,1,0:T(8,128)(2,1)S(1)}, u32[]{:S(2)}) %copy-start) | copy-done | bytes 8388632
  17.9 0.0 collective-permute-done.2
  17.9 0.0 collective-permute-done.1
  17.9 0.1 pad_maximum_fusion.coef_ref
  18.0 3.4 %copy-done.1 = bf16[32,4,128,256]{3,2,1,0:T(8,128)(2,1)S(1)} copy-done((bf16[32,4,128,256]{3,2,1,0:T(8,128)(2,1)S(1)}, bf16[32,4,128,256]{3,2,1,0:T(8,128)(2,1)}, u32[]{:S(2)}) %copy-start.1) | copy-done | bytes 8388632
  21.4 2.2 %copy-done.2 = bf16[32,256,256]{2,1,0:T(8,128)(2,1)S(1)} copy-done((bf16[32,256,256]{2,1,0:T(8,128)(2,1)S(1)}, bf16[32,256,256]{2,1,0:T(8,128)(2,1)}, u32[]{:S(2)}) %copy-start.2) | copy-done | bytes 4194328
  23.6 5.4 %shard_map.65 = (f32[4,128,128]{2,1,0:T(8,128)S(1)}, f32[4,128,128]{2,1,0:T(8,128)S(1)}, f32[4,128,128]{2,1,0:T(8,128)S(1)}, f32[4,128,128]{2,1,0:T(8,128)S(1)},...) custom-call(s32[32]{0:T(128)S(1)} %compare_select_fusion.shift_ref, ...), custom_call_target="tpu_custom_call" | custom-call | flops 2147483648 | bytes 12582912 | tf_op jit(solution)/shard_map/pallas_call | solution.py:91
  29.1 1.6 %collective-permute-start.4 = (bf16[4,128,128]{2,1,0:T(8,128)(2,1)S(1)}, bf16[4,128,128]{2,1,0:T(8,128)(2,1)S(1)}, u32[]{:S(2)}, u32[]{:S(2)}) collective-permute-start(bf16[4,128,128]{2,1,0:T(8,128)(2,1)S(1)} %get-tuple-element.16), channel_id=1, source_target_pairs={{0,2},{2,0},{1,3},{3,1},{4,6},{6,4},{5,7},{7,5},{8,10},{10,8},{9,1... | collective-permute-start | bytes 393224 | tf_op jit(solution)/shard_map/ppermute | solution.py:115
  30.6 0.5 %collective-permute-start.3 = (bf16[4,128,128]{2,1,0:T(8,128)(2,1)S(1)}, bf16[4,128,128]{2,1,0:T(8,128)(2,1)S(1)}, u32[]{:S(2)}, u32[]{:S(2)}) collective-permute-start(bf16[4,128,128]{2,1,0:T(8,128)(2,1)S(1)} %get-tuple-element.14), channel_id=1, source_target_pairs={{0,2},{2,0},{1,3},{3,1},{4,6},{6,4},{5,7},{7,5},{8,10},{10,8},{9,1... | collective-permute-start | bytes 393224 | tf_op jit(solution)/shard_map/ppermute | solution.py:115
  31.1 1.5 %collective-permute-start.6 = (bf16[4,128,128]{2,1,0:T(8,128)(2,1)S(1)}, bf16[4,128,128]{2,1,0:T(8,128)(2,1)S(1)}, u32[]{:S(2)}, u32[]{:S(2)}) collective-permute-start(bf16[4,128,128]{2,1,0:T(8,128)(2,1)S(1)} %get-tuple-element.18), channel_id=1, source_target_pairs={{0,2},{2,0},{1,3},{3,1},{4,6},{6,4},{5,7},{7,5},{8,10},{10,8},{9,1... | collective-permute-start | bytes 393224 | tf_op jit(solution)/shard_map/ppermute | solution.py:115
  32.6 0.5 %collective-permute-start.8 = (bf16[4,128,128]{2,1,0:T(8,128)(2,1)S(1)}, bf16[4,128,128]{2,1,0:T(8,128)(2,1)S(1)}, u32[]{:S(2)}, u32[]{:S(2)}) collective-permute-start(bf16[4,128,128]{2,1,0:T(8,128)(2,1)S(1)} %get-tuple-element.20), channel_id=1, source_target_pairs={{0,2},{2,0},{1,3},{3,1},{4,6},{6,4},{5,7},{7,5},{8,10},{10,8},{9,1... | collective-permute-start | bytes 393224 | tf_op jit(solution)/shard_map/ppermute | solution.py:115
  33.2 2.4 %collective-permute-done.4 = bf16[4,128,128]{2,1,0:T(8,128)(2,1)S(1)} collective-permute-done((bf16[4,128,128]{2,1,0:T(8,128)(2,1)S(1)}, bf16[4,128,128]{2,1,0:T(8,128)(2,1)S(1)}, u32[]{:S(2)}, u32[]{:S(2)}) %collective-permute-start.4) | collective-permute-done | bytes 131104 | tf_op jit(solution)/shard_map/ppermute | solution.py:115
  35.6 0.3 collective-permute-start.5
  35.9 4.7 %collective-permute-done.6 = bf16[4,128,128]{2,1,0:T(8,128)(2,1)S(1)} collective-permute-done((bf16[4,128,128]{2,1,0:T(8,128)(2,1)S(1)}, bf16[4,128,128]{2,1,0:T(8,128)(2,1)S(1)}, u32[]{:S(2)}, u32[]{:S(2)}) %collective-permute-start.6) | collective-permute-done | bytes 131104 | tf_op jit(solution)/shard_map/ppermute | solution.py:115
  40.6 0.7 %collective-permute-start.7 = (bf16[4,128,128]{2,1,0:T(8,128)(2,1)S(1)}, bf16[4,128,128]{2,1,0:T(8,128)(2,1)S(1)}, u32[]{:S(2)}, u32[]{:S(2)}) collective-permute-start(bf16[4,128,128]{2,1,0:T(8,128)(2,1)S(1)} %add_convert_fusion.1), channel_id=1, source_target_pairs={{0,4},{4,8},{8,12},{12,0},{1,5},{5,9},{9,13},{13,1},{2,6},{6,10},{... | collective-permute-start | bytes 393224 | tf_op jit(solution)/shard_map/ppermute | solution.py:115
  41.3 0.6 %collective-permute-done.8 = bf16[4,128,128]{2,1,0:T(8,128)(2,1)S(1)} collective-permute-done((bf16[4,128,128]{2,1,0:T(8,128)(2,1)S(1)}, bf16[4,128,128]{2,1,0:T(8,128)(2,1)S(1)}, u32[]{:S(2)}, u32[]{:S(2)}) %collective-permute-start.8) | collective-permute-done | bytes 131104 | tf_op jit(solution)/shard_map/ppermute | solution.py:115
  42.0 2.6 %collective-permute-start.9 = (bf16[4,128,128]{2,1,0:T(8,128)(2,1)S(1)}, bf16[4,128,128]{2,1,0:T(8,128)(2,1)S(1)}, u32[]{:S(2)}, u32[]{:S(2)}) collective-permute-start(bf16[4,128,128]{2,1,0:T(8,128)(2,1)S(1)} %add_convert_fusion), channel_id=1, source_target_pairs={{0,12},{4,0},{8,4},{12,8},{1,13},{5,1},{9,5},{13,9},{2,14},{6,2},{... | collective-permute-start | bytes 393224 | tf_op jit(solution)/shard_map/ppermute | solution.py:115
  44.6 0.0 collective-permute-done.3
  44.6 1.0 %collective-permute-done.5 = bf16[4,128,128]{2,1,0:T(8,128)(2,1)S(1)} collective-permute-done((bf16[4,128,128]{2,1,0:T(8,128)(2,1)S(1)}, bf16[4,128,128]{2,1,0:T(8,128)(2,1)S(1)}, u32[]{:S(2)}, u32[]{:S(2)}) %collective-permute-start.5) | collective-permute-done | bytes 131104 | tf_op jit(solution)/shard_map/ppermute | solution.py:115
  45.5 2.0 %collective-permute-done.7 = bf16[4,128,128]{2,1,0:T(8,128)(2,1)S(1)} collective-permute-done((bf16[4,128,128]{2,1,0:T(8,128)(2,1)S(1)}, bf16[4,128,128]{2,1,0:T(8,128)(2,1)S(1)}, u32[]{:S(2)}, u32[]{:S(2)}) %collective-permute-start.7) | collective-permute-done | bytes 131104 | tf_op jit(solution)/shard_map/ppermute | solution.py:115
  47.6 1.0 %collective-permute-done.9 = bf16[4,128,128]{2,1,0:T(8,128)(2,1)S(1)} collective-permute-done((bf16[4,128,128]{2,1,0:T(8,128)(2,1)S(1)}, bf16[4,128,128]{2,1,0:T(8,128)(2,1)S(1)}, u32[]{:S(2)}, u32[]{:S(2)}) %collective-permute-start.9) | collective-permute-done | bytes 131104 | tf_op jit(solution)/shard_map/ppermute | solution.py:115
  48.6 0.8 %convert_add_fusion = f32[4,128,128]{2,1,0:T(8,128)} fusion(bf16[4,128,128]{2,1,0:T(8,128)(2,1)S(1)} %collective-permute-done.9, bf16[4,128,128]{2,1,0:T(8,128)(2,1)S(1)} %collective-permute-done.7, bf16[4,128,128]{2,1,0:T(8,128)(2,1)S(1)} %collective-permute-done.5, f32[4,128,128]{2,1,0:T(8,128)S(1)} %get-tuple-element.13, ...), kind=kLoop, calls=%fused_computation | loop fusion | flops 524288 | bytes 1048576 | tf_op jit(solution)/shard_map/add | solution.py:138
  (10 shorter events, 0.1 us)
Async XLA Ops:
  1.6 16.4 %collective-permute-start.2 = (f32[32,4]{1,0:T(8,128)S(1)}, f32[32,4]{1,0:T(8,128)S(1)}, u32[]{:S(2)}, u32[]{:S(2)}) collective-permute-start(f32[32,4]{1,0:T(8,128)S(1)} %broadcast_select_fusion), channel_id=1, source_target_pairs={{0,4},{4,8},{8,12},{12,0},{1,5},{5,9},{9,13},{13,1},{2,6},{6,10},{... | collective-permute-start | bytes 1544 | tf_op jit(solution)/shard_map/ppermute | solution.py:115
  4.6 13.3 %collective-permute-start.1 = (f32[32,4]{1,0:T(8,128)S(1)}, f32[32,4]{1,0:T(8,128)S(1)}, u32[]{:S(2)}, u32[]{:S(2)}) collective-permute-start(f32[32,4]{1,0:T(8,128)S(1)} %broadcast_select_fusion), channel_id=1, source_target_pairs={{0,8},{4,12},{8,0},{12,4},{1,9},{5,13},{9,1},{13,5},{2,10},{6,14},... | collective-permute-start | bytes 1544 | tf_op jit(solution)/shard_map/ppermute | solution.py:115
  7.2 10.7 %collective-permute-start = (f32[32,4]{1,0:T(8,128)S(1)}, f32[32,4]{1,0:T(8,128)S(1)}, u32[]{:S(2)}, u32[]{:S(2)}) collective-permute-start(f32[32,4]{1,0:T(8,128)S(1)} %broadcast_select_fusion), channel_id=1, source_target_pairs={{0,12},{4,0},{8,4},{12,8},{1,13},{5,1},{9,5},{13,9},{2,14},{6,2},{... | collective-permute-start | bytes 1544 | tf_op jit(solution)/shard_map/ppermute | solution.py:115
  9.2 1.6 %copy-start.3 = (bf16[32,128,256]{2,1,0:T(8,128)(2,1)S(1)}, bf16[32,128,256]{2,1,0:T(8,128)(2,1)}, u32[]{:S(2)}) copy-start(bf16[32,128,256]{2,1,0:T(8,128)(2,1)} %left_ref.1) | copy-start | bytes 6291460
  10.8 1.0 %copy-start.4 = (bf16[4,256,256]{2,1,0:T(8,128)(2,1)S(1)}, bf16[4,256,256]{2,1,0:T(8,128)(2,1)}, u32[]{:S(2)}) copy-start(bf16[4,256,256]{2,1,0:T(8,128)(2,1)} %wave_ref.1) | copy-start | bytes 1572868
  14.7 3.2 %copy-start = (bf16[32,4,128,256]{3,2,1,0:T(8,128)(2,1)}, bf16[32,4,128,256]{3,2,1,0:T(8,128)(2,1)S(1)}, u32[]{:S(2)}) copy-start(bf16[32,4,128,256]{3,2,1,0:T(8,128)(2,1)S(1)} %shard_map.64.mixed_ref) | copy-start | bytes 25165828
  18.0 3.4 %copy-start.1 = (bf16[32,4,128,256]{3,2,1,0:T(8,128)(2,1)S(1)}, bf16[32,4,128,256]{3,2,1,0:T(8,128)(2,1)}, u32[]{:S(2)}) copy-start(bf16[32,4,128,256]{3,2,1,0:T(8,128)(2,1)} %copy-done) | copy-start | bytes 25165828
  21.4 2.2 %copy-start.2 = (bf16[32,256,256]{2,1,0:T(8,128)(2,1)S(1)}, bf16[32,256,256]{2,1,0:T(8,128)(2,1)}, u32[]{:S(2)}) copy-start(bf16[32,256,256]{2,1,0:T(8,128)(2,1)} %right_ref.1) | copy-start | bytes 12582916
  29.1 6.5 %collective-permute-start.4 = (bf16[4,128,128]{2,1,0:T(8,128)(2,1)S(1)}, bf16[4,128,128]{2,1,0:T(8,128)(2,1)S(1)}, u32[]{:S(2)}, u32[]{:S(2)}) collective-permute-start(bf16[4,128,128]{2,1,0:T(8,128)(2,1)S(1)} %get-tuple-element.16), channel_id=1, source_target_pairs={{0,2},{2,0},{1,3},{3,1},{4,6},{6,4},{5,7},{7,5},{8,10},{10,8},{9,1... | collective-permute-start | bytes 393224 | tf_op jit(solution)/shard_map/ppermute | solution.py:115
  30.6 13.9 %collective-permute-start.3 = (bf16[4,128,128]{2,1,0:T(8,128)(2,1)S(1)}, bf16[4,128,128]{2,1,0:T(8,128)(2,1)S(1)}, u32[]{:S(2)}, u32[]{:S(2)}) collective-permute-start(bf16[4,128,128]{2,1,0:T(8,128)(2,1)S(1)} %get-tuple-element.14), channel_id=1, source_target_pairs={{0,2},{2,0},{1,3},{3,1},{4,6},{6,4},{5,7},{7,5},{8,10},{10,8},{9,1... | collective-permute-start | bytes 393224 | tf_op jit(solution)/shard_map/ppermute | solution.py:115
  31.1 9.4 %collective-permute-start.6 = (bf16[4,128,128]{2,1,0:T(8,128)(2,1)S(1)}, bf16[4,128,128]{2,1,0:T(8,128)(2,1)S(1)}, u32[]{:S(2)}, u32[]{:S(2)}) collective-permute-start(bf16[4,128,128]{2,1,0:T(8,128)(2,1)S(1)} %get-tuple-element.18), channel_id=1, source_target_pairs={{0,2},{2,0},{1,3},{3,1},{4,6},{6,4},{5,7},{7,5},{8,10},{10,8},{9,1... | collective-permute-start | bytes 393224 | tf_op jit(solution)/shard_map/ppermute | solution.py:115
  32.6 9.3 %collective-permute-start.8 = (bf16[4,128,128]{2,1,0:T(8,128)(2,1)S(1)}, bf16[4,128,128]{2,1,0:T(8,128)(2,1)S(1)}, u32[]{:S(2)}, u32[]{:S(2)}) collective-permute-start(bf16[4,128,128]{2,1,0:T(8,128)(2,1)S(1)} %get-tuple-element.20), channel_id=1, source_target_pairs={{0,2},{2,0},{1,3},{3,1},{4,6},{6,4},{5,7},{7,5},{8,10},{10,8},{9,1... | collective-permute-start | bytes 393224 | tf_op jit(solution)/shard_map/ppermute | solution.py:115
  35.6 9.9 %collective-permute-start.5 = (bf16[4,128,128]{2,1,0:T(8,128)(2,1)S(1)}, bf16[4,128,128]{2,1,0:T(8,128)(2,1)S(1)}, u32[]{:S(2)}, u32[]{:S(2)}) collective-permute-start(bf16[4,128,128]{2,1,0:T(8,128)(2,1)S(1)} %add_convert_fusion.2), channel_id=1, source_target_pairs={{0,8},{4,12},{8,0},{12,4},{1,9},{5,13},{9,1},{13,5},{2,10},{6,14},... | collective-permute-start | bytes 393224 | tf_op jit(solution)/shard_map/ppermute | solution.py:115
  40.6 7.0 %collective-permute-start.7 = (bf16[4,128,128]{2,1,0:T(8,128)(2,1)S(1)}, bf16[4,128,128]{2,1,0:T(8,128)(2,1)S(1)}, u32[]{:S(2)}, u32[]{:S(2)}) collective-permute-start(bf16[4,128,128]{2,1,0:T(8,128)(2,1)S(1)} %add_convert_fusion.1), channel_id=1, source_target_pairs={{0,4},{4,8},{8,12},{12,0},{1,5},{5,9},{9,13},{13,1},{2,6},{6,10},{... | collective-permute-start | bytes 393224 | tf_op jit(solution)/shard_map/ppermute | solution.py:115
  42.0 6.6 %collective-permute-start.9 = (bf16[4,128,128]{2,1,0:T(8,128)(2,1)S(1)}, bf16[4,128,128]{2,1,0:T(8,128)(2,1)S(1)}, u32[]{:S(2)}, u32[]{:S(2)}) collective-permute-start(bf16[4,128,128]{2,1,0:T(8,128)(2,1)S(1)} %add_convert_fusion), channel_id=1, source_target_pairs={{0,12},{4,0},{8,4},{12,8},{1,13},{5,1},{9,5},{13,9},{2,14},{6,2},{... | collective-permute-start | bytes 393224 | tf_op jit(solution)/shard_map/ppermute | solution.py:115

commit v3 on v0

v3 whole, which is shorter than its diff:
```python
import functools

import jax
import jax.numpy as jnp
from jax import lax
from jax.experimental import pallas as pl
from jax.experimental.pallas import tpu as pltpu
from jax.sharding import PartitionSpec as P

MIX_TERMS = 8
SUM_TERMS = 4
MIB = 1024 * 1024


def mix_kernel(split, side_ref, wave_ref, left_ref, right_ref, mixed_ref, held_ref, wave, left, sems):
    sec_dev = wave.shape[0]
    terms, rows, width = left.shape
    chunks = terms // MIX_TERMS

    def left_copy(c):
        part = pl.ds(c * MIX_TERMS, MIX_TERMS)
        return pltpu.make_async_copy(left_ref.at[part], left.at[part], sems.at[3 + c])

    wave_copy = pltpu.make_async_copy(wave_ref, wave, sems.at[0])
    wave_copy.start()
    for c in range(chunks):
        left_copy(c).start()
    if split:
        half = width // 2
        mine = pl.multiple_of(side_ref[0] * half, half)
        theirs = pl.multiple_of((1 - side_ref[0]) * half, half)
        right_copies = [
            pltpu.make_async_copy(
                right_ref.at[:, pl.ds(theirs, half)], held_ref.at[:, pl.ds(0, half)], sems.at[1]
            ),
            pltpu.make_async_copy(
                right_ref.at[:, pl.ds(mine, half)], held_ref.at[:, pl.ds(half, half)], sems.at[2]
            ),
        ]
    else:
        right_copies = [pltpu.make_async_copy(right_ref, held_ref, sems.at[1])]
    for copy in right_copies:
        copy.start()
    wave_copy.wait()

    @pl.loop(0, chunks)
    def _(c):
        left_copy(c).wait()
        part = pl.ds(c * MIX_TERMS, MIX_TERMS)
        rows_in = left[part].reshape(MIX_TERMS * rows, width)
        for s in range(sec_dev):
            product = jnp.dot(rows_in, wave[s], preferred_element_type=jnp.float32)
            mixed_ref[part, s] = product.astype(jnp.bfloat16).reshape(MIX_TERMS, rows, width)

    for copy in right_copies:
        copy.wait()


def mix(side, wavefunction, left_ops, right_ops, split):
    k_dev, rows, width = left_ops.shape
    sec_dev = wavefunction.shape[0]
    return pl.pallas_call(
        functools.partial(mix_kernel, split),
        out_shape=[
            pltpu.VMEM((k_dev, sec_dev, rows, width), jnp.bfloat16),
            pltpu.VMEM(right_ops.shape, jnp.bfloat16),
        ],
        in_specs=[pl.BlockSpec(memory_space=pltpu.SMEM)] + [pl.BlockSpec(memory_space=pltpu.HBM)] * 3,
        out_specs=[pl.BlockSpec(memory_space=pltpu.VMEM)] * 2,
        scratch_shapes=[
            pltpu.VMEM(wavefunction.shape, jnp.bfloat16),
            pltpu.VMEM(left_ops.shape, jnp.bfloat16),
            pltpu.SemaphoreType.DMA((3 + k_dev // MIX_TERMS,)),
        ],
        compiler_params=pltpu.CompilerParams(vmem_limit_bytes=24 * MIB),
        cost_estimate=pl.CostEstimate(
            flops=2 * k_dev * sec_dev * rows * width * width,
            bytes_accessed=2 * (left_ops.size + right_ops.size),
            transcendentals=0,
        ),
    )(
        side,
        *(pltpu.with_memory_space_constraint(x, pltpu.HBM) for x in (wavefunction, left_ops, right_ops)),
    )


def sum_kernel(split, base_ref, shift_ref, coef_ref, mixed_ref, held_ref, *refs):
    terms, sec_dev, rows, width = mixed_ref.shape
    targets = coef_ref.shape[0]
    half = width // 2
    mine = refs[0]
    mine[...] = jnp.zeros_like(mine)
    if split:
        theirs, total = refs[1:-1], refs[-1]
        total[...] = jnp.zeros_like(total)

    @pl.loop(0, terms // SUM_TERMS)
    def _(step):
        for t in range(SUM_TERMS):
            k = step * SUM_TERMS + t
            product = lax.dot_general(
                mixed_ref[k].reshape(sec_dev * rows, width),
                held_ref[k],
                (((1,), (1,)), ((), ())),
                preferred_element_type=jnp.float32,
            )
            for s in range(sec_dev):
                target = lax.rem(base_ref[0] + s + targets - shift_ref[k], targets)
                scaled = coef_ref[target, k] * product[s * rows : (s + 1) * rows]
                if split:
                    total[target] += scaled[:, :half]
                    mine[target] += scaled[:, half:]
                else:
                    mine[target] += scaled

    if split:
        for g, out in enumerate(theirs):
            out[...] = total[g * sec_dev : (g + 1) * sec_dev].astype(jnp.bfloat16)


def summed(base, shift, coef, mixed, held, split):
    k_dev, sec_dev, rows, width = mixed.shape
    targets = coef.shape[0]
    if split:
        out_shape = [pltpu.VMEM((targets, rows, width // 2), jnp.float32)]
        out_shape += [pltpu.VMEM((sec_dev, rows, width // 2), jnp.bfloat16)] * (targets // sec_dev)
        scratch = [pltpu.VMEM((targets, rows, width // 2), jnp.float32)]
    else:
        out_shape = [pltpu.VMEM((targets, rows, width), jnp.float32)]
        scratch = []
    return pl.pallas_call(
        functools.partial(sum_kernel, split),
        out_shape=out_shape,
        in_specs=[pl.BlockSpec(memory_space=pltpu.SMEM)] * 3
        + [pl.BlockSpec(memory_space=pltpu.VMEM)] * 2,
        out_specs=[pl.BlockSpec(memory_space=pltpu.VMEM)] * len(out_shape),
        scratch_shapes=scratch,
        compiler_params=pltpu.CompilerParams(vmem_limit_bytes=24 * MIB),
        cost_estimate=pl.CostEstimate(
            flops=2 * k_dev * sec_dev * rows * width * width,
            bytes_accessed=2 * (mixed.size + held.size),
            transcendentals=0,
        ),
    )(
        base,
        shift,
        coef,
        pltpu.with_memory_space_constraint(mixed, pltpu.VMEM),
        pltpu.with_memory_space_constraint(held, pltpu.VMEM),
    )


def shift_by(value, axis, distance):
    size = lax.axis_size(axis)
    return lax.ppermute(value, axis, [(i, (i + distance) % size) for i in range(size)])


def after(value, other):
    return lax.optimization_barrier((value, other))[0]


def per_device(wavefunction, left_ops, right_ops, site_coef, coupled, sector_shift):
    sec_dev = wavefunction.shape[0]
    devices = lax.axis_size("sector")
    live = jnp.where(coupled.T > 0, site_coef.T, 0.0)
    shift = lax.rem(sector_shift, sec_dev * devices)
    side = jnp.reshape(lax.axis_index("op"), (1,)).astype(jnp.int32)
    me = lax.axis_index("sector")

    if lax.axis_size("op") == 2 and devices <= 4:
        coefs = [live] + [shift_by(live, "sector", -g) for g in range(1, devices)]
        mixed, held = mix(side, wavefunction, left_ops, right_ops, True)
        base = jnp.zeros((1,), jnp.int32)
        mine, *theirs = summed(base, shift, jnp.concatenate(coefs, axis=0), mixed, held, True)
        mine = [mine[g * sec_dev : (g + 1) * sec_dev] for g in range(devices)]
        order = sorted(range(1, devices), key=lambda g: abs(2 * g - devices))
        crossed = {g: shift_by(theirs[g], "op", 1) for g in order}
        arrived, both = [], None
        for g in order:
            other = crossed[g] if both is None else after(crossed[g], both)
            both = (mine[g] + other.astype(jnp.float32)).astype(jnp.bfloat16)
            if not arrived:
                theirs[0] = after(theirs[0], both)
            arrived.append(shift_by(both, "sector", g))
        sigma = mine[0] + shift_by(theirs[0], "op", 1).astype(jnp.float32)
        for other in arrived:
            sigma = sigma + other.astype(jnp.float32)
        return sigma

    coef = lax.all_gather(live, "sector", axis=0, tiled=True)
    mixed, held = mix(side, wavefunction, left_ops, right_ops, False)
    base = jnp.reshape(me * sec_dev, (1,)).astype(jnp.int32)
    (total,) = summed(base, shift, coef, mixed, held, False)
    total = lax.psum_scatter(total, "op", scatter_dimension=2, tiled=True)
    return lax.psum_scatter(total, "sector", scatter_dimension=0, tiled=True)


def solution(mesh):
    placed = (
        P(("groups", "sector"), None, None),
        P(("groups", "op"), "rep", None),
        P(("groups", "op"), None, None),
        P(("groups", "op"), "sector"),
        P(("groups", "op"), "sector"),
        P(("groups", "op")),
    )
    return jax.shard_map(
        per_device,
        mesh=mesh,
        in_specs=placed,
        out_specs=P(("groups", "sector"), "rep", "op"),
        check_vma=False,
    )
```

time: 159 us -> 36.5 us (0.23)
  waiting for transfers between devices: 76.8 us -> 9.84 us
  local copies, waits for them, and re-layouts: 48 us -> 0 us
  matrix products: 18.2 us -> 0 us
  starting transfers between devices: 0.04 us -> 15 us
  between operations: 13.4 us -> 0.07 us
  Pallas kernels: 0 us -> 9.19 us
    all_gather x1 -> x0, waiting for transfers between devices: 48.6 us -> none  [per_device(): everything = lax.all_gather(wavefunction, 'sector', axis=0, tiled=True)]
    gather x8 -> x0, local copies, waits for them, and re-layouts: 43.3 us -> none  [one_block(): source_blocks = jnp.take(everything, place, axis=0)]
    psum x1 -> x0, waiting for transfers between devices: 27.5 us -> none  [per_device(): summed = lax.psum(result, 'op')]
    dot_general x4 -> x0, matrix products: 18.2 us -> none  [one_block(): jnp.einsum('ksil,kml->ksim', mixed, right_part, preferred_element_type=jn...]
    ppermute x0 -> x10, starting transfers between devices: none -> 15 us  [shift_by(): lax.ppermute(value, axis, [(i, (i + distance) % size) for i in range(size)])]
    ppermute x0 -> x10, waiting for transfers between devices: none -> 9.84 us  [shift_by(): lax.ppermute(value, axis, [(i, (i + distance) % size) for i in range(size)])]
    pallas_call x0 -> x2, Pallas kernels: none -> 9.19 us  [the longest x1 5.08 us: summed(): pl.pallas_call(functools.partial(sum_kernel, split), out_shape=out_shape,...]
    dynamic_slice x5 -> x0, local copies, waits for them, and re-layouts: 1.69 us -> none  [the longest x1 1.67 us: per_device(): lax.dynamic_slice_in_dim(summed, lax.axis_index('op') * columns, columns, 2)]
  transfers between devices with their start and end apart: 2 -> 10, of which waited for: 2 -> 5; matrix products, arithmetic and copies ran while one was open for 1% -> 2% of each run, Pallas kernels for 0% -> 11%
where the time goes in v3:
time: 36.5 us; the launch traced here: 36.3 us
  starting transfers between devices  15 us (41%)
  waiting for transfers between devices  9.84 us (27%)
  Pallas kernels  9.19 us (25%)
  other arithmetic  2.26 us (6%)
    ppermute x10, starting transfers between devices, shift_by(): lax.ppermute(value, axis, [(i, (i + distance) % size) for i in range(size)])  15 us
    ppermute x10, waiting for transfers between devices, shift_by(): lax.ppermute(value, axis, [(i, (i + distance) % size) for i in range(size)])  9.84 us
    pallas_call x1, Pallas kernels, summed(): pl.pallas_call(functools.partial(sum_kernel, split), out_shape=out_shape,...  5.08 us
    pallas_call x1, Pallas kernels, mix(): pl.pallas_call(functools.partial(mix_kernel, split), out_shape=[pltpu.VME...  4.11 us
    add x1, other arithmetic, per_device(): sigma = sigma + other.astype(jnp.float32)  0.78 us
  transfers between devices with their start and end apart: 10, of which 5 were waited for; matrix products, arithmetic and copies ran while one was open for 2% of the time, Pallas kernels for 11%

profile of v3, /device:TPU:0, one launch (start us, length us, event | category | flops | bytes accessed | tf_op | source)
XLA Modules:
  0.0 36.3 jit_solution(17618921651392373495)
XLA Ops:
  0.0 0.7 %select_bitcast_fusion = f32[4,32]{1,0:T(4,128)S(1)} fusion(f32[32,4]{0,1:T(4,128)} %param.9, s32[32,4]{0,1:T(4,128)} %param.10), kind=kLoop, calls=%fused_computation.7 | loop fusion | flops 256 | bytes 1536 | tf_op jit(solution)/shard_map/jit(_where)/select_n | solution.py:165
  0.7 3.0 %collective-permute-start.2 = (f32[4,32]{1,0:T(4,128)S(1)}, f32[4,32]{1,0:T(4,128)S(1)}, u32[]{:S(2)}, u32[]{:S(2)}) collective-permute-start(f32[4,32]{1,0:T(4,128)S(1)} %select_bitcast_fusion), channel_id=1, source_target_pairs={{0,4},{4,8},{8,12},{12,0},{1,5},{5,9},{9,13},{13,1},{2,6},{6,10},{... | collective-permute-start | bytes 1544 | tf_op jit(solution)/shard_map/ppermute | solution.py:155
  3.7 2.6 %collective-permute-start.1 = (f32[4,32]{1,0:T(4,128)S(1)}, f32[4,32]{1,0:T(4,128)S(1)}, u32[]{:S(2)}, u32[]{:S(2)}) collective-permute-start(f32[4,32]{1,0:T(4,128)S(1)} %select_bitcast_fusion), channel_id=1, source_target_pairs={{0,8},{4,12},{8,0},{12,4},{1,9},{5,13},{9,1},{13,5},{2,10},{6,14},... | collective-permute-start | bytes 1544 | tf_op jit(solution)/shard_map/ppermute | solution.py:155
  6.3 1.3 %collective-permute-start = (f32[4,32]{1,0:T(4,128)S(1)}, f32[4,32]{1,0:T(4,128)S(1)}, u32[]{:S(2)}, u32[]{:S(2)}) collective-permute-start(f32[4,32]{1,0:T(4,128)S(1)} %select_bitcast_fusion), channel_id=1, source_target_pairs={{0,12},{4,0},{8,4},{12,8},{1,13},{5,1},{9,5},{13,9},{2,14},{6,2},{... | collective-permute-start | bytes 1544 | tf_op jit(solution)/shard_map/ppermute | solution.py:155
  7.7 0.7 %compare_select_fusion.shift_ref = s32[32]{0:T(128)S(1)} fusion(s32[32]{0:T(128)} %param.11), kind=kLoop, calls=%fused_computation.5 | loop fusion | flops 192 | bytes 256 | tf_op jit(solution)/shard_map/rem | solution.py:166
  8.3 4.1 %shard_map.64 = (bf16[32,4,128,256]{3,2,1,0:T(8,128)(2,1)S(1)}, bf16[32,256,256]{2,1,0:T(8,128)(2,1)S(1)}) custom-call(s32[1]{0:T(128)} %bitcast.1.side_ref, bf16[4,256,256]{2,1,0:T(8,128)(2,1)} %wave_ref.1, bf16[32,128,256]{2,1,0:T(8,128)(2,1)} %left_ref.1, bf16[32,256,256]{2,1,0:T(8,128)(2,1)} %right_ref.1), custom_call_target="tpu_custom_call" | custom-call | flops 2147483648 | bytes 6291456 | tf_op jit(solution)/shard_map/pallas_call | solution.py:62
  12.4 0.0 collective-permute-done.2
  12.5 0.0 collective-permute-done.1
  12.5 0.0 collective-permute-done
  12.5 5.1 %shard_map.65 = (f32[16,128,128]{2,1,0:T(8,128)S(1)}, bf16[4,128,128]{2,1,0:T(8,128)(2,1)S(1)}, bf16[4,128,128]{2,1,0:T(8,128)(2,1)S(1)}, bf16[4,128,128]{2,1,0:T(8,128)(2,1)S(1)}, bf16[4,128,128]{2,1,0:T(8,128)(2,1)S(1)}) custom-call(s32[1]{0:T(128)} %constant.4.clone.1.base_ref, s32[32]{0:T(128)S(1)} %compare_select_fusion.shift_ref, ...), custom_call_target="tpu_custom_call" | custom-call | flops 2147483648 | bytes 12582912 | tf_op jit(solution)/shard_map/pallas_call | solution.py:131
  17.6 1.6 %collective-permute-start.3 = (bf16[4,128,128]{2,1,0:T(8,128)(2,1)S(1)}, bf16[4,128,128]{2,1,0:T(8,128)(2,1)S(1)}, u32[]{:S(2)}, u32[]{:S(2)}) collective-permute-start(bf16[4,128,128]{2,1,0:T(8,128)(2,1)S(1)} %get-tuple-element.19), channel_id=1, source_target_pairs={{0,2},{2,0},{1,3},{3,1},{4,6},{6,4},{5,7},{7,5},{8,10},{10,8},{9,1... | collective-permute-start | bytes 393224 | tf_op jit(solution)/shard_map/ppermute | solution.py:155
  19.1 0.5 %collective-permute-start.6 = (bf16[4,128,128]{2,1,0:T(8,128)(2,1)S(1)}, bf16[4,128,128]{2,1,0:T(8,128)(2,1)S(1)}, u32[]{:S(2)}, u32[]{:S(2)}) collective-permute-start(bf16[4,128,128]{2,1,0:T(8,128)(2,1)S(1)} %get-tuple-element.21), channel_id=1, source_target_pairs={{0,2},{2,0},{1,3},{3,1},{4,6},{6,4},{5,7},{7,5},{8,10},{10,8},{9,1... | collective-permute-start | bytes 393224 | tf_op jit(solution)/shard_map/ppermute | solution.py:155
  19.7 1.5 %collective-permute-start.8 = (bf16[4,128,128]{2,1,0:T(8,128)(2,1)S(1)}, bf16[4,128,128]{2,1,0:T(8,128)(2,1)S(1)}, u32[]{:S(2)}, u32[]{:S(2)}) collective-permute-start(bf16[4,128,128]{2,1,0:T(8,128)(2,1)S(1)} %get-tuple-element.23), channel_id=1, source_target_pairs={{0,2},{2,0},{1,3},{3,1},{4,6},{6,4},{5,7},{7,5},{8,10},{10,8},{9,1... | collective-permute-start | bytes 393224 | tf_op jit(solution)/shard_map/ppermute | solution.py:155
  21.2 2.9 %collective-permute-done.3 = bf16[4,128,128]{2,1,0:T(8,128)(2,1)S(1)} collective-permute-done((bf16[4,128,128]{2,1,0:T(8,128)(2,1)S(1)}, bf16[4,128,128]{2,1,0:T(8,128)(2,1)S(1)}, u32[]{:S(2)}, u32[]{:S(2)}) %collective-permute-start.3) | collective-permute-done | bytes 131104 | tf_op jit(solution)/shard_map/ppermute | solution.py:155
  24.1 0.2 collective-permute-start.5
  24.3 1.7 %collective-permute-start.4 = (bf16[4,128,128]{2,1,0:T(8,128)(2,1)S(1)}, bf16[4,128,128]{2,1,0:T(8,128)(2,1)S(1)}, u32[]{:S(2)}, u32[]{:S(2)}) collective-permute-start(bf16[4,128,128]{2,1,0:T(8,128)(2,1)S(1)} %get-tuple-element.20), channel_id=1, source_target_pairs={{0,2},{2,0},{1,3},{3,1},{4,6},{6,4},{5,7},{7,5},{8,10},{10,8},{9,1... | collective-permute-start | bytes 393224 | tf_op jit(solution)/shard_map/ppermute | solution.py:155
  26.0 0.9 %collective-permute-done.6 = bf16[4,128,128]{2,1,0:T(8,128)(2,1)S(1)} collective-permute-done((bf16[4,128,128]{2,1,0:T(8,128)(2,1)S(1)}, bf16[4,128,128]{2,1,0:T(8,128)(2,1)S(1)}, u32[]{:S(2)}, u32[]{:S(2)}) %collective-permute-start.6) | collective-permute-done | bytes 131104 | tf_op jit(solution)/shard_map/ppermute | solution.py:155
  26.9 0.7 %collective-permute-start.7 = (bf16[4,128,128]{2,1,0:T(8,128)(2,1)S(1)}, bf16[4,128,128]{2,1,0:T(8,128)(2,1)S(1)}, u32[]{:S(2)}, u32[]{:S(2)}) collective-permute-start(bf16[4,128,128]{2,1,0:T(8,128)(2,1)S(1)} %add_convert_fusion.1), channel_id=1, source_target_pairs={{0,4},{4,8},{8,12},{12,0},{1,5},{5,9},{9,13},{13,1},{2,6},{6,10},{... | collective-permute-start | bytes 393224 | tf_op jit(solution)/shard_map/ppermute | solution.py:155
  27.7 1.4 %collective-permute-done.8 = bf16[4,128,128]{2,1,0:T(8,128)(2,1)S(1)} collective-permute-done((bf16[4,128,128]{2,1,0:T(8,128)(2,1)S(1)}, bf16[4,128,128]{2,1,0:T(8,128)(2,1)S(1)}, u32[]{:S(2)}, u32[]{:S(2)}) %collective-permute-start.8) | collective-permute-done | bytes 131104 | tf_op jit(solution)/shard_map/ppermute | solution.py:155
  29.1 1.8 %collective-permute-start.9 = (bf16[4,128,128]{2,1,0:T(8,128)(2,1)S(1)}, bf16[4,128,128]{2,1,0:T(8,128)(2,1)S(1)}, u32[]{:S(2)}, u32[]{:S(2)}) collective-permute-start(bf16[4,128,128]{2,1,0:T(8,128)(2,1)S(1)} %add_convert_fusion), channel_id=1, source_target_pairs={{0,12},{4,0},{8,4},{12,8},{1,13},{5,1},{9,5},{13,9},{2,14},{6,2},{... | collective-permute-start | bytes 393224 | tf_op jit(solution)/shard_map/ppermute | solution.py:155
  30.9 0.0 collective-permute-done.4
  30.9 3.5 %collective-permute-done.5 = bf16[4,128,128]{2,1,0:T(8,128)(2,1)S(1)} collective-permute-done((bf16[4,128,128]{2,1,0:T(8,128)(2,1)S(1)}, bf16[4,128,128]{2,1,0:T(8,128)(2,1)S(1)}, u32[]{:S(2)}, u32[]{:S(2)}) %collective-permute-start.5) | collective-permute-done | bytes 131104 | tf_op jit(solution)/shard_map/ppermute | solution.py:155
  34.4 0.0 collective-permute-done.7
  34.4 1.1 %collective-permute-done.9 = bf16[4,128,128]{2,1,0:T(8,128)(2,1)S(1)} collective-permute-done((bf16[4,128,128]{2,1,0:T(8,128)(2,1)S(1)}, bf16[4,128,128]{2,1,0:T(8,128)(2,1)S(1)}, u32[]{:S(2)}, u32[]{:S(2)}) %collective-permute-start.9) | collective-permute-done | bytes 131104 | tf_op jit(solution)/shard_map/ppermute | solution.py:155
  35.5 0.8 %convert_add_fusion = f32[4,128,128]{2,1,0:T(8,128)} fusion(bf16[4,128,128]{2,1,0:T(8,128)(2,1)S(1)} %collective-permute-done.9, bf16[4,128,128]{2,1,0:T(8,128)(2,1)S(1)} %collective-permute-done.7, bf16[4,128,128]{2,1,0:T(8,128)(2,1)S(1)} %collective-permute-done.5, bf16[4,128,128]{2,1,0:T(8,128)(2,1)S(1)} %collective-permute-done.4, ...), kind=kLoop, calls=%fused_computation | loop fusion | flops 524288 | bytes 1048576 | tf_op jit(solution)/shard_map/add | solution.py:187
  (4 shorter events, 0.1 us)
Async XLA Ops:
  0.7 11.7 %collective-permute-start.2 = (f32[4,32]{1,0:T(4,128)S(1)}, f32[4,32]{1,0:T(4,128)S(1)}, u32[]{:S(2)}, u32[]{:S(2)}) collective-permute-start(f32[4,32]{1,0:T(4,128)S(1)} %select_bitcast_fusion), channel_id=1, source_target_pairs={{0,4},{4,8},{8,12},{12,0},{1,5},{5,9},{9,13},{13,1},{2,6},{6,10},{... | collective-permute-start | bytes 1544 | tf_op jit(solution)/shard_map/ppermute | solution.py:155
  3.7 8.7 %collective-permute-start.1 = (f32[4,32]{1,0:T(4,128)S(1)}, f32[4,32]{1,0:T(4,128)S(1)}, u32[]{:S(2)}, u32[]{:S(2)}) collective-permute-start(f32[4,32]{1,0:T(4,128)S(1)} %select_bitcast_fusion), channel_id=1, source_target_pairs={{0,8},{4,12},{8,0},{12,4},{1,9},{5,13},{9,1},{13,5},{2,10},{6,14},... | collective-permute-start | bytes 1544 | tf_op jit(solution)/shard_map/ppermute | solution.py:155
  6.3 6.2 %collective-permute-start = (f32[4,32]{1,0:T(4,128)S(1)}, f32[4,32]{1,0:T(4,128)S(1)}, u32[]{:S(2)}, u32[]{:S(2)}) collective-permute-start(f32[4,32]{1,0:T(4,128)S(1)} %select_bitcast_fusion), channel_id=1, source_target_pairs={{0,12},{4,0},{8,4},{12,8},{1,13},{5,1},{9,5},{13,9},{2,14},{6,2},{... | collective-permute-start | bytes 1544 | tf_op jit(solution)/shard_map/ppermute | solution.py:155
  17.6 6.5 %collective-permute-start.3 = (bf16[4,128,128]{2,1,0:T(8,128)(2,1)S(1)}, bf16[4,128,128]{2,1,0:T(8,128)(2,1)S(1)}, u32[]{:S(2)}, u32[]{:S(2)}) collective-permute-start(bf16[4,128,128]{2,1,0:T(8,128)(2,1)S(1)} %get-tuple-element.19), channel_id=1, source_target_pairs={{0,2},{2,0},{1,3},{3,1},{4,6},{6,4},{5,7},{7,5},{8,10},{10,8},{9,1... | collective-permute-start | bytes 393224 | tf_op jit(solution)/shard_map/ppermute | solution.py:155
  19.1 7.8 %collective-permute-start.6 = (bf16[4,128,128]{2,1,0:T(8,128)(2,1)S(1)}, bf16[4,128,128]{2,1,0:T(8,128)(2,1)S(1)}, u32[]{:S(2)}, u32[]{:S(2)}) collective-permute-start(bf16[4,128,128]{2,1,0:T(8,128)(2,1)S(1)} %get-tuple-element.21), channel_id=1, source_target_pairs={{0,2},{2,0},{1,3},{3,1},{4,6},{6,4},{5,7},{7,5},{8,10},{10,8},{9,1... | collective-permute-start | bytes 393224 | tf_op jit(solution)/shard_map/ppermute | solution.py:155
  19.7 9.4 %collective-permute-start.8 = (bf16[4,128,128]{2,1,0:T(8,128)(2,1)S(1)}, bf16[4,128,128]{2,1,0:T(8,128)(2,1)S(1)}, u32[]{:S(2)}, u32[]{:S(2)}) collective-permute-start(bf16[4,128,128]{2,1,0:T(8,128)(2,1)S(1)} %get-tuple-element.23), channel_id=1, source_target_pairs={{0,2},{2,0},{1,3},{3,1},{4,6},{6,4},{5,7},{7,5},{8,10},{10,8},{9,1... | collective-permute-start | bytes 393224 | tf_op jit(solution)/shard_map/ppermute | solution.py:155
  24.1 10.3 %collective-permute-start.5 = (bf16[4,128,128]{2,1,0:T(8,128)(2,1)S(1)}, bf16[4,128,128]{2,1,0:T(8,128)(2,1)S(1)}, u32[]{:S(2)}, u32[]{:S(2)}) collective-permute-start(bf16[4,128,128]{2,1,0:T(8,128)(2,1)S(1)} %add_convert_fusion.2), channel_id=1, source_target_pairs={{0,8},{4,12},{8,0},{12,4},{1,9},{5,13},{9,1},{13,5},{2,10},{6,14},... | collective-permute-start | bytes 393224 | tf_op jit(solution)/shard_map/ppermute | solution.py:155
  24.3 6.6 %collective-permute-start.4 = (bf16[4,128,128]{2,1,0:T(8,128)(2,1)S(1)}, bf16[4,128,128]{2,1,0:T(8,128)(2,1)S(1)}, u32[]{:S(2)}, u32[]{:S(2)}) collective-permute-start(bf16[4,128,128]{2,1,0:T(8,128)(2,1)S(1)} %get-tuple-element.20), channel_id=1, source_target_pairs={{0,2},{2,0},{1,3},{3,1},{4,6},{6,4},{5,7},{7,5},{8,10},{10,8},{9,1... | collective-permute-start | bytes 393224 | tf_op jit(solution)/shard_map/ppermute | solution.py:155
  26.9 7.5 %collective-permute-start.7 = (bf16[4,128,128]{2,1,0:T(8,128)(2,1)S(1)}, bf16[4,128,128]{2,1,0:T(8,128)(2,1)S(1)}, u32[]{:S(2)}, u32[]{:S(2)}) collective-permute-start(bf16[4,128,128]{2,1,0:T(8,128)(2,1)S(1)} %add_convert_fusion.1), channel_id=1, source_target_pairs={{0,4},{4,8},{8,12},{12,0},{1,5},{5,9},{9,13},{13,1},{2,6},{6,10},{... | collective-permute-start | bytes 393224 | tf_op jit(solution)/shard_map/ppermute | solution.py:155
  29.1 6.4 %collective-permute-start.9 = (bf16[4,128,128]{2,1,0:T(8,128)(2,1)S(1)}, bf16[4,128,128]{2,1,0:T(8,128)(2,1)S(1)}, u32[]{:S(2)}, u32[]{:S(2)}) collective-permute-start(bf16[4,128,128]{2,1,0:T(8,128)(2,1)S(1)} %add_convert_fusion), channel_id=1, source_target_pairs={{0,12},{4,0},{8,4},{12,8},{1,13},{5,1},{9,5},{13,9},{2,14},{6,2},{... | collective-permute-start | bytes 393224 | tf_op jit(solution)/shard_map/ppermute | solution.py:155

commit v4 on v3

v4 whole, which is shorter than its diff:
```python
import functools

import jax
import jax.numpy as jnp
from jax import lax
from jax.experimental import pallas as pl
from jax.experimental.pallas import tpu as pltpu
from jax.sharding import PartitionSpec as P

MIX_TERMS = 8
PAIRS_A_STEP = 8
FIELD = 256
MIB = 1024 * 1024


def wrapped(value, size):
    if size & (size - 1) == 0:
        return value & (size - 1)
    return lax.rem(value + size, size)


def divided(value, size):
    if size & (size - 1) == 0:
        return value >> (size.bit_length() - 1)
    return lax.div(value, size)


def list_words(pairs):
    return pairs + 2 * PAIRS_A_STEP


def slot_of(target, batch, sec_dev):
    if len(batch) == 1:
        return divided(target, sec_dev) == batch[0], wrapped(target, sec_dev)
    if batch == list(range(len(batch))):
        return divided(target, sec_dev) < len(batch), target
    held, place = False, 0
    for at, group in enumerate(batch):
        here = divided(target, sec_dev) == group
        held = held | here
        place = jnp.where(here, at * sec_dev, place)
    return held, place + wrapped(target, sec_dev)


def mix_kernel(split, batches, targets, side_ref, shift_ref, wave_ref, left_ref, right_ref, *refs):
    mixed_ref, held_ref, lists, wave, left, sems = refs
    sec_dev = wave.shape[0]
    terms, rows, width = left.shape
    chunks = terms // MIX_TERMS
    words = list_words(terms * sec_dev)

    def left_copy(c):
        part = pl.ds(c * MIX_TERMS, MIX_TERMS)
        return pltpu.make_async_copy(left_ref.at[part], left.at[part], sems.at[3 + c])

    wave_copy = pltpu.make_async_copy(wave_ref, wave, sems.at[0])
    wave_copy.start()
    for c in range(chunks):
        left_copy(c).start()
    if split:
        half = width // 2
        mine = pl.multiple_of(side_ref[0] * half, half)
        theirs = pl.multiple_of((1 - side_ref[0]) * half, half)
        right_copies = [
            pltpu.make_async_copy(
                right_ref.at[:, pl.ds(theirs, half)], held_ref.at[:, pl.ds(0, half)], sems.at[1]
            ),
            pltpu.make_async_copy(
                right_ref.at[:, pl.ds(mine, half)], held_ref.at[:, pl.ds(half, half)], sems.at[2]
            ),
        ]
    else:
        right_copies = [pltpu.make_async_copy(right_ref, held_ref, sems.at[1])]
    for copy in right_copies:
        copy.start()

    def add_term(k, counts):
        counts = list(counts)
        for s in range(sec_dev):
            target = wrapped(s - shift_ref[k], targets)
            for b, batch in enumerate(batches):
                held, slot = slot_of(target, batch, sec_dev)
                lists[b * words + counts[b]] = ((k * sec_dev + s) * FIELD + slot) * FIELD + target
                counts[b] = counts[b] + jnp.where(held, 1, 0)
        return tuple(counts)

    counts = lax.fori_loop(0, terms, add_term, (0,) * len(batches))
    for b, count in enumerate(counts):
        lists[(b + 1) * words - 1] = count
    wave_copy.wait()

    @pl.loop(0, chunks)
    def _(c):
        left_copy(c).wait()
        part = pl.ds(c * MIX_TERMS, MIX_TERMS)
        rows_in = left[part].reshape(MIX_TERMS * rows, width)
        for s in range(sec_dev):
            product = jnp.dot(rows_in, wave[s], preferred_element_type=jnp.float32)
            mixed_ref[part, s] = product.astype(jnp.bfloat16).reshape(MIX_TERMS, rows, width)

    for copy in right_copies:
        copy.wait()


def mix(side, shift, wavefunction, left_ops, right_ops, batches, targets, split):
    k_dev, rows, width = left_ops.shape
    sec_dev = wavefunction.shape[0]
    arrays = (shift, wavefunction, left_ops, right_ops)
    return pl.pallas_call(
        functools.partial(mix_kernel, split, batches, targets),
        out_shape=[
            pltpu.VMEM((k_dev, sec_dev, rows, width), jnp.bfloat16),
            pltpu.VMEM(right_ops.shape, jnp.bfloat16),
            jax.ShapeDtypeStruct((len(batches) * list_words(k_dev * sec_dev),), jnp.int32),
        ],
        in_specs=[pl.BlockSpec(memory_space=pltpu.SMEM)] * 2
        + [pl.BlockSpec(memory_space=pltpu.HBM)] * 3,
        out_specs=[pl.BlockSpec(memory_space=pltpu.VMEM)] * 2
        + [pl.BlockSpec(memory_space=pltpu.SMEM)],
        scratch_shapes=[
            pltpu.VMEM(wavefunction.shape, jnp.bfloat16),
            pltpu.VMEM(left_ops.shape, jnp.bfloat16),
            pltpu.SemaphoreType.DMA((3 + k_dev // MIX_TERMS,)),
        ],
        compiler_params=pltpu.CompilerParams(vmem_limit_bytes=24 * MIB),
        cost_estimate=pl.CostEstimate(
            flops=2 * k_dev * sec_dev * rows * width * width,
            bytes_accessed=2 * (left_ops.size + right_ops.size),
            transcendentals=0,
        ),
    )(side, *(pltpu.with_memory_space_constraint(x, pltpu.HBM) for x in arrays))


def sum_kernel(split, number, coef_ref, lists_ref, mixed_ref, held_ref, *refs):
    pairs, weights = refs[-2:]
    terms, sec_dev, rows, width = mixed_ref.shape
    half = width // 2
    words = list_words(terms * sec_dev)
    start = number * words
    mine = refs[0]
    mine[...] = jnp.zeros_like(mine)
    if split:
        theirs, total = refs[1:-3], refs[-3]
        total[...] = jnp.zeros_like(total)

    def keep(i, kept):
        entry = lists_ref[start + i]
        k = divided(divided(entry, FIELD * FIELD), sec_dev)
        weight = coef_ref[wrapped(entry, FIELD), k]
        pairs[kept] = divided(entry, FIELD)
        weights[kept] = weight
        return kept + jnp.where(weight != 0.0, 1, 0)

    kept = lax.fori_loop(0, lists_ref[start + words - 1], keep, 0)
    for i in range(PAIRS_A_STEP):
        pairs[kept + i] = 0
        weights[kept + i] = 0.0

    @pl.loop(0, divided(kept + PAIRS_A_STEP - 1, PAIRS_A_STEP))
    def _(step):
        for i in range(PAIRS_A_STEP):
            pair = pairs[step * PAIRS_A_STEP + i]
            place = divided(pair, FIELD)
            slot = wrapped(pair, FIELD)
            k = divided(place, sec_dev)
            product = lax.dot_general(
                mixed_ref[k, wrapped(place, sec_dev)],
                held_ref[k],
                (((1,), (1,)), ((), ())),
                preferred_element_type=jnp.float32,
            )
            scaled = weights[step * PAIRS_A_STEP + i] * product
            if split:
                total[slot] += scaled[:, :half]
                mine[slot] += scaled[:, half:]
            else:
                mine[slot] += scaled

    if split:
        for g, out in enumerate(theirs):
            out[...] = total[g * sec_dev : (g + 1) * sec_dev].astype(jnp.bfloat16)


def summed(number, batch, coef, lists, mixed, held, split):
    k_dev, sec_dev, rows, width = mixed.shape
    words = list_words(k_dev * sec_dev)
    slots = len(batch) * sec_dev
    columns = width // 2 if split else width
    out_shape = [pltpu.VMEM((slots, rows, columns), jnp.float32)]
    scratch = [pltpu.SMEM((words,), jnp.int32), pltpu.SMEM((words,), jnp.float32)]
    if split:
        out_shape += [pltpu.VMEM((sec_dev, rows, columns), jnp.bfloat16)] * len(batch)
        scratch = [pltpu.VMEM((slots, rows, columns), jnp.float32)] + scratch
    return pl.pallas_call(
        functools.partial(sum_kernel, split, number),
        out_shape=out_shape,
        in_specs=[pl.BlockSpec(memory_space=pltpu.SMEM)] * 2
        + [pl.BlockSpec(memory_space=pltpu.VMEM)] * 2,
        out_specs=[pl.BlockSpec(memory_space=pltpu.VMEM)] * len(out_shape),
        scratch_shapes=scratch,
        compiler_params=pltpu.CompilerParams(vmem_limit_bytes=24 * MIB),
        cost_estimate=pl.CostEstimate(
            flops=2 * k_dev * slots * rows * width * width // 4,
            bytes_accessed=2 * (mixed.size + held.size),
            transcendentals=0,
        ),
    )(
        coef,
        lists,
        pltpu.with_memory_space_constraint(mixed, pltpu.VMEM),
        pltpu.with_memory_space_constraint(held, pltpu.VMEM),
    )


def shift_by(value, axis, distance):
    size = lax.axis_size(axis)
    return lax.ppermute(value, axis, [(i, (i + distance) % size) for i in range(size)])


def after(value, other):
    return lax.optimization_barrier((value, other))[0]


def per_device(wavefunction, left_ops, right_ops, site_coef, coupled, sector_shift):
    sec_dev = wavefunction.shape[0]
    devices = lax.axis_size("sector")
    live = jnp.where(coupled.T > 0, site_coef.T, 0.0)
    side = jnp.reshape(lax.axis_index("op"), (1,)).astype(jnp.int32)
    split = lax.axis_size("op") == 2 and devices <= 4

    if split:
        far, *near = sorted(range(1, devices), key=lambda g: abs(2 * g - devices))
        batches = [[far], near, [0]]
    else:
        batches = [list(range(devices))]
    targets = devices * sec_dev
    mixed, held, lists = mix(
        side, sector_shift, wavefunction, left_ops, right_ops, batches, targets, split
    )

    if split:
        coefs = [live] + [shift_by(live, "sector", -g) for g in range(1, devices)]
        coef = jnp.concatenate(coefs, axis=0)
        mine, crossed, arrived, both = {}, {}, [], None

        def pass_on(g):
            other = crossed[g] if both is None else after(crossed[g], both)
            summed_up = (mine[g] + other.astype(jnp.float32)).astype(jnp.bfloat16)
            arrived.append(shift_by(summed_up, "sector", g))
            return summed_up

        for number, batch in enumerate(batches):
            sums, *theirs = summed(number, batch, coef, lists, mixed, held, True)
            for at, g in enumerate(batch):
                mine[g] = sums[at * sec_dev : (at + 1) * sec_dev]
                crossed[g] = shift_by(theirs[at], "op", 1)
            coef = after(coef, sums)
            if number == 1:
                crossed[far] = after(crossed[far], sums)
                both = pass_on(far)
                coef = after(coef, both)
        for g in near:
            both = pass_on(g)
        sigma = mine[0] + crossed[0].astype(jnp.float32)
        for other in arrived:
            sigma = sigma + other.astype(jnp.float32)
        return sigma

    first = lax.axis_index("sector") * sec_dev
    coef = jnp.roll(lax.all_gather(live, "sector", axis=0, tiled=True), -first, axis=0)
    (total,) = summed(0, batches[0], coef, lists, mixed, held, False)
    total = jnp.roll(total, first, axis=0)
    total = lax.psum_scatter(total, "op", scatter_dimension=2, tiled=True)
    return lax.psum_scatter(total, "sector", scatter_dimension=0, tiled=True)


def solution(mesh):
    placed = (
        P(("groups", "sector"), None, None),
        P(("groups", "op"), "rep", None),
        P(("groups", "op"), None, None),
        P(("groups", "op"), "sector"),
        P(("groups", "op"), "sector"),
        P(("groups", "op")),
    )
    return jax.shard_map(
        per_device,
        mesh=mesh,
        in_specs=placed,
        out_specs=P(("groups", "sector"), "rep", "op"),
        check_vma=False,
    )
```

time: 36.5 us -> 37 us (1.014); the launches traced: 36.3 us -> 37.7 us
  Pallas kernels: 9.19 us -> 15.1 us
  starting transfers between devices: 15 us -> 12.8 us
  waiting for transfers between devices: 9.84 us -> 8.06 us
  other arithmetic: 2.26 us -> 1.6 us
    pallas_call x2 -> x4, Pallas kernels: 9.19 us -> 15.1 us  [the longest x3 9.5 us: summed(): pl.pallas_call(functools.partial(sum_kernel, split, number), out_shape=ou...]
    ppermute x10, starting transfers between devices: 15 us -> 12.8 us  [shift_by(): lax.ppermute(value, axis, [(i, (i + distance) % size) for i in range(size)])]
    ppermute x10, waiting for transfers between devices: 9.84 us -> 8.06 us  [shift_by(): lax.ppermute(value, axis, [(i, (i + distance) % size) for i in range(size)])]
    rem x1 -> x0, other arithmetic: 0.66 us -> none  [per_device(): shift = lax.rem(sector_shift, sec_dev * devices)]
  transfers between devices with their start and end apart: 10 -> 10, of which waited for: 5 -> 4; matrix products, arithmetic and copies ran while one was open for 2% -> 0% of each run, Pallas kernels for 11% -> 35%
where the time goes in v4:
time: 37 us; the launch traced here: 37.7 us
  Pallas kernels  15.1 us (41%)
  starting transfers between devices  12.8 us (35%)
  waiting for transfers between devices  8.06 us (22%)
  other arithmetic  1.6 us (4%)
    ppermute x10, starting transfers between devices, shift_by(): lax.ppermute(value, axis, [(i, (i + distance) % size) for i in range(size)])  12.8 us
    pallas_call x3, Pallas kernels, summed(): pl.pallas_call(functools.partial(sum_kernel, split, number), out_shape=ou...  9.5 us
    ppermute x10, waiting for transfers between devices, shift_by(): lax.ppermute(value, axis, [(i, (i + distance) % size) for i in range(size)])  8.06 us
    pallas_call x1, Pallas kernels, mix(): pl.pallas_call(functools.partial(mix_kernel, split, batches, targets), ou...  5.59 us
    add x1, other arithmetic, per_device(): sigma = sigma + other.astype(jnp.float32)  0.78 us
  transfers between devices with their start and end apart: 10, of which 4 were waited for; matrix products, arithmetic and copies ran while one was open for 0% of the time, Pallas kernels for 35%

profile of v4, /device:TPU:0, one launch (start us, length us, event | category | flops | bytes accessed | tf_op | source)
XLA Modules:
  0.0 37.7 jit_solution(13691461897464055862)
XLA Ops:
  0.0 0.7 %select_bitcast_fusion = f32[4,32]{1,0:T(4,128)S(1)} fusion(f32[32,4]{0,1:T(4,128)} %param.9, s32[32,4]{0,1:T(4,128)} %param.10), kind=kLoop, calls=%fused_computation.5 | loop fusion | flops 256 | bytes 1536 | tf_op jit(solution)/shard_map/jit(_where)/select_n | solution.py:227
  0.7 3.0 %collective-permute-start.2 = (f32[4,32]{1,0:T(4,128)S(1)}, f32[4,32]{1,0:T(4,128)S(1)}, u32[]{:S(2)}, u32[]{:S(2)}) collective-permute-start(f32[4,32]{1,0:T(4,128)S(1)} %select_bitcast_fusion), channel_id=1, source_target_pairs={{0,4},{4,8},{8,12},{12,0},{1,5},{5,9},{9,13},{13,1},{2,6},{6,10},{... | collective-permute-start | bytes 1544 | tf_op jit(solution)/shard_map/ppermute | solution.py:217
  3.7 2.6 %collective-permute-start.1 = (f32[4,32]{1,0:T(4,128)S(1)}, f32[4,32]{1,0:T(4,128)S(1)}, u32[]{:S(2)}, u32[]{:S(2)}) collective-permute-start(f32[4,32]{1,0:T(4,128)S(1)} %select_bitcast_fusion), channel_id=1, source_target_pairs={{0,8},{4,12},{8,0},{12,4},{1,9},{5,13},{9,1},{13,5},{2,10},{6,14},... | collective-permute-start | bytes 1544 | tf_op jit(solution)/shard_map/ppermute | solution.py:217
  6.3 1.3 %collective-permute-start = (f32[4,32]{1,0:T(4,128)S(1)}, f32[4,32]{1,0:T(4,128)S(1)}, u32[]{:S(2)}, u32[]{:S(2)}) collective-permute-start(f32[4,32]{1,0:T(4,128)S(1)} %select_bitcast_fusion), channel_id=1, source_target_pairs={{0,12},{4,0},{8,4},{12,8},{1,13},{5,1},{9,5},{13,9},{2,14},{6,2},{... | collective-permute-start | bytes 1544 | tf_op jit(solution)/shard_map/ppermute | solution.py:217
  7.7 5.6 %shard_map.64 = (bf16[32,4,128,256]{3,2,1,0:T(8,128)(2,1)S(1)}, bf16[32,256,256]{2,1,0:T(8,128)(2,1)S(1)}, s32[432]{0:T(512)S(1)}) custom-call(s32[1]{0:T(128)} %bitcast.1.side_ref, s32[32]{0:T(128)} %shift_ref.1, bf16[4,256,256]{2,1,0:T(8,128)(2,1)} %wave_ref.1, bf16[32,128,256]{2,1,0:T(8,128)(2,1)} %left_ref.1, bf16[32,256,256]{2,1,0:T(8,128)(2,1)} %right_ref.1), custom_call_target="tpu_custom_call" | custom-call | flops 2147483648 | bytes 6291456 | tf_op jit(solution)/shard_map/pallas_call | solution.py:109
  13.3 0.0 collective-permute-done.2
  13.3 0.0 collective-permute-done.1
  13.3 0.0 collective-permute-done
  13.3 2.0 %shard_map.65 = (f32[4,128,128]{2,1,0:T(8,128)S(1)}, bf16[4,128,128]{2,1,0:T(8,128)(2,1)S(1)}) custom-call(f32[16,32]{1,0:T(8,128)S(1)} %pad_maximum_fusion.coef_ref, s32[432]{0:T(512)S(1)} %get-tuple-element.21.lists_ref, bf16[32,4,128,256]{3,2,1,0:T(8,128)(2,1)S(1)} %get-tuple-element.22.mixed_ref, bf16[32,256,256]{2,1,0:T(8,128)(2,1)S(1)} %get-tuple-element.23.held_ref), custom_call_target="tpu_custom_call" | custom-call | flops 536870912 | bytes 12582912 | tf_op jit(solution)/shard_map/pallas_call | solution.py:194
  15.3 1.7 %collective-permute-start.3 = (bf16[4,128,128]{2,1,0:T(8,128)(2,1)S(1)}, bf16[4,128,128]{2,1,0:T(8,128)(2,1)S(1)}, u32[]{:S(2)}, u32[]{:S(2)}) collective-permute-start(bf16[4,128,128]{2,1,0:T(8,128)(2,1)S(1)} %get-tuple-element.28), channel_id=1, source_target_pairs={{0,2},{2,0},{1,3},{3,1},{4,6},{6,4},{5,7},{7,5},{8,10},{10,8},{9,1... | collective-permute-start | bytes 393224 | tf_op jit(solution)/shard_map/ppermute | solution.py:217
  17.0 5.3 %shard_map.66 = (f32[8,128,128]{2,1,0:T(8,128)S(1)}, bf16[4,128,128]{2,1,0:T(8,128)(2,1)S(1)}, bf16[4,128,128]{2,1,0:T(8,128)(2,1)S(1)}) custom-call(f32[16,32]{1,0:T(8,128)S(1)} %pad_maximum_fusion.coef_ref, s32[432]{0:T(512)S(1)} %get-tuple-element.21.lists_ref, bf16[32,4,128,256]{3,2,1,0:T(8,128)(2,1)S(1)} %get-tuple-element.22.mixed_ref, ...), custom_call_target="tpu_custom_call" | custom-call | flops 1073741824 | bytes 12582912 | tf_op jit(solution)/shard_map/pallas_call | solution.py:194
  22.3 0.1 collective-permute-start.6
  22.4 2.0 %collective-permute-start.8 = (bf16[4,128,128]{2,1,0:T(8,128)(2,1)S(1)}, bf16[4,128,128]{2,1,0:T(8,128)(2,1)S(1)}, u32[]{:S(2)}, u32[]{:S(2)}) collective-permute-start(bf16[4,128,128]{2,1,0:T(8,128)(2,1)S(1)} %get-tuple-element.35), channel_id=1, source_target_pairs={{0,2},{2,0},{1,3},{3,1},{4,6},{6,4},{5,7},{7,5},{8,10},{10,8},{9,1... | collective-permute-start | bytes 393224 | tf_op jit(solution)/shard_map/ppermute | solution.py:217
  24.4 0.0 collective-permute-done.3
  24.5 0.1 collective-permute-start.5
  24.5 2.2 %shard_map.67 = (f32[4,128,128]{2,1,0:T(8,128)S(1)}, bf16[4,128,128]{2,1,0:T(8,128)(2,1)S(1)}) custom-call(f32[16,32]{1,0:T(8,128)S(1)} %pad_maximum_fusion.coef_ref, s32[432]{0:T(512)S(1)} %get-tuple-element.21.lists_ref, bf16[32,4,128,256]{3,2,1,0:T(8,128)(2,1)S(1)} %get-tuple-element.22.mixed_ref, bf16[32,256,256]{2,1,0:T(8,128)(2,1)S(1)} %get-tuple-element.23.held_ref), custom_call_target="tpu_custom_call" | custom-call | flops 536870912 | bytes 12582912 | tf_op jit(solution)/shard_map/pallas_call | solution.py:194
  26.7 0.1 collective-permute-start.4
  26.9 1.3 %collective-permute-done.6 = bf16[4,128,128]{2,1,0:T(8,128)(2,1)S(1)} collective-permute-done((bf16[4,128,128]{2,1,0:T(8,128)(2,1)S(1)}, bf16[4,128,128]{2,1,0:T(8,128)(2,1)S(1)}, u32[]{:S(2)}, u32[]{:S(2)}) %collective-permute-start.6) | collective-permute-done | bytes 131104 | tf_op jit(solution)/shard_map/ppermute | solution.py:217
  28.2 0.4 %collective-permute-start.7 = (bf16[4,128,128]{2,1,0:T(8,128)(2,1)S(1)}, bf16[4,128,128]{2,1,0:T(8,128)(2,1)S(1)}, u32[]{:S(2)}, u32[]{:S(2)}) collective-permute-start(bf16[4,128,128]{2,1,0:T(8,128)(2,1)S(1)} %add_convert_fusion.1), channel_id=1, source_target_pairs={{0,4},{4,8},{8,12},{12,0},{1,5},{5,9},{9,13},{13,1},{2,6},{6,10},{... | collective-permute-start | bytes 393224 | tf_op jit(solution)/shard_map/ppermute | solution.py:217
  28.7 2.0 %collective-permute-done.8 = bf16[4,128,128]{2,1,0:T(8,128)(2,1)S(1)} collective-permute-done((bf16[4,128,128]{2,1,0:T(8,128)(2,1)S(1)}, bf16[4,128,128]{2,1,0:T(8,128)(2,1)S(1)}, u32[]{:S(2)}, u32[]{:S(2)}) %collective-permute-start.8) | collective-permute-done | bytes 131104 | tf_op jit(solution)/shard_map/ppermute | solution.py:217
  30.7 1.4 %collective-permute-start.9 = (bf16[4,128,128]{2,1,0:T(8,128)(2,1)S(1)}, bf16[4,128,128]{2,1,0:T(8,128)(2,1)S(1)}, u32[]{:S(2)}, u32[]{:S(2)}) collective-permute-start(bf16[4,128,128]{2,1,0:T(8,128)(2,1)S(1)} %add_convert_fusion), channel_id=1, source_target_pairs={{0,12},{4,0},{8,4},{12,8},{1,13},{5,1},{9,5},{13,9},{2,14},{6,2},{... | collective-permute-start | bytes 393224 | tf_op jit(solution)/shard_map/ppermute | solution.py:217
  32.2 0.0 collective-permute-done.4
  32.2 3.6 %collective-permute-done.5 = bf16[4,128,128]{2,1,0:T(8,128)(2,1)S(1)} collective-permute-done((bf16[4,128,128]{2,1,0:T(8,128)(2,1)S(1)}, bf16[4,128,128]{2,1,0:T(8,128)(2,1)S(1)}, u32[]{:S(2)}, u32[]{:S(2)}) %collective-permute-start.5) | collective-permute-done | bytes 131104 | tf_op jit(solution)/shard_map/ppermute | solution.py:217
  35.8 0.0 collective-permute-done.7
  35.8 1.1 %collective-permute-done.9 = bf16[4,128,128]{2,1,0:T(8,128)(2,1)S(1)} collective-permute-done((bf16[4,128,128]{2,1,0:T(8,128)(2,1)S(1)}, bf16[4,128,128]{2,1,0:T(8,128)(2,1)S(1)}, u32[]{:S(2)}, u32[]{:S(2)}) %collective-permute-start.9) | collective-permute-done | bytes 131104 | tf_op jit(solution)/shard_map/ppermute | solution.py:217
  36.9 0.8 %convert_add_fusion = f32[4,128,128]{2,1,0:T(8,128)} fusion(bf16[4,128,128]{2,1,0:T(8,128)(2,1)S(1)} %collective-permute-done.9, bf16[4,128,128]{2,1,0:T(8,128)(2,1)S(1)} %collective-permute-done.7, bf16[4,128,128]{2,1,0:T(8,128)(2,1)S(1)} %collective-permute-done.5, f32[4,128,128]{2,1,0:T(8,128)S(1)} %get-tuple-element.31, ...), kind=kLoop, calls=%fused_computation | loop fusion | flops 524288 | bytes 1048576 | tf_op jit(solution)/shard_map/add | solution.py:266
  (4 shorter events, 0.1 us)
Async XLA Ops:
  0.7 12.6 %collective-permute-start.2 = (f32[4,32]{1,0:T(4,128)S(1)}, f32[4,32]{1,0:T(4,128)S(1)}, u32[]{:S(2)}, u32[]{:S(2)}) collective-permute-start(f32[4,32]{1,0:T(4,128)S(1)} %select_bitcast_fusion), channel_id=1, source_target_pairs={{0,4},{4,8},{8,12},{12,0},{1,5},{5,9},{9,13},{13,1},{2,6},{6,10},{... | collective-permute-start | bytes 1544 | tf_op jit(solution)/shard_map/ppermute | solution.py:217
  3.7 9.5 %collective-permute-start.1 = (f32[4,32]{1,0:T(4,128)S(1)}, f32[4,32]{1,0:T(4,128)S(1)}, u32[]{:S(2)}, u32[]{:S(2)}) collective-permute-start(f32[4,32]{1,0:T(4,128)S(1)} %select_bitcast_fusion), channel_id=1, source_target_pairs={{0,8},{4,12},{8,0},{12,4},{1,9},{5,13},{9,1},{13,5},{2,10},{6,14},... | collective-permute-start | bytes 1544 | tf_op jit(solution)/shard_map/ppermute | solution.py:217
  6.3 7.0 %collective-permute-start = (f32[4,32]{1,0:T(4,128)S(1)}, f32[4,32]{1,0:T(4,128)S(1)}, u32[]{:S(2)}, u32[]{:S(2)}) collective-permute-start(f32[4,32]{1,0:T(4,128)S(1)} %select_bitcast_fusion), channel_id=1, source_target_pairs={{0,12},{4,0},{8,4},{12,8},{1,13},{5,1},{9,5},{13,9},{2,14},{6,2},{... | collective-permute-start | bytes 1544 | tf_op jit(solution)/shard_map/ppermute | solution.py:217
  15.3 9.1 %collective-permute-start.3 = (bf16[4,128,128]{2,1,0:T(8,128)(2,1)S(1)}, bf16[4,128,128]{2,1,0:T(8,128)(2,1)S(1)}, u32[]{:S(2)}, u32[]{:S(2)}) collective-permute-start(bf16[4,128,128]{2,1,0:T(8,128)(2,1)S(1)} %get-tuple-element.28), channel_id=1, source_target_pairs={{0,2},{2,0},{1,3},{3,1},{4,6},{6,4},{5,7},{7,5},{8,10},{10,8},{9,1... | collective-permute-start | bytes 393224 | tf_op jit(solution)/shard_map/ppermute | solution.py:217
  22.3 5.9 %collective-permute-start.6 = (bf16[4,128,128]{2,1,0:T(8,128)(2,1)S(1)}, bf16[4,128,128]{2,1,0:T(8,128)(2,1)S(1)}, u32[]{:S(2)}, u32[]{:S(2)}) collective-permute-start(bf16[4,128,128]{2,1,0:T(8,128)(2,1)S(1)} %get-tuple-element.33), channel_id=1, source_target_pairs={{0,2},{2,0},{1,3},{3,1},{4,6},{6,4},{5,7},{7,5},{8,10},{10,8},{9,1... | collective-permute-start | bytes 393224 | tf_op jit(solution)/shard_map/ppermute | solution.py:217
  22.4 8.3 %collective-permute-start.8 = (bf16[4,128,128]{2,1,0:T(8,128)(2,1)S(1)}, bf16[4,128,128]{2,1,0:T(8,128)(2,1)S(1)}, u32[]{:S(2)}, u32[]{:S(2)}) collective-permute-start(bf16[4,128,128]{2,1,0:T(8,128)(2,1)S(1)} %get-tuple-element.35), channel_id=1, source_target_pairs={{0,2},{2,0},{1,3},{3,1},{4,6},{6,4},{5,7},{7,5},{8,10},{10,8},{9,1... | collective-permute-start | bytes 393224 | tf_op jit(solution)/shard_map/ppermute | solution.py:217
  24.5 11.3 %collective-permute-start.5 = (bf16[4,128,128]{2,1,0:T(8,128)(2,1)S(1)}, bf16[4,128,128]{2,1,0:T(8,128)(2,1)S(1)}, u32[]{:S(2)}, u32[]{:S(2)}) collective-permute-start(bf16[4,128,128]{2,1,0:T(8,128)(2,1)S(1)} %add_convert_fusion.2), channel_id=1, source_target_pairs={{0,8},{4,12},{8,0},{12,4},{1,9},{5,13},{9,1},{13,5},{2,10},{6,14},... | collective-permute-start | bytes 393224 | tf_op jit(solution)/shard_map/ppermute | solution.py:217
  26.7 5.4 %collective-permute-start.4 = (bf16[4,128,128]{2,1,0:T(8,128)(2,1)S(1)}, bf16[4,128,128]{2,1,0:T(8,128)(2,1)S(1)}, u32[]{:S(2)}, u32[]{:S(2)}) collective-permute-start(bf16[4,128,128]{2,1,0:T(8,128)(2,1)S(1)} %get-tuple-element.32), channel_id=1, source_target_pairs={{0,2},{2,0},{1,3},{3,1},{4,6},{6,4},{5,7},{7,5},{8,10},{10,8},{9,1... | collective-permute-start | bytes 393224 | tf_op jit(solution)/shard_map/ppermute | solution.py:217
  28.2 7.6 %collective-permute-start.7 = (bf16[4,128,128]{2,1,0:T(8,128)(2,1)S(1)}, bf16[4,128,128]{2,1,0:T(8,128)(2,1)S(1)}, u32[]{:S(2)}, u32[]{:S(2)}) collective-permute-start(bf16[4,128,128]{2,1,0:T(8,128)(2,1)S(1)} %add_convert_fusion.1), channel_id=1, source_target_pairs={{0,4},{4,8},{8,12},{12,0},{1,5},{5,9},{9,13},{13,1},{2,6},{6,10},{... | collective-permute-start | bytes 393224 | tf_op jit(solution)/shard_map/ppermute | solution.py:217
  30.7 6.1 %collective-permute-start.9 = (bf16[4,128,128]{2,1,0:T(8,128)(2,1)S(1)}, bf16[4,128,128]{2,1,0:T(8,128)(2,1)S(1)}, u32[]{:S(2)}, u32[]{:S(2)}) collective-permute-start(bf16[4,128,128]{2,1,0:T(8,128)(2,1)S(1)} %add_convert_fusion), channel_id=1, source_target_pairs={{0,12},{4,0},{8,4},{12,8},{1,13},{5,1},{9,5},{13,9},{2,14},{6,2},{... | collective-permute-start | bytes 393224 | tf_op jit(solution)/shard_map/ppermute | solution.py:217

commit v5 on v0

v5 whole, which is shorter than its diff:
```python
import functools

import jax
import jax.numpy as jnp
from jax import lax
from jax.experimental import pallas as pl
from jax.experimental.pallas import tpu as pltpu
from jax.sharding import PartitionSpec as P

BLOCK_TERMS = 8
MIB = 1024 * 1024


def wrapped(value, size):
    if size & (size - 1) == 0:
        return value & (size - 1)
    return lax.rem(value + size, size)


def sigma_kernel(split, side_ref, shift_ref, coef_ref, wave_ref, left_ref, right_ref, *refs):
    wave, left, right, even, odd, wave_sem, left_sems, right_sems = refs[-8:]
    terms, rows, width = left.shape
    sec_dev = wave.shape[0]
    targets = coef_ref.shape[0]
    blocks = terms // BLOCK_TERMS
    half = width // 2
    mine = refs[0]

    def part(block):
        return pl.ds(block * BLOCK_TERMS, BLOCK_TERMS)

    def left_copy(block):
        return pltpu.make_async_copy(
            left_ref.at[part(block)], left.at[part(block)], left_sems.at[block]
        )

    def right_copies(block):
        if not split:
            source, target = right_ref.at[part(block)], right.at[part(block)]
            return [pltpu.make_async_copy(source, target, right_sems.at[0, block])]
        copies = []
        for at, side in enumerate((1 - side_ref[0], side_ref[0])):
            source = right_ref.at[part(block), pl.ds(pl.multiple_of(side * half, half), half)]
            target = right.at[part(block), pl.ds(at * half, half)]
            copies.append(pltpu.make_async_copy(source, target, right_sems.at[at, block]))
        return copies

    def first_product(block, mixed):
        rows_in = left[part(block)].reshape(BLOCK_TERMS * rows, width)
        for s in range(sec_dev):
            product = jnp.dot(rows_in, wave[s], preferred_element_type=jnp.float32)
            mixed[:, s] = product.astype(jnp.bfloat16).reshape(BLOCK_TERMS, rows, width)

    def second_product(block, mixed):
        for t in range(BLOCK_TERMS):
            k = block * BLOCK_TERMS + t
            product = lax.dot_general(
                mixed[t].reshape(sec_dev * rows, width),
                right[k],
                (((1,), (1,)), ((), ())),
                preferred_element_type=jnp.float32,
            )
            for s in range(sec_dev):
                target = wrapped(s - shift_ref[k], targets)
                scaled = coef_ref[target, k] * product[s * rows : (s + 1) * rows]
                if split:
                    total[target] += scaled[:, :half]
                    mine[target] += scaled[:, half:]
                else:
                    mine[target] += scaled

    wave_copy = pltpu.make_async_copy(wave_ref, wave, wave_sem)
    wave_copy.start()
    for block in range(blocks):
        left_copy(block).start()
        for copy in right_copies(block):
            copy.start()
    mine[...] = jnp.zeros_like(mine)
    if split:
        theirs, total = refs[1:-9], refs[-9]
        total[...] = jnp.zeros_like(total)
    wave_copy.wait()
    left_copy(0).wait()
    first_product(0, even)

    @pl.loop(0, blocks // 2)
    def _(step):
        block = 2 * step
        left_copy(block + 1).wait()
        for copy in right_copies(block):
            copy.wait()
        first_product(block + 1, odd)
        second_product(block, even)
        for copy in right_copies(block + 1):
            copy.wait()

        @pl.when(block + 2 < blocks)
        def _():
            left_copy(block + 2).wait()
            first_product(block + 2, even)

        second_product(block + 1, odd)

    if split:
        for g, out in enumerate(theirs):
            out[...] = total[g * sec_dev : (g + 1) * sec_dev].astype(jnp.bfloat16)


def partial_sums(side, shift, coef, wavefunction, left_ops, right_ops, split):
    k_dev, rows, width = left_ops.shape
    sec_dev = wavefunction.shape[0]
    targets = coef.shape[0]
    blocks = k_dev // BLOCK_TERMS
    scratch = [pltpu.VMEM(x.shape, x.dtype) for x in (wavefunction, left_ops, right_ops)]
    scratch += [pltpu.VMEM((BLOCK_TERMS, sec_dev, rows, width), jnp.bfloat16)] * 2
    scratch += [
        pltpu.SemaphoreType.DMA(()),
        pltpu.SemaphoreType.DMA((blocks,)),
        pltpu.SemaphoreType.DMA((2, blocks)),
    ]
    if split:
        out_shape = [pltpu.VMEM((targets, rows, width // 2), jnp.float32)]
        out_shape += [pltpu.VMEM((sec_dev, rows, width // 2), jnp.bfloat16)] * (targets // sec_dev)
        scratch = [pltpu.VMEM((targets, rows, width // 2), jnp.float32)] + scratch
    else:
        out_shape = [pltpu.VMEM((targets, rows, width), jnp.float32)]
    return pl.pallas_call(
        functools.partial(sigma_kernel, split),
        out_shape=out_shape,
        in_specs=[pl.BlockSpec(memory_space=pltpu.SMEM)] * 3
        + [pl.BlockSpec(memory_space=pltpu.HBM)] * 3,
        out_specs=[pl.BlockSpec(memory_space=pltpu.VMEM)] * len(out_shape),
        scratch_shapes=scratch,
        compiler_params=pltpu.CompilerParams(vmem_limit_bytes=40 * MIB),
        cost_estimate=pl.CostEstimate(
            flops=4 * k_dev * sec_dev * rows * width * width,
            bytes_accessed=2 * (left_ops.size + right_ops.size),
            transcendentals=0,
        ),
    )(
        side,
        pltpu.with_memory_space_constraint(shift, pltpu.HBM),
        coef,
        *(pltpu.with_memory_space_constraint(x, pltpu.HBM) for x in (wavefunction, left_ops, right_ops)),
    )


def shift_by(value, axis, distance):
    size = lax.axis_size(axis)
    return lax.ppermute(value, axis, [(i, (i + distance) % size) for i in range(size)])


def after(value, other):
    return lax.optimization_barrier((value, other))[0]


def per_device(wavefunction, left_ops, right_ops, site_coef, coupled, sector_shift):
    sec_dev = wavefunction.shape[0]
    devices = lax.axis_size("sector")
    live = jnp.where(coupled.T > 0, site_coef.T, 0.0)
    side = jnp.reshape(lax.axis_index("op"), (1,)).astype(jnp.int32)
    arrays = (wavefunction, left_ops, right_ops)

    if lax.axis_size("op") == 2 and devices <= 4:
        coefs = [live] + [shift_by(live, "sector", -g) for g in range(1, devices)]
        coef = jnp.concatenate(coefs, axis=0)
        mine, *theirs = partial_sums(side, sector_shift, coef, *arrays, True)
        mine = [mine[g * sec_dev : (g + 1) * sec_dev] for g in range(devices)]
        order = sorted(range(1, devices), key=lambda g: abs(2 * g - devices))
        crossed = {g: shift_by(theirs[g], "op", 1) for g in order}
        arrived, both = [], None
        for g in order:
            other = crossed[g] if both is None else after(crossed[g], both)
            both = (mine[g] + other.astype(jnp.float32)).astype(jnp.bfloat16)
            if not arrived:
                theirs[0] = after(theirs[0], both)
            arrived.append(shift_by(both, "sector", g))
        sigma = mine[0] + after(shift_by(theirs[0], "op", 1), both).astype(jnp.float32)
        for other in arrived:
            sigma = lax.optimization_barrier(sigma) + other.astype(jnp.float32)
        return sigma

    first = lax.axis_index("sector") * sec_dev
    coef = jnp.roll(lax.all_gather(live, "sector", axis=0, tiled=True), -first, axis=0)
    (total,) = partial_sums(side, sector_shift, coef, *arrays, False)
    total = jnp.roll(total, first, axis=0)
    total = lax.psum_scatter(total, "op", scatter_dimension=2, tiled=True)
    return lax.psum_scatter(total, "sector", scatter_dimension=0, tiled=True)


def solution(mesh):
    placed = (
        P(("groups", "sector"), None, None),
        P(("groups", "op"), "rep", None),
        P(("groups", "op"), None, None),
        P(("groups", "op"), "sector"),
        P(("groups", "op"), "sector"),
        P(("groups", "op")),
    )
    return jax.shard_map(
        per_device,
        mesh=mesh,
        in_specs=placed,
        out_specs=P(("groups", "sector"), "rep", "op"),
        check_vma=False,
    )
```

time: 159 us -> 37.2 us (0.23)
  waiting for transfers between devices: 76.8 us -> 12.1 us
  local copies, waits for them, and re-layouts: 48 us -> 0 us
  matrix products: 18.2 us -> 0 us
  starting transfers between devices: 0.04 us -> 14.9 us
  between operations: 13.4 us -> 0.05 us
  Pallas kernels: 0 us -> 8.36 us
    all_gather x1 -> x0, waiting for transfers between devices: 48.6 us -> none  [per_device(): everything = lax.all_gather(wavefunction, 'sector', axis=0, tiled=True)]
    gather x8 -> x0, local copies, waits for them, and re-layouts: 43.3 us -> none  [one_block(): source_blocks = jnp.take(everything, place, axis=0)]
    psum x1 -> x0, waiting for transfers between devices: 27.5 us -> none  [per_device(): summed = lax.psum(result, 'op')]
    dot_general x4 -> x0, matrix products: 18.2 us -> none  [one_block(): jnp.einsum('ksil,kml->ksim', mixed, right_part, preferred_element_type=jn...]
    ppermute x0 -> x10, starting transfers between devices: none -> 14.9 us  [shift_by(): lax.ppermute(value, axis, [(i, (i + distance) % size) for i in range(size)])]
    ppermute x0 -> x10, waiting for transfers between devices: none -> 12.1 us  [shift_by(): lax.ppermute(value, axis, [(i, (i + distance) % size) for i in range(size)])]
    pallas_call x0 -> x1, Pallas kernels: none -> 8.36 us  [partial_sums(): pl.pallas_call(functools.partial(sigma_kernel, split), out_shape=out_shap...]
    dynamic_slice x5 -> x0, local copies, waits for them, and re-layouts: 1.69 us -> none  [the longest x1 1.67 us: per_device(): lax.dynamic_slice_in_dim(summed, lax.axis_index('op') * columns, columns, 2)]
  transfers between devices with their start and end apart: 2 -> 10, of which waited for: 2 -> 9; matrix products, arithmetic and copies ran while one was open for 1% -> 1% of each run, Pallas kernels for 0% -> 0%
where the time goes in v5:
time: 37.2 us; the launch traced here: 37.1 us
  starting transfers between devices  14.9 us (40%)
  waiting for transfers between devices  12.1 us (33%)
  Pallas kernels  8.36 us (22%)
  other arithmetic  1.66 us (4%)
    ppermute x10, starting transfers between devices, shift_by(): lax.ppermute(value, axis, [(i, (i + distance) % size) for i in range(size)])  14.9 us
    ppermute x10, waiting for transfers between devices, shift_by(): lax.ppermute(value, axis, [(i, (i + distance) % size) for i in range(size)])  12.1 us
    pallas_call x1, Pallas kernels, partial_sums(): pl.pallas_call(functools.partial(sigma_kernel, split), out_shape=out_shap...  8.36 us
    add x3, other arithmetic, per_device(): sigma = lax.optimization_barrier(sigma) + other.astype(jnp.float32)  0.8 us
  transfers between devices with their start and end apart: 10, of which 9 were waited for; matrix products, arithmetic and copies ran while one was open for 1% of the time, Pallas kernels for 0%

profile of v5, /device:TPU:0, one launch (start us, length us, event | category | flops | bytes accessed | tf_op | source)
XLA Modules:
  0.0 37.1 jit_solution(1887449320973131501)
XLA Ops:
  0.0 0.7 %select_bitcast_fusion = f32[4,32]{1,0:T(4,128)S(1)} fusion(f32[32,4]{0,1:T(4,128)} %param.9, s32[32,4]{0,1:T(4,128)} %param.10), kind=kLoop, calls=%fused_computation.8 | loop fusion | flops 256 | bytes 1536 | tf_op jit(solution)/shard_map/jit(_where)/select_n | solution.py:160
  0.7 5.0 %collective-permute-start = (f32[4,32]{1,0:T(4,128)S(1)}, f32[4,32]{1,0:T(4,128)S(1)}, u32[]{:S(2)}, u32[]{:S(2)}) collective-permute-start(f32[4,32]{1,0:T(4,128)S(1)} %select_bitcast_fusion), channel_id=1, source_target_pairs={{0,12},{4,0},{8,4},{12,8},{1,13},{5,1},{9,5},{13,9},{2,14},{6,2},{... | collective-permute-start | bytes 1544 | tf_op jit(solution)/shard_map/ppermute | solution.py:150
  5.8 0.0 collective-permute-start.1
  5.8 1.0 %collective-permute-start.2 = (f32[4,32]{1,0:T(4,128)S(1)}, f32[4,32]{1,0:T(4,128)S(1)}, u32[]{:S(2)}, u32[]{:S(2)}) collective-permute-start(f32[4,32]{1,0:T(4,128)S(1)} %select_bitcast_fusion), channel_id=1, source_target_pairs={{0,4},{4,8},{8,12},{12,0},{1,5},{5,9},{9,13},{13,1},{2,6},{6,10},{... | collective-permute-start | bytes 1544 | tf_op jit(solution)/shard_map/ppermute | solution.py:150
  6.8 0.3 collective-permute-done
  7.1 3.2 %collective-permute-done.1 = f32[4,32]{1,0:T(4,128)S(1)} collective-permute-done((f32[4,32]{1,0:T(4,128)S(1)}, f32[4,32]{1,0:T(4,128)S(1)}, u32[]{:S(2)}, u32[]{:S(2)}) %collective-permute-start.1) | collective-permute-done | bytes 544 | tf_op jit(solution)/shard_map/ppermute | solution.py:150
  10.2 0.9 %collective-permute-done.2 = f32[4,32]{1,0:T(4,128)S(1)} collective-permute-done((f32[4,32]{1,0:T(4,128)S(1)}, f32[4,32]{1,0:T(4,128)S(1)}, u32[]{:S(2)}, u32[]{:S(2)}) %collective-permute-start.2) | collective-permute-done | bytes 544 | tf_op jit(solution)/shard_map/ppermute | solution.py:150
  11.1 8.4 %shard_map.64 = (f32[16,128,128]{2,1,0:T(8,128)S(1)}, bf16[4,128,128]{2,1,0:T(8,128)(2,1)S(1)}, bf16[4,128,128]{2,1,0:T(8,128)(2,1)S(1)}, bf16[4,128,128]{2,1,0:T(8,128)(2,1)S(1)}, bf16[4,128,128]{2,1,0:T(8,128)(2,1)S(1)}) custom-call(s32[1]{0:T(128)} %bitcast.side_ref, s32[32]{0:T(128)} %shift_ref.1, f32[16,32]{1,0:T(8,128)S(1)} %pad_maximum_fusion.coef_ref, ...), custom_call_target="tpu_custom_call" | custom-call | flops 4294967296 | bytes 6291456 | tf_op jit(solution)/shard_map/pallas_call | solution.py:127
  19.5 1.6 %collective-permute-start.3 = (bf16[4,128,128]{2,1,0:T(8,128)(2,1)S(1)}, bf16[4,128,128]{2,1,0:T(8,128)(2,1)S(1)}, u32[]{:S(2)}, u32[]{:S(2)}) collective-permute-start(bf16[4,128,128]{2,1,0:T(8,128)(2,1)S(1)} %get-tuple-element.16), channel_id=1, source_target_pairs={{0,2},{2,0},{1,3},{3,1},{4,6},{6,4},{5,7},{7,5},{8,10},{10,8},{9,1... | collective-permute-start | bytes 393224 | tf_op jit(solution)/shard_map/ppermute | solution.py:150
  21.1 0.5 %collective-permute-start.6 = (bf16[4,128,128]{2,1,0:T(8,128)(2,1)S(1)}, bf16[4,128,128]{2,1,0:T(8,128)(2,1)S(1)}, u32[]{:S(2)}, u32[]{:S(2)}) collective-permute-start(bf16[4,128,128]{2,1,0:T(8,128)(2,1)S(1)} %get-tuple-element.19), channel_id=1, source_target_pairs={{0,2},{2,0},{1,3},{3,1},{4,6},{6,4},{5,7},{7,5},{8,10},{10,8},{9,1... | collective-permute-start | bytes 393224 | tf_op jit(solution)/shard_map/ppermute | solution.py:150
  21.6 1.5 %collective-permute-start.5 = (bf16[4,128,128]{2,1,0:T(8,128)(2,1)S(1)}, bf16[4,128,128]{2,1,0:T(8,128)(2,1)S(1)}, u32[]{:S(2)}, u32[]{:S(2)}) collective-permute-start(bf16[4,128,128]{2,1,0:T(8,128)(2,1)S(1)} %get-tuple-element.18), channel_id=1, source_target_pairs={{0,2},{2,0},{1,3},{3,1},{4,6},{6,4},{5,7},{7,5},{8,10},{10,8},{9,1... | collective-permute-start | bytes 393224 | tf_op jit(solution)/shard_map/ppermute | solution.py:150
  23.1 2.9 %collective-permute-done.3 = bf16[4,128,128]{2,1,0:T(8,128)(2,1)S(1)} collective-permute-done((bf16[4,128,128]{2,1,0:T(8,128)(2,1)S(1)}, bf16[4,128,128]{2,1,0:T(8,128)(2,1)S(1)}, u32[]{:S(2)}, u32[]{:S(2)}) %collective-permute-start.3) | collective-permute-done | bytes 131104 | tf_op jit(solution)/shard_map/ppermute | solution.py:150
  26.1 1.1 %collective-permute-start.7 = (bf16[4,128,128]{2,1,0:T(8,128)(2,1)S(1)}, bf16[4,128,128]{2,1,0:T(8,128)(2,1)S(1)}, u32[]{:S(2)}, u32[]{:S(2)}) collective-permute-start(bf16[4,128,128]{2,1,0:T(8,128)(2,1)S(1)} %add_convert_fusion.2), channel_id=1, source_target_pairs={{0,8},{4,12},{8,0},{12,4},{1,9},{5,13},{9,1},{13,5},{2,10},{6,14},... | collective-permute-start | bytes 393224 | tf_op jit(solution)/shard_map/ppermute | solution.py:150
  27.2 0.4 %collective-permute-done.6 = bf16[4,128,128]{2,1,0:T(8,128)(2,1)S(1)} collective-permute-done((bf16[4,128,128]{2,1,0:T(8,128)(2,1)S(1)}, bf16[4,128,128]{2,1,0:T(8,128)(2,1)S(1)}, u32[]{:S(2)}, u32[]{:S(2)}) %collective-permute-start.6) | collective-permute-done | bytes 131104 | tf_op jit(solution)/shard_map/ppermute | solution.py:150
  27.6 0.1 collective-permute-start.8
  27.7 1.3 %collective-permute-done.5 = bf16[4,128,128]{2,1,0:T(8,128)(2,1)S(1)} collective-permute-done((bf16[4,128,128]{2,1,0:T(8,128)(2,1)S(1)}, bf16[4,128,128]{2,1,0:T(8,128)(2,1)S(1)}, u32[]{:S(2)}, u32[]{:S(2)}) %collective-permute-start.5) | collective-permute-done | bytes 131104 | tf_op jit(solution)/shard_map/ppermute | solution.py:150
  29.0 1.5 %collective-permute-start.4 = (bf16[4,128,128]{2,1,0:T(8,128)(2,1)S(1)}, bf16[4,128,128]{2,1,0:T(8,128)(2,1)S(1)}, u32[]{:S(2)}, u32[]{:S(2)}) collective-permute-start(bf16[4,128,128]{2,1,0:T(8,128)(2,1)S(1)} %get-tuple-element.17), channel_id=1, source_target_pairs={{0,2},{2,0},{1,3},{3,1},{4,6},{6,4},{5,7},{7,5},{8,10},{10,8},{9,1... | collective-permute-start | bytes 393224 | tf_op jit(solution)/shard_map/ppermute | solution.py:150
  30.5 2.6 %collective-permute-start.9 = (bf16[4,128,128]{2,1,0:T(8,128)(2,1)S(1)}, bf16[4,128,128]{2,1,0:T(8,128)(2,1)S(1)}, u32[]{:S(2)}, u32[]{:S(2)}) collective-permute-start(bf16[4,128,128]{2,1,0:T(8,128)(2,1)S(1)} %add_convert_fusion), channel_id=1, source_target_pairs={{0,12},{4,0},{8,4},{12,8},{1,13},{5,1},{9,5},{13,9},{2,14},{6,2},{... | collective-permute-start | bytes 393224 | tf_op jit(solution)/shard_map/ppermute | solution.py:150
  33.1 0.9 %collective-permute-done.4 = bf16[4,128,128]{2,1,0:T(8,128)(2,1)S(1)} collective-permute-done((bf16[4,128,128]{2,1,0:T(8,128)(2,1)S(1)}, bf16[4,128,128]{2,1,0:T(8,128)(2,1)S(1)}, u32[]{:S(2)}, u32[]{:S(2)}) %collective-permute-start.4) | collective-permute-done | bytes 131104 | tf_op jit(solution)/shard_map/ppermute | solution.py:150
  34.0 1.2 %collective-permute-done.7 = bf16[4,128,128]{2,1,0:T(8,128)(2,1)S(1)} collective-permute-done((bf16[4,128,128]{2,1,0:T(8,128)(2,1)S(1)}, bf16[4,128,128]{2,1,0:T(8,128)(2,1)S(1)}, u32[]{:S(2)}, u32[]{:S(2)}) %collective-permute-start.7) | collective-permute-done | bytes 131104 | tf_op jit(solution)/shard_map/ppermute | solution.py:150
  35.2 0.0 collective-permute-done.8
  35.3 1.1 %collective-permute-done.9 = bf16[4,128,128]{2,1,0:T(8,128)(2,1)S(1)} collective-permute-done((bf16[4,128,128]{2,1,0:T(8,128)(2,1)S(1)}, bf16[4,128,128]{2,1,0:T(8,128)(2,1)S(1)}, u32[]{:S(2)}, u32[]{:S(2)}) %collective-permute-start.9) | collective-permute-done | bytes 131104 | tf_op jit(solution)/shard_map/ppermute | solution.py:150
  36.3 0.7 %convert_add_fusion = f32[4,128,128]{2,1,0:T(8,128)} fusion(f32[4,128,128]{2,1,0:T(8,128)S(1)} %convert_add_fusion.1, bf16[4,128,128]{2,1,0:T(8,128)(2,1)S(1)} %collective-permute-done.9), kind=kLoop, calls=%fused_computation | loop fusion | flops 131072 | bytes 655360 | tf_op jit(solution)/shard_map/add | solution.py:180
  (7 shorter events, 0.2 us)
Async XLA Ops:
  0.7 6.4 %collective-permute-start = (f32[4,32]{1,0:T(4,128)S(1)}, f32[4,32]{1,0:T(4,128)S(1)}, u32[]{:S(2)}, u32[]{:S(2)}) collective-permute-start(f32[4,32]{1,0:T(4,128)S(1)} %select_bitcast_fusion), channel_id=1, source_target_pairs={{0,12},{4,0},{8,4},{12,8},{1,13},{5,1},{9,5},{13,9},{2,14},{6,2},{... | collective-permute-start | bytes 1544 | tf_op jit(solution)/shard_map/ppermute | solution.py:150
  5.8 4.5 %collective-permute-start.1 = (f32[4,32]{1,0:T(4,128)S(1)}, f32[4,32]{1,0:T(4,128)S(1)}, u32[]{:S(2)}, u32[]{:S(2)}) collective-permute-start(f32[4,32]{1,0:T(4,128)S(1)} %select_bitcast_fusion), channel_id=1, source_target_pairs={{0,8},{4,12},{8,0},{12,4},{1,9},{5,13},{9,1},{13,5},{2,10},{6,14},... | collective-permute-start | bytes 1544 | tf_op jit(solution)/shard_map/ppermute | solution.py:150
  5.8 5.4 %collective-permute-start.2 = (f32[4,32]{1,0:T(4,128)S(1)}, f32[4,32]{1,0:T(4,128)S(1)}, u32[]{:S(2)}, u32[]{:S(2)}) collective-permute-start(f32[4,32]{1,0:T(4,128)S(1)} %select_bitcast_fusion), channel_id=1, source_target_pairs={{0,4},{4,8},{8,12},{12,0},{1,5},{5,9},{9,13},{13,1},{2,6},{6,10},{... | collective-permute-start | bytes 1544 | tf_op jit(solution)/shard_map/ppermute | solution.py:150
  19.5 6.5 %collective-permute-start.3 = (bf16[4,128,128]{2,1,0:T(8,128)(2,1)S(1)}, bf16[4,128,128]{2,1,0:T(8,128)(2,1)S(1)}, u32[]{:S(2)}, u32[]{:S(2)}) collective-permute-start(bf16[4,128,128]{2,1,0:T(8,128)(2,1)S(1)} %get-tuple-element.16), channel_id=1, source_target_pairs={{0,2},{2,0},{1,3},{3,1},{4,6},{6,4},{5,7},{7,5},{8,10},{10,8},{9,1... | collective-permute-start | bytes 393224 | tf_op jit(solution)/shard_map/ppermute | solution.py:150
  21.1 6.5 %collective-permute-start.6 = (bf16[4,128,128]{2,1,0:T(8,128)(2,1)S(1)}, bf16[4,128,128]{2,1,0:T(8,128)(2,1)S(1)}, u32[]{:S(2)}, u32[]{:S(2)}) collective-permute-start(bf16[4,128,128]{2,1,0:T(8,128)(2,1)S(1)} %get-tuple-element.19), channel_id=1, source_target_pairs={{0,2},{2,0},{1,3},{3,1},{4,6},{6,4},{5,7},{7,5},{8,10},{10,8},{9,1... | collective-permute-start | bytes 393224 | tf_op jit(solution)/shard_map/ppermute | solution.py:150
  21.6 7.4 %collective-permute-start.5 = (bf16[4,128,128]{2,1,0:T(8,128)(2,1)S(1)}, bf16[4,128,128]{2,1,0:T(8,128)(2,1)S(1)}, u32[]{:S(2)}, u32[]{:S(2)}) collective-permute-start(bf16[4,128,128]{2,1,0:T(8,128)(2,1)S(1)} %get-tuple-element.18), channel_id=1, source_target_pairs={{0,2},{2,0},{1,3},{3,1},{4,6},{6,4},{5,7},{7,5},{8,10},{10,8},{9,1... | collective-permute-start | bytes 393224 | tf_op jit(solution)/shard_map/ppermute | solution.py:150
  26.1 9.1 %collective-permute-start.7 = (bf16[4,128,128]{2,1,0:T(8,128)(2,1)S(1)}, bf16[4,128,128]{2,1,0:T(8,128)(2,1)S(1)}, u32[]{:S(2)}, u32[]{:S(2)}) collective-permute-start(bf16[4,128,128]{2,1,0:T(8,128)(2,1)S(1)} %add_convert_fusion.2), channel_id=1, source_target_pairs={{0,8},{4,12},{8,0},{12,4},{1,9},{5,13},{9,1},{13,5},{2,10},{6,14},... | collective-permute-start | bytes 393224 | tf_op jit(solution)/shard_map/ppermute | solution.py:150
  27.6 7.6 %collective-permute-start.8 = (bf16[4,128,128]{2,1,0:T(8,128)(2,1)S(1)}, bf16[4,128,128]{2,1,0:T(8,128)(2,1)S(1)}, u32[]{:S(2)}, u32[]{:S(2)}) collective-permute-start(bf16[4,128,128]{2,1,0:T(8,128)(2,1)S(1)} %add_convert_fusion.1), channel_id=1, source_target_pairs={{0,4},{4,8},{8,12},{12,0},{1,5},{5,9},{9,13},{13,1},{2,6},{6,10},{... | collective-permute-start | bytes 393224 | tf_op jit(solution)/shard_map/ppermute | solution.py:150
  29.0 5.0 %collective-permute-start.4 = (bf16[4,128,128]{2,1,0:T(8,128)(2,1)S(1)}, bf16[4,128,128]{2,1,0:T(8,128)(2,1)S(1)}, u32[]{:S(2)}, u32[]{:S(2)}) collective-permute-start(bf16[4,128,128]{2,1,0:T(8,128)(2,1)S(1)} %get-tuple-element.17), channel_id=1, source_target_pairs={{0,2},{2,0},{1,3},{3,1},{4,6},{6,4},{5,7},{7,5},{8,10},{10,8},{9,1... | collective-permute-start | bytes 393224 | tf_op jit(solution)/shard_map/ppermute | solution.py:150
  30.5 5.8 %collective-permute-start.9 = (bf16[4,128,128]{2,1,0:T(8,128)(2,1)S(1)}, bf16[4,128,128]{2,1,0:T(8,128)(2,1)S(1)}, u32[]{:S(2)}, u32[]{:S(2)}) collective-permute-start(bf16[4,128,128]{2,1,0:T(8,128)(2,1)S(1)} %add_convert_fusion), channel_id=1, source_target_pairs={{0,12},{4,0},{8,4},{12,8},{1,13},{5,1},{9,5},{13,9},{2,14},{6,2},{... | collective-permute-start | bytes 393224 | tf_op jit(solution)/shard_map/ppermute | solution.py:150

commit v6 on v3

v6 whole, which is shorter than its diff:
```python
import functools

import jax
import jax.numpy as jnp
from jax import lax
from jax.experimental import pallas as pl
from jax.experimental.pallas import tpu as pltpu
from jax.sharding import PartitionSpec as P

MIX_TERMS = 8
SUM_TERMS = 4
MIB = 1024 * 1024


def wrapped(value, size):
    if size & (size - 1) == 0:
        return value & (size - 1)
    return lax.rem(value + size, size)


def mix_kernel(split, side_ref, wave_ref, left_ref, right_ref, mixed_ref, turned_ref, *refs):
    wave, left, right, wave_sem, left_sems, right_sems = refs
    sec_dev = wave.shape[0]
    terms, rows, width = left.shape
    blocks = terms // MIX_TERMS
    half = width // 2

    def part(block):
        return pl.ds(block * MIX_TERMS, MIX_TERMS)

    def left_copy(block):
        return pltpu.make_async_copy(
            left_ref.at[part(block)], left.at[part(block)], left_sems.at[block]
        )

    def right_copies(block):
        if not split:
            source, target = right_ref.at[part(block)], right.at[part(block)]
            return [pltpu.make_async_copy(source, target, right_sems.at[0, block])]
        copies = []
        for at, side in enumerate((1 - side_ref[0], side_ref[0])):
            source = right_ref.at[part(block), pl.ds(pl.multiple_of(side * half, half), half)]
            target = right.at[part(block), pl.ds(at * half, half)]
            copies.append(pltpu.make_async_copy(source, target, right_sems.at[at, block]))
        return copies

    wave_copy = pltpu.make_async_copy(wave_ref, wave, wave_sem)
    wave_copy.start()
    for block in range(blocks):
        left_copy(block).start()
        for copy in right_copies(block):
            copy.start()
    wave_copy.wait()

    @pl.loop(0, blocks)
    def _(block):
        left_copy(block).wait()
        for copy in right_copies(block):
            copy.wait()
        rows_in = left[part(block)].reshape(MIX_TERMS * rows, width)
        for s in range(sec_dev):
            product = jnp.dot(rows_in, wave[s], preferred_element_type=jnp.float32)
            mixed_ref[part(block), s] = product.astype(jnp.bfloat16).reshape(MIX_TERMS, rows, width)
        for t in range(MIX_TERMS):
            k = block * MIX_TERMS + t
            turned_ref[k] = right[k].T


def mix(side, wavefunction, left_ops, right_ops, split):
    k_dev, rows, width = left_ops.shape
    sec_dev = wavefunction.shape[0]
    blocks = k_dev // MIX_TERMS
    arrays = (wavefunction, left_ops, right_ops)
    return pl.pallas_call(
        functools.partial(mix_kernel, split),
        out_shape=[
            pltpu.VMEM((k_dev, sec_dev, rows, width), jnp.bfloat16),
            pltpu.VMEM(right_ops.shape, jnp.bfloat16),
        ],
        in_specs=[pl.BlockSpec(memory_space=pltpu.SMEM)] + [pl.BlockSpec(memory_space=pltpu.HBM)] * 3,
        out_specs=[pl.BlockSpec(memory_space=pltpu.VMEM)] * 2,
        scratch_shapes=[pltpu.VMEM(x.shape, x.dtype) for x in arrays]
        + [
            pltpu.SemaphoreType.DMA(()),
            pltpu.SemaphoreType.DMA((blocks,)),
            pltpu.SemaphoreType.DMA((2, blocks)),
        ],
        compiler_params=pltpu.CompilerParams(vmem_limit_bytes=32 * MIB),
        cost_estimate=pl.CostEstimate(
            flops=2 * k_dev * sec_dev * rows * width * width,
            bytes_accessed=2 * (left_ops.size + right_ops.size),
            transcendentals=0,
        ),
    )(side, *(pltpu.with_memory_space_constraint(x, pltpu.HBM) for x in arrays))


def sum_kernel(split, shift_ref, coef_ref, mixed_ref, turned_ref, *refs):
    terms, sec_dev, rows, width = mixed_ref.shape
    targets = coef_ref.shape[0]
    half = width // 2
    mine = refs[0]
    mine[...] = jnp.zeros_like(mine)
    if split:
        theirs, total = refs[1:-1], refs[-1]
        total[...] = jnp.zeros_like(total)

    @pl.loop(0, terms // SUM_TERMS)
    def _(step):
        for t in range(SUM_TERMS):
            k = step * SUM_TERMS + t
            product = jnp.dot(
                mixed_ref[k].reshape(sec_dev * rows, width),
                turned_ref[k],
                preferred_element_type=jnp.float32,
            )
            for s in range(sec_dev):
                target = wrapped(s - shift_ref[k], targets)
                scaled = coef_ref[target, k] * product[s * rows : (s + 1) * rows]
                if split:
                    total[target] += scaled[:, :half]
                    mine[target] += scaled[:, half:]
                else:
                    mine[target] += scaled

    if split:
        for g, out in enumerate(theirs):
            out[...] = total[g * sec_dev : (g + 1) * sec_dev].astype(jnp.bfloat16)


def summed(shift, coef, mixed, turned, split):
    k_dev, sec_dev, rows, width = mixed.shape
    targets = coef.shape[0]
    if split:
        out_shape = [pltpu.VMEM((targets, rows, width // 2), jnp.float32)]
        out_shape += [pltpu.VMEM((sec_dev, rows, width // 2), jnp.bfloat16)] * (targets // sec_dev)
        scratch = [pltpu.VMEM((targets, rows, width // 2), jnp.float32)]
    else:
        out_shape = [pltpu.VMEM((targets, rows, width), jnp.float32)]
        scratch = []
    return pl.pallas_call(
        functools.partial(sum_kernel, split),
        out_shape=out_shape,
        in_specs=[pl.BlockSpec(memory_space=pltpu.SMEM)] * 2
        + [pl.BlockSpec(memory_space=pltpu.VMEM)] * 2,
        out_specs=[pl.BlockSpec(memory_space=pltpu.VMEM)] * len(out_shape),
        scratch_shapes=scratch,
        compiler_params=pltpu.CompilerParams(vmem_limit_bytes=24 * MIB),
        cost_estimate=pl.CostEstimate(
            flops=2 * k_dev * sec_dev * rows * width * width,
            bytes_accessed=2 * (mixed.size + turned.size),
            transcendentals=0,
        ),
    )(
        pltpu.with_memory_space_constraint(shift, pltpu.HBM),
        coef,
        pltpu.with_memory_space_constraint(mixed, pltpu.VMEM),
        pltpu.with_memory_space_constraint(turned, pltpu.VMEM),
    )


def shift_by(value, axis, distance):
    size = lax.axis_size(axis)
    return lax.ppermute(value, axis, [(i, (i + distance) % size) for i in range(size)])


def after(value, other):
    return lax.optimization_barrier((value, other))[0]


def per_device(wavefunction, left_ops, right_ops, site_coef, coupled, sector_shift):
    sec_dev = wavefunction.shape[0]
    devices = lax.axis_size("sector")
    live = jnp.where(coupled.T > 0, site_coef.T, 0.0)
    side = jnp.reshape(lax.axis_index("op"), (1,)).astype(jnp.int32)
    split = lax.axis_size("op") == 2 and devices <= 4

    if split:
        coefs = [live] + [shift_by(live, "sector", -g) for g in range(1, devices)]
        coef = jnp.concatenate(coefs, axis=0)
        mixed, turned = mix(side, wavefunction, left_ops, right_ops, True)
        mine, *theirs = summed(sector_shift, coef, mixed, turned, True)
        mine = [mine[g * sec_dev : (g + 1) * sec_dev] for g in range(devices)]
        order = sorted(range(1, devices), key=lambda g: abs(2 * g - devices))
        crossed = {g: shift_by(theirs[g], "op", 1) for g in order}
        arrived, both = [], None
        for g in order:
            other = crossed[g] if both is None else after(crossed[g], both)
            both = (mine[g] + other.astype(jnp.float32)).astype(jnp.bfloat16)
            if not arrived:
                theirs[0] = after(theirs[0], both)
            arrived.append(shift_by(both, "sector", g))
        sigma = mine[0] + after(shift_by(theirs[0], "op", 1), both).astype(jnp.float32)
        for other in arrived:
            sigma = lax.optimization_barrier(sigma) + other.astype(jnp.float32)
        return sigma

    first = lax.axis_index("sector") * sec_dev
    coef = jnp.roll(lax.all_gather(live, "sector", axis=0, tiled=True), -first, axis=0)
    mixed, turned = mix(side, wavefunction, left_ops, right_ops, False)
    (total,) = summed(sector_shift, coef, mixed, turned, False)
    total = jnp.roll(total, first, axis=0)
    total = lax.psum_scatter(total, "op", scatter_dimension=2, tiled=True)
    return lax.psum_scatter(total, "sector", scatter_dimension=0, tiled=True)


def solution(mesh):
    placed = (
        P(("groups", "sector"), None, None),
        P(("groups", "op"), "rep", None),
        P(("groups", "op"), None, None),
        P(("groups", "op"), "sector"),
        P(("groups", "op"), "sector"),
        P(("groups", "op")),
    )
    return jax.shard_map(
        per_device,
        mesh=mesh,
        in_specs=placed,
        out_specs=P(("groups", "sector"), "rep", "op"),
        check_vma=False,
    )
```

time: 36.5 us -> 38.3 us (1.049)
  Pallas kernels: 9.19 us -> 10.7 us
  starting transfers between devices: 15 us -> 16.4 us
  other arithmetic: 2.26 us -> 1.65 us
  waiting for transfers between devices: 9.84 us -> 9.39 us
    pallas_call x1, Pallas kernels: 4.11 us -> 5.59 us  [mix(): pl.pallas_call(functools.partial(mix_kernel, split), out_shape=[pltpu.VME...]
    ppermute x10, starting transfers between devices: 15 us -> 16.4 us  [shift_by(): lax.ppermute(value, axis, [(i, (i + distance) % size) for i in range(size)])]
    rem x1 -> x0, other arithmetic: 0.66 us -> none  [per_device(): shift = lax.rem(sector_shift, sec_dev * devices)]
    ppermute x10, waiting for transfers between devices: 9.84 us -> 9.39 us  [shift_by(): lax.ppermute(value, axis, [(i, (i + distance) % size) for i in range(size)])]
    add x1 -> x4, other arithmetic: 0.78 us -> 0.82 us  [the longest x3 0.79 us: per_device(): sigma = lax.optimization_barrier(sigma) + other.astype(jnp.float32)]
  transfers between devices with their start and end apart: 10 -> 10, of which waited for: 5 -> 5; matrix products, arithmetic and copies ran while one was open for 2% -> 1% of each run, Pallas kernels for 11% -> 15%
where the time goes in v6:
time: 38.3 us; the launch traced here: 38.2 us
  starting transfers between devices  16.4 us (43%)
  Pallas kernels  10.7 us (28%)
  waiting for transfers between devices  9.39 us (25%)
  other arithmetic  1.65 us (4%)
    ppermute x10, starting transfers between devices, shift_by(): lax.ppermute(value, axis, [(i, (i + distance) % size) for i in range(size)])  16.4 us
    ppermute x10, waiting for transfers between devices, shift_by(): lax.ppermute(value, axis, [(i, (i + distance) % size) for i in range(size)])  9.39 us
    pallas_call x1, Pallas kernels, mix(): pl.pallas_call(functools.partial(mix_kernel, split), out_shape=[pltpu.VME...  5.59 us
    pallas_call x1, Pallas kernels, summed(): pl.pallas_call(functools.partial(sum_kernel, split), out_shape=out_shape,...  5.1 us
    add x3, other arithmetic, per_device(): sigma = lax.optimization_barrier(sigma) + other.astype(jnp.float32)  0.79 us
  transfers between devices with their start and end apart: 10, of which 5 were waited for; matrix products, arithmetic and copies ran while one was open for 1% of the time, Pallas kernels for 15%

profile of v6, /device:TPU:0, one launch (start us, length us, event | category | flops | bytes accessed | tf_op | source)
XLA Modules:
  0.0 38.2 jit_solution(8097550195790648710)
XLA Ops:
  0.0 0.7 %select_bitcast_fusion = f32[4,32]{1,0:T(4,128)S(1)} fusion(f32[32,4]{0,1:T(4,128)} %param.9, s32[32,4]{0,1:T(4,128)} %param.10), kind=kLoop, calls=%fused_computation.8 | loop fusion | flops 256 | bytes 1536 | tf_op jit(solution)/shard_map/jit(_where)/select_n | solution.py:173
  0.7 3.0 %collective-permute-start.2 = (f32[4,32]{1,0:T(4,128)S(1)}, f32[4,32]{1,0:T(4,128)S(1)}, u32[]{:S(2)}, u32[]{:S(2)}) collective-permute-start(f32[4,32]{1,0:T(4,128)S(1)} %select_bitcast_fusion), channel_id=1, source_target_pairs={{0,4},{4,8},{8,12},{12,0},{1,5},{5,9},{9,13},{13,1},{2,6},{6,10},{... | collective-permute-start | bytes 1544 | tf_op jit(solution)/shard_map/ppermute | solution.py:163
  3.7 2.6 %collective-permute-start.1 = (f32[4,32]{1,0:T(4,128)S(1)}, f32[4,32]{1,0:T(4,128)S(1)}, u32[]{:S(2)}, u32[]{:S(2)}) collective-permute-start(f32[4,32]{1,0:T(4,128)S(1)} %select_bitcast_fusion), channel_id=1, source_target_pairs={{0,8},{4,12},{8,0},{12,4},{1,9},{5,13},{9,1},{13,5},{2,10},{6,14},... | collective-permute-start | bytes 1544 | tf_op jit(solution)/shard_map/ppermute | solution.py:163
  6.3 1.3 %collective-permute-start = (f32[4,32]{1,0:T(4,128)S(1)}, f32[4,32]{1,0:T(4,128)S(1)}, u32[]{:S(2)}, u32[]{:S(2)}) collective-permute-start(f32[4,32]{1,0:T(4,128)S(1)} %select_bitcast_fusion), channel_id=1, source_target_pairs={{0,12},{4,0},{8,4},{12,8},{1,13},{5,1},{9,5},{13,9},{2,14},{6,2},{... | collective-permute-start | bytes 1544 | tf_op jit(solution)/shard_map/ppermute | solution.py:163
  7.7 5.6 %shard_map.64 = (bf16[32,4,128,256]{3,2,1,0:T(8,128)(2,1)S(1)}, bf16[32,256,256]{2,1,0:T(8,128)(2,1)S(1)}) custom-call(s32[1]{0:T(128)} %bitcast.1.side_ref, bf16[4,256,256]{2,1,0:T(8,128)(2,1)} %wave_ref.1, bf16[32,128,256]{2,1,0:T(8,128)(2,1)} %left_ref.1, bf16[32,256,256]{2,1,0:T(8,128)(2,1)} %right_ref.1), custom_call_target="tpu_custom_call" | custom-call | flops 2147483648 | bytes 6291456 | tf_op jit(solution)/shard_map/pallas_call | solution.py:74
  13.3 0.0 collective-permute-done.2
  13.3 0.0 collective-permute-done.1
  13.3 0.0 collective-permute-done
  13.3 5.1 %shard_map.65 = (f32[16,128,128]{2,1,0:T(8,128)S(1)}, bf16[4,128,128]{2,1,0:T(8,128)(2,1)S(1)}, bf16[4,128,128]{2,1,0:T(8,128)(2,1)S(1)}, bf16[4,128,128]{2,1,0:T(8,128)(2,1)S(1)}, bf16[4,128,128]{2,1,0:T(8,128)(2,1)S(1)}) custom-call(s32[32]{0:T(128)} %shift_ref.1, f32[16,32]{1,0:T(8,128)S(1)} %pad_maximum_fusion.coef_ref, ...), custom_call_target="tpu_custom_call" | custom-call | flops 2147483648 | bytes 12582912 | tf_op jit(solution)/shard_map/pallas_call | solution.py:140
  18.4 1.6 %collective-permute-start.3 = (bf16[4,128,128]{2,1,0:T(8,128)(2,1)S(1)}, bf16[4,128,128]{2,1,0:T(8,128)(2,1)S(1)}, u32[]{:S(2)}, u32[]{:S(2)}) collective-permute-start(bf16[4,128,128]{2,1,0:T(8,128)(2,1)S(1)} %get-tuple-element.20), channel_id=1, source_target_pairs={{0,2},{2,0},{1,3},{3,1},{4,6},{6,4},{5,7},{7,5},{8,10},{10,8},{9,1... | collective-permute-start | bytes 393224 | tf_op jit(solution)/shard_map/ppermute | solution.py:163
  20.0 0.5 %collective-permute-start.5 = (bf16[4,128,128]{2,1,0:T(8,128)(2,1)S(1)}, bf16[4,128,128]{2,1,0:T(8,128)(2,1)S(1)}, u32[]{:S(2)}, u32[]{:S(2)}) collective-permute-start(bf16[4,128,128]{2,1,0:T(8,128)(2,1)S(1)} %get-tuple-element.22), channel_id=1, source_target_pairs={{0,2},{2,0},{1,3},{3,1},{4,6},{6,4},{5,7},{7,5},{8,10},{10,8},{9,1... | collective-permute-start | bytes 393224 | tf_op jit(solution)/shard_map/ppermute | solution.py:163
  20.5 1.5 %collective-permute-start.6 = (bf16[4,128,128]{2,1,0:T(8,128)(2,1)S(1)}, bf16[4,128,128]{2,1,0:T(8,128)(2,1)S(1)}, u32[]{:S(2)}, u32[]{:S(2)}) collective-permute-start(bf16[4,128,128]{2,1,0:T(8,128)(2,1)S(1)} %get-tuple-element.23), channel_id=1, source_target_pairs={{0,2},{2,0},{1,3},{3,1},{4,6},{6,4},{5,7},{7,5},{8,10},{10,8},{9,1... | collective-permute-start | bytes 393224 | tf_op jit(solution)/shard_map/ppermute | solution.py:163
  22.0 2.9 %collective-permute-done.3 = bf16[4,128,128]{2,1,0:T(8,128)(2,1)S(1)} collective-permute-done((bf16[4,128,128]{2,1,0:T(8,128)(2,1)S(1)}, bf16[4,128,128]{2,1,0:T(8,128)(2,1)S(1)}, u32[]{:S(2)}, u32[]{:S(2)}) %collective-permute-start.3) | collective-permute-done | bytes 131104 | tf_op jit(solution)/shard_map/ppermute | solution.py:163
  25.0 0.2 collective-permute-start.7
  25.1 1.7 %collective-permute-start.4 = (bf16[4,128,128]{2,1,0:T(8,128)(2,1)S(1)}, bf16[4,128,128]{2,1,0:T(8,128)(2,1)S(1)}, u32[]{:S(2)}, u32[]{:S(2)}) collective-permute-start(bf16[4,128,128]{2,1,0:T(8,128)(2,1)S(1)} %get-tuple-element.21), channel_id=1, source_target_pairs={{0,2},{2,0},{1,3},{3,1},{4,6},{6,4},{5,7},{7,5},{8,10},{10,8},{9,1... | collective-permute-start | bytes 393224 | tf_op jit(solution)/shard_map/ppermute | solution.py:163
  26.9 3.1 %collective-permute-done.6 = bf16[4,128,128]{2,1,0:T(8,128)(2,1)S(1)} collective-permute-done((bf16[4,128,128]{2,1,0:T(8,128)(2,1)S(1)}, bf16[4,128,128]{2,1,0:T(8,128)(2,1)S(1)}, u32[]{:S(2)}, u32[]{:S(2)}) %collective-permute-start.6) | collective-permute-done | bytes 131104 | tf_op jit(solution)/shard_map/ppermute | solution.py:163
  30.0 0.7 %collective-permute-start.8 = (bf16[4,128,128]{2,1,0:T(8,128)(2,1)S(1)}, bf16[4,128,128]{2,1,0:T(8,128)(2,1)S(1)}, u32[]{:S(2)}, u32[]{:S(2)}) collective-permute-start(bf16[4,128,128]{2,1,0:T(8,128)(2,1)S(1)} %add_convert_fusion.1), channel_id=1, source_target_pairs={{0,4},{4,8},{8,12},{12,0},{1,5},{5,9},{9,13},{13,1},{2,6},{6,10},{... | collective-permute-start | bytes 393224 | tf_op jit(solution)/shard_map/ppermute | solution.py:163
  30.7 0.0 collective-permute-done.5
  30.7 3.2 %collective-permute-start.9 = (bf16[4,128,128]{2,1,0:T(8,128)(2,1)S(1)}, bf16[4,128,128]{2,1,0:T(8,128)(2,1)S(1)}, u32[]{:S(2)}, u32[]{:S(2)}) collective-permute-start(bf16[4,128,128]{2,1,0:T(8,128)(2,1)S(1)} %add_convert_fusion), channel_id=1, source_target_pairs={{0,12},{4,0},{8,4},{12,8},{1,13},{5,1},{9,5},{13,9},{2,14},{6,2},{... | collective-permute-start | bytes 393224 | tf_op jit(solution)/shard_map/ppermute | solution.py:163
  33.9 0.0 collective-permute-done.4
  34.0 0.9 %collective-permute-done.7 = bf16[4,128,128]{2,1,0:T(8,128)(2,1)S(1)} collective-permute-done((bf16[4,128,128]{2,1,0:T(8,128)(2,1)S(1)}, bf16[4,128,128]{2,1,0:T(8,128)(2,1)S(1)}, u32[]{:S(2)}, u32[]{:S(2)}) %collective-permute-start.7) | collective-permute-done | bytes 131104 | tf_op jit(solution)/shard_map/ppermute | solution.py:163
  34.9 2.0 %collective-permute-done.8 = bf16[4,128,128]{2,1,0:T(8,128)(2,1)S(1)} collective-permute-done((bf16[4,128,128]{2,1,0:T(8,128)(2,1)S(1)}, bf16[4,128,128]{2,1,0:T(8,128)(2,1)S(1)}, u32[]{:S(2)}, u32[]{:S(2)}) %collective-permute-start.8) | collective-permute-done | bytes 131104 | tf_op jit(solution)/shard_map/ppermute | solution.py:163
  37.0 0.5 %collective-permute-done.9 = bf16[4,128,128]{2,1,0:T(8,128)(2,1)S(1)} collective-permute-done((bf16[4,128,128]{2,1,0:T(8,128)(2,1)S(1)}, bf16[4,128,128]{2,1,0:T(8,128)(2,1)S(1)}, u32[]{:S(2)}, u32[]{:S(2)}) %collective-permute-start.9) | collective-permute-done | bytes 131104 | tf_op jit(solution)/shard_map/ppermute | solution.py:163
  37.4 0.7 %convert_add_fusion = f32[4,128,128]{2,1,0:T(8,128)} fusion(f32[4,128,128]{2,1,0:T(8,128)S(1)} %convert_add_fusion.1, bf16[4,128,128]{2,1,0:T(8,128)(2,1)S(1)} %collective-permute-done.9), kind=kLoop, calls=%fused_computation | loop fusion | flops 131072 | bytes 655360 | tf_op jit(solution)/shard_map/add | solution.py:194
  (7 shorter events, 0.2 us)
Async XLA Ops:
  0.7 12.6 %collective-permute-start.2 = (f32[4,32]{1,0:T(4,128)S(1)}, f32[4,32]{1,0:T(4,128)S(1)}, u32[]{:S(2)}, u32[]{:S(2)}) collective-permute-start(f32[4,32]{1,0:T(4,128)S(1)} %select_bitcast_fusion), channel_id=1, source_target_pairs={{0,4},{4,8},{8,12},{12,0},{1,5},{5,9},{9,13},{13,1},{2,6},{6,10},{... | collective-permute-start | bytes 1544 | tf_op jit(solution)/shard_map/ppermute | solution.py:163
  3.7 9.6 %collective-permute-start.1 = (f32[4,32]{1,0:T(4,128)S(1)}, f32[4,32]{1,0:T(4,128)S(1)}, u32[]{:S(2)}, u32[]{:S(2)}) collective-permute-start(f32[4,32]{1,0:T(4,128)S(1)} %select_bitcast_fusion), channel_id=1, source_target_pairs={{0,8},{4,12},{8,0},{12,4},{1,9},{5,13},{9,1},{13,5},{2,10},{6,14},... | collective-permute-start | bytes 1544 | tf_op jit(solution)/shard_map/ppermute | solution.py:163
  6.3 7.0 %collective-permute-start = (f32[4,32]{1,0:T(4,128)S(1)}, f32[4,32]{1,0:T(4,128)S(1)}, u32[]{:S(2)}, u32[]{:S(2)}) collective-permute-start(f32[4,32]{1,0:T(4,128)S(1)} %select_bitcast_fusion), channel_id=1, source_target_pairs={{0,12},{4,0},{8,4},{12,8},{1,13},{5,1},{9,5},{13,9},{2,14},{6,2},{... | collective-permute-start | bytes 1544 | tf_op jit(solution)/shard_map/ppermute | solution.py:163
  18.4 6.5 %collective-permute-start.3 = (bf16[4,128,128]{2,1,0:T(8,128)(2,1)S(1)}, bf16[4,128,128]{2,1,0:T(8,128)(2,1)S(1)}, u32[]{:S(2)}, u32[]{:S(2)}) collective-permute-start(bf16[4,128,128]{2,1,0:T(8,128)(2,1)S(1)} %get-tuple-element.20), channel_id=1, source_target_pairs={{0,2},{2,0},{1,3},{3,1},{4,6},{6,4},{5,7},{7,5},{8,10},{10,8},{9,1... | collective-permute-start | bytes 393224 | tf_op jit(solution)/shard_map/ppermute | solution.py:163
  20.0 10.7 %collective-permute-start.5 = (bf16[4,128,128]{2,1,0:T(8,128)(2,1)S(1)}, bf16[4,128,128]{2,1,0:T(8,128)(2,1)S(1)}, u32[]{:S(2)}, u32[]{:S(2)}) collective-permute-start(bf16[4,128,128]{2,1,0:T(8,128)(2,1)S(1)} %get-tuple-element.22), channel_id=1, source_target_pairs={{0,2},{2,0},{1,3},{3,1},{4,6},{6,4},{5,7},{7,5},{8,10},{10,8},{9,1... | collective-permute-start | bytes 393224 | tf_op jit(solution)/shard_map/ppermute | solution.py:163
  20.5 9.4 %collective-permute-start.6 = (bf16[4,128,128]{2,1,0:T(8,128)(2,1)S(1)}, bf16[4,128,128]{2,1,0:T(8,128)(2,1)S(1)}, u32[]{:S(2)}, u32[]{:S(2)}) collective-permute-start(bf16[4,128,128]{2,1,0:T(8,128)(2,1)S(1)} %get-tuple-element.23), channel_id=1, source_target_pairs={{0,2},{2,0},{1,3},{3,1},{4,6},{6,4},{5,7},{7,5},{8,10},{10,8},{9,1... | collective-permute-start | bytes 393224 | tf_op jit(solution)/shard_map/ppermute | solution.py:163
  25.0 9.9 %collective-permute-start.7 = (bf16[4,128,128]{2,1,0:T(8,128)(2,1)S(1)}, bf16[4,128,128]{2,1,0:T(8,128)(2,1)S(1)}, u32[]{:S(2)}, u32[]{:S(2)}) collective-permute-start(bf16[4,128,128]{2,1,0:T(8,128)(2,1)S(1)} %add_convert_fusion.2), channel_id=1, source_target_pairs={{0,8},{4,12},{8,0},{12,4},{1,9},{5,13},{9,1},{13,5},{2,10},{6,14},... | collective-permute-start | bytes 393224 | tf_op jit(solution)/shard_map/ppermute | solution.py:163
  25.1 8.8 %collective-permute-start.4 = (bf16[4,128,128]{2,1,0:T(8,128)(2,1)S(1)}, bf16[4,128,128]{2,1,0:T(8,128)(2,1)S(1)}, u32[]{:S(2)}, u32[]{:S(2)}) collective-permute-start(bf16[4,128,128]{2,1,0:T(8,128)(2,1)S(1)} %get-tuple-element.21), channel_id=1, source_target_pairs={{0,2},{2,0},{1,3},{3,1},{4,6},{6,4},{5,7},{7,5},{8,10},{10,8},{9,1... | collective-permute-start | bytes 393224 | tf_op jit(solution)/shard_map/ppermute | solution.py:163
  30.0 7.0 %collective-permute-start.8 = (bf16[4,128,128]{2,1,0:T(8,128)(2,1)S(1)}, bf16[4,128,128]{2,1,0:T(8,128)(2,1)S(1)}, u32[]{:S(2)}, u32[]{:S(2)}) collective-permute-start(bf16[4,128,128]{2,1,0:T(8,128)(2,1)S(1)} %add_convert_fusion.1), channel_id=1, source_target_pairs={{0,4},{4,8},{8,12},{12,0},{1,5},{5,9},{9,13},{13,1},{2,6},{6,10},{... | collective-permute-start | bytes 393224 | tf_op jit(solution)/shard_map/ppermute | solution.py:163
  30.7 6.7 %collective-permute-start.9 = (bf16[4,128,128]{2,1,0:T(8,128)(2,1)S(1)}, bf16[4,128,128]{2,1,0:T(8,128)(2,1)S(1)}, u32[]{:S(2)}, u32[]{:S(2)}) collective-permute-start(bf16[4,128,128]{2,1,0:T(8,128)(2,1)S(1)} %add_convert_fusion), channel_id=1, source_target_pairs={{0,12},{4,0},{8,4},{12,8},{1,13},{5,1},{9,5},{13,9},{2,14},{6,2},{... | collective-permute-start | bytes 393224 | tf_op jit(solution)/shard_map/ppermute | solution.py:163

commit v7 on v3

--- a/solution.py
+++ b/solution.py
@@ -10,6 +10,12 @@
 MIX_TERMS = 8
 SUM_TERMS = 4
 MIB = 1024 * 1024
+
+
+def wrapped(value, size):
+    if size & (size - 1) == 0:
+        return value & (size - 1)
+    return lax.rem(value + size, size)
 
 
 def mix_kernel(split, side_ref, wave_ref, left_ref, right_ref, mixed_ref, held_ref, wave, left, sems):
@@ -39,13 +45,17 @@
         ]
     else:
         right_copies = [pltpu.make_async_copy(right_ref, held_ref, sems.at[1])]
-    for copy in right_copies:
-        copy.start()
     wave_copy.wait()
 
     @pl.loop(0, chunks)
     def _(c):
         left_copy(c).wait()
+
+        @pl.when(c == 0)
+        def _():
+            for copy in right_copies:
+                copy.start()
+
         part = pl.ds(c * MIX_TERMS, MIX_TERMS)
         rows_in = left[part].reshape(MIX_TERMS * rows, width)
         for s in range(sec_dev):
@@ -84,14 +94,14 @@
     )
 
 
-def sum_kernel(split, base_ref, shift_ref, coef_ref, mixed_ref, held_ref, *refs):
+def sum_kernel(split, shift_ref, coef_ref, mixed_ref, held_ref, *refs):
     terms, sec_dev, rows, width = mixed_ref.shape
     targets = coef_ref.shape[0]
     half = width // 2
-    mine = refs[0]
-    mine[...] = jnp.zeros_like(mine)
-    if split:
-        theirs, total = refs[1:-1], refs[-1]
+    spill = sec_dev - 1
+    sums = refs[-2:] if split else refs[-1:]
+    outs = refs[: len(refs) - len(sums)]
+    for total in sums:
         total[...] = jnp.zeros_like(total)
 
     @pl.loop(0, terms // SUM_TERMS)
@@ -103,35 +113,41 @@
                 held_ref[k],
                 (((1,), (1,)), ((), ())),
                 preferred_element_type=jnp.float32,
+            ).reshape(sec_dev, rows, width)
+            first = wrapped(-shift_ref[k], targets)
+            scaled = jnp.stack(
+                [coef_ref[wrapped(first + s, targets), k] * product[s] for s in range(sec_dev)]
             )
-            for s in range(sec_dev):
-                target = lax.rem(base_ref[0] + s + targets - shift_ref[k], targets)
-                scaled = coef_ref[target, k] * product[s * rows : (s + 1) * rows]
-                if split:
-                    total[target] += scaled[:, :half]
-                    mine[target] += scaled[:, half:]
-                else:
-                    mine[target] += scaled
-
-    if split:
-        for g, out in enumerate(theirs):
-            out[...] = total[g * sec_dev : (g + 1) * sec_dev].astype(jnp.bfloat16)
-
-
-def summed(base, shift, coef, mixed, held, split):
+            place = pl.ds(first, sec_dev)
+            if split:
+                sums[0][place] += scaled[:, :, :half]
+                sums[1][place] += scaled[:, :, half:]
+            else:
+                sums[0][place] += scaled
+
+    for total in sums:
+        total[:spill] += total[targets:]
+    if split:
+        outs[0][...] = sums[1][:targets]
+        for g, out in enumerate(outs[1:]):
+            out[...] = sums[0][g * sec_dev : (g + 1) * sec_dev].astype(jnp.bfloat16)
+    else:
+        outs[0][...] = sums[0][:targets]
+
+
+def summed(shift, coef, mixed, held, split):
     k_dev, sec_dev, rows, width = mixed.shape
     targets = coef.shape[0]
-    if split:
-        out_shape = [pltpu.VMEM((targets, rows, width // 2), jnp.float32)]
-        out_shape += [pltpu.VMEM((sec_dev, rows, width // 2), jnp.bfloat16)] * (targets // sec_dev)
-        scratch = [pltpu.VMEM((targets, rows, width // 2), jnp.float32)]
-    else:
-        out_shape = [pltpu.VMEM((targets, rows, width), jnp.float32)]
-        scratch = []
+    columns = width // 2 if split else width
+    out_shape = [pltpu.VMEM((targets, rows, columns), jnp.float32)]
+    scratch = [pltpu.VMEM((targets + sec_dev - 1, rows, columns), jnp.float32)]
+    if split:
+        out_shape += [pltpu.VMEM((sec_dev, rows, columns), jnp.bfloat16)] * (targets // sec_dev)
+        scratch = scratch * 2
     return pl.pallas_call(
         functools.partial(sum_kernel, split),
         out_shape=out_shape,
-        in_specs=[pl.BlockSpec(memory_space=pltpu.SMEM)] * 3
+        in_specs=[pl.BlockSpec(memory_space=pltpu.SMEM)] * 2
         + [pl.BlockSpec(memory_space=pltpu.VMEM)] * 2,
         out_specs=[pl.BlockSpec(memory_space=pltpu.VMEM)] * len(out_shape),
         scratch_shapes=scratch,
@@ -142,8 +158,7 @@
             transcendentals=0,
         ),
     )(
-        base,
-        shift,
+        pltpu.with_memory_space_constraint(shift, pltpu.HBM),
         coef,
         pltpu.with_memory_space_constraint(mixed, pltpu.VMEM),
         pltpu.with_memory_space_constraint(held, pltpu.VMEM),
@@ -163,15 +178,14 @@
     sec_dev = wavefunction.shape[0]
     devices = lax.axis_size("sector")
     live = jnp.where(coupled.T > 0, site_coef.T, 0.0)
-    shift = lax.rem(sector_shift, sec_dev * devices)
     side = jnp.reshape(lax.axis_index("op"), (1,)).astype(jnp.int32)
-    me = lax.axis_index("sector")
-
-    if lax.axis_size("op") == 2 and devices <= 4:
+    split = lax.axis_size("op") == 2 and devices <= 4
+
+    if split:
         coefs = [live] + [shift_by(live, "sector", -g) for g in range(1, devices)]
+        coef = jnp.concatenate(coefs, axis=0)
         mixed, held = mix(side, wavefunction, left_ops, right_ops, True)
-        base = jnp.zeros((1,), jnp.int32)
-        mine, *theirs = summed(base, shift, jnp.concatenate(coefs, axis=0), mixed, held, True)
+        mine, *theirs = summed(sector_shift, coef, mixed, held, True)
         mine = [mine[g * sec_dev : (g + 1) * sec_dev] for g in range(devices)]
         order = sorted(range(1, devices), key=lambda g: abs(2 * g - devices))
         crossed = {g: shift_by(theirs[g], "op", 1) for g in order}
@@ -182,15 +196,16 @@
             if not arrived:
                 theirs[0] = after(theirs[0], both)
             arrived.append(shift_by(both, "sector", g))
-        sigma = mine[0] + shift_by(theirs[0], "op", 1).astype(jnp.float32)
+        sigma = mine[0] + after(shift_by(theirs[0], "op", 1), both).astype(jnp.float32)
         for other in arrived:
-            sigma = sigma + other.astype(jnp.float32)
+            sigma = lax.optimization_barrier(sigma) + other.astype(jnp.float32)
         return sigma
 
-    coef = lax.all_gather(live, "sector", axis=0, tiled=True)
+    first = lax.axis_index("sector") * sec_dev
+    coef = jnp.roll(lax.all_gather(live, "sector", axis=0, tiled=True), -first, axis=0)
     mixed, held = mix(side, wavefunction, left_ops, right_ops, False)
-    base = jnp.reshape(me * sec_dev, (1,)).astype(jnp.int32)
-    (total,) = summed(base, shift, coef, mixed, held, False)
+    (total,) = summed(sector_shift, coef, mixed, held, False)
+    total = jnp.roll(total, first, axis=0)
     total = lax.psum_scatter(total, "op", scatter_dimension=2, tiled=True)
     return lax.psum_scatter(total, "sector", scatter_dimension=0, tiled=True)
 

time: 36.5 us -> 37.3 us (1.022)
  starting transfers between devices: 15 us -> 16.4 us
  other arithmetic: 2.26 us -> 1.65 us
  Pallas kernels: 9.19 us -> 9.67 us
  waiting for transfers between devices: 9.84 us -> 9.39 us
    ppermute x10, starting transfers between devices: 15 us -> 16.4 us  [shift_by(): lax.ppermute(value, axis, [(i, (i + distance) % size) for i in range(size)])]
    rem x1 -> x0, other arithmetic: 0.66 us -> none  [per_device(): shift = lax.rem(sector_shift, sec_dev * devices)]
    pallas_call x1, Pallas kernels: 5.08 us -> 5.57 us  [summed(): pl.pallas_call(functools.partial(sum_kernel, split), out_shape=out_shape,...]
    ppermute x10, waiting for transfers between devices: 9.84 us -> 9.39 us  [shift_by(): lax.ppermute(value, axis, [(i, (i + distance) % size) for i in range(size)])]
    add x1 -> x4, other arithmetic: 0.78 us -> 0.82 us  [the longest x3 0.79 us: per_device(): sigma = lax.optimization_barrier(sigma) + other.astype(jnp.float32)]
  transfers between devices with their start and end apart: 10 -> 10, of which waited for: 5 -> 5; matrix products, arithmetic and copies ran while one was open for 2% -> 1% of each run, Pallas kernels for 11% -> 11%
where the time goes in v7:
time: 37.3 us; the launch traced here: 37.1 us
  starting transfers between devices  16.4 us (44%)
  Pallas kernels  9.67 us (26%)
  waiting for transfers between devices  9.39 us (25%)
  other arithmetic  1.65 us (4%)
    ppermute x10, starting transfers between devices, shift_by(): lax.ppermute(value, axis, [(i, (i + distance) % size) for i in range(size)])  16.4 us
    ppermute x10, waiting for transfers between devices, shift_by(): lax.ppermute(value, axis, [(i, (i + distance) % size) for i in range(size)])  9.39 us
    pallas_call x1, Pallas kernels, summed(): pl.pallas_call(functools.partial(sum_kernel, split), out_shape=out_shape,...  5.57 us
    pallas_call x1, Pallas kernels, mix(): pl.pallas_call(functools.partial(mix_kernel, split), out_shape=[pltpu.VME...  4.11 us
    add x3, other arithmetic, per_device(): sigma = lax.optimization_barrier(sigma) + other.astype(jnp.float32)  0.79 us
  transfers between devices with their start and end apart: 10, of which 5 were waited for; matrix products, arithmetic and copies ran while one was open for 1% of the time, Pallas kernels for 11%

profile of v7, /device:TPU:0, one launch (start us, length us, event | category | flops | bytes accessed | tf_op | source)
XLA Modules:
  0.0 37.1 jit_solution(9566522862557593263)
XLA Ops:
  0.0 0.7 %select_bitcast_fusion = f32[4,32]{1,0:T(4,128)S(1)} fusion(f32[32,4]{0,1:T(4,128)} %param.9, s32[32,4]{0,1:T(4,128)} %param.10), kind=kLoop, calls=%fused_computation.8 | loop fusion | flops 256 | bytes 1536 | tf_op jit(solution)/shard_map/jit(_where)/select_n | solution.py:180
  0.7 3.0 %collective-permute-start.2 = (f32[4,32]{1,0:T(4,128)S(1)}, f32[4,32]{1,0:T(4,128)S(1)}, u32[]{:S(2)}, u32[]{:S(2)}) collective-permute-start(f32[4,32]{1,0:T(4,128)S(1)} %select_bitcast_fusion), channel_id=1, source_target_pairs={{0,4},{4,8},{8,12},{12,0},{1,5},{5,9},{9,13},{13,1},{2,6},{6,10},{... | collective-permute-start | bytes 1544 | tf_op jit(solution)/shard_map/ppermute | solution.py:170
  3.7 2.6 %collective-permute-start.1 = (f32[4,32]{1,0:T(4,128)S(1)}, f32[4,32]{1,0:T(4,128)S(1)}, u32[]{:S(2)}, u32[]{:S(2)}) collective-permute-start(f32[4,32]{1,0:T(4,128)S(1)} %select_bitcast_fusion), channel_id=1, source_target_pairs={{0,8},{4,12},{8,0},{12,4},{1,9},{5,13},{9,1},{13,5},{2,10},{6,14},... | collective-permute-start | bytes 1544 | tf_op jit(solution)/shard_map/ppermute | solution.py:170
  6.3 1.3 %collective-permute-start = (f32[4,32]{1,0:T(4,128)S(1)}, f32[4,32]{1,0:T(4,128)S(1)}, u32[]{:S(2)}, u32[]{:S(2)}) collective-permute-start(f32[4,32]{1,0:T(4,128)S(1)} %select_bitcast_fusion), channel_id=1, source_target_pairs={{0,12},{4,0},{8,4},{12,8},{1,13},{5,1},{9,5},{13,9},{2,14},{6,2},{... | collective-permute-start | bytes 1544 | tf_op jit(solution)/shard_map/ppermute | solution.py:170
  7.7 4.1 %shard_map.64 = (bf16[32,4,128,256]{3,2,1,0:T(8,128)(2,1)S(1)}, bf16[32,256,256]{2,1,0:T(8,128)(2,1)S(1)}) custom-call(s32[1]{0:T(128)} %bitcast.1.side_ref, bf16[4,256,256]{2,1,0:T(8,128)(2,1)} %wave_ref.1, bf16[32,128,256]{2,1,0:T(8,128)(2,1)} %left_ref.1, bf16[32,256,256]{2,1,0:T(8,128)(2,1)} %right_ref.1), custom_call_target="tpu_custom_call" | custom-call | flops 2147483648 | bytes 6291456 | tf_op jit(solution)/shard_map/pallas_call | solution.py:72
  11.8 0.0 collective-permute-done.2
  11.8 0.0 collective-permute-done.1
  11.8 0.0 collective-permute-done
  11.8 5.6 %shard_map.65 = (f32[16,128,128]{2,1,0:T(8,128)S(1)}, bf16[4,128,128]{2,1,0:T(8,128)(2,1)S(1)}, bf16[4,128,128]{2,1,0:T(8,128)(2,1)S(1)}, bf16[4,128,128]{2,1,0:T(8,128)(2,1)S(1)}, bf16[4,128,128]{2,1,0:T(8,128)(2,1)S(1)}) custom-call(s32[32]{0:T(128)} %shift_ref.1, f32[16,32]{1,0:T(8,128)S(1)} %pad_maximum_fusion.coef_ref, ...), custom_call_target="tpu_custom_call" | custom-call | flops 2147483648 | bytes 12582912 | tf_op jit(solution)/shard_map/pallas_call | solution.py:147
  17.4 1.6 %collective-permute-start.3 = (bf16[4,128,128]{2,1,0:T(8,128)(2,1)S(1)}, bf16[4,128,128]{2,1,0:T(8,128)(2,1)S(1)}, u32[]{:S(2)}, u32[]{:S(2)}) collective-permute-start(bf16[4,128,128]{2,1,0:T(8,128)(2,1)S(1)} %get-tuple-element.20), channel_id=1, source_target_pairs={{0,2},{2,0},{1,3},{3,1},{4,6},{6,4},{5,7},{7,5},{8,10},{10,8},{9,1... | collective-permute-start | bytes 393224 | tf_op jit(solution)/shard_map/ppermute | solution.py:170
  19.0 0.5 %collective-permute-start.5 = (bf16[4,128,128]{2,1,0:T(8,128)(2,1)S(1)}, bf16[4,128,128]{2,1,0:T(8,128)(2,1)S(1)}, u32[]{:S(2)}, u32[]{:S(2)}) collective-permute-start(bf16[4,128,128]{2,1,0:T(8,128)(2,1)S(1)} %get-tuple-element.22), channel_id=1, source_target_pairs={{0,2},{2,0},{1,3},{3,1},{4,6},{6,4},{5,7},{7,5},{8,10},{10,8},{9,1... | collective-permute-start | bytes 393224 | tf_op jit(solution)/shard_map/ppermute | solution.py:170
  19.5 1.5 %collective-permute-start.6 = (bf16[4,128,128]{2,1,0:T(8,128)(2,1)S(1)}, bf16[4,128,128]{2,1,0:T(8,128)(2,1)S(1)}, u32[]{:S(2)}, u32[]{:S(2)}) collective-permute-start(bf16[4,128,128]{2,1,0:T(8,128)(2,1)S(1)} %get-tuple-element.23), channel_id=1, source_target_pairs={{0,2},{2,0},{1,3},{3,1},{4,6},{6,4},{5,7},{7,5},{8,10},{10,8},{9,1... | collective-permute-start | bytes 393224 | tf_op jit(solution)/shard_map/ppermute | solution.py:170
  21.0 2.9 %collective-permute-done.3 = bf16[4,128,128]{2,1,0:T(8,128)(2,1)S(1)} collective-permute-done((bf16[4,128,128]{2,1,0:T(8,128)(2,1)S(1)}, bf16[4,128,128]{2,1,0:T(8,128)(2,1)S(1)}, u32[]{:S(2)}, u32[]{:S(2)}) %collective-permute-start.3) | collective-permute-done | bytes 131104 | tf_op jit(solution)/shard_map/ppermute | solution.py:170
  23.9 0.2 collective-permute-start.7
  24.1 1.7 %collective-permute-start.4 = (bf16[4,128,128]{2,1,0:T(8,128)(2,1)S(1)}, bf16[4,128,128]{2,1,0:T(8,128)(2,1)S(1)}, u32[]{:S(2)}, u32[]{:S(2)}) collective-permute-start(bf16[4,128,128]{2,1,0:T(8,128)(2,1)S(1)} %get-tuple-element.21), channel_id=1, source_target_pairs={{0,2},{2,0},{1,3},{3,1},{4,6},{6,4},{5,7},{7,5},{8,10},{10,8},{9,1... | collective-permute-start | bytes 393224 | tf_op jit(solution)/shard_map/ppermute | solution.py:170
  25.8 3.1 %collective-permute-done.6 = bf16[4,128,128]{2,1,0:T(8,128)(2,1)S(1)} collective-permute-done((bf16[4,128,128]{2,1,0:T(8,128)(2,1)S(1)}, bf16[4,128,128]{2,1,0:T(8,128)(2,1)S(1)}, u32[]{:S(2)}, u32[]{:S(2)}) %collective-permute-start.6) | collective-permute-done | bytes 131104 | tf_op jit(solution)/shard_map/ppermute | solution.py:170
  28.9 0.7 %collective-permute-start.8 = (bf16[4,128,128]{2,1,0:T(8,128)(2,1)S(1)}, bf16[4,128,128]{2,1,0:T(8,128)(2,1)S(1)}, u32[]{:S(2)}, u32[]{:S(2)}) collective-permute-start(bf16[4,128,128]{2,1,0:T(8,128)(2,1)S(1)} %add_convert_fusion.1), channel_id=1, source_target_pairs={{0,4},{4,8},{8,12},{12,0},{1,5},{5,9},{9,13},{13,1},{2,6},{6,10},{... | collective-permute-start | bytes 393224 | tf_op jit(solution)/shard_map/ppermute | solution.py:170
  29.7 0.0 collective-permute-done.5
  29.7 3.2 %collective-permute-start.9 = (bf16[4,128,128]{2,1,0:T(8,128)(2,1)S(1)}, bf16[4,128,128]{2,1,0:T(8,128)(2,1)S(1)}, u32[]{:S(2)}, u32[]{:S(2)}) collective-permute-start(bf16[4,128,128]{2,1,0:T(8,128)(2,1)S(1)} %add_convert_fusion), channel_id=1, source_target_pairs={{0,12},{4,0},{8,4},{12,8},{1,13},{5,1},{9,5},{13,9},{2,14},{6,2},{... | collective-permute-start | bytes 393224 | tf_op jit(solution)/shard_map/ppermute | solution.py:170
  32.9 0.0 collective-permute-done.4
  32.9 0.9 %collective-permute-done.7 = bf16[4,128,128]{2,1,0:T(8,128)(2,1)S(1)} collective-permute-done((bf16[4,128,128]{2,1,0:T(8,128)(2,1)S(1)}, bf16[4,128,128]{2,1,0:T(8,128)(2,1)S(1)}, u32[]{:S(2)}, u32[]{:S(2)}) %collective-permute-start.7) | collective-permute-done | bytes 131104 | tf_op jit(solution)/shard_map/ppermute | solution.py:170
  33.9 2.0 %collective-permute-done.8 = bf16[4,128,128]{2,1,0:T(8,128)(2,1)S(1)} collective-permute-done((bf16[4,128,128]{2,1,0:T(8,128)(2,1)S(1)}, bf16[4,128,128]{2,1,0:T(8,128)(2,1)S(1)}, u32[]{:S(2)}, u32[]{:S(2)}) %collective-permute-start.8) | collective-permute-done | bytes 131104 | tf_op jit(solution)/shard_map/ppermute | solution.py:170
  35.9 0.5 %collective-permute-done.9 = bf16[4,128,128]{2,1,0:T(8,128)(2,1)S(1)} collective-permute-done((bf16[4,128,128]{2,1,0:T(8,128)(2,1)S(1)}, bf16[4,128,128]{2,1,0:T(8,128)(2,1)S(1)}, u32[]{:S(2)}, u32[]{:S(2)}) %collective-permute-start.9) | collective-permute-done | bytes 131104 | tf_op jit(solution)/shard_map/ppermute | solution.py:170
  36.4 0.7 %convert_add_fusion = f32[4,128,128]{2,1,0:T(8,128)} fusion(f32[4,128,128]{2,1,0:T(8,128)S(1)} %convert_add_fusion.1, bf16[4,128,128]{2,1,0:T(8,128)(2,1)S(1)} %collective-permute-done.9), kind=kLoop, calls=%fused_computation | loop fusion | flops 131072 | bytes 655360 | tf_op jit(solution)/shard_map/add | solution.py:201
  (7 shorter events, 0.2 us)
Async XLA Ops:
  0.7 11.1 %collective-permute-start.2 = (f32[4,32]{1,0:T(4,128)S(1)}, f32[4,32]{1,0:T(4,128)S(1)}, u32[]{:S(2)}, u32[]{:S(2)}) collective-permute-start(f32[4,32]{1,0:T(4,128)S(1)} %select_bitcast_fusion), channel_id=1, source_target_pairs={{0,4},{4,8},{8,12},{12,0},{1,5},{5,9},{9,13},{13,1},{2,6},{6,10},{... | collective-permute-start | bytes 1544 | tf_op jit(solution)/shard_map/ppermute | solution.py:170
  3.7 8.1 %collective-permute-start.1 = (f32[4,32]{1,0:T(4,128)S(1)}, f32[4,32]{1,0:T(4,128)S(1)}, u32[]{:S(2)}, u32[]{:S(2)}) collective-permute-start(f32[4,32]{1,0:T(4,128)S(1)} %select_bitcast_fusion), channel_id=1, source_target_pairs={{0,8},{4,12},{8,0},{12,4},{1,9},{5,13},{9,1},{13,5},{2,10},{6,14},... | collective-permute-start | bytes 1544 | tf_op jit(solution)/shard_map/ppermute | solution.py:170
  6.3 5.5 %collective-permute-start = (f32[4,32]{1,0:T(4,128)S(1)}, f32[4,32]{1,0:T(4,128)S(1)}, u32[]{:S(2)}, u32[]{:S(2)}) collective-permute-start(f32[4,32]{1,0:T(4,128)S(1)} %select_bitcast_fusion), channel_id=1, source_target_pairs={{0,12},{4,0},{8,4},{12,8},{1,13},{5,1},{9,5},{13,9},{2,14},{6,2},{... | collective-permute-start | bytes 1544 | tf_op jit(solution)/shard_map/ppermute | solution.py:170
  17.4 6.5 %collective-permute-start.3 = (bf16[4,128,128]{2,1,0:T(8,128)(2,1)S(1)}, bf16[4,128,128]{2,1,0:T(8,128)(2,1)S(1)}, u32[]{:S(2)}, u32[]{:S(2)}) collective-permute-start(bf16[4,128,128]{2,1,0:T(8,128)(2,1)S(1)} %get-tuple-element.20), channel_id=1, source_target_pairs={{0,2},{2,0},{1,3},{3,1},{4,6},{6,4},{5,7},{7,5},{8,10},{10,8},{9,1... | collective-permute-start | bytes 393224 | tf_op jit(solution)/shard_map/ppermute | solution.py:170
  19.0 10.7 %collective-permute-start.5 = (bf16[4,128,128]{2,1,0:T(8,128)(2,1)S(1)}, bf16[4,128,128]{2,1,0:T(8,128)(2,1)S(1)}, u32[]{:S(2)}, u32[]{:S(2)}) collective-permute-start(bf16[4,128,128]{2,1,0:T(8,128)(2,1)S(1)} %get-tuple-element.22), channel_id=1, source_target_pairs={{0,2},{2,0},{1,3},{3,1},{4,6},{6,4},{5,7},{7,5},{8,10},{10,8},{9,1... | collective-permute-start | bytes 393224 | tf_op jit(solution)/shard_map/ppermute | solution.py:170
  19.5 9.4 %collective-permute-start.6 = (bf16[4,128,128]{2,1,0:T(8,128)(2,1)S(1)}, bf16[4,128,128]{2,1,0:T(8,128)(2,1)S(1)}, u32[]{:S(2)}, u32[]{:S(2)}) collective-permute-start(bf16[4,128,128]{2,1,0:T(8,128)(2,1)S(1)} %get-tuple-element.23), channel_id=1, source_target_pairs={{0,2},{2,0},{1,3},{3,1},{4,6},{6,4},{5,7},{7,5},{8,10},{10,8},{9,1... | collective-permute-start | bytes 393224 | tf_op jit(solution)/shard_map/ppermute | solution.py:170
  23.9 9.9 %collective-permute-start.7 = (bf16[4,128,128]{2,1,0:T(8,128)(2,1)S(1)}, bf16[4,128,128]{2,1,0:T(8,128)(2,1)S(1)}, u32[]{:S(2)}, u32[]{:S(2)}) collective-permute-start(bf16[4,128,128]{2,1,0:T(8,128)(2,1)S(1)} %add_convert_fusion.2), channel_id=1, source_target_pairs={{0,8},{4,12},{8,0},{12,4},{1,9},{5,13},{9,1},{13,5},{2,10},{6,14},... | collective-permute-start | bytes 393224 | tf_op jit(solution)/shard_map/ppermute | solution.py:170
  24.1 8.8 %collective-permute-start.4 = (bf16[4,128,128]{2,1,0:T(8,128)(2,1)S(1)}, bf16[4,128,128]{2,1,0:T(8,128)(2,1)S(1)}, u32[]{:S(2)}, u32[]{:S(2)}) collective-permute-start(bf16[4,128,128]{2,1,0:T(8,128)(2,1)S(1)} %get-tuple-element.21), channel_id=1, source_target_pairs={{0,2},{2,0},{1,3},{3,1},{4,6},{6,4},{5,7},{7,5},{8,10},{10,8},{9,1... | collective-permute-start | bytes 393224 | tf_op jit(solution)/shard_map/ppermute | solution.py:170
  28.9 7.0 %collective-permute-start.8 = (bf16[4,128,128]{2,1,0:T(8,128)(2,1)S(1)}, bf16[4,128,128]{2,1,0:T(8,128)(2,1)S(1)}, u32[]{:S(2)}, u32[]{:S(2)}) collective-permute-start(bf16[4,128,128]{2,1,0:T(8,128)(2,1)S(1)} %add_convert_fusion.1), channel_id=1, source_target_pairs={{0,4},{4,8},{8,12},{12,0},{1,5},{5,9},{9,13},{13,1},{2,6},{6,10},{... | collective-permute-start | bytes 393224 | tf_op jit(solution)/shard_map/ppermute | solution.py:170
  29.7 6.7 %collective-permute-start.9 = (bf16[4,128,128]{2,1,0:T(8,128)(2,1)S(1)}, bf16[4,128,128]{2,1,0:T(8,128)(2,1)S(1)}, u32[]{:S(2)}, u32[]{:S(2)}) collective-permute-start(bf16[4,128,128]{2,1,0:T(8,128)(2,1)S(1)} %add_convert_fusion), channel_id=1, source_target_pairs={{0,12},{4,0},{8,4},{12,8},{1,13},{5,1},{9,5},{13,9},{2,14},{6,2},{... | collective-permute-start | bytes 393224 | tf_op jit(solution)/shard_map/ppermute | solution.py:170

commit v8 on v7

--- a/solution.py
+++ b/solution.py
@@ -8,7 +8,7 @@
 from jax.sharding import PartitionSpec as P
 
 MIX_TERMS = 8
-SUM_TERMS = 4
+SUM_TERMS = 8
 MIB = 1024 * 1024
 
 
@@ -94,15 +94,12 @@
     )
 
 
-def sum_kernel(split, shift_ref, coef_ref, mixed_ref, held_ref, *refs):
+def sum_kernel(theirs, at, shift_ref, coef_ref, mixed_ref, held_ref, *refs):
     terms, sec_dev, rows, width = mixed_ref.shape
     targets = coef_ref.shape[0]
-    half = width // 2
-    spill = sec_dev - 1
-    sums = refs[-2:] if split else refs[-1:]
-    outs = refs[: len(refs) - len(sums)]
-    for total in sums:
-        total[...] = jnp.zeros_like(total)
+    total = refs[-1]
+    columns = total.shape[2]
+    total[...] = jnp.zeros_like(total)
 
     @pl.loop(0, terms // SUM_TERMS)
     def _(step):
@@ -110,42 +107,32 @@
             k = step * SUM_TERMS + t
             product = lax.dot_general(
                 mixed_ref[k].reshape(sec_dev * rows, width),
-                held_ref[k],
+                held_ref[k, at * columns : (at + 1) * columns],
                 (((1,), (1,)), ((), ())),
                 preferred_element_type=jnp.float32,
-            ).reshape(sec_dev, rows, width)
-            first = wrapped(-shift_ref[k], targets)
-            scaled = jnp.stack(
-                [coef_ref[wrapped(first + s, targets), k] * product[s] for s in range(sec_dev)]
             )
-            place = pl.ds(first, sec_dev)
-            if split:
-                sums[0][place] += scaled[:, :, :half]
-                sums[1][place] += scaled[:, :, half:]
-            else:
-                sums[0][place] += scaled
-
-    for total in sums:
-        total[:spill] += total[targets:]
-    if split:
-        outs[0][...] = sums[1][:targets]
-        for g, out in enumerate(outs[1:]):
-            out[...] = sums[0][g * sec_dev : (g + 1) * sec_dev].astype(jnp.bfloat16)
-    else:
-        outs[0][...] = sums[0][:targets]
-
-
-def summed(shift, coef, mixed, held, split):
+            for s in range(sec_dev):
+                target = wrapped(s - shift_ref[k], targets)
+                total[target] += coef_ref[target, k] * product[s * rows : (s + 1) * rows]
+
+    if theirs:
+        for g, out in enumerate(refs[:-1]):
+            out[...] = total[g * sec_dev : (g + 1) * sec_dev].astype(jnp.bfloat16)
+
+
+def summed(shift, coef, mixed, held, parts, at, theirs):
     k_dev, sec_dev, rows, width = mixed.shape
     targets = coef.shape[0]
-    columns = width // 2 if split else width
-    out_shape = [pltpu.VMEM((targets, rows, columns), jnp.float32)]
-    scratch = [pltpu.VMEM((targets + sec_dev - 1, rows, columns), jnp.float32)]
-    if split:
-        out_shape += [pltpu.VMEM((sec_dev, rows, columns), jnp.bfloat16)] * (targets // sec_dev)
-        scratch = scratch * 2
+    shape = (targets, rows, width // parts)
+    if theirs:
+        group = (sec_dev, rows, width // parts)
+        out_shape = [pltpu.VMEM(group, jnp.bfloat16)] * (targets // sec_dev)
+        scratch = [pltpu.VMEM(shape, jnp.float32)]
+    else:
+        out_shape = [pltpu.VMEM(shape, jnp.float32)]
+        scratch = []
     return pl.pallas_call(
-        functools.partial(sum_kernel, split),
+        functools.partial(sum_kernel, theirs, at),
         out_shape=out_shape,
         in_specs=[pl.BlockSpec(memory_space=pltpu.SMEM)] * 2
         + [pl.BlockSpec(memory_space=pltpu.VMEM)] * 2,
@@ -153,7 +140,7 @@
         scratch_shapes=scratch,
         compiler_params=pltpu.CompilerParams(vmem_limit_bytes=24 * MIB),
         cost_estimate=pl.CostEstimate(
-            flops=2 * k_dev * sec_dev * rows * width * width,
+            flops=2 * k_dev * sec_dev * rows * width * width // parts,
             bytes_accessed=2 * (mixed.size + held.size),
             transcendentals=0,
         ),
@@ -185,18 +172,18 @@
         coefs = [live] + [shift_by(live, "sector", -g) for g in range(1, devices)]
         coef = jnp.concatenate(coefs, axis=0)
         mixed, held = mix(side, wavefunction, left_ops, right_ops, True)
-        mine, *theirs = summed(sector_shift, coef, mixed, held, True)
+        theirs = summed(sector_shift, coef, mixed, held, 2, 0, True)
+        far, *near = sorted(range(1, devices), key=lambda g: abs(2 * g - devices))
+        crossed = shift_by(theirs[far], "op", 1)
+        (mine,) = summed(sector_shift, after(coef, theirs[far]), mixed, held, 2, 1, False)
         mine = [mine[g * sec_dev : (g + 1) * sec_dev] for g in range(devices)]
-        order = sorted(range(1, devices), key=lambda g: abs(2 * g - devices))
-        crossed = {g: shift_by(theirs[g], "op", 1) for g in order}
-        arrived, both = [], None
-        for g in order:
-            other = crossed[g] if both is None else after(crossed[g], both)
-            both = (mine[g] + other.astype(jnp.float32)).astype(jnp.bfloat16)
-            if not arrived:
-                theirs[0] = after(theirs[0], both)
+        both = (mine[far] + crossed.astype(jnp.float32)).astype(jnp.bfloat16)
+        arrived = [shift_by(both, "sector", far)]
+        crossed = {g: shift_by(after(theirs[g], both), "op", 1) for g in near + [0]}
+        for g in near:
+            both = (mine[g] + after(crossed[g], both).astype(jnp.float32)).astype(jnp.bfloat16)
             arrived.append(shift_by(both, "sector", g))
-        sigma = mine[0] + after(shift_by(theirs[0], "op", 1), both).astype(jnp.float32)
+        sigma = mine[0] + after(crossed[0], both).astype(jnp.float32)
         for other in arrived:
             sigma = lax.optimization_barrier(sigma) + other.astype(jnp.float32)
         return sigma
@@ -204,7 +191,7 @@
     first = lax.axis_index("sector") * sec_dev
     coef = jnp.roll(lax.all_gather(live, "sector", axis=0, tiled=True), -first, axis=0)
     mixed, held = mix(side, wavefunction, left_ops, right_ops, False)
-    (total,) = summed(sector_shift, coef, mixed, held, False)
+    (total,) = summed(sector_shift, coef, mixed, held, 1, 0, False)
     total = jnp.roll(total, first, axis=0)
     total = lax.psum_scatter(total, "op", scatter_dimension=2, tiled=True)
     return lax.psum_scatter(total, "sector", scatter_dimension=0, tiled=True)

time: 37.3 us -> 37 us (level)
  Pallas kernels: 9.67 us -> 11.8 us
  starting transfers between devices: 16.4 us -> 14.5 us
  waiting for transfers between devices: 9.39 us -> 8.79 us
    pallas_call x1 -> x2, Pallas kernels: 5.57 us -> 7.67 us  [summed(): pl.pallas_call(functools.partial(sum_kernel, theirs, at), out_shape=out_s...]
    ppermute x10, starting transfers between devices: 16.4 us -> 14.5 us  [shift_by(): lax.ppermute(value, axis, [(i, (i + distance) % size) for i in range(size)])]
    ppermute x10, waiting for transfers between devices: 9.39 us -> 8.79 us  [shift_by(): lax.ppermute(value, axis, [(i, (i + distance) % size) for i in range(size)])]
  transfers between devices with their start and end apart: 10 -> 10, of which waited for: 5 -> 4; matrix products, arithmetic and copies ran while one was open for 1% -> 0% of each run, Pallas kernels for 11% -> 21%
where the time goes in v8:
time: 37 us; the launch traced here: 36.8 us
  starting transfers between devices  14.5 us (39%)
  Pallas kernels  11.8 us (32%)
  waiting for transfers between devices  8.79 us (24%)
  other arithmetic  1.65 us (4%)
    ppermute x10, starting transfers between devices, shift_by(): lax.ppermute(value, axis, [(i, (i + distance) % size) for i in range(size)])  14.5 us
    ppermute x10, waiting for transfers between devices, shift_by(): lax.ppermute(value, axis, [(i, (i + distance) % size) for i in range(size)])  8.79 us
    pallas_call x2, Pallas kernels, summed(): pl.pallas_call(functools.partial(sum_kernel, theirs, at), out_shape=out_s...  7.67 us
    pallas_call x1, Pallas kernels, mix(): pl.pallas_call(functools.partial(mix_kernel, split), out_shape=[pltpu.VME...  4.11 us
    add x3, other arithmetic, per_device(): sigma = lax.optimization_barrier(sigma) + other.astype(jnp.float32)  0.8 us
  transfers between devices with their start and end apart: 10, of which 4 were waited for; matrix products, arithmetic and copies ran while one was open for 0% of the time, Pallas kernels for 21%

profile of v8, /device:TPU:0, one launch (start us, length us, event | category | flops | bytes accessed | tf_op | source)
XLA Modules:
  0.0 36.8 jit_solution(15079975443725977732)
XLA Ops:
  0.0 0.7 %select_bitcast_fusion = f32[4,32]{1,0:T(4,128)S(1)} fusion(f32[32,4]{0,1:T(4,128)} %param.9, s32[32,4]{0,1:T(4,128)} %param.10), kind=kLoop, calls=%fused_computation.11 | loop fusion | flops 256 | bytes 1536 | tf_op jit(solution)/shard_map/jit(_where)/select_n | solution.py:167
  0.7 3.0 %collective-permute-start.2 = (f32[4,32]{1,0:T(4,128)S(1)}, f32[4,32]{1,0:T(4,128)S(1)}, u32[]{:S(2)}, u32[]{:S(2)}) collective-permute-start(f32[4,32]{1,0:T(4,128)S(1)} %select_bitcast_fusion), channel_id=1, source_target_pairs={{0,4},{4,8},{8,12},{12,0},{1,5},{5,9},{9,13},{13,1},{2,6},{6,10},{... | collective-permute-start | bytes 1544 | tf_op jit(solution)/shard_map/ppermute | solution.py:157
  3.7 2.6 %collective-permute-start.1 = (f32[4,32]{1,0:T(4,128)S(1)}, f32[4,32]{1,0:T(4,128)S(1)}, u32[]{:S(2)}, u32[]{:S(2)}) collective-permute-start(f32[4,32]{1,0:T(4,128)S(1)} %select_bitcast_fusion), channel_id=1, source_target_pairs={{0,8},{4,12},{8,0},{12,4},{1,9},{5,13},{9,1},{13,5},{2,10},{6,14},... | collective-permute-start | bytes 1544 | tf_op jit(solution)/shard_map/ppermute | solution.py:157
  6.3 1.3 %collective-permute-start = (f32[4,32]{1,0:T(4,128)S(1)}, f32[4,32]{1,0:T(4,128)S(1)}, u32[]{:S(2)}, u32[]{:S(2)}) collective-permute-start(f32[4,32]{1,0:T(4,128)S(1)} %select_bitcast_fusion), channel_id=1, source_target_pairs={{0,12},{4,0},{8,4},{12,8},{1,13},{5,1},{9,5},{13,9},{2,14},{6,2},{... | collective-permute-start | bytes 1544 | tf_op jit(solution)/shard_map/ppermute | solution.py:157
  7.7 4.1 %shard_map.64 = (bf16[32,4,128,256]{3,2,1,0:T(8,128)(2,1)S(1)}, bf16[32,256,256]{2,1,0:T(8,128)(2,1)S(1)}) custom-call(s32[1]{0:T(128)} %bitcast.1.side_ref, bf16[4,256,256]{2,1,0:T(8,128)(2,1)} %wave_ref.1, bf16[32,128,256]{2,1,0:T(8,128)(2,1)} %left_ref.1, bf16[32,256,256]{2,1,0:T(8,128)(2,1)} %right_ref.1), custom_call_target="tpu_custom_call" | custom-call | flops 2147483648 | bytes 6291456 | tf_op jit(solution)/shard_map/pallas_call | solution.py:72
  11.8 0.0 collective-permute-done.2
  11.8 0.0 collective-permute-done.1
  11.8 0.0 collective-permute-done
  11.8 3.9 %shard_map.65 = (bf16[4,128,128]{2,1,0:T(8,128)(2,1)S(1)}, bf16[4,128,128]{2,1,0:T(8,128)(2,1)S(1)}, bf16[4,128,128]{2,1,0:T(8,128)(2,1)S(1)}, bf16[4,128,128]{2,1,0:T(8,128)(2,1)S(1)}) custom-call(s32[32]{0:T(128)} %shift_ref.3, f32[16,32]{1,0:T(8,128)S(1)} %pad_maximum_fusion.coef_ref, bf16[32,4,128,256]{3,2,1,0:T(8,128)(2,1)S(1)} %get-tuple-element.18.mixed_ref, ...), custom_call_target="tpu_custom_call" | custom-call | flops 1073741824 | bytes 12582912 | tf_op jit(solution)/shard_map/pallas_call | solution.py:134
  15.8 1.6 %collective-permute-start.3 = (bf16[4,128,128]{2,1,0:T(8,128)(2,1)S(1)}, bf16[4,128,128]{2,1,0:T(8,128)(2,1)S(1)}, u32[]{:S(2)}, u32[]{:S(2)}) collective-permute-start(bf16[4,128,128]{2,1,0:T(8,128)(2,1)S(1)} %get-tuple-element.20), channel_id=1, source_target_pairs={{0,2},{2,0},{1,3},{3,1},{4,6},{6,4},{5,7},{7,5},{8,10},{10,8},{9,1... | collective-permute-start | bytes 393224 | tf_op jit(solution)/shard_map/ppermute | solution.py:157
  17.3 3.8 %shard_map.66 = f32[16,128,128]{2,1,0:T(8,128)S(1)} custom-call(s32[32]{0:T(128)} %shift_ref.3, f32[16,32]{1,0:T(8,128)S(1)} %pad_maximum_fusion.coef_ref, bf16[32,4,128,256]{3,2,1,0:T(8,128)(2,1)S(1)} %get-tuple-element.18.mixed_ref, bf16[32,256,256]{2,1,0:T(8,128)(2,1)S(1)} %get-tuple-element.19.held_ref), custom_call_target="tpu_custom_call" | custom-call | flops 1073741824 | bytes 12582912 | tf_op jit(solution)/shard_map/pallas_call | solution.py:134
  21.1 0.0 collective-permute-done.3
  21.1 1.3 %collective-permute-start.6 = (bf16[4,128,128]{2,1,0:T(8,128)(2,1)S(1)}, bf16[4,128,128]{2,1,0:T(8,128)(2,1)S(1)}, u32[]{:S(2)}, u32[]{:S(2)}) collective-permute-start(bf16[4,128,128]{2,1,0:T(8,128)(2,1)S(1)} %get-tuple-element.27), channel_id=1, source_target_pairs={{0,2},{2,0},{1,3},{3,1},{4,6},{6,4},{5,7},{7,5},{8,10},{10,8},{9,1... | collective-permute-start | bytes 393224 | tf_op jit(solution)/shard_map/ppermute | solution.py:157
  22.4 0.3 collective-permute-start.7
  22.7 0.8 %collective-permute-start.4 = (bf16[4,128,128]{2,1,0:T(8,128)(2,1)S(1)}, bf16[4,128,128]{2,1,0:T(8,128)(2,1)S(1)}, u32[]{:S(2)}, u32[]{:S(2)}) collective-permute-start(bf16[4,128,128]{2,1,0:T(8,128)(2,1)S(1)} %get-tuple-element.23), channel_id=1, source_target_pairs={{0,2},{2,0},{1,3},{3,1},{4,6},{6,4},{5,7},{7,5},{8,10},{10,8},{9,1... | collective-permute-start | bytes 393224 | tf_op jit(solution)/shard_map/ppermute | solution.py:157
  23.6 1.2 %collective-permute-start.5 = (bf16[4,128,128]{2,1,0:T(8,128)(2,1)S(1)}, bf16[4,128,128]{2,1,0:T(8,128)(2,1)S(1)}, u32[]{:S(2)}, u32[]{:S(2)}) collective-permute-start(bf16[4,128,128]{2,1,0:T(8,128)(2,1)S(1)} %get-tuple-element.25), channel_id=1, source_target_pairs={{0,2},{2,0},{1,3},{3,1},{4,6},{6,4},{5,7},{7,5},{8,10},{10,8},{9,1... | collective-permute-start | bytes 393224 | tf_op jit(solution)/shard_map/ppermute | solution.py:157
  24.7 2.9 %collective-permute-done.6 = bf16[4,128,128]{2,1,0:T(8,128)(2,1)S(1)} collective-permute-done((bf16[4,128,128]{2,1,0:T(8,128)(2,1)S(1)}, bf16[4,128,128]{2,1,0:T(8,128)(2,1)S(1)}, u32[]{:S(2)}, u32[]{:S(2)}) %collective-permute-start.6) | collective-permute-done | bytes 131104 | tf_op jit(solution)/shard_map/ppermute | solution.py:157
  27.7 0.7 %collective-permute-start.8 = (bf16[4,128,128]{2,1,0:T(8,128)(2,1)S(1)}, bf16[4,128,128]{2,1,0:T(8,128)(2,1)S(1)}, u32[]{:S(2)}, u32[]{:S(2)}) collective-permute-start(bf16[4,128,128]{2,1,0:T(8,128)(2,1)S(1)} %fusion), channel_id=1, source_target_pairs={{0,4},{4,8},{8,12},{12,0},{1,5},{5,9},{9,13},{13,1},{2,6},{6,10},{... | collective-permute-start | bytes 393224 | tf_op jit(solution)/shard_map/ppermute | solution.py:157
  28.4 2.5 %collective-permute-done.5 = bf16[4,128,128]{2,1,0:T(8,128)(2,1)S(1)} collective-permute-done((bf16[4,128,128]{2,1,0:T(8,128)(2,1)S(1)}, bf16[4,128,128]{2,1,0:T(8,128)(2,1)S(1)}, u32[]{:S(2)}, u32[]{:S(2)}) %collective-permute-start.5) | collective-permute-done | bytes 131104 | tf_op jit(solution)/shard_map/ppermute | solution.py:157
  31.0 1.7 %collective-permute-start.9 = (bf16[4,128,128]{2,1,0:T(8,128)(2,1)S(1)}, bf16[4,128,128]{2,1,0:T(8,128)(2,1)S(1)}, u32[]{:S(2)}, u32[]{:S(2)}) collective-permute-start(bf16[4,128,128]{2,1,0:T(8,128)(2,1)S(1)} %fusion.1), channel_id=1, source_target_pairs={{0,12},{4,0},{8,4},{12,8},{1,13},{5,1},{9,5},{13,9},{2,14},{6,2},{... | collective-permute-start | bytes 393224 | tf_op jit(solution)/shard_map/ppermute | solution.py:157
  32.6 0.0 collective-permute-done.4
  32.7 0.0 collective-permute-done.7
  32.7 2.0 %collective-permute-done.8 = bf16[4,128,128]{2,1,0:T(8,128)(2,1)S(1)} collective-permute-done((bf16[4,128,128]{2,1,0:T(8,128)(2,1)S(1)}, bf16[4,128,128]{2,1,0:T(8,128)(2,1)S(1)}, u32[]{:S(2)}, u32[]{:S(2)}) %collective-permute-start.8) | collective-permute-done | bytes 131104 | tf_op jit(solution)/shard_map/ppermute | solution.py:157
  34.7 1.4 %collective-permute-done.9 = bf16[4,128,128]{2,1,0:T(8,128)(2,1)S(1)} collective-permute-done((bf16[4,128,128]{2,1,0:T(8,128)(2,1)S(1)}, bf16[4,128,128]{2,1,0:T(8,128)(2,1)S(1)}, u32[]{:S(2)}, u32[]{:S(2)}) %collective-permute-start.9) | collective-permute-done | bytes 131104 | tf_op jit(solution)/shard_map/ppermute | solution.py:157
  36.1 0.7 %convert_add_fusion = f32[4,128,128]{2,1,0:T(8,128)} fusion(f32[4,128,128]{2,1,0:T(8,128)S(1)} %convert_add_fusion.1, bf16[4,128,128]{2,1,0:T(8,128)(2,1)S(1)} %collective-permute-done.9), kind=kLoop, calls=%fused_computation.7 | loop fusion | flops 131072 | bytes 655360 | tf_op jit(solution)/shard_map/add | solution.py:188
  (7 shorter events, 0.2 us)
Async XLA Ops:
  0.7 11.1 %collective-permute-start.2 = (f32[4,32]{1,0:T(4,128)S(1)}, f32[4,32]{1,0:T(4,128)S(1)}, u32[]{:S(2)}, u32[]{:S(2)}) collective-permute-start(f32[4,32]{1,0:T(4,128)S(1)} %select_bitcast_fusion), channel_id=1, source_target_pairs={{0,4},{4,8},{8,12},{12,0},{1,5},{5,9},{9,13},{13,1},{2,6},{6,10},{... | collective-permute-start | bytes 1544 | tf_op jit(solution)/shard_map/ppermute | solution.py:157
  3.7 8.1 %collective-permute-start.1 = (f32[4,32]{1,0:T(4,128)S(1)}, f32[4,32]{1,0:T(4,128)S(1)}, u32[]{:S(2)}, u32[]{:S(2)}) collective-permute-start(f32[4,32]{1,0:T(4,128)S(1)} %select_bitcast_fusion), channel_id=1, source_target_pairs={{0,8},{4,12},{8,0},{12,4},{1,9},{5,13},{9,1},{13,5},{2,10},{6,14},... | collective-permute-start | bytes 1544 | tf_op jit(solution)/shard_map/ppermute | solution.py:157
  6.3 5.5 %collective-permute-start = (f32[4,32]{1,0:T(4,128)S(1)}, f32[4,32]{1,0:T(4,128)S(1)}, u32[]{:S(2)}, u32[]{:S(2)}) collective-permute-start(f32[4,32]{1,0:T(4,128)S(1)} %select_bitcast_fusion), channel_id=1, source_target_pairs={{0,12},{4,0},{8,4},{12,8},{1,13},{5,1},{9,5},{13,9},{2,14},{6,2},{... | collective-permute-start | bytes 1544 | tf_op jit(solution)/shard_map/ppermute | solution.py:157
  15.8 5.3 %collective-permute-start.3 = (bf16[4,128,128]{2,1,0:T(8,128)(2,1)S(1)}, bf16[4,128,128]{2,1,0:T(8,128)(2,1)S(1)}, u32[]{:S(2)}, u32[]{:S(2)}) collective-permute-start(bf16[4,128,128]{2,1,0:T(8,128)(2,1)S(1)} %get-tuple-element.20), channel_id=1, source_target_pairs={{0,2},{2,0},{1,3},{3,1},{4,6},{6,4},{5,7},{7,5},{8,10},{10,8},{9,1... | collective-permute-start | bytes 393224 | tf_op jit(solution)/shard_map/ppermute | solution.py:157
  21.1 6.5 %collective-permute-start.6 = (bf16[4,128,128]{2,1,0:T(8,128)(2,1)S(1)}, bf16[4,128,128]{2,1,0:T(8,128)(2,1)S(1)}, u32[]{:S(2)}, u32[]{:S(2)}) collective-permute-start(bf16[4,128,128]{2,1,0:T(8,128)(2,1)S(1)} %get-tuple-element.27), channel_id=1, source_target_pairs={{0,2},{2,0},{1,3},{3,1},{4,6},{6,4},{5,7},{7,5},{8,10},{10,8},{9,1... | collective-permute-start | bytes 393224 | tf_op jit(solution)/shard_map/ppermute | solution.py:157
  22.4 10.3 %collective-permute-start.7 = (bf16[4,128,128]{2,1,0:T(8,128)(2,1)S(1)}, bf16[4,128,128]{2,1,0:T(8,128)(2,1)S(1)}, u32[]{:S(2)}, u32[]{:S(2)}) collective-permute-start(bf16[4,128,128]{2,1,0:T(8,128)(2,1)S(1)} %fusion.2), channel_id=1, source_target_pairs={{0,8},{4,12},{8,0},{12,4},{1,9},{5,13},{9,1},{13,5},{2,10},{6,14},... | collective-permute-start | bytes 393224 | tf_op jit(solution)/shard_map/ppermute | solution.py:157
  22.7 9.9 %collective-permute-start.4 = (bf16[4,128,128]{2,1,0:T(8,128)(2,1)S(1)}, bf16[4,128,128]{2,1,0:T(8,128)(2,1)S(1)}, u32[]{:S(2)}, u32[]{:S(2)}) collective-permute-start(bf16[4,128,128]{2,1,0:T(8,128)(2,1)S(1)} %get-tuple-element.23), channel_id=1, source_target_pairs={{0,2},{2,0},{1,3},{3,1},{4,6},{6,4},{5,7},{7,5},{8,10},{10,8},{9,1... | collective-permute-start | bytes 393224 | tf_op jit(solution)/shard_map/ppermute | solution.py:157
  23.6 7.4 %collective-permute-start.5 = (bf16[4,128,128]{2,1,0:T(8,128)(2,1)S(1)}, bf16[4,128,128]{2,1,0:T(8,128)(2,1)S(1)}, u32[]{:S(2)}, u32[]{:S(2)}) collective-permute-start(bf16[4,128,128]{2,1,0:T(8,128)(2,1)S(1)} %get-tuple-element.25), channel_id=1, source_target_pairs={{0,2},{2,0},{1,3},{3,1},{4,6},{6,4},{5,7},{7,5},{8,10},{10,8},{9,1... | collective-permute-start | bytes 393224 | tf_op jit(solution)/shard_map/ppermute | solution.py:157
  27.7 7.0 %collective-permute-start.8 = (bf16[4,128,128]{2,1,0:T(8,128)(2,1)S(1)}, bf16[4,128,128]{2,1,0:T(8,128)(2,1)S(1)}, u32[]{:S(2)}, u32[]{:S(2)}) collective-permute-start(bf16[4,128,128]{2,1,0:T(8,128)(2,1)S(1)} %fusion), channel_id=1, source_target_pairs={{0,4},{4,8},{8,12},{12,0},{1,5},{5,9},{9,13},{13,1},{2,6},{6,10},{... | collective-permute-start | bytes 393224 | tf_op jit(solution)/shard_map/ppermute | solution.py:157
  31.0 5.1 %collective-permute-start.9 = (bf16[4,128,128]{2,1,0:T(8,128)(2,1)S(1)}, bf16[4,128,128]{2,1,0:T(8,128)(2,1)S(1)}, u32[]{:S(2)}, u32[]{:S(2)}) collective-permute-start(bf16[4,128,128]{2,1,0:T(8,128)(2,1)S(1)} %fusion.1), channel_id=1, source_target_pairs={{0,12},{4,0},{8,4},{12,8},{1,13},{5,1},{9,5},{13,9},{2,14},{6,2},{... | collective-permute-start | bytes 393224 | tf_op jit(solution)/shard_map/ppermute | solution.py:157

commit v9 on v7

--- a/solution.py
+++ b/solution.py
@@ -8,7 +8,7 @@
 from jax.sharding import PartitionSpec as P
 
 MIX_TERMS = 8
-SUM_TERMS = 4
+SUM_TERMS = 8
 MIB = 1024 * 1024
 
 
@@ -98,41 +98,41 @@
     terms, sec_dev, rows, width = mixed_ref.shape
     targets = coef_ref.shape[0]
     half = width // 2
-    spill = sec_dev - 1
-    sums = refs[-2:] if split else refs[-1:]
-    outs = refs[: len(refs) - len(sums)]
-    for total in sums:
+    mine = refs[0]
+    mine[...] = jnp.zeros_like(mine)
+    if split:
+        theirs, total = refs[1:-1], refs[-1]
         total[...] = jnp.zeros_like(total)
+
+    def add(k, s, product):
+        target = wrapped(s - shift_ref[k], targets)
+        scaled = coef_ref[target, k] * product
+        if split:
+            total[target] += scaled[:, :half]
+            mine[target] += scaled[:, half:]
+        else:
+            mine[target] += scaled
 
     @pl.loop(0, terms // SUM_TERMS)
     def _(step):
+        waiting = None
         for t in range(SUM_TERMS):
             k = step * SUM_TERMS + t
-            product = lax.dot_general(
-                mixed_ref[k].reshape(sec_dev * rows, width),
-                held_ref[k],
-                (((1,), (1,)), ((), ())),
-                preferred_element_type=jnp.float32,
-            ).reshape(sec_dev, rows, width)
-            first = wrapped(-shift_ref[k], targets)
-            scaled = jnp.stack(
-                [coef_ref[wrapped(first + s, targets), k] * product[s] for s in range(sec_dev)]
-            )
-            place = pl.ds(first, sec_dev)
-            if split:
-                sums[0][place] += scaled[:, :, :half]
-                sums[1][place] += scaled[:, :, half:]
-            else:
-                sums[0][place] += scaled
-
-    for total in sums:
-        total[:spill] += total[targets:]
-    if split:
-        outs[0][...] = sums[1][:targets]
-        for g, out in enumerate(outs[1:]):
-            out[...] = sums[0][g * sec_dev : (g + 1) * sec_dev].astype(jnp.bfloat16)
-    else:
-        outs[0][...] = sums[0][:targets]
+            for s in range(sec_dev):
+                product = lax.dot_general(
+                    mixed_ref[k, s],
+                    held_ref[k],
+                    (((1,), (1,)), ((), ())),
+                    preferred_element_type=jnp.float32,
+                )
+                if waiting is not None:
+                    add(*waiting)
+                waiting = (k, s, product)
+        add(*waiting)
+
+    if split:
+        for g, out in enumerate(theirs):
+            out[...] = total[g * sec_dev : (g + 1) * sec_dev].astype(jnp.bfloat16)
 
 
 def summed(shift, coef, mixed, held, split):
@@ -140,10 +140,10 @@
     targets = coef.shape[0]
     columns = width // 2 if split else width
     out_shape = [pltpu.VMEM((targets, rows, columns), jnp.float32)]
-    scratch = [pltpu.VMEM((targets + sec_dev - 1, rows, columns), jnp.float32)]
+    scratch = []
     if split:
         out_shape += [pltpu.VMEM((sec_dev, rows, columns), jnp.bfloat16)] * (targets // sec_dev)
-        scratch = scratch * 2
+        scratch = [pltpu.VMEM((targets, rows, columns), jnp.float32)]
     return pl.pallas_call(
         functools.partial(sum_kernel, split),
         out_shape=out_shape,

time: 37.3 us -> 38.6 us (1.035)
  Pallas kernels: 9.67 us -> 11 us
    pallas_call x1, Pallas kernels: 5.57 us -> 6.89 us  [summed(): pl.pallas_call(functools.partial(sum_kernel, split), out_shape=out_shape,...]
where the time goes in v9:
time: 38.6 us; the launch traced here: 38.5 us
  starting transfers between devices  16.4 us (42%)
  Pallas kernels  11 us (28%)
  waiting for transfers between devices  9.33 us (24%)
  other arithmetic  1.65 us (4%)
    ppermute x10, starting transfers between devices, shift_by(): lax.ppermute(value, axis, [(i, (i + distance) % size) for i in range(size)])  16.4 us
    ppermute x10, waiting for transfers between devices, shift_by(): lax.ppermute(value, axis, [(i, (i + distance) % size) for i in range(size)])  9.33 us
    pallas_call x1, Pallas kernels, summed(): pl.pallas_call(functools.partial(sum_kernel, split), out_shape=out_shape,...  6.89 us
    pallas_call x1, Pallas kernels, mix(): pl.pallas_call(functools.partial(mix_kernel, split), out_shape=[pltpu.VME...  4.11 us
    add x3, other arithmetic, per_device(): sigma = lax.optimization_barrier(sigma) + other.astype(jnp.float32)  0.79 us
  transfers between devices with their start and end apart: 10, of which 5 were waited for; matrix products, arithmetic and copies ran while one was open for 1% of the time, Pallas kernels for 11%

profile of v9, /device:TPU:0, one launch (start us, length us, event | category | flops | bytes accessed | tf_op | source)
XLA Modules:
  0.0 38.5 jit_solution(2654952983375919059)
XLA Ops:
  0.0 0.7 %select_bitcast_fusion = f32[4,32]{1,0:T(4,128)S(1)} fusion(f32[32,4]{0,1:T(4,128)} %param.9, s32[32,4]{0,1:T(4,128)} %param.10), kind=kLoop, calls=%fused_computation.8 | loop fusion | flops 256 | bytes 1536 | tf_op jit(solution)/shard_map/jit(_where)/select_n | solution.py:180
  0.7 3.0 %collective-permute-start.2 = (f32[4,32]{1,0:T(4,128)S(1)}, f32[4,32]{1,0:T(4,128)S(1)}, u32[]{:S(2)}, u32[]{:S(2)}) collective-permute-start(f32[4,32]{1,0:T(4,128)S(1)} %select_bitcast_fusion), channel_id=1, source_target_pairs={{0,4},{4,8},{8,12},{12,0},{1,5},{5,9},{9,13},{13,1},{2,6},{6,10},{... | collective-permute-start | bytes 1544 | tf_op jit(solution)/shard_map/ppermute | solution.py:170
  3.7 2.6 %collective-permute-start.1 = (f32[4,32]{1,0:T(4,128)S(1)}, f32[4,32]{1,0:T(4,128)S(1)}, u32[]{:S(2)}, u32[]{:S(2)}) collective-permute-start(f32[4,32]{1,0:T(4,128)S(1)} %select_bitcast_fusion), channel_id=1, source_target_pairs={{0,8},{4,12},{8,0},{12,4},{1,9},{5,13},{9,1},{13,5},{2,10},{6,14},... | collective-permute-start | bytes 1544 | tf_op jit(solution)/shard_map/ppermute | solution.py:170
  6.3 1.3 %collective-permute-start = (f32[4,32]{1,0:T(4,128)S(1)}, f32[4,32]{1,0:T(4,128)S(1)}, u32[]{:S(2)}, u32[]{:S(2)}) collective-permute-start(f32[4,32]{1,0:T(4,128)S(1)} %select_bitcast_fusion), channel_id=1, source_target_pairs={{0,12},{4,0},{8,4},{12,8},{1,13},{5,1},{9,5},{13,9},{2,14},{6,2},{... | collective-permute-start | bytes 1544 | tf_op jit(solution)/shard_map/ppermute | solution.py:170
  7.7 4.1 %shard_map.64 = (bf16[32,4,128,256]{3,2,1,0:T(8,128)(2,1)S(1)}, bf16[32,256,256]{2,1,0:T(8,128)(2,1)S(1)}) custom-call(s32[1]{0:T(128)} %bitcast.1.side_ref, bf16[4,256,256]{2,1,0:T(8,128)(2,1)} %wave_ref.1, bf16[32,128,256]{2,1,0:T(8,128)(2,1)} %left_ref.1, bf16[32,256,256]{2,1,0:T(8,128)(2,1)} %right_ref.1), custom_call_target="tpu_custom_call" | custom-call | flops 2147483648 | bytes 6291456 | tf_op jit(solution)/shard_map/pallas_call | solution.py:72
  11.8 0.0 collective-permute-done.2
  11.8 0.0 collective-permute-done.1
  11.8 0.0 collective-permute-done
  11.8 6.9 %shard_map.65 = (f32[16,128,128]{2,1,0:T(8,128)S(1)}, bf16[4,128,128]{2,1,0:T(8,128)(2,1)S(1)}, bf16[4,128,128]{2,1,0:T(8,128)(2,1)S(1)}, bf16[4,128,128]{2,1,0:T(8,128)(2,1)S(1)}, bf16[4,128,128]{2,1,0:T(8,128)(2,1)S(1)}) custom-call(s32[32]{0:T(128)} %shift_ref.1, f32[16,32]{1,0:T(8,128)S(1)} %pad_maximum_fusion.coef_ref, ...), custom_call_target="tpu_custom_call" | custom-call | flops 2147483648 | bytes 12582912 | tf_op jit(solution)/shard_map/pallas_call | solution.py:147
  18.7 1.6 %collective-permute-start.3 = (bf16[4,128,128]{2,1,0:T(8,128)(2,1)S(1)}, bf16[4,128,128]{2,1,0:T(8,128)(2,1)S(1)}, u32[]{:S(2)}, u32[]{:S(2)}) collective-permute-start(bf16[4,128,128]{2,1,0:T(8,128)(2,1)S(1)} %get-tuple-element.20), channel_id=1, source_target_pairs={{0,2},{2,0},{1,3},{3,1},{4,6},{6,4},{5,7},{7,5},{8,10},{10,8},{9,1... | collective-permute-start | bytes 393224 | tf_op jit(solution)/shard_map/ppermute | solution.py:170
  20.3 0.5 %collective-permute-start.5 = (bf16[4,128,128]{2,1,0:T(8,128)(2,1)S(1)}, bf16[4,128,128]{2,1,0:T(8,128)(2,1)S(1)}, u32[]{:S(2)}, u32[]{:S(2)}) collective-permute-start(bf16[4,128,128]{2,1,0:T(8,128)(2,1)S(1)} %get-tuple-element.22), channel_id=1, source_target_pairs={{0,2},{2,0},{1,3},{3,1},{4,6},{6,4},{5,7},{7,5},{8,10},{10,8},{9,1... | collective-permute-start | bytes 393224 | tf_op jit(solution)/shard_map/ppermute | solution.py:170
  20.8 1.5 %collective-permute-start.6 = (bf16[4,128,128]{2,1,0:T(8,128)(2,1)S(1)}, bf16[4,128,128]{2,1,0:T(8,128)(2,1)S(1)}, u32[]{:S(2)}, u32[]{:S(2)}) collective-permute-start(bf16[4,128,128]{2,1,0:T(8,128)(2,1)S(1)} %get-tuple-element.23), channel_id=1, source_target_pairs={{0,2},{2,0},{1,3},{3,1},{4,6},{6,4},{5,7},{7,5},{8,10},{10,8},{9,1... | collective-permute-start | bytes 393224 | tf_op jit(solution)/shard_map/ppermute | solution.py:170
  22.3 2.9 %collective-permute-done.3 = bf16[4,128,128]{2,1,0:T(8,128)(2,1)S(1)} collective-permute-done((bf16[4,128,128]{2,1,0:T(8,128)(2,1)S(1)}, bf16[4,128,128]{2,1,0:T(8,128)(2,1)S(1)}, u32[]{:S(2)}, u32[]{:S(2)}) %collective-permute-start.3) | collective-permute-done | bytes 131104 | tf_op jit(solution)/shard_map/ppermute | solution.py:170
  25.3 0.2 collective-permute-start.7
  25.5 1.7 %collective-permute-start.4 = (bf16[4,128,128]{2,1,0:T(8,128)(2,1)S(1)}, bf16[4,128,128]{2,1,0:T(8,128)(2,1)S(1)}, u32[]{:S(2)}, u32[]{:S(2)}) collective-permute-start(bf16[4,128,128]{2,1,0:T(8,128)(2,1)S(1)} %get-tuple-element.21), channel_id=1, source_target_pairs={{0,2},{2,0},{1,3},{3,1},{4,6},{6,4},{5,7},{7,5},{8,10},{10,8},{9,1... | collective-permute-start | bytes 393224 | tf_op jit(solution)/shard_map/ppermute | solution.py:170
  27.2 3.1 %collective-permute-done.6 = bf16[4,128,128]{2,1,0:T(8,128)(2,1)S(1)} collective-permute-done((bf16[4,128,128]{2,1,0:T(8,128)(2,1)S(1)}, bf16[4,128,128]{2,1,0:T(8,128)(2,1)S(1)}, u32[]{:S(2)}, u32[]{:S(2)}) %collective-permute-start.6) | collective-permute-done | bytes 131104 | tf_op jit(solution)/shard_map/ppermute | solution.py:170
  30.3 0.7 %collective-permute-start.8 = (bf16[4,128,128]{2,1,0:T(8,128)(2,1)S(1)}, bf16[4,128,128]{2,1,0:T(8,128)(2,1)S(1)}, u32[]{:S(2)}, u32[]{:S(2)}) collective-permute-start(bf16[4,128,128]{2,1,0:T(8,128)(2,1)S(1)} %add_convert_fusion.1), channel_id=1, source_target_pairs={{0,4},{4,8},{8,12},{12,0},{1,5},{5,9},{9,13},{13,1},{2,6},{6,10},{... | collective-permute-start | bytes 393224 | tf_op jit(solution)/shard_map/ppermute | solution.py:170
  31.0 0.0 collective-permute-done.5
  31.0 3.2 %collective-permute-start.9 = (bf16[4,128,128]{2,1,0:T(8,128)(2,1)S(1)}, bf16[4,128,128]{2,1,0:T(8,128)(2,1)S(1)}, u32[]{:S(2)}, u32[]{:S(2)}) collective-permute-start(bf16[4,128,128]{2,1,0:T(8,128)(2,1)S(1)} %add_convert_fusion), channel_id=1, source_target_pairs={{0,12},{4,0},{8,4},{12,8},{1,13},{5,1},{9,5},{13,9},{2,14},{6,2},{... | collective-permute-start | bytes 393224 | tf_op jit(solution)/shard_map/ppermute | solution.py:170
  34.3 0.0 collective-permute-done.4
  34.3 0.9 %collective-permute-done.7 = bf16[4,128,128]{2,1,0:T(8,128)(2,1)S(1)} collective-permute-done((bf16[4,128,128]{2,1,0:T(8,128)(2,1)S(1)}, bf16[4,128,128]{2,1,0:T(8,128)(2,1)S(1)}, u32[]{:S(2)}, u32[]{:S(2)}) %collective-permute-start.7) | collective-permute-done | bytes 131104 | tf_op jit(solution)/shard_map/ppermute | solution.py:170
  35.2 2.0 %collective-permute-done.8 = bf16[4,128,128]{2,1,0:T(8,128)(2,1)S(1)} collective-permute-done((bf16[4,128,128]{2,1,0:T(8,128)(2,1)S(1)}, bf16[4,128,128]{2,1,0:T(8,128)(2,1)S(1)}, u32[]{:S(2)}, u32[]{:S(2)}) %collective-permute-start.8) | collective-permute-done | bytes 131104 | tf_op jit(solution)/shard_map/ppermute | solution.py:170
  37.3 0.4 %collective-permute-done.9 = bf16[4,128,128]{2,1,0:T(8,128)(2,1)S(1)} collective-permute-done((bf16[4,128,128]{2,1,0:T(8,128)(2,1)S(1)}, bf16[4,128,128]{2,1,0:T(8,128)(2,1)S(1)}, u32[]{:S(2)}, u32[]{:S(2)}) %collective-permute-start.9) | collective-permute-done | bytes 131104 | tf_op jit(solution)/shard_map/ppermute | solution.py:170
  37.7 0.7 %convert_add_fusion = f32[4,128,128]{2,1,0:T(8,128)} fusion(f32[4,128,128]{2,1,0:T(8,128)S(1)} %convert_add_fusion.1, bf16[4,128,128]{2,1,0:T(8,128)(2,1)S(1)} %collective-permute-done.9), kind=kLoop, calls=%fused_computation | loop fusion | flops 131072 | bytes 655360 | tf_op jit(solution)/shard_map/add | solution.py:201
  (7 shorter events, 0.2 us)
Async XLA Ops:
  0.7 11.1 %collective-permute-start.2 = (f32[4,32]{1,0:T(4,128)S(1)}, f32[4,32]{1,0:T(4,128)S(1)}, u32[]{:S(2)}, u32[]{:S(2)}) collective-permute-start(f32[4,32]{1,0:T(4,128)S(1)} %select_bitcast_fusion), channel_id=1, source_target_pairs={{0,4},{4,8},{8,12},{12,0},{1,5},{5,9},{9,13},{13,1},{2,6},{6,10},{... | collective-permute-start | bytes 1544 | tf_op jit(solution)/shard_map/ppermute | solution.py:170
  3.7 8.1 %collective-permute-start.1 = (f32[4,32]{1,0:T(4,128)S(1)}, f32[4,32]{1,0:T(4,128)S(1)}, u32[]{:S(2)}, u32[]{:S(2)}) collective-permute-start(f32[4,32]{1,0:T(4,128)S(1)} %select_bitcast_fusion), channel_id=1, source_target_pairs={{0,8},{4,12},{8,0},{12,4},{1,9},{5,13},{9,1},{13,5},{2,10},{6,14},... | collective-permute-start | bytes 1544 | tf_op jit(solution)/shard_map/ppermute | solution.py:170
  6.3 5.5 %collective-permute-start = (f32[4,32]{1,0:T(4,128)S(1)}, f32[4,32]{1,0:T(4,128)S(1)}, u32[]{:S(2)}, u32[]{:S(2)}) collective-permute-start(f32[4,32]{1,0:T(4,128)S(1)} %select_bitcast_fusion), channel_id=1, source_target_pairs={{0,12},{4,0},{8,4},{12,8},{1,13},{5,1},{9,5},{13,9},{2,14},{6,2},{... | collective-permute-start | bytes 1544 | tf_op jit(solution)/shard_map/ppermute | solution.py:170
  18.7 6.5 %collective-permute-start.3 = (bf16[4,128,128]{2,1,0:T(8,128)(2,1)S(1)}, bf16[4,128,128]{2,1,0:T(8,128)(2,1)S(1)}, u32[]{:S(2)}, u32[]{:S(2)}) collective-permute-start(bf16[4,128,128]{2,1,0:T(8,128)(2,1)S(1)} %get-tuple-element.20), channel_id=1, source_target_pairs={{0,2},{2,0},{1,3},{3,1},{4,6},{6,4},{5,7},{7,5},{8,10},{10,8},{9,1... | collective-permute-start | bytes 393224 | tf_op jit(solution)/shard_map/ppermute | solution.py:170
  20.3 10.7 %collective-permute-start.5 = (bf16[4,128,128]{2,1,0:T(8,128)(2,1)S(1)}, bf16[4,128,128]{2,1,0:T(8,128)(2,1)S(1)}, u32[]{:S(2)}, u32[]{:S(2)}) collective-permute-start(bf16[4,128,128]{2,1,0:T(8,128)(2,1)S(1)} %get-tuple-element.22), channel_id=1, source_target_pairs={{0,2},{2,0},{1,3},{3,1},{4,6},{6,4},{5,7},{7,5},{8,10},{10,8},{9,1... | collective-permute-start | bytes 393224 | tf_op jit(solution)/shard_map/ppermute | solution.py:170
  20.8 9.4 %collective-permute-start.6 = (bf16[4,128,128]{2,1,0:T(8,128)(2,1)S(1)}, bf16[4,128,128]{2,1,0:T(8,128)(2,1)S(1)}, u32[]{:S(2)}, u32[]{:S(2)}) collective-permute-start(bf16[4,128,128]{2,1,0:T(8,128)(2,1)S(1)} %get-tuple-element.23), channel_id=1, source_target_pairs={{0,2},{2,0},{1,3},{3,1},{4,6},{6,4},{5,7},{7,5},{8,10},{10,8},{9,1... | collective-permute-start | bytes 393224 | tf_op jit(solution)/shard_map/ppermute | solution.py:170
  25.3 9.9 %collective-permute-start.7 = (bf16[4,128,128]{2,1,0:T(8,128)(2,1)S(1)}, bf16[4,128,128]{2,1,0:T(8,128)(2,1)S(1)}, u32[]{:S(2)}, u32[]{:S(2)}) collective-permute-start(bf16[4,128,128]{2,1,0:T(8,128)(2,1)S(1)} %add_convert_fusion.2), channel_id=1, source_target_pairs={{0,8},{4,12},{8,0},{12,4},{1,9},{5,13},{9,1},{13,5},{2,10},{6,14},... | collective-permute-start | bytes 393224 | tf_op jit(solution)/shard_map/ppermute | solution.py:170
  25.5 8.8 %collective-permute-start.4 = (bf16[4,128,128]{2,1,0:T(8,128)(2,1)S(1)}, bf16[4,128,128]{2,1,0:T(8,128)(2,1)S(1)}, u32[]{:S(2)}, u32[]{:S(2)}) collective-permute-start(bf16[4,128,128]{2,1,0:T(8,128)(2,1)S(1)} %get-tuple-element.21), channel_id=1, source_target_pairs={{0,2},{2,0},{1,3},{3,1},{4,6},{6,4},{5,7},{7,5},{8,10},{10,8},{9,1... | collective-permute-start | bytes 393224 | tf_op jit(solution)/shard_map/ppermute | solution.py:170
  30.3 7.0 %collective-permute-start.8 = (bf16[4,128,128]{2,1,0:T(8,128)(2,1)S(1)}, bf16[4,128,128]{2,1,0:T(8,128)(2,1)S(1)}, u32[]{:S(2)}, u32[]{:S(2)}) collective-permute-start(bf16[4,128,128]{2,1,0:T(8,128)(2,1)S(1)} %add_convert_fusion.1), channel_id=1, source_target_pairs={{0,4},{4,8},{8,12},{12,0},{1,5},{5,9},{9,13},{13,1},{2,6},{6,10},{... | collective-permute-start | bytes 393224 | tf_op jit(solution)/shard_map/ppermute | solution.py:170
  31.0 6.7 %collective-permute-start.9 = (bf16[4,128,128]{2,1,0:T(8,128)(2,1)S(1)}, bf16[4,128,128]{2,1,0:T(8,128)(2,1)S(1)}, u32[]{:S(2)}, u32[]{:S(2)}) collective-permute-start(bf16[4,128,128]{2,1,0:T(8,128)(2,1)S(1)} %add_convert_fusion), channel_id=1, source_target_pairs={{0,12},{4,0},{8,4},{12,8},{1,13},{5,1},{9,5},{13,9},{2,14},{6,2},{... | collective-permute-start | bytes 393224 | tf_op jit(solution)/shard_map/ppermute | solution.py:170

commit v10 on v3

--- a/solution.py
+++ b/solution.py
@@ -10,6 +10,12 @@
 MIX_TERMS = 8
 SUM_TERMS = 4
 MIB = 1024 * 1024
+
+
+def wrapped(value, size):
+    if size & (size - 1) == 0:
+        return value & (size - 1)
+    return lax.rem(value + size, size)
 
 
 def mix_kernel(split, side_ref, wave_ref, left_ref, right_ref, mixed_ref, held_ref, wave, left, sems):
@@ -39,13 +45,17 @@
         ]
     else:
         right_copies = [pltpu.make_async_copy(right_ref, held_ref, sems.at[1])]
-    for copy in right_copies:
-        copy.start()
     wave_copy.wait()
 
     @pl.loop(0, chunks)
     def _(c):
         left_copy(c).wait()
+
+        @pl.when(c == 0)
+        def _():
+            for copy in right_copies:
+                copy.start()
+
         part = pl.ds(c * MIX_TERMS, MIX_TERMS)
         rows_in = left[part].reshape(MIX_TERMS * rows, width)
         for s in range(sec_dev):
@@ -84,10 +94,11 @@
     )
 
 
-def sum_kernel(split, base_ref, shift_ref, coef_ref, mixed_ref, held_ref, *refs):
+def sum_kernel(split, me_ref, shift_ref, coef_ref, mixed_ref, held_ref, *refs):
     terms, sec_dev, rows, width = mixed_ref.shape
     targets = coef_ref.shape[0]
     half = width // 2
+    first = me_ref[0] * sec_dev
     mine = refs[0]
     mine[...] = jnp.zeros_like(mine)
     if split:
@@ -105,29 +116,29 @@
                 preferred_element_type=jnp.float32,
             )
             for s in range(sec_dev):
-                target = lax.rem(base_ref[0] + s + targets - shift_ref[k], targets)
-                scaled = coef_ref[target, k] * product[s * rows : (s + 1) * rows]
+                target = wrapped(first + s - shift_ref[k], targets)
                 if split:
-                    total[target] += scaled[:, :half]
-                    mine[target] += scaled[:, half:]
+                    slot = target ^ first
+                    scaled = coef_ref[slot, k] * product[s * rows : (s + 1) * rows]
+                    total[slot] += scaled[:, :half]
+                    mine[slot] += scaled[:, half:]
                 else:
-                    mine[target] += scaled
+                    mine[target] += coef_ref[target, k] * product[s * rows : (s + 1) * rows]
 
     if split:
         for g, out in enumerate(theirs):
             out[...] = total[g * sec_dev : (g + 1) * sec_dev].astype(jnp.bfloat16)
 
 
-def summed(base, shift, coef, mixed, held, split):
+def summed(me, shift, coef, mixed, held, split):
     k_dev, sec_dev, rows, width = mixed.shape
     targets = coef.shape[0]
-    if split:
-        out_shape = [pltpu.VMEM((targets, rows, width // 2), jnp.float32)]
-        out_shape += [pltpu.VMEM((sec_dev, rows, width // 2), jnp.bfloat16)] * (targets // sec_dev)
-        scratch = [pltpu.VMEM((targets, rows, width // 2), jnp.float32)]
-    else:
-        out_shape = [pltpu.VMEM((targets, rows, width), jnp.float32)]
-        scratch = []
+    columns = width // 2 if split else width
+    out_shape = [pltpu.VMEM((targets, rows, columns), jnp.float32)]
+    scratch = []
+    if split:
+        out_shape += [pltpu.VMEM((sec_dev, rows, columns), jnp.bfloat16)] * (targets // sec_dev)
+        scratch = [pltpu.VMEM((targets, rows, columns), jnp.float32)]
     return pl.pallas_call(
         functools.partial(sum_kernel, split),
         out_shape=out_shape,
@@ -142,17 +153,16 @@
             transcendentals=0,
         ),
     )(
-        base,
-        shift,
+        me,
+        pltpu.with_memory_space_constraint(shift, pltpu.HBM),
         coef,
         pltpu.with_memory_space_constraint(mixed, pltpu.VMEM),
         pltpu.with_memory_space_constraint(held, pltpu.VMEM),
     )
 
 
-def shift_by(value, axis, distance):
-    size = lax.axis_size(axis)
-    return lax.ppermute(value, axis, [(i, (i + distance) % size) for i in range(size)])
+def swap(value, axis, mask):
+    return lax.ppermute(value, axis, [(i, i ^ mask) for i in range(lax.axis_size(axis))])
 
 
 def after(value, other):
@@ -163,34 +173,31 @@
     sec_dev = wavefunction.shape[0]
     devices = lax.axis_size("sector")
     live = jnp.where(coupled.T > 0, site_coef.T, 0.0)
-    shift = lax.rem(sector_shift, sec_dev * devices)
     side = jnp.reshape(lax.axis_index("op"), (1,)).astype(jnp.int32)
-    me = lax.axis_index("sector")
-
-    if lax.axis_size("op") == 2 and devices <= 4:
-        coefs = [live] + [shift_by(live, "sector", -g) for g in range(1, devices)]
-        mixed, held = mix(side, wavefunction, left_ops, right_ops, True)
-        base = jnp.zeros((1,), jnp.int32)
-        mine, *theirs = summed(base, shift, jnp.concatenate(coefs, axis=0), mixed, held, True)
-        mine = [mine[g * sec_dev : (g + 1) * sec_dev] for g in range(devices)]
-        order = sorted(range(1, devices), key=lambda g: abs(2 * g - devices))
-        crossed = {g: shift_by(theirs[g], "op", 1) for g in order}
-        arrived, both = [], None
-        for g in order:
-            other = crossed[g] if both is None else after(crossed[g], both)
-            both = (mine[g] + other.astype(jnp.float32)).astype(jnp.bfloat16)
-            if not arrived:
-                theirs[0] = after(theirs[0], both)
-            arrived.append(shift_by(both, "sector", g))
-        sigma = mine[0] + shift_by(theirs[0], "op", 1).astype(jnp.float32)
-        for other in arrived:
-            sigma = sigma + other.astype(jnp.float32)
-        return sigma
+    me = jnp.reshape(lax.axis_index("sector"), (1,)).astype(jnp.int32)
+    split = lax.axis_size("op") == 2 and devices == 4 and sec_dev & (sec_dev - 1) == 0
+    mixed, held = mix(side, wavefunction, left_ops, right_ops, split)
+
+    if split:
+        coef = jnp.concatenate([live] + [swap(live, "sector", g) for g in (1, 2, 3)], axis=0)
+        mine, *theirs = summed(me, sector_shift, coef, mixed, held, True)
+        mine = [mine[g * sec_dev : (g + 1) * sec_dev] for g in range(4)]
+        crossed = {g: swap(theirs[g], "op", 1) for g in (3, 2)}
+        third = (mine[3] + crossed[3].astype(jnp.float32)).astype(jnp.bfloat16)
+        relayed = swap(third, "sector", 1)
+        crossed |= {g: swap(after(theirs[g], third), "op", 1) for g in (1, 0)}
+        second = mine[2] + after(crossed[2], third).astype(jnp.float32)
+        second = lax.optimization_barrier(second) + relayed.astype(jnp.float32)
+        second = second.astype(jnp.bfloat16)
+        far = swap(second, "sector", 2)
+        first = (mine[1] + after(crossed[1], second).astype(jnp.float32)).astype(jnp.bfloat16)
+        near = swap(first, "sector", 1)
+        sigma = mine[0] + after(crossed[0], first).astype(jnp.float32)
+        sigma = lax.optimization_barrier(sigma) + near.astype(jnp.float32)
+        return lax.optimization_barrier(sigma) + far.astype(jnp.float32)
 
     coef = lax.all_gather(live, "sector", axis=0, tiled=True)
-    mixed, held = mix(side, wavefunction, left_ops, right_ops, False)
-    base = jnp.reshape(me * sec_dev, (1,)).astype(jnp.int32)
-    (total,) = summed(base, shift, coef, mixed, held, False)
+    (total,) = summed(me, sector_shift, coef, mixed, held, False)
     total = lax.psum_scatter(total, "op", scatter_dimension=2, tiled=True)
     return lax.psum_scatter(total, "sector", scatter_dimension=0, tiled=True)
 

time: 36.5 us -> 48.6 us (1.33)
  local copies, waits for them, and re-layouts: 0 us -> 10.7 us
  waiting for transfers between devices: 9.84 us -> 11.9 us
  other arithmetic: 2.26 us -> 1.64 us
    unnamed x0 -> x8, local copies, waits for them, and re-layouts: none -> 10.7 us
    ppermute x10, waiting for transfers between devices: 9.84 us -> 11.9 us  [swap(): lax.ppermute(value, axis, [(i, i ^ mask) for i in range(lax.axis_size(axi...]
    rem x1 -> x0, other arithmetic: 0.66 us -> none  [per_device(): shift = lax.rem(sector_shift, sec_dev * devices)]
  transfers between devices with their start and end apart: 10 -> 10, of which waited for: 5 -> 3; matrix products, arithmetic and copies ran while one was open for 2% -> 0% of each run, Pallas kernels for 11% -> 9%
where the time goes in v10:
time: 48.6 us; the launch traced here: 48.3 us
  starting transfers between devices  14.7 us (30%)
  waiting for transfers between devices  11.9 us (24%)
  local copies, waits for them, and re-layouts  10.7 us (22%)
  Pallas kernels  9.32 us (19%)
  other arithmetic  1.64 us (3%)
    ppermute x10, starting transfers between devices, swap(): lax.ppermute(value, axis, [(i, i ^ mask) for i in range(lax.axis_size(axi...  14.7 us
    ppermute x10, waiting for transfers between devices, swap(): lax.ppermute(value, axis, [(i, i ^ mask) for i in range(lax.axis_size(axi...  11.9 us
    unnamed x8, local copies, waits for them, and re-layouts  10.7 us
    pallas_call x1, Pallas kernels, summed(): pl.pallas_call(functools.partial(sum_kernel, split), out_shape=out_shape,...  5.21 us
    pallas_call x1, Pallas kernels, mix(): pl.pallas_call(functools.partial(mix_kernel, split), out_shape=[pltpu.VME...  4.11 us
  transfers between devices with their start and end apart: 10, of which 3 were waited for; matrix products, arithmetic and copies ran while one was open for 0% of the time, Pallas kernels for 9%

profile of v10, /device:TPU:0, one launch (start us, length us, event | category | flops | bytes accessed | tf_op | source)
XLA Modules:
  0.0 48.3 jit_solution(2957690014100704435)
XLA Ops:
  0.0 0.7 %select_bitcast_fusion = f32[4,32]{1,0:T(4,128)S(1)} fusion(f32[32,4]{0,1:T(4,128)} %param.9, s32[32,4]{0,1:T(4,128)} %param.10), kind=kLoop, calls=%fused_computation.8 | loop fusion | flops 256 | bytes 1536 | tf_op jit(solution)/shard_map/jit(_where)/select_n | solution.py:175
  0.7 5.0 %collective-permute-start.2 = (f32[4,32]{1,0:T(4,128)S(1)}, f32[4,32]{1,0:T(4,128)S(1)}, u32[]{:S(2)}, u32[]{:S(2)}) collective-permute-start(f32[4,32]{1,0:T(4,128)S(1)} %select_bitcast_fusion), channel_id=1, source_target_pairs={{0,12},{4,8},{8,4},{12,0},{1,13},{5,9},{9,5},{13,1},{2,14},{6,10},... | collective-permute-start | bytes 1544 | tf_op jit(solution)/shard_map/ppermute | solution.py:165
  5.8 0.0 collective-permute-start.1
  5.8 0.6 %collective-permute-start = (f32[4,32]{1,0:T(4,128)S(1)}, f32[4,32]{1,0:T(4,128)S(1)}, u32[]{:S(2)}, u32[]{:S(2)}) collective-permute-start(f32[4,32]{1,0:T(4,128)S(1)} %select_bitcast_fusion), channel_id=1, source_target_pairs={{0,4},{4,0},{8,12},{12,8},{1,5},{5,1},{9,13},{13,9},{2,6},{6,2},{1... | collective-permute-start | bytes 1544 | tf_op jit(solution)/shard_map/ppermute | solution.py:165
  6.3 4.1 %shard_map.64 = (bf16[32,4,128,256]{3,2,1,0:T(8,128)(2,1)S(1)}, bf16[32,256,256]{2,1,0:T(8,128)(2,1)S(1)}) custom-call(s32[1]{0:T(128)} %bitcast.2.side_ref, bf16[4,256,256]{2,1,0:T(8,128)(2,1)} %wave_ref.1, bf16[32,128,256]{2,1,0:T(8,128)(2,1)} %left_ref.1, bf16[32,256,256]{2,1,0:T(8,128)(2,1)} %right_ref.1), custom_call_target="tpu_custom_call" | custom-call | flops 2147483648 | bytes 6291456 | tf_op jit(solution)/shard_map/pallas_call | solution.py:72
  10.4 0.0 copy-start
  10.5 3.2 %copy-done = bf16[32,4,128,256]{3,2,1,0:T(8,128)(2,1)} copy-done((bf16[32,4,128,256]{3,2,1,0:T(8,128)(2,1)}, bf16[32,4,128,256]{3,2,1,0:T(8,128)(2,1)S(1)}, u32[]{:S(2)}) %copy-start) | copy-done | bytes 8388632
  13.7 0.0 copy-start.2
  13.7 2.0 %copy-done.2 = bf16[32,256,256]{2,1,0:T(8,128)(2,1)} copy-done((bf16[32,256,256]{2,1,0:T(8,128)(2,1)}, bf16[32,256,256]{2,1,0:T(8,128)(2,1)S(1)}, u32[]{:S(2)}) %copy-start.2) | copy-done | bytes 4194328
  15.6 0.0 collective-permute-done.2
  15.6 0.0 collective-permute-done.1
  15.6 0.0 collective-permute-done
  15.6 0.0 copy-start.1
  15.7 3.4 %copy-done.1 = bf16[32,4,128,256]{3,2,1,0:T(8,128)(2,1)S(1)} copy-done((bf16[32,4,128,256]{3,2,1,0:T(8,128)(2,1)S(1)}, bf16[32,4,128,256]{3,2,1,0:T(8,128)(2,1)}, u32[]{:S(2)}) %copy-start.1) | copy-done | bytes 8388632
  19.0 0.0 copy-start.3
  19.0 2.2 %copy-done.3 = bf16[32,256,256]{2,1,0:T(8,128)(2,1)S(1)} copy-done((bf16[32,256,256]{2,1,0:T(8,128)(2,1)S(1)}, bf16[32,256,256]{2,1,0:T(8,128)(2,1)}, u32[]{:S(2)}) %copy-start.3) | copy-done | bytes 4194328
  21.2 5.2 %shard_map.65 = (f32[16,128,128]{2,1,0:T(8,128)S(1)}, bf16[4,128,128]{2,1,0:T(8,128)(2,1)S(1)}, bf16[4,128,128]{2,1,0:T(8,128)(2,1)S(1)}, bf16[4,128,128]{2,1,0:T(8,128)(2,1)S(1)}, bf16[4,128,128]{2,1,0:T(8,128)(2,1)S(1)}) custom-call(s32[1]{0:T(128)} %bitcast.me_ref, s32[32]{0:T(128)} %shift_ref.1, f32[16,32]{1,0:T(8,128)S(1)} %pad_maximum_fusion.coef_ref, ...), custom_call_target="tpu_custom_call" | custom-call | flops 2147483648 | bytes 12582912 | tf_op jit(solution)/shard_map/pallas_call | solution.py:142
  26.4 1.8 %collective-permute-start.3 = (bf16[4,128,128]{2,1,0:T(8,128)(2,1)S(1)}, bf16[4,128,128]{2,1,0:T(8,128)(2,1)S(1)}, u32[]{:S(2)}, u32[]{:S(2)}) collective-permute-start(bf16[4,128,128]{2,1,0:T(8,128)(2,1)S(1)} %get-tuple-element.21), channel_id=1, source_target_pairs={{0,2},{2,0},{1,3},{3,1},{4,6},{6,4},{5,7},{7,5},{8,10},{10,8},{9,1... | collective-permute-start | bytes 393224 | tf_op jit(solution)/shard_map/ppermute | solution.py:165
  28.2 0.3 collective-permute-start.6
  28.5 4.1 %collective-permute-done.3 = bf16[4,128,128]{2,1,0:T(8,128)(2,1)S(1)} collective-permute-done((bf16[4,128,128]{2,1,0:T(8,128)(2,1)S(1)}, bf16[4,128,128]{2,1,0:T(8,128)(2,1)S(1)}, u32[]{:S(2)}, u32[]{:S(2)}) %collective-permute-start.3) | collective-permute-done | bytes 131104 | tf_op jit(solution)/shard_map/ppermute | solution.py:165
  32.6 1.5 %collective-permute-start.7 = (bf16[4,128,128]{2,1,0:T(8,128)(2,1)S(1)}, bf16[4,128,128]{2,1,0:T(8,128)(2,1)S(1)}, u32[]{:S(2)}, u32[]{:S(2)}) collective-permute-start(bf16[4,128,128]{2,1,0:T(8,128)(2,1)S(1)} %add_convert_fusion.2), channel_id=1, source_target_pairs={{0,4},{4,0},{8,12},{12,8},{1,5},{5,1},{9,13},{13,9},{2,6},{6,2},{1... | collective-permute-start | bytes 393224 | tf_op jit(solution)/shard_map/ppermute | solution.py:165
  34.2 1.5 %collective-permute-start.4 = (bf16[4,128,128]{2,1,0:T(8,128)(2,1)S(1)}, bf16[4,128,128]{2,1,0:T(8,128)(2,1)S(1)}, u32[]{:S(2)}, u32[]{:S(2)}) collective-permute-start(bf16[4,128,128]{2,1,0:T(8,128)(2,1)S(1)} %get-tuple-element.22), channel_id=1, source_target_pairs={{0,2},{2,0},{1,3},{3,1},{4,6},{6,4},{5,7},{7,5},{8,10},{10,8},{9,1... | collective-permute-start | bytes 393224 | tf_op jit(solution)/shard_map/ppermute | solution.py:165
  35.6 0.5 %collective-permute-start.5 = (bf16[4,128,128]{2,1,0:T(8,128)(2,1)S(1)}, bf16[4,128,128]{2,1,0:T(8,128)(2,1)S(1)}, u32[]{:S(2)}, u32[]{:S(2)}) collective-permute-start(bf16[4,128,128]{2,1,0:T(8,128)(2,1)S(1)} %get-tuple-element.24), channel_id=1, source_target_pairs={{0,2},{2,0},{1,3},{3,1},{4,6},{6,4},{5,7},{7,5},{8,10},{10,8},{9,1... | collective-permute-start | bytes 393224 | tf_op jit(solution)/shard_map/ppermute | solution.py:165
  36.2 0.0 collective-permute-done.6
  36.2 2.6 %collective-permute-done.7 = bf16[4,128,128]{2,1,0:T(8,128)(2,1)S(1)} collective-permute-done((bf16[4,128,128]{2,1,0:T(8,128)(2,1)S(1)}, bf16[4,128,128]{2,1,0:T(8,128)(2,1)S(1)}, u32[]{:S(2)}, u32[]{:S(2)}) %collective-permute-start.7) | collective-permute-done | bytes 131104 | tf_op jit(solution)/shard_map/ppermute | solution.py:165
  38.8 2.4 %collective-permute-start.9 = (bf16[4,128,128]{2,1,0:T(8,128)(2,1)S(1)}, bf16[4,128,128]{2,1,0:T(8,128)(2,1)S(1)}, u32[]{:S(2)}, u32[]{:S(2)}) collective-permute-start(bf16[4,128,128]{2,1,0:T(8,128)(2,1)S(1)} %add_convert_fusion.1), channel_id=1, source_target_pairs={{0,8},{4,12},{8,0},{12,4},{1,9},{5,13},{9,1},{13,5},{2,10},{6,14},... | collective-permute-start | bytes 393224 | tf_op jit(solution)/shard_map/ppermute | solution.py:165
  41.3 0.0 collective-permute-done.5
  41.3 1.0 %collective-permute-start.8 = (bf16[4,128,128]{2,1,0:T(8,128)(2,1)S(1)}, bf16[4,128,128]{2,1,0:T(8,128)(2,1)S(1)}, u32[]{:S(2)}, u32[]{:S(2)}) collective-permute-start(bf16[4,128,128]{2,1,0:T(8,128)(2,1)S(1)} %add_convert_fusion), channel_id=1, source_target_pairs={{0,4},{4,0},{8,12},{12,8},{1,5},{5,1},{9,13},{13,9},{2,6},{6,2},{1... | collective-permute-start | bytes 393224 | tf_op jit(solution)/shard_map/ppermute | solution.py:165
  42.3 0.0 collective-permute-done.4
  42.3 5.2 %collective-permute-done.8 = bf16[4,128,128]{2,1,0:T(8,128)(2,1)S(1)} collective-permute-done((bf16[4,128,128]{2,1,0:T(8,128)(2,1)S(1)}, bf16[4,128,128]{2,1,0:T(8,128)(2,1)S(1)}, u32[]{:S(2)}, u32[]{:S(2)}) %collective-permute-start.8) | collective-permute-done | bytes 131104 | tf_op jit(solution)/shard_map/ppermute | solution.py:165
  47.6 0.0 collective-permute-done.9
  47.6 0.7 %convert_add_fusion = f32[4,128,128]{2,1,0:T(8,128)} fusion(f32[4,128,128]{2,1,0:T(8,128)S(1)} %convert_add_fusion.1, bf16[4,128,128]{2,1,0:T(8,128)(2,1)S(1)} %collective-permute-done.9), kind=kLoop, calls=%fused_computation | loop fusion | flops 131072 | bytes 655360 | tf_op jit(solution)/shard_map/add | solution.py:197
  (7 shorter events, 0.2 us)
Async XLA Ops:
  0.7 14.9 %collective-permute-start.2 = (f32[4,32]{1,0:T(4,128)S(1)}, f32[4,32]{1,0:T(4,128)S(1)}, u32[]{:S(2)}, u32[]{:S(2)}) collective-permute-start(f32[4,32]{1,0:T(4,128)S(1)} %select_bitcast_fusion), channel_id=1, source_target_pairs={{0,12},{4,8},{8,4},{12,0},{1,13},{5,9},{9,5},{13,1},{2,14},{6,10},... | collective-permute-start | bytes 1544 | tf_op jit(solution)/shard_map/ppermute | solution.py:165
  5.8 9.9 %collective-permute-start.1 = (f32[4,32]{1,0:T(4,128)S(1)}, f32[4,32]{1,0:T(4,128)S(1)}, u32[]{:S(2)}, u32[]{:S(2)}) collective-permute-start(f32[4,32]{1,0:T(4,128)S(1)} %select_bitcast_fusion), channel_id=1, source_target_pairs={{0,8},{4,12},{8,0},{12,4},{1,9},{5,13},{9,1},{13,5},{2,10},{6,14},... | collective-permute-start | bytes 1544 | tf_op jit(solution)/shard_map/ppermute | solution.py:165
  5.8 9.9 %collective-permute-start = (f32[4,32]{1,0:T(4,128)S(1)}, f32[4,32]{1,0:T(4,128)S(1)}, u32[]{:S(2)}, u32[]{:S(2)}) collective-permute-start(f32[4,32]{1,0:T(4,128)S(1)} %select_bitcast_fusion), channel_id=1, source_target_pairs={{0,4},{4,0},{8,12},{12,8},{1,5},{5,1},{9,13},{13,9},{2,6},{6,2},{1... | collective-permute-start | bytes 1544 | tf_op jit(solution)/shard_map/ppermute | solution.py:165
  10.4 3.2 %copy-start = (bf16[32,4,128,256]{3,2,1,0:T(8,128)(2,1)}, bf16[32,4,128,256]{3,2,1,0:T(8,128)(2,1)S(1)}, u32[]{:S(2)}) copy-start(bf16[32,4,128,256]{3,2,1,0:T(8,128)(2,1)S(1)} %get-tuple-element.17.mixed_ref) | copy-start | bytes 25165828
  13.7 2.0 %copy-start.2 = (bf16[32,256,256]{2,1,0:T(8,128)(2,1)}, bf16[32,256,256]{2,1,0:T(8,128)(2,1)S(1)}, u32[]{:S(2)}) copy-start(bf16[32,256,256]{2,1,0:T(8,128)(2,1)S(1)} %get-tuple-element.18.held_ref) | copy-start | bytes 12582916
  15.6 3.4 %copy-start.1 = (bf16[32,4,128,256]{3,2,1,0:T(8,128)(2,1)S(1)}, bf16[32,4,128,256]{3,2,1,0:T(8,128)(2,1)}, u32[]{:S(2)}) copy-start(bf16[32,4,128,256]{3,2,1,0:T(8,128)(2,1)} %copy-done) | copy-start | bytes 25165828
  19.0 2.2 %copy-start.3 = (bf16[32,256,256]{2,1,0:T(8,128)(2,1)S(1)}, bf16[32,256,256]{2,1,0:T(8,128)(2,1)}, u32[]{:S(2)}) copy-start(bf16[32,256,256]{2,1,0:T(8,128)(2,1)} %copy-done.2) | copy-start | bytes 12582916
  26.4 6.1 %collective-permute-start.3 = (bf16[4,128,128]{2,1,0:T(8,128)(2,1)S(1)}, bf16[4,128,128]{2,1,0:T(8,128)(2,1)S(1)}, u32[]{:S(2)}, u32[]{:S(2)}) collective-permute-start(bf16[4,128,128]{2,1,0:T(8,128)(2,1)S(1)} %get-tuple-element.21), channel_id=1, source_target_pairs={{0,2},{2,0},{1,3},{3,1},{4,6},{6,4},{5,7},{7,5},{8,10},{10,8},{9,1... | collective-permute-start | bytes 393224 | tf_op jit(solution)/shard_map/ppermute | solution.py:165
  28.2 8.0 %collective-permute-start.6 = (bf16[4,128,128]{2,1,0:T(8,128)(2,1)S(1)}, bf16[4,128,128]{2,1,0:T(8,128)(2,1)S(1)}, u32[]{:S(2)}, u32[]{:S(2)}) collective-permute-start(bf16[4,128,128]{2,1,0:T(8,128)(2,1)S(1)} %get-tuple-element.25), channel_id=1, source_target_pairs={{0,2},{2,0},{1,3},{3,1},{4,6},{6,4},{5,7},{7,5},{8,10},{10,8},{9,1... | collective-permute-start | bytes 393224 | tf_op jit(solution)/shard_map/ppermute | solution.py:165
  32.6 6.2 %collective-permute-start.7 = (bf16[4,128,128]{2,1,0:T(8,128)(2,1)S(1)}, bf16[4,128,128]{2,1,0:T(8,128)(2,1)S(1)}, u32[]{:S(2)}, u32[]{:S(2)}) collective-permute-start(bf16[4,128,128]{2,1,0:T(8,128)(2,1)S(1)} %add_convert_fusion.2), channel_id=1, source_target_pairs={{0,4},{4,0},{8,12},{12,8},{1,5},{5,1},{9,13},{13,9},{2,6},{6,2},{1... | collective-permute-start | bytes 393224 | tf_op jit(solution)/shard_map/ppermute | solution.py:165
  34.2 8.2 %collective-permute-start.4 = (bf16[4,128,128]{2,1,0:T(8,128)(2,1)S(1)}, bf16[4,128,128]{2,1,0:T(8,128)(2,1)S(1)}, u32[]{:S(2)}, u32[]{:S(2)}) collective-permute-start(bf16[4,128,128]{2,1,0:T(8,128)(2,1)S(1)} %get-tuple-element.22), channel_id=1, source_target_pairs={{0,2},{2,0},{1,3},{3,1},{4,6},{6,4},{5,7},{7,5},{8,10},{10,8},{9,1... | collective-permute-start | bytes 393224 | tf_op jit(solution)/shard_map/ppermute | solution.py:165
  35.6 5.6 %collective-permute-start.5 = (bf16[4,128,128]{2,1,0:T(8,128)(2,1)S(1)}, bf16[4,128,128]{2,1,0:T(8,128)(2,1)S(1)}, u32[]{:S(2)}, u32[]{:S(2)}) collective-permute-start(bf16[4,128,128]{2,1,0:T(8,128)(2,1)S(1)} %get-tuple-element.24), channel_id=1, source_target_pairs={{0,2},{2,0},{1,3},{3,1},{4,6},{6,4},{5,7},{7,5},{8,10},{10,8},{9,1... | collective-permute-start | bytes 393224 | tf_op jit(solution)/shard_map/ppermute | solution.py:165
  38.8 8.8 %collective-permute-start.9 = (bf16[4,128,128]{2,1,0:T(8,128)(2,1)S(1)}, bf16[4,128,128]{2,1,0:T(8,128)(2,1)S(1)}, u32[]{:S(2)}, u32[]{:S(2)}) collective-permute-start(bf16[4,128,128]{2,1,0:T(8,128)(2,1)S(1)} %add_convert_fusion.1), channel_id=1, source_target_pairs={{0,8},{4,12},{8,0},{12,4},{1,9},{5,13},{9,1},{13,5},{2,10},{6,14},... | collective-permute-start | bytes 393224 | tf_op jit(solution)/shard_map/ppermute | solution.py:165
  41.3 6.2 %collective-permute-start.8 = (bf16[4,128,128]{2,1,0:T(8,128)(2,1)S(1)}, bf16[4,128,128]{2,1,0:T(8,128)(2,1)S(1)}, u32[]{:S(2)}, u32[]{:S(2)}) collective-permute-start(bf16[4,128,128]{2,1,0:T(8,128)(2,1)S(1)} %add_convert_fusion), channel_id=1, source_target_pairs={{0,4},{4,0},{8,12},{12,8},{1,5},{5,1},{9,13},{13,9},{2,6},{6,2},{1... | collective-permute-start | bytes 393224 | tf_op jit(solution)/shard_map/ppermute | solution.py:165

commit v11 on v8

--- a/solution.py
+++ b/solution.py
@@ -8,7 +8,7 @@
 from jax.sharding import PartitionSpec as P
 
 MIX_TERMS = 8
-SUM_TERMS = 8
+SUM_TERMS = 4
 MIB = 1024 * 1024
 
 
@@ -82,7 +82,7 @@
             pltpu.VMEM(left_ops.shape, jnp.bfloat16),
             pltpu.SemaphoreType.DMA((3 + k_dev // MIX_TERMS,)),
         ],
-        compiler_params=pltpu.CompilerParams(vmem_limit_bytes=24 * MIB),
+        compiler_params=pltpu.CompilerParams(vmem_limit_bytes=16 * MIB),
         cost_estimate=pl.CostEstimate(
             flops=2 * k_dev * sec_dev * rows * width * width,
             bytes_accessed=2 * (left_ops.size + right_ops.size),
@@ -94,61 +94,73 @@
     )
 
 
-def sum_kernel(theirs, at, shift_ref, coef_ref, mixed_ref, held_ref, *refs):
-    terms, sec_dev, rows, width = mixed_ref.shape
+def sum_kernel(low, order, shift_ref, coef_ref, mixed_ref, held_ref, *refs):
+    terms, sec_dev, _, width = mixed_ref.shape
     targets = coef_ref.shape[0]
-    total = refs[-1]
-    columns = total.shape[2]
-    total[...] = jnp.zeros_like(total)
+    half = width // 2
+    if order:
+        *before, mine = refs[: -1 - len(order)]
+        theirs, total = refs[-1 - len(order) : -1], refs[-1]
+        total[...] = jnp.zeros_like(total)
+    else:
+        (mine,) = refs
+    rows = mine.shape[1]
+    mine[...] = jnp.zeros_like(mine)
 
     @pl.loop(0, terms // SUM_TERMS)
     def _(step):
         for t in range(SUM_TERMS):
             k = step * SUM_TERMS + t
             product = lax.dot_general(
-                mixed_ref[k].reshape(sec_dev * rows, width),
-                held_ref[k, at * columns : (at + 1) * columns],
+                mixed_ref[k, :, low : low + rows].reshape(sec_dev * rows, width),
+                held_ref[k],
                 (((1,), (1,)), ((), ())),
                 preferred_element_type=jnp.float32,
             )
             for s in range(sec_dev):
                 target = wrapped(s - shift_ref[k], targets)
-                total[target] += coef_ref[target, k] * product[s * rows : (s + 1) * rows]
-
-    if theirs:
-        for g, out in enumerate(refs[:-1]):
-            out[...] = total[g * sec_dev : (g + 1) * sec_dev].astype(jnp.bfloat16)
-
-
-def summed(shift, coef, mixed, held, parts, at, theirs):
-    k_dev, sec_dev, rows, width = mixed.shape
+                scaled = coef_ref[target, k] * product[s * rows : (s + 1) * rows]
+                if order:
+                    total[target] += scaled[:, :half]
+                    mine[target] += scaled[:, half:]
+                else:
+                    mine[target] += scaled
+
+    for out, groups in zip(theirs if order else (), order):
+        for at, g in enumerate(groups):
+            sums = total[g * sec_dev : (g + 1) * sec_dev].astype(jnp.bfloat16)
+            out[at * sec_dev : (at + 1) * sec_dev, out.shape[1] - rows :] = sums
+    if order and before:
+        theirs[-1][:, :low] = before[0][...]
+
+
+def summed(shift, coef, mixed, held, low, rows, order, before=()):
+    k_dev, sec_dev, _, width = mixed.shape
     targets = coef.shape[0]
-    shape = (targets, rows, width // parts)
-    if theirs:
-        group = (sec_dev, rows, width // parts)
-        out_shape = [pltpu.VMEM(group, jnp.bfloat16)] * (targets // sec_dev)
-        scratch = [pltpu.VMEM(shape, jnp.float32)]
-    else:
-        out_shape = [pltpu.VMEM(shape, jnp.float32)]
-        scratch = []
+    columns = width // 2 if order else width
+    shape = (targets, rows, columns)
+    out_shape = [pltpu.VMEM(shape, jnp.float32)]
+    for number, groups in enumerate(order):
+        height = low + rows if before and number == len(order) - 1 else rows
+        out_shape.append(pltpu.VMEM((len(groups) * sec_dev, height, columns), jnp.bfloat16))
+    held_in_vmem = (mixed, held, *before)
     return pl.pallas_call(
-        functools.partial(sum_kernel, theirs, at),
+        functools.partial(sum_kernel, low, order),
         out_shape=out_shape,
         in_specs=[pl.BlockSpec(memory_space=pltpu.SMEM)] * 2
-        + [pl.BlockSpec(memory_space=pltpu.VMEM)] * 2,
+        + [pl.BlockSpec(memory_space=pltpu.VMEM)] * len(held_in_vmem),
         out_specs=[pl.BlockSpec(memory_space=pltpu.VMEM)] * len(out_shape),
-        scratch_shapes=scratch,
-        compiler_params=pltpu.CompilerParams(vmem_limit_bytes=24 * MIB),
+        scratch_shapes=[pltpu.VMEM(shape, jnp.float32)] if order else [],
+        compiler_params=pltpu.CompilerParams(vmem_limit_bytes=16 * MIB),
         cost_estimate=pl.CostEstimate(
-            flops=2 * k_dev * sec_dev * rows * width * width // parts,
+            flops=2 * k_dev * sec_dev * rows * width * width,
             bytes_accessed=2 * (mixed.size + held.size),
             transcendentals=0,
         ),
     )(
         pltpu.with_memory_space_constraint(shift, pltpu.HBM),
         coef,
-        pltpu.with_memory_space_constraint(mixed, pltpu.VMEM),
-        pltpu.with_memory_space_constraint(held, pltpu.VMEM),
+        *(pltpu.with_memory_space_constraint(x, pltpu.VMEM) for x in held_in_vmem),
     )
 
 
@@ -172,26 +184,48 @@
         coefs = [live] + [shift_by(live, "sector", -g) for g in range(1, devices)]
         coef = jnp.concatenate(coefs, axis=0)
         mixed, held = mix(side, wavefunction, left_ops, right_ops, True)
-        theirs = summed(sector_shift, coef, mixed, held, 2, 0, True)
         far, *near = sorted(range(1, devices), key=lambda g: abs(2 * g - devices))
-        crossed = shift_by(theirs[far], "op", 1)
-        (mine,) = summed(sector_shift, after(coef, theirs[far]), mixed, held, 2, 1, False)
-        mine = [mine[g * sec_dev : (g + 1) * sec_dev] for g in range(devices)]
-        both = (mine[far] + crossed.astype(jnp.float32)).astype(jnp.bfloat16)
-        arrived = [shift_by(both, "sector", far)]
-        crossed = {g: shift_by(after(theirs[g], both), "op", 1) for g in near + [0]}
-        for g in near:
-            both = (mine[g] + after(crossed[g], both).astype(jnp.float32)).astype(jnp.bfloat16)
-            arrived.append(shift_by(both, "sector", g))
-        sigma = mine[0] + after(crossed[0], both).astype(jnp.float32)
-        for other in arrived:
-            sigma = lax.optimization_barrier(sigma) + other.astype(jnp.float32)
-        return sigma
+        order = ((far,), tuple(near), (0,))
+        rows = left_ops.shape[1] // 2
+
+        def own(mine, g):
+            return mine[g * sec_dev : (g + 1) * sec_dev]
+
+        mine, *theirs = summed(sector_shift, coef, mixed, held, 0, rows, order)
+        crossed = [shift_by(x, "op", 1) for x in theirs[:2]]
+        lower, *rest = summed(sector_shift, coef, mixed, held, rows, rows, order, theirs[2:])
+
+        def pass_on(mine, crossed, last):
+            arrived = []
+            for at, g in enumerate([far, *near]):
+                other = crossed[0] if at == 0 else own(crossed[1], at - 1)
+                other = other if last is None else after(other, last)
+                last = (own(mine, g) + other.astype(jnp.float32)).astype(jnp.bfloat16)
+                arrived.append(shift_by(last, "sector", g))
+                if at == 0:
+                    first = last
+            return arrived, first, last
+
+        upper_arrived, first, last = pass_on(mine, crossed, None)
+        crossed = [shift_by(after(x, first), "op", 1) for x in rest[:2]]
+        whole = shift_by(after(rest[2], last), "op", 1)
+        lower_arrived, _, last = pass_on(lower, crossed, last)
+        whole = after(whole, last).astype(jnp.float32)
+        parts = []
+        for own_sums, arrived, other in (
+            (mine, upper_arrived, whole[:, :rows]),
+            (lower, lower_arrived, whole[:, rows:]),
+        ):
+            sigma = own(own_sums, 0) + other
+            for other in arrived:
+                sigma = lax.optimization_barrier(sigma) + other.astype(jnp.float32)
+            parts.append(sigma)
+        return jnp.concatenate(parts, axis=1)
 
     first = lax.axis_index("sector") * sec_dev
     coef = jnp.roll(lax.all_gather(live, "sector", axis=0, tiled=True), -first, axis=0)
     mixed, held = mix(side, wavefunction, left_ops, right_ops, False)
-    (total,) = summed(sector_shift, coef, mixed, held, 1, 0, False)
+    (total,) = summed(sector_shift, coef, mixed, held, 0, left_ops.shape[1], ())
     total = jnp.roll(total, first, axis=0)
     total = lax.psum_scatter(total, "op", scatter_dimension=2, tiled=True)
     return lax.psum_scatter(total, "sector", scatter_dimension=0, tiled=True)

time: 37 us -> 41.2 us (1.11)
  starting transfers between devices: 14.5 us -> 21.1 us
  waiting for transfers between devices: 8.79 us -> 6.58 us
    ppermute x10 -> x14, starting transfers between devices: 14.5 us -> 21.1 us  [shift_by(): lax.ppermute(value, axis, [(i, (i + distance) % size) for i in range(size)])]
    ppermute x10 -> x14, waiting for transfers between devices: 8.79 us -> 6.58 us  [shift_by(): lax.ppermute(value, axis, [(i, (i + distance) % size) for i in range(size)])]
    concatenate x0 -> x1, other arithmetic: none -> 0.72 us  [per_device(): return jnp.concatenate(parts, axis=1)]
    add x3 -> x6, other arithmetic: 0.8 us -> 0.09 us  [per_device(): sigma = lax.optimization_barrier(sigma) + other.astype(jnp.float32)]
  transfers between devices with their start and end apart: 10 -> 14, of which waited for: 4 -> 3; matrix products, arithmetic and copies ran while one was open for 0% -> 1% of each run, Pallas kernels for 21% -> 19%
where the time goes in v11:
time: 41.2 us; the launch traced here: 41 us
  starting transfers between devices  21.1 us (51%)
  Pallas kernels  11.4 us (28%)
  waiting for transfers between devices  6.58 us (16%)
  other arithmetic  1.7 us (4%)
    ppermute x14, starting transfers between devices, shift_by(): lax.ppermute(value, axis, [(i, (i + distance) % size) for i in range(size)])  21.1 us
    pallas_call x2, Pallas kernels, summed(): pl.pallas_call(functools.partial(sum_kernel, low, order), out_shape=out_s...  7.33 us
    ppermute x14, waiting for transfers between devices, shift_by(): lax.ppermute(value, axis, [(i, (i + distance) % size) for i in range(size)])  6.58 us
    pallas_call x1, Pallas kernels, mix(): pl.pallas_call(functools.partial(mix_kernel, split), out_shape=[pltpu.VME...  4.11 us
  transfers between devices with their start and end apart: 14, of which 3 were waited for; matrix products, arithmetic and copies ran while one was open for 1% of the time, Pallas kernels for 19%

profile of v11, /device:TPU:0, one launch (start us, length us, event | category | flops | bytes accessed | tf_op | source)
XLA Modules:
  0.0 41.0 jit_solution(15162120183883536508)
XLA Ops:
  0.0 0.7 %select_bitcast_fusion = f32[4,32]{1,0:T(4,128)S(1)} fusion(f32[32,4]{0,1:T(4,128)} %param.9, s32[32,4]{0,1:T(4,128)} %param.10), kind=kLoop, calls=%fused_computation.16 | loop fusion | flops 256 | bytes 1536 | tf_op jit(solution)/shard_map/jit(_where)/select_n | solution.py:179
  0.7 3.0 %collective-permute-start.2 = (f32[4,32]{1,0:T(4,128)S(1)}, f32[4,32]{1,0:T(4,128)S(1)}, u32[]{:S(2)}, u32[]{:S(2)}) collective-permute-start(f32[4,32]{1,0:T(4,128)S(1)} %select_bitcast_fusion), channel_id=1, source_target_pairs={{0,4},{4,8},{8,12},{12,0},{1,5},{5,9},{9,13},{13,1},{2,6},{6,10},{... | collective-permute-start | bytes 1544 | tf_op jit(solution)/shard_map/ppermute | solution.py:169
  3.7 2.6 %collective-permute-start.1 = (f32[4,32]{1,0:T(4,128)S(1)}, f32[4,32]{1,0:T(4,128)S(1)}, u32[]{:S(2)}, u32[]{:S(2)}) collective-permute-start(f32[4,32]{1,0:T(4,128)S(1)} %select_bitcast_fusion), channel_id=1, source_target_pairs={{0,8},{4,12},{8,0},{12,4},{1,9},{5,13},{9,1},{13,5},{2,10},{6,14},... | collective-permute-start | bytes 1544 | tf_op jit(solution)/shard_map/ppermute | solution.py:169
  6.3 1.3 %collective-permute-start = (f32[4,32]{1,0:T(4,128)S(1)}, f32[4,32]{1,0:T(4,128)S(1)}, u32[]{:S(2)}, u32[]{:S(2)}) collective-permute-start(f32[4,32]{1,0:T(4,128)S(1)} %select_bitcast_fusion), channel_id=1, source_target_pairs={{0,12},{4,0},{8,4},{12,8},{1,13},{5,1},{9,5},{13,9},{2,14},{6,2},{... | collective-permute-start | bytes 1544 | tf_op jit(solution)/shard_map/ppermute | solution.py:169
  7.7 4.1 %shard_map.64 = (bf16[32,4,128,256]{3,2,1,0:T(8,128)(2,1)S(1)}, bf16[32,256,256]{2,1,0:T(8,128)(2,1)S(1)}) custom-call(s32[1]{0:T(128)} %bitcast.1.side_ref, bf16[4,256,256]{2,1,0:T(8,128)(2,1)} %wave_ref.1, bf16[32,128,256]{2,1,0:T(8,128)(2,1)} %left_ref.1, bf16[32,256,256]{2,1,0:T(8,128)(2,1)} %right_ref.1), custom_call_target="tpu_custom_call" | custom-call | flops 2147483648 | bytes 6291456 | tf_op jit(solution)/shard_map/pallas_call | solution.py:72
  11.8 0.0 collective-permute-done.2
  11.8 0.0 collective-permute-done.1
  11.8 0.0 collective-permute-done
  11.8 3.7 %shard_map.65 = (f32[16,64,128]{2,1,0:T(8,128)S(1)}, bf16[4,64,128]{2,1,0:T(8,128)(2,1)S(1)}, bf16[8,64,128]{2,1,0:T(8,128)(2,1)S(1)}, bf16[4,64,128]{2,1,0:T(8,128)(2,1)S(1)}) custom-call(s32[32]{0:T(128)} %shift_ref.3, f32[16,32]{1,0:T(8,128)S(1)} %pad_maximum_fusion.1.coef_ref, bf16[32,4,128,256]{3,2,1,0:T(8,128)(2,1)S(1)} %get-tuple-element.24.mixed_ref, ...), custom_call_target="tpu_custom_call" | custom-call | flops 1073741824 | bytes 12582912 | tf_op jit(solution)/shard_map/pallas_call | solution.py:147
  15.5 1.6 %collective-permute-start.4 = (bf16[4,64,128]{2,1,0:T(8,128)(2,1)S(1)}, bf16[4,64,128]{2,1,0:T(8,128)(2,1)S(1)}, u32[]{:S(2)}, u32[]{:S(2)}) collective-permute-start(bf16[4,64,128]{2,1,0:T(8,128)(2,1)S(1)} %get-tuple-element.30), channel_id=1, source_target_pairs={{0,2},{2,0},{1,3},{3,1},{4,6},{6,4},{5,7},{7,5},{8,10},{10,8},{9,1... | collective-permute-start | bytes 196616 | tf_op jit(solution)/shard_map/ppermute | solution.py:169
  17.1 0.5 %collective-permute-start.3 = (bf16[8,64,128]{2,1,0:T(8,128)(2,1)S(1)}, bf16[8,64,128]{2,1,0:T(8,128)(2,1)S(1)}, u32[]{:S(2)}, u32[]{:S(2)}) collective-permute-start(bf16[8,64,128]{2,1,0:T(8,128)(2,1)S(1)} %get-tuple-element.29), channel_id=1, source_target_pairs={{0,2},{2,0},{1,3},{3,1},{4,6},{6,4},{5,7},{7,5},{8,10},{10,8},{9,1... | collective-permute-start | bytes 393224 | tf_op jit(solution)/shard_map/ppermute | solution.py:169
  17.6 3.7 %shard_map.66 = (f32[16,64,128]{2,1,0:T(8,128)S(1)}, bf16[4,64,128]{2,1,0:T(8,128)(2,1)S(1)}, bf16[8,64,128]{2,1,0:T(8,128)(2,1)S(1)}, bf16[4,128,128]{2,1,0:T(8,128)(2,1)S(1)}) custom-call(s32[32]{0:T(128)} %shift_ref.3, f32[16,32]{1,0:T(8,128)S(1)} %pad_maximum_fusion.1.coef_ref, bf16[32,4,128,256]{3,2,1,0:T(8,128)(2,1)S(1)} %get-tuple-element.24.mixed_ref, ...), custom_call_target="tpu_custom_call" | custom-call | flops 1073741824 | bytes 12582912 | tf_op jit(solution)/shard_map/pallas_call | solution.py:147
  21.3 0.0 collective-permute-done.4
  21.3 0.2 collective-permute-start.8
  21.5 1.7 %collective-permute-start.7 = (bf16[4,64,128]{2,1,0:T(8,128)(2,1)S(1)}, bf16[4,64,128]{2,1,0:T(8,128)(2,1)S(1)}, u32[]{:S(2)}, u32[]{:S(2)}) collective-permute-start(bf16[4,64,128]{2,1,0:T(8,128)(2,1)S(1)} %get-tuple-element.38), channel_id=1, source_target_pairs={{0,2},{2,0},{1,3},{3,1},{4,6},{6,4},{5,7},{7,5},{8,10},{10,8},{9,1... | collective-permute-start | bytes 196616 | tf_op jit(solution)/shard_map/ppermute | solution.py:169
  23.2 0.3 collective-permute-start.6
  23.5 0.0 collective-permute-done.3
  23.6 1.7 %collective-permute-start.9 = (bf16[4,64,128]{2,1,0:T(8,128)(2,1)S(1)}, bf16[4,64,128]{2,1,0:T(8,128)(2,1)S(1)}, u32[]{:S(2)}, u32[]{:S(2)}) collective-permute-start(bf16[4,64,128]{2,1,0:T(8,128)(2,1)S(1)} %add_convert_fusion.4), channel_id=1, source_target_pairs={{0,4},{4,8},{8,12},{12,0},{1,5},{5,9},{9,13},{13,1},{2,6},{6,10},{... | collective-permute-start | bytes 196616 | tf_op jit(solution)/shard_map/ppermute | solution.py:169
  25.3 2.2 %collective-permute-start.10 = (bf16[4,64,128]{2,1,0:T(8,128)(2,1)S(1)}, bf16[4,64,128]{2,1,0:T(8,128)(2,1)S(1)}, u32[]{:S(2)}, u32[]{:S(2)}) collective-permute-start(bf16[4,64,128]{2,1,0:T(8,128)(2,1)S(1)} %add_convert_fusion.3), channel_id=1, source_target_pairs={{0,12},{4,0},{8,4},{12,8},{1,13},{5,1},{9,5},{13,9},{2,14},{6,2},{... | collective-permute-start | bytes 196616 | tf_op jit(solution)/shard_map/ppermute | solution.py:169
  27.5 0.0 collective-permute-done.7
  27.5 1.7 %collective-permute-start.5 = (bf16[4,128,128]{2,1,0:T(8,128)(2,1)S(1)}, bf16[4,128,128]{2,1,0:T(8,128)(2,1)S(1)}, u32[]{:S(2)}, u32[]{:S(2)}) collective-permute-start(bf16[4,128,128]{2,1,0:T(8,128)(2,1)S(1)} %get-tuple-element.33), channel_id=1, source_target_pairs={{0,2},{2,0},{1,3},{3,1},{4,6},{6,4},{5,7},{7,5},{8,10},{10,8},{9,1... | collective-permute-start | bytes 393224 | tf_op jit(solution)/shard_map/ppermute | solution.py:169
  29.2 0.0 collective-permute-done.6
  29.3 2.1 %collective-permute-start.11 = (bf16[4,64,128]{2,1,0:T(8,128)(2,1)S(1)}, bf16[4,64,128]{2,1,0:T(8,128)(2,1)S(1)}, u32[]{:S(2)}, u32[]{:S(2)}) collective-permute-start(bf16[4,64,128]{2,1,0:T(8,128)(2,1)S(1)} %add_convert_fusion.2), channel_id=1, source_target_pairs={{0,8},{4,12},{8,0},{12,4},{1,9},{5,13},{9,1},{13,5},{2,10},{6,14},... | collective-permute-start | bytes 196616 | tf_op jit(solution)/shard_map/ppermute | solution.py:169
  31.4 1.0 %collective-permute-done.5 = bf16[4,128,128]{2,1,0:T(8,128)(2,1)S(1)} collective-permute-done((bf16[4,128,128]{2,1,0:T(8,128)(2,1)S(1)}, bf16[4,128,128]{2,1,0:T(8,128)(2,1)S(1)}, u32[]{:S(2)}, u32[]{:S(2)}) %collective-permute-start.5) | collective-permute-done | bytes 131104 | tf_op jit(solution)/shard_map/ppermute | solution.py:169
  32.5 1.6 %collective-permute-start.13 = (bf16[4,64,128]{2,1,0:T(8,128)(2,1)S(1)}, bf16[4,64,128]{2,1,0:T(8,128)(2,1)S(1)}, u32[]{:S(2)}, u32[]{:S(2)}) collective-permute-start(bf16[4,64,128]{2,1,0:T(8,128)(2,1)S(1)} %add_convert_fusion), channel_id=1, source_target_pairs={{0,12},{4,0},{8,4},{12,8},{1,13},{5,1},{9,5},{13,9},{2,14},{6,2},{... | collective-permute-start | bytes 196616 | tf_op jit(solution)/shard_map/ppermute | solution.py:169
  34.1 0.0 collective-permute-done.8
  34.1 0.5 %collective-permute-start.12 = (bf16[4,64,128]{2,1,0:T(8,128)(2,1)S(1)}, bf16[4,64,128]{2,1,0:T(8,128)(2,1)S(1)}, u32[]{:S(2)}, u32[]{:S(2)}) collective-permute-start(bf16[4,64,128]{2,1,0:T(8,128)(2,1)S(1)} %add_convert_fusion.1), channel_id=1, source_target_pairs={{0,4},{4,8},{8,12},{12,0},{1,5},{5,9},{9,13},{13,1},{2,6},{6,10},{... | collective-permute-start | bytes 196616 | tf_op jit(solution)/shard_map/ppermute | solution.py:169
  34.7 0.0 collective-permute-done.9
  34.7 1.2 %collective-permute-done.11 = bf16[4,64,128]{2,1,0:T(8,128)(2,1)S(1)} collective-permute-done((bf16[4,64,128]{2,1,0:T(8,128)(2,1)S(1)}, bf16[4,64,128]{2,1,0:T(8,128)(2,1)S(1)}, u32[]{:S(2)}, u32[]{:S(2)}) %collective-permute-start.11) | collective-permute-done | bytes 65568 | tf_op jit(solution)/shard_map/ppermute | solution.py:169
  35.9 4.3 %collective-permute-done.12 = bf16[4,64,128]{2,1,0:T(8,128)(2,1)S(1)} collective-permute-done((bf16[4,64,128]{2,1,0:T(8,128)(2,1)S(1)}, bf16[4,64,128]{2,1,0:T(8,128)(2,1)S(1)}, u32[]{:S(2)}, u32[]{:S(2)}) %collective-permute-start.12) | collective-permute-done | bytes 65568 | tf_op jit(solution)/shard_map/ppermute | solution.py:169
  40.3 0.0 collective-permute-done.13
  40.3 0.7 %pad_maximum_fusion = f32[4,128,128]{2,1,0:T(8,128)} fusion(f32[4,64,128]{2,1,0:T(8,128)S(1)} %convert_add_fusion, f32[4,64,128]{2,1,0:T(8,128)S(1)} %convert_add_fusion.3), kind=kLoop, calls=%fused_computation | loop fusion | flops 65536 | bytes 524288 | tf_op jit(solution)/shard_map/concatenate | solution.py:223
  (18 shorter events, 0.3 us)
Async XLA Ops:
  0.7 11.1 %collective-permute-start.2 = (f32[4,32]{1,0:T(4,128)S(1)}, f32[4,32]{1,0:T(4,128)S(1)}, u32[]{:S(2)}, u32[]{:S(2)}) collective-permute-start(f32[4,32]{1,0:T(4,128)S(1)} %select_bitcast_fusion), channel_id=1, source_target_pairs={{0,4},{4,8},{8,12},{12,0},{1,5},{5,9},{9,13},{13,1},{2,6},{6,10},{... | collective-permute-start | bytes 1544 | tf_op jit(solution)/shard_map/ppermute | solution.py:169
  3.7 8.1 %collective-permute-start.1 = (f32[4,32]{1,0:T(4,128)S(1)}, f32[4,32]{1,0:T(4,128)S(1)}, u32[]{:S(2)}, u32[]{:S(2)}) collective-permute-start(f32[4,32]{1,0:T(4,128)S(1)} %select_bitcast_fusion), channel_id=1, source_target_pairs={{0,8},{4,12},{8,0},{12,4},{1,9},{5,13},{9,1},{13,5},{2,10},{6,14},... | collective-permute-start | bytes 1544 | tf_op jit(solution)/shard_map/ppermute | solution.py:169
  6.3 5.5 %collective-permute-start = (f32[4,32]{1,0:T(4,128)S(1)}, f32[4,32]{1,0:T(4,128)S(1)}, u32[]{:S(2)}, u32[]{:S(2)}) collective-permute-start(f32[4,32]{1,0:T(4,128)S(1)} %select_bitcast_fusion), channel_id=1, source_target_pairs={{0,12},{4,0},{8,4},{12,8},{1,13},{5,1},{9,5},{13,9},{2,14},{6,2},{... | collective-permute-start | bytes 1544 | tf_op jit(solution)/shard_map/ppermute | solution.py:169
  15.5 5.8 %collective-permute-start.4 = (bf16[4,64,128]{2,1,0:T(8,128)(2,1)S(1)}, bf16[4,64,128]{2,1,0:T(8,128)(2,1)S(1)}, u32[]{:S(2)}, u32[]{:S(2)}) collective-permute-start(bf16[4,64,128]{2,1,0:T(8,128)(2,1)S(1)} %get-tuple-element.30), channel_id=1, source_target_pairs={{0,2},{2,0},{1,3},{3,1},{4,6},{6,4},{5,7},{7,5},{8,10},{10,8},{9,1... | collective-permute-start | bytes 196616 | tf_op jit(solution)/shard_map/ppermute | solution.py:169
  17.1 6.5 %collective-permute-start.3 = (bf16[8,64,128]{2,1,0:T(8,128)(2,1)S(1)}, bf16[8,64,128]{2,1,0:T(8,128)(2,1)S(1)}, u32[]{:S(2)}, u32[]{:S(2)}) collective-permute-start(bf16[8,64,128]{2,1,0:T(8,128)(2,1)S(1)} %get-tuple-element.29), channel_id=1, source_target_pairs={{0,2},{2,0},{1,3},{3,1},{4,6},{6,4},{5,7},{7,5},{8,10},{10,8},{9,1... | collective-permute-start | bytes 393224 | tf_op jit(solution)/shard_map/ppermute | solution.py:169
  21.3 12.8 %collective-permute-start.8 = (bf16[4,64,128]{2,1,0:T(8,128)(2,1)S(1)}, bf16[4,64,128]{2,1,0:T(8,128)(2,1)S(1)}, u32[]{:S(2)}, u32[]{:S(2)}) collective-permute-start(bf16[4,64,128]{2,1,0:T(8,128)(2,1)S(1)} %add_convert_fusion.5), channel_id=1, source_target_pairs={{0,8},{4,12},{8,0},{12,4},{1,9},{5,13},{9,1},{13,5},{2,10},{6,14},... | collective-permute-start | bytes 196616 | tf_op jit(solution)/shard_map/ppermute | solution.py:169
  21.5 6.0 %collective-permute-start.7 = (bf16[4,64,128]{2,1,0:T(8,128)(2,1)S(1)}, bf16[4,64,128]{2,1,0:T(8,128)(2,1)S(1)}, u32[]{:S(2)}, u32[]{:S(2)}) collective-permute-start(bf16[4,64,128]{2,1,0:T(8,128)(2,1)S(1)} %get-tuple-element.38), channel_id=1, source_target_pairs={{0,2},{2,0},{1,3},{3,1},{4,6},{6,4},{5,7},{7,5},{8,10},{10,8},{9,1... | collective-permute-start | bytes 196616 | tf_op jit(solution)/shard_map/ppermute | solution.py:169
  23.2 6.1 %collective-permute-start.6 = (bf16[8,64,128]{2,1,0:T(8,128)(2,1)S(1)}, bf16[8,64,128]{2,1,0:T(8,128)(2,1)S(1)}, u32[]{:S(2)}, u32[]{:S(2)}) collective-permute-start(bf16[8,64,128]{2,1,0:T(8,128)(2,1)S(1)} %get-tuple-element.36), channel_id=1, source_target_pairs={{0,2},{2,0},{1,3},{3,1},{4,6},{6,4},{5,7},{7,5},{8,10},{10,8},{9,1... | collective-permute-start | bytes 393224 | tf_op jit(solution)/shard_map/ppermute | solution.py:169
  23.6 11.1 %collective-permute-start.9 = (bf16[4,64,128]{2,1,0:T(8,128)(2,1)S(1)}, bf16[4,64,128]{2,1,0:T(8,128)(2,1)S(1)}, u32[]{:S(2)}, u32[]{:S(2)}) collective-permute-start(bf16[4,64,128]{2,1,0:T(8,128)(2,1)S(1)} %add_convert_fusion.4), channel_id=1, source_target_pairs={{0,4},{4,8},{8,12},{12,0},{1,5},{5,9},{9,13},{13,1},{2,6},{6,10},{... | collective-permute-start | bytes 196616 | tf_op jit(solution)/shard_map/ppermute | solution.py:169
  25.3 9.4 %collective-permute-start.10 = (bf16[4,64,128]{2,1,0:T(8,128)(2,1)S(1)}, bf16[4,64,128]{2,1,0:T(8,128)(2,1)S(1)}, u32[]{:S(2)}, u32[]{:S(2)}) collective-permute-start(bf16[4,64,128]{2,1,0:T(8,128)(2,1)S(1)} %add_convert_fusion.3), channel_id=1, source_target_pairs={{0,12},{4,0},{8,4},{12,8},{1,13},{5,1},{9,5},{13,9},{2,14},{6,2},{... | collective-permute-start | bytes 196616 | tf_op jit(solution)/shard_map/ppermute | solution.py:169
  27.5 5.0 %collective-permute-start.5 = (bf16[4,128,128]{2,1,0:T(8,128)(2,1)S(1)}, bf16[4,128,128]{2,1,0:T(8,128)(2,1)S(1)}, u32[]{:S(2)}, u32[]{:S(2)}) collective-permute-start(bf16[4,128,128]{2,1,0:T(8,128)(2,1)S(1)} %get-tuple-element.33), channel_id=1, source_target_pairs={{0,2},{2,0},{1,3},{3,1},{4,6},{6,4},{5,7},{7,5},{8,10},{10,8},{9,1... | collective-permute-start | bytes 393224 | tf_op jit(solution)/shard_map/ppermute | solution.py:169
  29.3 6.6 %collective-permute-start.11 = (bf16[4,64,128]{2,1,0:T(8,128)(2,1)S(1)}, bf16[4,64,128]{2,1,0:T(8,128)(2,1)S(1)}, u32[]{:S(2)}, u32[]{:S(2)}) collective-permute-start(bf16[4,64,128]{2,1,0:T(8,128)(2,1)S(1)} %add_convert_fusion.2), channel_id=1, source_target_pairs={{0,8},{4,12},{8,0},{12,4},{1,9},{5,13},{9,1},{13,5},{2,10},{6,14},... | collective-permute-start | bytes 196616 | tf_op jit(solution)/shard_map/ppermute | solution.py:169
  32.5 7.8 %collective-permute-start.13 = (bf16[4,64,128]{2,1,0:T(8,128)(2,1)S(1)}, bf16[4,64,128]{2,1,0:T(8,128)(2,1)S(1)}, u32[]{:S(2)}, u32[]{:S(2)}) collective-permute-start(bf16[4,64,128]{2,1,0:T(8,128)(2,1)S(1)} %add_convert_fusion), channel_id=1, source_target_pairs={{0,12},{4,0},{8,4},{12,8},{1,13},{5,1},{9,5},{13,9},{2,14},{6,2},{... | collective-permute-start | bytes 196616 | tf_op jit(solution)/shard_map/ppermute | solution.py:169
  34.1 6.1 %collective-permute-start.12 = (bf16[4,64,128]{2,1,0:T(8,128)(2,1)S(1)}, bf16[4,64,128]{2,1,0:T(8,128)(2,1)S(1)}, u32[]{:S(2)}, u32[]{:S(2)}) collective-permute-start(bf16[4,64,128]{2,1,0:T(8,128)(2,1)S(1)} %add_convert_fusion.1), channel_id=1, source_target_pairs={{0,4},{4,8},{8,12},{12,0},{1,5},{5,9},{9,13},{13,1},{2,6},{6,10},{... | collective-permute-start | bytes 196616 | tf_op jit(solution)/shard_map/ppermute | solution.py:169

commit v12 on v8

v12 whole, which is shorter than its diff:
```python
import functools

import jax
import jax.numpy as jnp
from jax import lax
from jax.experimental import pallas as pl
from jax.experimental.pallas import tpu as pltpu
from jax.sharding import PartitionSpec as P

MIX_TERMS = 8
SUM_TERMS = 4
MIB = 1024 * 1024


def wrapped(value, size):
    if size & (size - 1) == 0:
        return value & (size - 1)
    return lax.rem(value + size, size)


def mix_kernel(split, wave_ref, left_ref, right_ref, mixed_ref, held_ref, wave, left, sems):
    sec_dev = wave.shape[0]
    terms, rows, width = left.shape
    chunks = terms // MIX_TERMS

    def left_copy(c):
        part = pl.ds(c * MIX_TERMS, MIX_TERMS)
        return pltpu.make_async_copy(left_ref.at[part], left.at[part], sems.at[3 + c])

    wave_copy = pltpu.make_async_copy(wave_ref, wave, sems.at[0])
    wave_copy.start()
    for c in range(chunks):
        left_copy(c).start()
    if split:
        half = width // 2
        side = lax.axis_index("op")
        mine = pl.multiple_of(side * half, half)
        theirs = pl.multiple_of((1 - side) * half, half)
        right_copies = [
            pltpu.make_async_copy(
                right_ref.at[:, pl.ds(theirs, half)], held_ref.at[:, pl.ds(0, half)], sems.at[1]
            ),
            pltpu.make_async_copy(
                right_ref.at[:, pl.ds(mine, half)], held_ref.at[:, pl.ds(half, half)], sems.at[2]
            ),
        ]
    else:
        right_copies = [pltpu.make_async_copy(right_ref, held_ref, sems.at[1])]
    for copy in right_copies:
        copy.start()
    wave_copy.wait()

    @pl.loop(0, chunks)
    def _(c):
        left_copy(c).wait()
        part = pl.ds(c * MIX_TERMS, MIX_TERMS)
        rows_in = left[part].reshape(MIX_TERMS * rows, width)
        for s in range(sec_dev):
            product = jnp.dot(rows_in, wave[s], preferred_element_type=jnp.float32)
            mixed_ref[part, s] = product.astype(jnp.bfloat16).reshape(MIX_TERMS, rows, width)

    for copy in right_copies:
        copy.wait()


def mix(wavefunction, left_ops, right_ops, split):
    k_dev, rows, width = left_ops.shape
    sec_dev = wavefunction.shape[0]
    return pl.pallas_call(
        functools.partial(mix_kernel, split),
        out_shape=[
            pltpu.VMEM((k_dev, sec_dev, rows, width), jnp.bfloat16),
            pltpu.VMEM(right_ops.shape, jnp.bfloat16),
        ],
        in_specs=[pl.BlockSpec(memory_space=pltpu.HBM)] * 3,
        out_specs=[pl.BlockSpec(memory_space=pltpu.VMEM)] * 2,
        scratch_shapes=[
            pltpu.VMEM(wavefunction.shape, jnp.bfloat16),
            pltpu.VMEM(left_ops.shape, jnp.bfloat16),
            pltpu.SemaphoreType.DMA((3 + k_dev // MIX_TERMS,)),
        ],
        compiler_params=pltpu.CompilerParams(vmem_limit_bytes=24 * MIB),
        cost_estimate=pl.CostEstimate(
            flops=2 * k_dev * sec_dev * rows * width * width,
            bytes_accessed=2 * (left_ops.size + right_ops.size),
            transcendentals=0,
        ),
    )(*(pltpu.with_memory_space_constraint(x, pltpu.HBM) for x in (wavefunction, left_ops, right_ops)))


def reaches(shift, group, sec_dev, targets):
    return wrapped(-shift - group * sec_dev + sec_dev - 1, targets) < 2 * sec_dev - 1


def sum_kernel(far, stage, shift_ref, coef_ref, mixed_ref, held_ref, *refs):
    terms, sec_dev, rows, width = mixed_ref.shape
    targets = coef_ref.shape[0]
    groups = targets // sec_dev
    half = width // 2
    picked = refs[-1]

    def pick(k, count):
        picked[count] = k
        if stage is None:
            return count + 1
        wanted = reaches(shift_ref[k], far, sec_dev, targets) == (stage == 0)
        return count + jnp.where(wanted, 1, 0)

    count = lax.fori_loop(0, terms, pick, 0)
    for i in range(SUM_TERMS):
        picked[count + i] = 0

    if stage is None:
        sums = refs[:1]
    elif stage == 0:
        sums, rounded = refs[:2], refs[2]
    else:
        before, sums, rounded = refs[:2], (refs[2], refs[-2]), refs[3:-2]
    for total in sums:
        total[...] = jnp.zeros_like(total)

    @pl.loop(0, lax.div(count + SUM_TERMS - 1, SUM_TERMS))
    def _(step):
        for t in range(SUM_TERMS):
            at = step * SUM_TERMS + t
            k = picked[at]
            product = lax.dot_general(
                mixed_ref[k].reshape(sec_dev * rows, width),
                held_ref[k],
                (((1,), (1,)), ((), ())),
                preferred_element_type=jnp.float32,
            )
            for s in range(sec_dev):
                target = wrapped(s - shift_ref[k], targets)
                weight = jnp.where(at < count, coef_ref[target, k], 0.0)
                scaled = weight * product[s * rows : (s + 1) * rows]
                if stage is None:
                    sums[0][target] += scaled
                else:
                    sums[0][target] += scaled[:, half:]
                    sums[1][target] += scaled[:, :half]

    def part(ref, g):
        return ref[g * sec_dev : (g + 1) * sec_dev]

    if stage == 0:
        rounded[...] = part(sums[1], far).astype(jnp.bfloat16)
    elif stage == 1:
        near = [g for g in range(1, groups) if g != far]
        for g in near:
            sums[0][g * sec_dev : (g + 1) * sec_dev] += part(before[0], g)
        for g, out in zip([0] + near, rounded):
            theirs = part(sums[1], g)
            out[...] = (theirs if g == 0 else theirs + part(before[1], g)).astype(jnp.bfloat16)


def summed(shift, coef, mixed, held, far, stage, before=()):
    k_dev, sec_dev, rows, width = mixed.shape
    targets = coef.shape[0]
    columns = width if stage is None else width // 2
    whole = pltpu.VMEM((targets, rows, columns), jnp.float32)
    rounded = pltpu.VMEM((sec_dev, rows, columns), jnp.bfloat16)
    scratch = [pltpu.SMEM((k_dev + SUM_TERMS,), jnp.int32)]
    out_shape = [whole]
    if stage == 0:
        out_shape = [whole, whole, rounded]
    elif stage == 1:
        out_shape = [whole] + [rounded] * (targets // sec_dev - 1)
        scratch = [whole] + scratch
    in_vmem = (mixed, held, *before)
    return pl.pallas_call(
        functools.partial(sum_kernel, far, stage),
        out_shape=out_shape,
        in_specs=[pl.BlockSpec(memory_space=pltpu.SMEM)] * 2
        + [pl.BlockSpec(memory_space=pltpu.VMEM)] * len(in_vmem),
        out_specs=[pl.BlockSpec(memory_space=pltpu.VMEM)] * len(out_shape),
        scratch_shapes=scratch,
        compiler_params=pltpu.CompilerParams(vmem_limit_bytes=24 * MIB),
        cost_estimate=pl.CostEstimate(
            flops=k_dev * sec_dev * rows * width * width,
            bytes_accessed=mixed.size + held.size,
            transcendentals=0,
        ),
    )(
        pltpu.with_memory_space_constraint(shift, pltpu.HBM),
        coef,
        *(pltpu.with_memory_space_constraint(x, pltpu.VMEM) for x in in_vmem),
    )


def shift_by(value, axis, distance):
    size = lax.axis_size(axis)
    return lax.ppermute(value, axis, [(i, (i + distance) % size) for i in range(size)])


def after(value, other):
    return lax.optimization_barrier((value, other))[0]


def per_device(wavefunction, left_ops, right_ops, site_coef, coupled, sector_shift):
    sec_dev = wavefunction.shape[0]
    devices = lax.axis_size("sector")
    live = jnp.where(coupled.T > 0, site_coef.T, 0.0)
    split = lax.axis_size("op") == 2 and devices == 4
    mixed, held = mix(wavefunction, left_ops, right_ops, split)

    if split:
        coefs = [live] + [shift_by(live, "sector", -g) for g in range(1, devices)]
        coef = jnp.concatenate(coefs, axis=0)
        far, near = 2, (1, 3)

        def own(sums, g):
            return sums[g * sec_dev : (g + 1) * sec_dev]

        *first, theirs = summed(sector_shift, coef, mixed, held, far, 0)
        crossed = shift_by(theirs, "op", 1)
        mine, *theirs = summed(sector_shift, coef, mixed, held, far, 1, first)
        other = after(crossed, mine).astype(jnp.float32)
        both = (own(first[0], far) + other).astype(jnp.bfloat16)
        arrived = [shift_by(both, "sector", far)]
        crossed = {g: shift_by(after(theirs[at], both), "op", 1) for at, g in enumerate(near, 1)}
        for g in near:
            if g == near[1]:
                crossed[0] = shift_by(after(theirs[0], both), "op", 1)
            other = after(crossed[g], both).astype(jnp.float32)
            both = (own(mine, g) + other).astype(jnp.bfloat16)
            arrived.append(shift_by(both, "sector", g))
        sigma = own(mine, 0) + after(crossed[0], both).astype(jnp.float32)
        for other in arrived:
            sigma = lax.optimization_barrier(sigma) + other.astype(jnp.float32)
        return sigma

    first = lax.axis_index("sector") * sec_dev
    coef = jnp.roll(lax.all_gather(live, "sector", axis=0, tiled=True), -first, axis=0)
    (total,) = summed(sector_shift, coef, mixed, held, None, None)
    total = jnp.roll(total, first, axis=0)
    total = lax.psum_scatter(total, "op", scatter_dimension=2, tiled=True)
    return lax.psum_scatter(total, "sector", scatter_dimension=0, tiled=True)


def solution(mesh):
    placed = (
        P(("groups", "sector"), None, None),
        P(("groups", "op"), "rep", None),
        P(("groups", "op"), None, None),
        P(("groups", "op"), "sector"),
        P(("groups", "op"), "sector"),
        P(("groups", "op")),
    )
    return jax.shard_map(
        per_device,
        mesh=mesh,
        in_specs=placed,
        out_specs=P(("groups", "sector"), "rep", "op"),
        check_vma=False,
    )
```

time: 37 us -> 36.1 us (0.976); the launches traced: 36.8 us -> 36.4 us
  starting transfers between devices: 14.5 us -> 15.3 us
  waiting for transfers between devices: 8.79 us -> 8.04 us
  Pallas kernels: 11.8 us -> 11.4 us
    ppermute x10, waiting for transfers between devices: 8.79 us -> 8.04 us  [shift_by(): lax.ppermute(value, axis, [(i, (i + distance) % size) for i in range(size)])]
    ppermute x10, starting transfers between devices: 14.5 us -> 15.3 us  [shift_by(): lax.ppermute(value, axis, [(i, (i + distance) % size) for i in range(size)])]
    pallas_call x2, Pallas kernels: 7.67 us -> 7.27 us  [summed(): pl.pallas_call(functools.partial(sum_kernel, far, stage), out_shape=out_s...]
  transfers between devices with their start and end apart: 10 -> 10, of which waited for: 4 -> 5; matrix products, arithmetic and copies ran while one was open for 0% -> 0% of each run, Pallas kernels for 21% -> 24%
where the time goes in v12:
time: 36.1 us; the launch traced here: 36.4 us
  starting transfers between devices  15.3 us (42%)
  Pallas kernels  11.4 us (32%)
  waiting for transfers between devices  8.04 us (22%)
  other arithmetic  1.64 us (5%)
    ppermute x10, starting transfers between devices, shift_by(): lax.ppermute(value, axis, [(i, (i + distance) % size) for i in range(size)])  15.3 us
    ppermute x10, waiting for transfers between devices, shift_by(): lax.ppermute(value, axis, [(i, (i + distance) % size) for i in range(size)])  8.04 us
    pallas_call x2, Pallas kernels, summed(): pl.pallas_call(functools.partial(sum_kernel, far, stage), out_shape=out_s...  7.27 us
    pallas_call x1, Pallas kernels, mix(): pl.pallas_call(functools.partial(mix_kernel, split), out_shape=[pltpu.VME...  4.11 us
    add x3, other arithmetic, per_device(): sigma = lax.optimization_barrier(sigma) + other.astype(jnp.float32)  0.78 us
  transfers between devices with their start and end apart: 10, of which 5 were waited for; matrix products, arithmetic and copies ran while one was open for 0% of the time, Pallas kernels for 24%

profile of v12, /device:TPU:0, one launch (start us, length us, event | category | flops | bytes accessed | tf_op | source)
XLA Modules:
  0.0 36.4 jit_solution(13526948392979869236)
XLA Ops:
  0.0 0.7 %select_bitcast_fusion = f32[4,32]{1,0:T(4,128)S(1)} fusion(f32[32,4]{0,1:T(4,128)} %param.9, s32[32,4]{0,1:T(4,128)} %param.10), kind=kLoop, calls=%fused_computation.8 | loop fusion | flops 256 | bytes 1536 | tf_op jit(solution)/shard_map/jit(_where)/select_n | solution.py:203
  0.7 3.0 %collective-permute-start.2 = (f32[4,32]{1,0:T(4,128)S(1)}, f32[4,32]{1,0:T(4,128)S(1)}, u32[]{:S(2)}, u32[]{:S(2)}) collective-permute-start(f32[4,32]{1,0:T(4,128)S(1)} %select_bitcast_fusion), channel_id=1, source_target_pairs={{0,4},{4,8},{8,12},{12,0},{1,5},{5,9},{9,13},{13,1},{2,6},{6,10},{... | collective-permute-start | bytes 1544 | tf_op jit(solution)/shard_map/ppermute | solution.py:193
  3.7 2.6 %collective-permute-start.1 = (f32[4,32]{1,0:T(4,128)S(1)}, f32[4,32]{1,0:T(4,128)S(1)}, u32[]{:S(2)}, u32[]{:S(2)}) collective-permute-start(f32[4,32]{1,0:T(4,128)S(1)} %select_bitcast_fusion), channel_id=1, source_target_pairs={{0,8},{4,12},{8,0},{12,4},{1,9},{5,13},{9,1},{13,5},{2,10},{6,14},... | collective-permute-start | bytes 1544 | tf_op jit(solution)/shard_map/ppermute | solution.py:193
  6.3 1.3 %collective-permute-start = (f32[4,32]{1,0:T(4,128)S(1)}, f32[4,32]{1,0:T(4,128)S(1)}, u32[]{:S(2)}, u32[]{:S(2)}) collective-permute-start(f32[4,32]{1,0:T(4,128)S(1)} %select_bitcast_fusion), channel_id=1, source_target_pairs={{0,12},{4,0},{8,4},{12,8},{1,13},{5,1},{9,5},{13,9},{2,14},{6,2},{... | collective-permute-start | bytes 1544 | tf_op jit(solution)/shard_map/ppermute | solution.py:193
  7.7 4.1 %shard_map.64 = (bf16[32,4,128,256]{3,2,1,0:T(8,128)(2,1)S(1)}, bf16[32,256,256]{2,1,0:T(8,128)(2,1)S(1)}) custom-call(bf16[4,256,256]{2,1,0:T(8,128)(2,1)} %wave_ref.1, bf16[32,128,256]{2,1,0:T(8,128)(2,1)} %left_ref.1, bf16[32,256,256]{2,1,0:T(8,128)(2,1)} %right_ref.1), custom_call_target="tpu_custom_call" | custom-call | flops 2147483648 | bytes 6291456 | tf_op jit(solution)/shard_map/pallas_call | solution.py:69
  11.8 0.0 collective-permute-done.2
  11.8 0.0 collective-permute-done.1
  11.8 0.0 collective-permute-done
  11.8 2.7 %shard_map.65 = (f32[16,128,128]{2,1,0:T(8,128)S(1)}, f32[16,128,128]{2,1,0:T(8,128)S(1)}, bf16[4,128,128]{2,1,0:T(8,128)(2,1)S(1)}) custom-call(s32[32]{0:T(128)} %shift_ref.3, f32[16,32]{1,0:T(8,128)S(1)} %pad_maximum_fusion.coef_ref, bf16[32,4,128,256]{3,2,1,0:T(8,128)(2,1)S(1)} %get-tuple-element.21.mixed_ref, ...), custom_call_target="tpu_custom_call" | custom-call | flops 1073741824 | bytes 6291456 | tf_op jit(solution)/shard_map/pallas_call | solution.py:171
  14.6 2.7 %collective-permute-start.3 = (bf16[4,128,128]{2,1,0:T(8,128)(2,1)S(1)}, bf16[4,128,128]{2,1,0:T(8,128)(2,1)S(1)}, u32[]{:S(2)}, u32[]{:S(2)}) collective-permute-start(bf16[4,128,128]{2,1,0:T(8,128)(2,1)S(1)} %get-tuple-element.28), channel_id=1, source_target_pairs={{0,2},{2,0},{1,3},{3,1},{4,6},{6,4},{5,7},{7,5},{8,10},{10,8},{9,1... | collective-permute-start | bytes 393224 | tf_op jit(solution)/shard_map/ppermute | solution.py:193
  17.2 4.5 %shard_map.66 = (f32[16,128,128]{2,1,0:T(8,128)S(1)}, bf16[4,128,128]{2,1,0:T(8,128)(2,1)S(1)}, bf16[4,128,128]{2,1,0:T(8,128)(2,1)S(1)}, bf16[4,128,128]{2,1,0:T(8,128)(2,1)S(1)}) custom-call(s32[32]{0:T(128)} %shift_ref.3, f32[16,32]{1,0:T(8,128)S(1)} %pad_maximum_fusion.coef_ref, bf16[32,4,128,256]{3,2,1,0:T(8,128)(2,1)S(1)} %get-tuple-element.21.mixed_ref, ...), custom_call_target="tpu_custom_call" | custom-call | flops 1073741824 | bytes 6291456 | tf_op jit(solution)/shard_map/pallas_call | solution.py:171
  21.8 0.0 collective-permute-done.3
  21.8 0.5 %collective-permute-start.4 = (bf16[4,128,128]{2,1,0:T(8,128)(2,1)S(1)}, bf16[4,128,128]{2,1,0:T(8,128)(2,1)S(1)}, u32[]{:S(2)}, u32[]{:S(2)}) collective-permute-start(bf16[4,128,128]{2,1,0:T(8,128)(2,1)S(1)} %get-tuple-element.30), channel_id=1, source_target_pairs={{0,2},{2,0},{1,3},{3,1},{4,6},{6,4},{5,7},{7,5},{8,10},{10,8},{9,1... | collective-permute-start | bytes 393224 | tf_op jit(solution)/shard_map/ppermute | solution.py:193
  22.3 0.3 collective-permute-start.7
  22.6 1.6 %collective-permute-start.6 = (bf16[4,128,128]{2,1,0:T(8,128)(2,1)S(1)}, bf16[4,128,128]{2,1,0:T(8,128)(2,1)S(1)}, u32[]{:S(2)}, u32[]{:S(2)}) collective-permute-start(bf16[4,128,128]{2,1,0:T(8,128)(2,1)S(1)} %get-tuple-element.34), channel_id=1, source_target_pairs={{0,2},{2,0},{1,3},{3,1},{4,6},{6,4},{5,7},{7,5},{8,10},{10,8},{9,1... | collective-permute-start | bytes 393224 | tf_op jit(solution)/shard_map/ppermute | solution.py:193
  24.2 3.2 %collective-permute-done.4 = bf16[4,128,128]{2,1,0:T(8,128)(2,1)S(1)} collective-permute-done((bf16[4,128,128]{2,1,0:T(8,128)(2,1)S(1)}, bf16[4,128,128]{2,1,0:T(8,128)(2,1)S(1)}, u32[]{:S(2)}, u32[]{:S(2)}) %collective-permute-start.4) | collective-permute-done | bytes 131104 | tf_op jit(solution)/shard_map/ppermute | solution.py:193
  27.4 0.9 %collective-permute-start.8 = (bf16[4,128,128]{2,1,0:T(8,128)(2,1)S(1)}, bf16[4,128,128]{2,1,0:T(8,128)(2,1)S(1)}, u32[]{:S(2)}, u32[]{:S(2)}) collective-permute-start(bf16[4,128,128]{2,1,0:T(8,128)(2,1)S(1)} %add_convert_fusion.1), channel_id=1, source_target_pairs={{0,4},{4,8},{8,12},{12,0},{1,5},{5,9},{9,13},{13,1},{2,6},{6,10},{... | collective-permute-start | bytes 393224 | tf_op jit(solution)/shard_map/ppermute | solution.py:193
  28.3 0.5 %collective-permute-start.5 = (bf16[4,128,128]{2,1,0:T(8,128)(2,1)S(1)}, bf16[4,128,128]{2,1,0:T(8,128)(2,1)S(1)}, u32[]{:S(2)}, u32[]{:S(2)}) collective-permute-start(bf16[4,128,128]{2,1,0:T(8,128)(2,1)S(1)} %get-tuple-element.32), channel_id=1, source_target_pairs={{0,2},{2,0},{1,3},{3,1},{4,6},{6,4},{5,7},{7,5},{8,10},{10,8},{9,1... | collective-permute-start | bytes 393224 | tf_op jit(solution)/shard_map/ppermute | solution.py:193
  28.8 1.2 %collective-permute-done.6 = bf16[4,128,128]{2,1,0:T(8,128)(2,1)S(1)} collective-permute-done((bf16[4,128,128]{2,1,0:T(8,128)(2,1)S(1)}, bf16[4,128,128]{2,1,0:T(8,128)(2,1)S(1)}, u32[]{:S(2)}, u32[]{:S(2)}) %collective-permute-start.6) | collective-permute-done | bytes 131104 | tf_op jit(solution)/shard_map/ppermute | solution.py:193
  30.1 1.8 %collective-permute-start.9 = (bf16[4,128,128]{2,1,0:T(8,128)(2,1)S(1)}, bf16[4,128,128]{2,1,0:T(8,128)(2,1)S(1)}, u32[]{:S(2)}, u32[]{:S(2)}) collective-permute-start(bf16[4,128,128]{2,1,0:T(8,128)(2,1)S(1)} %add_convert_fusion), channel_id=1, source_target_pairs={{0,12},{4,0},{8,4},{12,8},{1,13},{5,1},{9,5},{13,9},{2,14},{6,2},{... | collective-permute-start | bytes 393224 | tf_op jit(solution)/shard_map/ppermute | solution.py:193
  31.9 1.4 %collective-permute-done.5 = bf16[4,128,128]{2,1,0:T(8,128)(2,1)S(1)} collective-permute-done((bf16[4,128,128]{2,1,0:T(8,128)(2,1)S(1)}, bf16[4,128,128]{2,1,0:T(8,128)(2,1)S(1)}, u32[]{:S(2)}, u32[]{:S(2)}) %collective-permute-start.5) | collective-permute-done | bytes 131104 | tf_op jit(solution)/shard_map/ppermute | solution.py:193
  33.3 0.0 collective-permute-done.7
  33.4 0.9 %collective-permute-done.8 = bf16[4,128,128]{2,1,0:T(8,128)(2,1)S(1)} collective-permute-done((bf16[4,128,128]{2,1,0:T(8,128)(2,1)S(1)}, bf16[4,128,128]{2,1,0:T(8,128)(2,1)S(1)}, u32[]{:S(2)}, u32[]{:S(2)}) %collective-permute-start.8) | collective-permute-done | bytes 131104 | tf_op jit(solution)/shard_map/ppermute | solution.py:193
  34.4 1.3 %collective-permute-done.9 = bf16[4,128,128]{2,1,0:T(8,128)(2,1)S(1)} collective-permute-done((bf16[4,128,128]{2,1,0:T(8,128)(2,1)S(1)}, bf16[4,128,128]{2,1,0:T(8,128)(2,1)S(1)}, u32[]{:S(2)}, u32[]{:S(2)}) %collective-permute-start.9) | collective-permute-done | bytes 131104 | tf_op jit(solution)/shard_map/ppermute | solution.py:193
  35.7 0.7 %convert_add_fusion = f32[4,128,128]{2,1,0:T(8,128)} fusion(f32[4,128,128]{2,1,0:T(8,128)S(1)} %convert_add_fusion.1, bf16[4,128,128]{2,1,0:T(8,128)(2,1)S(1)} %collective-permute-done.9), kind=kLoop, calls=%fused_computation | loop fusion | flops 131072 | bytes 655360 | tf_op jit(solution)/shard_map/add | solution.py:230
  (7 shorter events, 0.2 us)
Async XLA Ops:
  0.7 11.1 %collective-permute-start.2 = (f32[4,32]{1,0:T(4,128)S(1)}, f32[4,32]{1,0:T(4,128)S(1)}, u32[]{:S(2)}, u32[]{:S(2)}) collective-permute-start(f32[4,32]{1,0:T(4,128)S(1)} %select_bitcast_fusion), channel_id=1, source_target_pairs={{0,4},{4,8},{8,12},{12,0},{1,5},{5,9},{9,13},{13,1},{2,6},{6,10},{... | collective-permute-start | bytes 1544 | tf_op jit(solution)/shard_map/ppermute | solution.py:193
  3.7 8.1 %collective-permute-start.1 = (f32[4,32]{1,0:T(4,128)S(1)}, f32[4,32]{1,0:T(4,128)S(1)}, u32[]{:S(2)}, u32[]{:S(2)}) collective-permute-start(f32[4,32]{1,0:T(4,128)S(1)} %select_bitcast_fusion), channel_id=1, source_target_pairs={{0,8},{4,12},{8,0},{12,4},{1,9},{5,13},{9,1},{13,5},{2,10},{6,14},... | collective-permute-start | bytes 1544 | tf_op jit(solution)/shard_map/ppermute | solution.py:193
  6.3 5.5 %collective-permute-start = (f32[4,32]{1,0:T(4,128)S(1)}, f32[4,32]{1,0:T(4,128)S(1)}, u32[]{:S(2)}, u32[]{:S(2)}) collective-permute-start(f32[4,32]{1,0:T(4,128)S(1)} %select_bitcast_fusion), channel_id=1, source_target_pairs={{0,12},{4,0},{8,4},{12,8},{1,13},{5,1},{9,5},{13,9},{2,14},{6,2},{... | collective-permute-start | bytes 1544 | tf_op jit(solution)/shard_map/ppermute | solution.py:193
  14.6 7.2 %collective-permute-start.3 = (bf16[4,128,128]{2,1,0:T(8,128)(2,1)S(1)}, bf16[4,128,128]{2,1,0:T(8,128)(2,1)S(1)}, u32[]{:S(2)}, u32[]{:S(2)}) collective-permute-start(bf16[4,128,128]{2,1,0:T(8,128)(2,1)S(1)} %get-tuple-element.28), channel_id=1, source_target_pairs={{0,2},{2,0},{1,3},{3,1},{4,6},{6,4},{5,7},{7,5},{8,10},{10,8},{9,1... | collective-permute-start | bytes 393224 | tf_op jit(solution)/shard_map/ppermute | solution.py:193
  21.8 5.6 %collective-permute-start.4 = (bf16[4,128,128]{2,1,0:T(8,128)(2,1)S(1)}, bf16[4,128,128]{2,1,0:T(8,128)(2,1)S(1)}, u32[]{:S(2)}, u32[]{:S(2)}) collective-permute-start(bf16[4,128,128]{2,1,0:T(8,128)(2,1)S(1)} %get-tuple-element.30), channel_id=1, source_target_pairs={{0,2},{2,0},{1,3},{3,1},{4,6},{6,4},{5,7},{7,5},{8,10},{10,8},{9,1... | collective-permute-start | bytes 393224 | tf_op jit(solution)/shard_map/ppermute | solution.py:193
  22.3 11.0 %collective-permute-start.7 = (bf16[4,128,128]{2,1,0:T(8,128)(2,1)S(1)}, bf16[4,128,128]{2,1,0:T(8,128)(2,1)S(1)}, u32[]{:S(2)}, u32[]{:S(2)}) collective-permute-start(bf16[4,128,128]{2,1,0:T(8,128)(2,1)S(1)} %add_convert_fusion.2), channel_id=1, source_target_pairs={{0,8},{4,12},{8,0},{12,4},{1,9},{5,13},{9,1},{13,5},{2,10},{6,14},... | collective-permute-start | bytes 393224 | tf_op jit(solution)/shard_map/ppermute | solution.py:193
  22.6 7.4 %collective-permute-start.6 = (bf16[4,128,128]{2,1,0:T(8,128)(2,1)S(1)}, bf16[4,128,128]{2,1,0:T(8,128)(2,1)S(1)}, u32[]{:S(2)}, u32[]{:S(2)}) collective-permute-start(bf16[4,128,128]{2,1,0:T(8,128)(2,1)S(1)} %get-tuple-element.34), channel_id=1, source_target_pairs={{0,2},{2,0},{1,3},{3,1},{4,6},{6,4},{5,7},{7,5},{8,10},{10,8},{9,1... | collective-permute-start | bytes 393224 | tf_op jit(solution)/shard_map/ppermute | solution.py:193
  27.4 6.9 %collective-permute-start.8 = (bf16[4,128,128]{2,1,0:T(8,128)(2,1)S(1)}, bf16[4,128,128]{2,1,0:T(8,128)(2,1)S(1)}, u32[]{:S(2)}, u32[]{:S(2)}) collective-permute-start(bf16[4,128,128]{2,1,0:T(8,128)(2,1)S(1)} %add_convert_fusion.1), channel_id=1, source_target_pairs={{0,4},{4,8},{8,12},{12,0},{1,5},{5,9},{9,13},{13,1},{2,6},{6,10},{... | collective-permute-start | bytes 393224 | tf_op jit(solution)/shard_map/ppermute | solution.py:193
  28.3 5.0 %collective-permute-start.5 = (bf16[4,128,128]{2,1,0:T(8,128)(2,1)S(1)}, bf16[4,128,128]{2,1,0:T(8,128)(2,1)S(1)}, u32[]{:S(2)}, u32[]{:S(2)}) collective-permute-start(bf16[4,128,128]{2,1,0:T(8,128)(2,1)S(1)} %get-tuple-element.32), channel_id=1, source_target_pairs={{0,2},{2,0},{1,3},{3,1},{4,6},{6,4},{5,7},{7,5},{8,10},{10,8},{9,1... | collective-permute-start | bytes 393224 | tf_op jit(solution)/shard_map/ppermute | solution.py:193
  30.1 5.6 %collective-permute-start.9 = (bf16[4,128,128]{2,1,0:T(8,128)(2,1)S(1)}, bf16[4,128,128]{2,1,0:T(8,128)(2,1)S(1)}, u32[]{:S(2)}, u32[]{:S(2)}) collective-permute-start(bf16[4,128,128]{2,1,0:T(8,128)(2,1)S(1)} %add_convert_fusion), channel_id=1, source_target_pairs={{0,12},{4,0},{8,4},{12,8},{1,13},{5,1},{9,5},{13,9},{2,14},{6,2},{... | collective-permute-start | bytes 393224 | tf_op jit(solution)/shard_map/ppermute | solution.py:193

commit v13 on v12

--- a/solution.py
+++ b/solution.py
@@ -7,7 +7,7 @@
 from jax.experimental.pallas import tpu as pltpu
 from jax.sharding import PartitionSpec as P
 
-MIX_TERMS = 8
+MIX_TERMS = 16
 SUM_TERMS = 4
 MIB = 1024 * 1024
 
@@ -92,10 +92,9 @@
     return wrapped(-shift - group * sec_dev + sec_dev - 1, targets) < 2 * sec_dev - 1
 
 
-def sum_kernel(far, stage, shift_ref, coef_ref, mixed_ref, held_ref, *refs):
+def sum_kernel(order, stage, shift_ref, coef_ref, mixed_ref, held_ref, *refs):
     terms, sec_dev, rows, width = mixed_ref.shape
     targets = coef_ref.shape[0]
-    groups = targets // sec_dev
     half = width // 2
     picked = refs[-1]
 
@@ -103,7 +102,12 @@
         picked[count] = k
         if stage is None:
             return count + 1
-        wanted = reaches(shift_ref[k], far, sec_dev, targets) == (stage == 0)
+        wanted = True
+        for at, groups in enumerate(order[: stage + 1]):
+            if at < stage:
+                wanted &= ~reaches(shift_ref[k], groups[0], sec_dev, targets)
+            elif at < len(order) - 1:
+                wanted &= reaches(shift_ref[k], groups[0], sec_dev, targets)
         return count + jnp.where(wanted, 1, 0)
 
     count = lax.fori_loop(0, terms, pick, 0)
@@ -113,11 +117,12 @@
     if stage is None:
         sums = refs[:1]
     elif stage == 0:
-        sums, rounded = refs[:2], refs[2]
+        sums, outs = refs[:2], refs[2:-1]
     else:
-        before, sums, rounded = refs[:2], (refs[2], refs[-2]), refs[3:-2]
-    for total in sums:
-        total[...] = jnp.zeros_like(total)
+        sums, outs = refs[2:4], refs[4:-1]
+    if not stage:
+        for total in sums:
+            total[...] = jnp.zeros_like(total)
 
     @pl.loop(0, lax.div(count + SUM_TERMS - 1, SUM_TERMS))
     def _(step):
@@ -140,41 +145,33 @@
                     sums[0][target] += scaled[:, half:]
                     sums[1][target] += scaled[:, :half]
 
-    def part(ref, g):
-        return ref[g * sec_dev : (g + 1) * sec_dev]
-
-    if stage == 0:
-        rounded[...] = part(sums[1], far).astype(jnp.bfloat16)
-    elif stage == 1:
-        near = [g for g in range(1, groups) if g != far]
-        for g in near:
-            sums[0][g * sec_dev : (g + 1) * sec_dev] += part(before[0], g)
-        for g, out in zip([0] + near, rounded):
-            theirs = part(sums[1], g)
-            out[...] = (theirs if g == 0 else theirs + part(before[1], g)).astype(jnp.bfloat16)
-
-
-def summed(shift, coef, mixed, held, far, stage, before=()):
+    if stage is not None:
+        for at, g in enumerate(order[stage]):
+            part = slice(g * sec_dev, (g + 1) * sec_dev)
+            outs[2 * at][...] = sums[0][part]
+            outs[2 * at + 1][...] = sums[1][part].astype(jnp.bfloat16)
+
+
+def summed(shift, coef, mixed, held, order, stage, sums=()):
     k_dev, sec_dev, rows, width = mixed.shape
     targets = coef.shape[0]
     columns = width if stage is None else width // 2
     whole = pltpu.VMEM((targets, rows, columns), jnp.float32)
-    rounded = pltpu.VMEM((sec_dev, rows, columns), jnp.bfloat16)
-    scratch = [pltpu.SMEM((k_dev + SUM_TERMS,), jnp.int32)]
     out_shape = [whole]
-    if stage == 0:
-        out_shape = [whole, whole, rounded]
-    elif stage == 1:
-        out_shape = [whole] + [rounded] * (targets // sec_dev - 1)
-        scratch = [whole] + scratch
-    in_vmem = (mixed, held, *before)
+    if stage is not None:
+        out_shape = [whole] * 2
+        for _ in order[stage]:
+            for dtype in (jnp.float32, jnp.bfloat16):
+                out_shape.append(pltpu.VMEM((sec_dev, rows, columns), dtype))
+    in_vmem = (mixed, held, *sums)
     return pl.pallas_call(
-        functools.partial(sum_kernel, far, stage),
+        functools.partial(sum_kernel, order, stage),
         out_shape=out_shape,
         in_specs=[pl.BlockSpec(memory_space=pltpu.SMEM)] * 2
         + [pl.BlockSpec(memory_space=pltpu.VMEM)] * len(in_vmem),
         out_specs=[pl.BlockSpec(memory_space=pltpu.VMEM)] * len(out_shape),
-        scratch_shapes=scratch,
+        input_output_aliases={4 + i: i for i in range(len(sums))},
+        scratch_shapes=[pltpu.SMEM((k_dev + SUM_TERMS,), jnp.int32)],
         compiler_params=pltpu.CompilerParams(vmem_limit_bytes=24 * MIB),
         cost_estimate=pl.CostEstimate(
             flops=k_dev * sec_dev * rows * width * width,
@@ -207,32 +204,30 @@
     if split:
         coefs = [live] + [shift_by(live, "sector", -g) for g in range(1, devices)]
         coef = jnp.concatenate(coefs, axis=0)
-        far, near = 2, (1, 3)
-
-        def own(sums, g):
-            return sums[g * sec_dev : (g + 1) * sec_dev]
-
-        *first, theirs = summed(sector_shift, coef, mixed, held, far, 0)
-        crossed = shift_by(theirs, "op", 1)
-        mine, *theirs = summed(sector_shift, coef, mixed, held, far, 1, first)
-        other = after(crossed, mine).astype(jnp.float32)
-        both = (own(first[0], far) + other).astype(jnp.bfloat16)
-        arrived = [shift_by(both, "sector", far)]
-        crossed = {g: shift_by(after(theirs[at], both), "op", 1) for at, g in enumerate(near, 1)}
-        for g in near:
-            if g == near[1]:
-                crossed[0] = shift_by(after(theirs[0], both), "op", 1)
-            other = after(crossed[g], both).astype(jnp.float32)
-            both = (own(mine, g) + other).astype(jnp.bfloat16)
-            arrived.append(shift_by(both, "sector", g))
-        sigma = own(mine, 0) + after(crossed[0], both).astype(jnp.float32)
-        for other in arrived:
+        order = ((2,), (3,), (1, 0))
+        *sums, mine_2, theirs_2 = summed(sector_shift, coef, mixed, held, order, 0)
+        crossed_2 = shift_by(theirs_2, "op", 1)
+        *sums, mine_3, theirs_3 = summed(sector_shift, coef, mixed, held, order, 1, sums)
+        crossed_3 = shift_by(theirs_3, "op", 1)
+        both_2 = (mine_2 + after(crossed_2, mine_3).astype(jnp.float32)).astype(jnp.bfloat16)
+        arrived_2 = shift_by(both_2, "sector", 2)
+        _, _, mine_1, theirs_1, mine_0, theirs_0 = summed(
+            sector_shift, after(coef, both_2), mixed, held, order, 2, sums
+        )
+        crossed_1 = shift_by(theirs_1, "op", 1)
+        both_3 = (mine_3 + after(crossed_3, mine_1).astype(jnp.float32)).astype(jnp.bfloat16)
+        arrived_3 = shift_by(both_3, "sector", 3)
+        crossed_0 = shift_by(after(theirs_0, both_3), "op", 1)
+        both_1 = (mine_1 + after(crossed_1, both_3).astype(jnp.float32)).astype(jnp.bfloat16)
+        arrived_1 = shift_by(both_1, "sector", 1)
+        sigma = mine_0 + after(crossed_0, both_1).astype(jnp.float32)
+        for other in (arrived_2, arrived_3, arrived_1):
             sigma = lax.optimization_barrier(sigma) + other.astype(jnp.float32)
         return sigma
 
     first = lax.axis_index("sector") * sec_dev
     coef = jnp.roll(lax.all_gather(live, "sector", axis=0, tiled=True), -first, axis=0)
-    (total,) = summed(sector_shift, coef, mixed, held, None, None)
+    (total,) = summed(sector_shift, coef, mixed, held, (), None)
     total = jnp.roll(total, first, axis=0)
     total = lax.psum_scatter(total, "op", scatter_dimension=2, tiled=True)
     return lax.psum_scatter(total, "sector", scatter_dimension=0, tiled=True)

time: 36.1 us -> 36.7 us (1.017)
  Pallas kernels: 11.4 us -> 12.6 us
  waiting for transfers between devices: 8.04 us -> 7.15 us
    pallas_call x2 -> x3, Pallas kernels: 7.27 us -> 8.61 us  [summed(): pl.pallas_call(functools.partial(sum_kernel, order, stage), out_shape=out...]
    ppermute x10, waiting for transfers between devices: 8.04 us -> 7.15 us  [shift_by(): lax.ppermute(value, axis, [(i, (i + distance) % size) for i in range(size)])]
  transfers between devices with their start and end apart: 10 -> 10, of which waited for: 5 -> 5; matrix products, arithmetic and copies ran while one was open for 0% -> 1% of each run, Pallas kernels for 24% -> 25%
where the time goes in v13:
time: 36.7 us
  starting transfers between devices  15.2 us (41%)
  Pallas kernels  12.6 us (34%)
  waiting for transfers between devices  7.15 us (19%)
  other arithmetic  1.66 us (5%)
    ppermute x10, starting transfers between devices, shift_by(): lax.ppermute(value, axis, [(i, (i + distance) % size) for i in range(size)])  15.2 us
    pallas_call x3, Pallas kernels, summed(): pl.pallas_call(functools.partial(sum_kernel, order, stage), out_shape=out...  8.61 us
    ppermute x10, waiting for transfers between devices, shift_by(): lax.ppermute(value, axis, [(i, (i + distance) % size) for i in range(size)])  7.15 us
    pallas_call x1, Pallas kernels, mix(): pl.pallas_call(functools.partial(mix_kernel, split), out_shape=[pltpu.VME...  3.95 us
    add x3, other arithmetic, per_device(): sigma = lax.optimization_barrier(sigma) + other.astype(jnp.float32)  0.8 us
  transfers between devices with their start and end apart: 10, of which 5 were waited for; matrix products, arithmetic and copies ran while one was open for 1% of the time, Pallas kernels for 25%

profile of v13, /device:TPU:0, one launch (start us, length us, event | category | flops | bytes accessed | tf_op | source)
XLA Modules:
  0.0 36.7 jit_solution(16858776228417751890)
XLA Ops:
  0.0 0.7 %select_bitcast_fusion = f32[4,32]{1,0:T(4,128)S(1)} fusion(f32[32,4]{0,1:T(4,128)} %param.9, s32[32,4]{0,1:T(4,128)} %param.10), kind=kLoop, calls=%fused_computation.8 | loop fusion | flops 256 | bytes 1536 | tf_op jit(solution)/shard_map/jit(_where)/select_n | solution.py:200
  0.7 3.0 %collective-permute-start.2 = (f32[4,32]{1,0:T(4,128)S(1)}, f32[4,32]{1,0:T(4,128)S(1)}, u32[]{:S(2)}, u32[]{:S(2)}) collective-permute-start(f32[4,32]{1,0:T(4,128)S(1)} %select_bitcast_fusion), channel_id=1, source_target_pairs={{0,4},{4,8},{8,12},{12,0},{1,5},{5,9},{9,13},{13,1},{2,6},{6,10},{... | collective-permute-start | bytes 1544 | tf_op jit(solution)/shard_map/ppermute | solution.py:190
  3.7 2.6 %collective-permute-start.1 = (f32[4,32]{1,0:T(4,128)S(1)}, f32[4,32]{1,0:T(4,128)S(1)}, u32[]{:S(2)}, u32[]{:S(2)}) collective-permute-start(f32[4,32]{1,0:T(4,128)S(1)} %select_bitcast_fusion), channel_id=1, source_target_pairs={{0,8},{4,12},{8,0},{12,4},{1,9},{5,13},{9,1},{13,5},{2,10},{6,14},... | collective-permute-start | bytes 1544 | tf_op jit(solution)/shard_map/ppermute | solution.py:190
  6.3 1.3 %collective-permute-start = (f32[4,32]{1,0:T(4,128)S(1)}, f32[4,32]{1,0:T(4,128)S(1)}, u32[]{:S(2)}, u32[]{:S(2)}) collective-permute-start(f32[4,32]{1,0:T(4,128)S(1)} %select_bitcast_fusion), channel_id=1, source_target_pairs={{0,12},{4,0},{8,4},{12,8},{1,13},{5,1},{9,5},{13,9},{2,14},{6,2},{... | collective-permute-start | bytes 1544 | tf_op jit(solution)/shard_map/ppermute | solution.py:190
  7.7 4.0 %shard_map.64 = (bf16[32,4,128,256]{3,2,1,0:T(8,128)(2,1)S(1)}, bf16[32,256,256]{2,1,0:T(8,128)(2,1)S(1)}) custom-call(bf16[4,256,256]{2,1,0:T(8,128)(2,1)} %wave_ref.1, bf16[32,128,256]{2,1,0:T(8,128)(2,1)} %left_ref.1, bf16[32,256,256]{2,1,0:T(8,128)(2,1)} %right_ref.1), custom_call_target="tpu_custom_call" | custom-call | flops 2147483648 | bytes 6291456 | tf_op jit(solution)/shard_map/pallas_call | solution.py:69
  11.6 0.0 collective-permute-done.2
  11.6 0.0 collective-permute-done.1
  11.6 0.0 collective-permute-done
  11.7 3.3 %shard_map.65 = (f32[16,128,128]{2,1,0:T(8,128)S(1)}, f32[16,128,128]{2,1,0:T(8,128)S(1)}, f32[4,128,128]{2,1,0:T(8,128)S(1)}, bf16[4,128,128]{2,1,0:T(8,128)(2,1)S(1)}) custom-call(s32[32]{0:T(128)} %shift_ref.5, f32[16,32]{1,0:T(8,128)S(1)} %pad_maximum_fusion.coef_ref, bf16[32,4,128,256]{3,2,1,0:T(8,128)(2,1)S(1)} %get-tuple-element.25.mixed_ref, ...), custom_call_target="tpu_custom_call" | custom-call | flops 1073741824 | bytes 6291456 | tf_op jit(solution)/shard_map/pallas_call | solution.py:167
  15.0 1.6 %collective-permute-start.3 = (bf16[4,128,128]{2,1,0:T(8,128)(2,1)S(1)}, bf16[4,128,128]{2,1,0:T(8,128)(2,1)S(1)}, u32[]{:S(2)}, u32[]{:S(2)}) collective-permute-start(bf16[4,128,128]{2,1,0:T(8,128)(2,1)S(1)} %get-tuple-element.28), channel_id=1, source_target_pairs={{0,2},{2,0},{1,3},{3,1},{4,6},{6,4},{5,7},{7,5},{8,10},{10,8},{9,1... | collective-permute-start | bytes 393224 | tf_op jit(solution)/shard_map/ppermute | solution.py:190
  16.5 2.6 %shard_map.66 = (f32[16,128,128]{2,1,0:T(8,128)S(1)}, f32[16,128,128]{2,1,0:T(8,128)S(1)}, f32[4,128,128]{2,1,0:T(8,128)S(1)}, bf16[4,128,128]{2,1,0:T(8,128)(2,1)S(1)}) custom-call(s32[32]{0:T(128)} %shift_ref.5, f32[16,32]{1,0:T(8,128)S(1)} %pad_maximum_fusion.coef_ref, ...), custom_call_target="tpu_custom_call", output_to_operand_aliasing={{0}: (4, {}), {1}: (5, {})} | custom-call | flops 1073741824 | bytes 6291456 | tf_op jit(solution)/shard_map/pallas_call | solution.py:167
  19.2 0.6 %collective-permute-start.4 = (bf16[4,128,128]{2,1,0:T(8,128)(2,1)S(1)}, bf16[4,128,128]{2,1,0:T(8,128)(2,1)S(1)}, u32[]{:S(2)}, u32[]{:S(2)}) collective-permute-start(bf16[4,128,128]{2,1,0:T(8,128)(2,1)S(1)} %get-tuple-element.38), channel_id=1, source_target_pairs={{0,2},{2,0},{1,3},{3,1},{4,6},{6,4},{5,7},{7,5},{8,10},{10,8},{9,1... | collective-permute-start | bytes 393224 | tf_op jit(solution)/shard_map/ppermute | solution.py:190
  19.8 0.2 collective-permute-done.3
  20.1 0.2 collective-permute-start.7
  20.2 2.7 %shard_map.67 = (f32[16,128,128]{2,1,0:T(8,128)S(1)}, f32[16,128,128]{2,1,0:T(8,128)S(1)}, f32[4,128,128]{2,1,0:T(8,128)S(1)}, bf16[4,128,128]{2,1,0:T(8,128)(2,...) custom-call(s32[32]{0:T(128)} %shift_ref.5, ...), custom_call_target="tpu_custom_call", output_to_operand_aliasing={{0}: (4, {}), {1}: (5, {})} | custom-call | flops 1073741824 | bytes 6291456 | tf_op jit(solution)/shard_map/pallas_call | solution.py:167
  22.9 1.6 %collective-permute-start.6 = (bf16[4,128,128]{2,1,0:T(8,128)(2,1)S(1)}, bf16[4,128,128]{2,1,0:T(8,128)(2,1)S(1)}, u32[]{:S(2)}, u32[]{:S(2)}) collective-permute-start(bf16[4,128,128]{2,1,0:T(8,128)(2,1)S(1)} %get-tuple-element.42), channel_id=1, source_target_pairs={{0,2},{2,0},{1,3},{3,1},{4,6},{6,4},{5,7},{7,5},{8,10},{10,8},{9,1... | collective-permute-start | bytes 393224 | tf_op jit(solution)/shard_map/ppermute | solution.py:190
  24.5 0.2 collective-permute-done.4
  24.7 2.6 %collective-permute-start.8 = (bf16[4,128,128]{2,1,0:T(8,128)(2,1)S(1)}, bf16[4,128,128]{2,1,0:T(8,128)(2,1)S(1)}, u32[]{:S(2)}, u32[]{:S(2)}) collective-permute-start(bf16[4,128,128]{2,1,0:T(8,128)(2,1)S(1)} %add_convert_fusion.1), channel_id=1, source_target_pairs={{0,12},{4,0},{8,4},{12,8},{1,13},{5,1},{9,5},{13,9},{2,14},{6,2},{... | collective-permute-start | bytes 393224 | tf_op jit(solution)/shard_map/ppermute | solution.py:190
  27.4 0.7 %collective-permute-start.5 = (bf16[4,128,128]{2,1,0:T(8,128)(2,1)S(1)}, bf16[4,128,128]{2,1,0:T(8,128)(2,1)S(1)}, u32[]{:S(2)}, u32[]{:S(2)}) collective-permute-start(bf16[4,128,128]{2,1,0:T(8,128)(2,1)S(1)} %get-tuple-element.41), channel_id=1, source_target_pairs={{0,2},{2,0},{1,3},{3,1},{4,6},{6,4},{5,7},{7,5},{8,10},{10,8},{9,1... | collective-permute-start | bytes 393224 | tf_op jit(solution)/shard_map/ppermute | solution.py:190
  28.0 1.1 %collective-permute-done.6 = bf16[4,128,128]{2,1,0:T(8,128)(2,1)S(1)} collective-permute-done((bf16[4,128,128]{2,1,0:T(8,128)(2,1)S(1)}, bf16[4,128,128]{2,1,0:T(8,128)(2,1)S(1)}, u32[]{:S(2)}, u32[]{:S(2)}) %collective-permute-start.6) | collective-permute-done | bytes 131104 | tf_op jit(solution)/shard_map/ppermute | solution.py:190
  29.1 1.1 %collective-permute-start.9 = (bf16[4,128,128]{2,1,0:T(8,128)(2,1)S(1)}, bf16[4,128,128]{2,1,0:T(8,128)(2,1)S(1)}, u32[]{:S(2)}, u32[]{:S(2)}) collective-permute-start(bf16[4,128,128]{2,1,0:T(8,128)(2,1)S(1)} %add_convert_fusion), channel_id=1, source_target_pairs={{0,4},{4,8},{8,12},{12,0},{1,5},{5,9},{9,13},{13,1},{2,6},{6,10},{... | collective-permute-start | bytes 393224 | tf_op jit(solution)/shard_map/ppermute | solution.py:190
  30.2 2.1 %collective-permute-done.5 = bf16[4,128,128]{2,1,0:T(8,128)(2,1)S(1)} collective-permute-done((bf16[4,128,128]{2,1,0:T(8,128)(2,1)S(1)}, bf16[4,128,128]{2,1,0:T(8,128)(2,1)S(1)}, u32[]{:S(2)}, u32[]{:S(2)}) %collective-permute-start.5) | collective-permute-done | bytes 131104 | tf_op jit(solution)/shard_map/ppermute | solution.py:190
  32.4 0.0 collective-permute-done.7
  32.4 0.0 collective-permute-done.8
  32.5 3.5 %collective-permute-done.9 = bf16[4,128,128]{2,1,0:T(8,128)(2,1)S(1)} collective-permute-done((bf16[4,128,128]{2,1,0:T(8,128)(2,1)S(1)}, bf16[4,128,128]{2,1,0:T(8,128)(2,1)S(1)}, u32[]{:S(2)}, u32[]{:S(2)}) %collective-permute-start.9) | collective-permute-done | bytes 131104 | tf_op jit(solution)/shard_map/ppermute | solution.py:190
  35.9 0.7 %convert_add_fusion = f32[4,128,128]{2,1,0:T(8,128)} fusion(f32[4,128,128]{2,1,0:T(8,128)S(1)} %convert_add_fusion.1, bf16[4,128,128]{2,1,0:T(8,128)(2,1)S(1)} %collective-permute-done.9), kind=kLoop, calls=%fused_computation | loop fusion | flops 131072 | bytes 655360 | tf_op jit(solution)/shard_map/add | solution.py:225
  (7 shorter events, 0.2 us)
Async XLA Ops:
  0.7 10.9 %collective-permute-start.2 = (f32[4,32]{1,0:T(4,128)S(1)}, f32[4,32]{1,0:T(4,128)S(1)}, u32[]{:S(2)}, u32[]{:S(2)}) collective-permute-start(f32[4,32]{1,0:T(4,128)S(1)} %select_bitcast_fusion), channel_id=1, source_target_pairs={{0,4},{4,8},{8,12},{12,0},{1,5},{5,9},{9,13},{13,1},{2,6},{6,10},{... | collective-permute-start | bytes 1544 | tf_op jit(solution)/shard_map/ppermute | solution.py:190
  3.7 7.9 %collective-permute-start.1 = (f32[4,32]{1,0:T(4,128)S(1)}, f32[4,32]{1,0:T(4,128)S(1)}, u32[]{:S(2)}, u32[]{:S(2)}) collective-permute-start(f32[4,32]{1,0:T(4,128)S(1)} %select_bitcast_fusion), channel_id=1, source_target_pairs={{0,8},{4,12},{8,0},{12,4},{1,9},{5,13},{9,1},{13,5},{2,10},{6,14},... | collective-permute-start | bytes 1544 | tf_op jit(solution)/shard_map/ppermute | solution.py:190
  6.3 5.3 %collective-permute-start = (f32[4,32]{1,0:T(4,128)S(1)}, f32[4,32]{1,0:T(4,128)S(1)}, u32[]{:S(2)}, u32[]{:S(2)}) collective-permute-start(f32[4,32]{1,0:T(4,128)S(1)} %select_bitcast_fusion), channel_id=1, source_target_pairs={{0,12},{4,0},{8,4},{12,8},{1,13},{5,1},{9,5},{13,9},{2,14},{6,2},{... | collective-permute-start | bytes 1544 | tf_op jit(solution)/shard_map/ppermute | solution.py:190
  15.0 5.0 %collective-permute-start.3 = (bf16[4,128,128]{2,1,0:T(8,128)(2,1)S(1)}, bf16[4,128,128]{2,1,0:T(8,128)(2,1)S(1)}, u32[]{:S(2)}, u32[]{:S(2)}) collective-permute-start(bf16[4,128,128]{2,1,0:T(8,128)(2,1)S(1)} %get-tuple-element.28), channel_id=1, source_target_pairs={{0,2},{2,0},{1,3},{3,1},{4,6},{6,4},{5,7},{7,5},{8,10},{10,8},{9,1... | collective-permute-start | bytes 393224 | tf_op jit(solution)/shard_map/ppermute | solution.py:190
  19.2 5.5 %collective-permute-start.4 = (bf16[4,128,128]{2,1,0:T(8,128)(2,1)S(1)}, bf16[4,128,128]{2,1,0:T(8,128)(2,1)S(1)}, u32[]{:S(2)}, u32[]{:S(2)}) collective-permute-start(bf16[4,128,128]{2,1,0:T(8,128)(2,1)S(1)} %get-tuple-element.38), channel_id=1, source_target_pairs={{0,2},{2,0},{1,3},{3,1},{4,6},{6,4},{5,7},{7,5},{8,10},{10,8},{9,1... | collective-permute-start | bytes 393224 | tf_op jit(solution)/shard_map/ppermute | solution.py:190
  20.1 12.3 %collective-permute-start.7 = (bf16[4,128,128]{2,1,0:T(8,128)(2,1)S(1)}, bf16[4,128,128]{2,1,0:T(8,128)(2,1)S(1)}, u32[]{:S(2)}, u32[]{:S(2)}) collective-permute-start(bf16[4,128,128]{2,1,0:T(8,128)(2,1)S(1)} %add_convert_fusion.2), channel_id=1, source_target_pairs={{0,8},{4,12},{8,0},{12,4},{1,9},{5,13},{9,1},{13,5},{2,10},{6,14},... | collective-permute-start | bytes 393224 | tf_op jit(solution)/shard_map/ppermute | solution.py:190
  22.9 6.2 %collective-permute-start.6 = (bf16[4,128,128]{2,1,0:T(8,128)(2,1)S(1)}, bf16[4,128,128]{2,1,0:T(8,128)(2,1)S(1)}, u32[]{:S(2)}, u32[]{:S(2)}) collective-permute-start(bf16[4,128,128]{2,1,0:T(8,128)(2,1)S(1)} %get-tuple-element.42), channel_id=1, source_target_pairs={{0,2},{2,0},{1,3},{3,1},{4,6},{6,4},{5,7},{7,5},{8,10},{10,8},{9,1... | collective-permute-start | bytes 393224 | tf_op jit(solution)/shard_map/ppermute | solution.py:190
  24.7 7.7 %collective-permute-start.8 = (bf16[4,128,128]{2,1,0:T(8,128)(2,1)S(1)}, bf16[4,128,128]{2,1,0:T(8,128)(2,1)S(1)}, u32[]{:S(2)}, u32[]{:S(2)}) collective-permute-start(bf16[4,128,128]{2,1,0:T(8,128)(2,1)S(1)} %add_convert_fusion.1), channel_id=1, source_target_pairs={{0,12},{4,0},{8,4},{12,8},{1,13},{5,1},{9,5},{13,9},{2,14},{6,2},{... | collective-permute-start | bytes 393224 | tf_op jit(solution)/shard_map/ppermute | solution.py:190
  27.4 5.0 %collective-permute-start.5 = (bf16[4,128,128]{2,1,0:T(8,128)(2,1)S(1)}, bf16[4,128,128]{2,1,0:T(8,128)(2,1)S(1)}, u32[]{:S(2)}, u32[]{:S(2)}) collective-permute-start(bf16[4,128,128]{2,1,0:T(8,128)(2,1)S(1)} %get-tuple-element.41), channel_id=1, source_target_pairs={{0,2},{2,0},{1,3},{3,1},{4,6},{6,4},{5,7},{7,5},{8,10},{10,8},{9,1... | collective-permute-start | bytes 393224 | tf_op jit(solution)/shard_map/ppermute | solution.py:190
  29.1 6.8 %collective-permute-start.9 = (bf16[4,128,128]{2,1,0:T(8,128)(2,1)S(1)}, bf16[4,128,128]{2,1,0:T(8,128)(2,1)S(1)}, u32[]{:S(2)}, u32[]{:S(2)}) collective-permute-start(bf16[4,128,128]{2,1,0:T(8,128)(2,1)S(1)} %add_convert_fusion), channel_id=1, source_target_pairs={{0,4},{4,8},{8,12},{12,0},{1,5},{5,9},{9,13},{13,1},{2,6},{6,10},{... | collective-permute-start | bytes 393224 | tf_op jit(solution)/shard_map/ppermute | solution.py:190

commit v14 on v13

--- a/solution.py
+++ b/solution.py
@@ -204,24 +204,23 @@
     if split:
         coefs = [live] + [shift_by(live, "sector", -g) for g in range(1, devices)]
         coef = jnp.concatenate(coefs, axis=0)
-        order = ((2,), (3,), (1, 0))
+        order = ((2,), (1, 3, 0))
         *sums, mine_2, theirs_2 = summed(sector_shift, coef, mixed, held, order, 0)
         crossed_2 = shift_by(theirs_2, "op", 1)
-        *sums, mine_3, theirs_3 = summed(sector_shift, coef, mixed, held, order, 1, sums)
-        crossed_3 = shift_by(theirs_3, "op", 1)
-        both_2 = (mine_2 + after(crossed_2, mine_3).astype(jnp.float32)).astype(jnp.bfloat16)
+        _, _, mine_1, theirs_1, mine_3, theirs_3, mine_0, theirs_0 = summed(
+            sector_shift, after(coef, theirs_2), mixed, held, order, 1, sums
+        )
+        both_2 = (mine_2 + after(crossed_2, mine_1).astype(jnp.float32)).astype(jnp.bfloat16)
         arrived_2 = shift_by(both_2, "sector", 2)
-        _, _, mine_1, theirs_1, mine_0, theirs_0 = summed(
-            sector_shift, after(coef, both_2), mixed, held, order, 2, sums
-        )
-        crossed_1 = shift_by(theirs_1, "op", 1)
-        both_3 = (mine_3 + after(crossed_3, mine_1).astype(jnp.float32)).astype(jnp.bfloat16)
+        crossed_1 = shift_by(after(theirs_1, both_2), "op", 1)
+        crossed_3 = shift_by(after(theirs_3, both_2), "op", 1)
+        both_1 = (mine_1 + after(crossed_1, both_2).astype(jnp.float32)).astype(jnp.bfloat16)
+        arrived_1 = shift_by(both_1, "sector", 1)
+        crossed_0 = shift_by(after(theirs_0, both_1), "op", 1)
+        both_3 = (mine_3 + after(crossed_3, both_1).astype(jnp.float32)).astype(jnp.bfloat16)
         arrived_3 = shift_by(both_3, "sector", 3)
-        crossed_0 = shift_by(after(theirs_0, both_3), "op", 1)
-        both_1 = (mine_1 + after(crossed_1, both_3).astype(jnp.float32)).astype(jnp.bfloat16)
-        arrived_1 = shift_by(both_1, "sector", 1)
-        sigma = mine_0 + after(crossed_0, both_1).astype(jnp.float32)
-        for other in (arrived_2, arrived_3, arrived_1):
+        sigma = mine_0 + after(crossed_0, both_3).astype(jnp.float32)
+        for other in (arrived_2, arrived_1, arrived_3):
             sigma = lax.optimization_barrier(sigma) + other.astype(jnp.float32)
         return sigma
 

time: 36.7 us -> 35.3 us (0.962)
  Pallas kernels: 12.6 us -> 11 us
  waiting for transfers between devices: 7.15 us -> 7.95 us
  starting transfers between devices: 15.2 us -> 14.5 us
    pallas_call x3 -> x2, Pallas kernels: 8.61 us -> 7.09 us  [summed(): pl.pallas_call(functools.partial(sum_kernel, order, stage), out_shape=out...]
    ppermute x10, waiting for transfers between devices: 7.15 us -> 7.95 us  [shift_by(): lax.ppermute(value, axis, [(i, (i + distance) % size) for i in range(size)])]
    ppermute x10, starting transfers between devices: 15.2 us -> 14.5 us  [shift_by(): lax.ppermute(value, axis, [(i, (i + distance) % size) for i in range(size)])]
  transfers between devices with their start and end apart: 10 -> 10, of which waited for: 5 -> 5; matrix products, arithmetic and copies ran while one was open for 1% -> 0% of each run, Pallas kernels for 25% -> 22%
where the time goes in v14:
time: 35.3 us; the launch traced here: 35.2 us
  starting transfers between devices  14.5 us (41%)
  Pallas kernels  11 us (31%)
  waiting for transfers between devices  7.95 us (23%)
  other arithmetic  1.64 us (5%)
    ppermute x10, starting transfers between devices, shift_by(): lax.ppermute(value, axis, [(i, (i + distance) % size) for i in range(size)])  14.5 us
    ppermute x10, waiting for transfers between devices, shift_by(): lax.ppermute(value, axis, [(i, (i + distance) % size) for i in range(size)])  7.95 us
    pallas_call x2, Pallas kernels, summed(): pl.pallas_call(functools.partial(sum_kernel, order, stage), out_shape=out...  7.09 us
    pallas_call x1, Pallas kernels, mix(): pl.pallas_call(functools.partial(mix_kernel, split), out_shape=[pltpu.VME...  3.95 us
    add x3, other arithmetic, per_device(): sigma = lax.optimization_barrier(sigma) + other.astype(jnp.float32)  0.78 us
  transfers between devices with their start and end apart: 10, of which 5 were waited for; matrix products, arithmetic and copies ran while one was open for 0% of the time, Pallas kernels for 22%

profile of v14, /device:TPU:0, one launch (start us, length us, event | category | flops | bytes accessed | tf_op | source)
XLA Modules:
  0.0 35.2 jit_solution(7448152268516576129)
XLA Ops:
  0.0 0.7 %select_bitcast_fusion = f32[4,32]{1,0:T(4,128)S(1)} fusion(f32[32,4]{0,1:T(4,128)} %param.9, s32[32,4]{0,1:T(4,128)} %param.10), kind=kLoop, calls=%fused_computation.8 | loop fusion | flops 256 | bytes 1536 | tf_op jit(solution)/shard_map/jit(_where)/select_n | solution.py:200
  0.7 3.0 %collective-permute-start.2 = (f32[4,32]{1,0:T(4,128)S(1)}, f32[4,32]{1,0:T(4,128)S(1)}, u32[]{:S(2)}, u32[]{:S(2)}) collective-permute-start(f32[4,32]{1,0:T(4,128)S(1)} %select_bitcast_fusion), channel_id=1, source_target_pairs={{0,4},{4,8},{8,12},{12,0},{1,5},{5,9},{9,13},{13,1},{2,6},{6,10},{... | collective-permute-start | bytes 1544 | tf_op jit(solution)/shard_map/ppermute | solution.py:190
  3.7 2.6 %collective-permute-start.1 = (f32[4,32]{1,0:T(4,128)S(1)}, f32[4,32]{1,0:T(4,128)S(1)}, u32[]{:S(2)}, u32[]{:S(2)}) collective-permute-start(f32[4,32]{1,0:T(4,128)S(1)} %select_bitcast_fusion), channel_id=1, source_target_pairs={{0,8},{4,12},{8,0},{12,4},{1,9},{5,13},{9,1},{13,5},{2,10},{6,14},... | collective-permute-start | bytes 1544 | tf_op jit(solution)/shard_map/ppermute | solution.py:190
  6.3 1.3 %collective-permute-start = (f32[4,32]{1,0:T(4,128)S(1)}, f32[4,32]{1,0:T(4,128)S(1)}, u32[]{:S(2)}, u32[]{:S(2)}) collective-permute-start(f32[4,32]{1,0:T(4,128)S(1)} %select_bitcast_fusion), channel_id=1, source_target_pairs={{0,12},{4,0},{8,4},{12,8},{1,13},{5,1},{9,5},{13,9},{2,14},{6,2},{... | collective-permute-start | bytes 1544 | tf_op jit(solution)/shard_map/ppermute | solution.py:190
  7.7 4.0 %shard_map.64 = (bf16[32,4,128,256]{3,2,1,0:T(8,128)(2,1)S(1)}, bf16[32,256,256]{2,1,0:T(8,128)(2,1)S(1)}) custom-call(bf16[4,256,256]{2,1,0:T(8,128)(2,1)} %wave_ref.1, bf16[32,128,256]{2,1,0:T(8,128)(2,1)} %left_ref.1, bf16[32,256,256]{2,1,0:T(8,128)(2,1)} %right_ref.1), custom_call_target="tpu_custom_call" | custom-call | flops 2147483648 | bytes 6291456 | tf_op jit(solution)/shard_map/pallas_call | solution.py:69
  11.6 0.0 collective-permute-done.2
  11.6 0.0 collective-permute-done.1
  11.6 0.0 collective-permute-done
  11.7 3.3 %shard_map.65 = (f32[16,128,128]{2,1,0:T(8,128)S(1)}, f32[16,128,128]{2,1,0:T(8,128)S(1)}, f32[4,128,128]{2,1,0:T(8,128)S(1)}, bf16[4,128,128]{2,1,0:T(8,128)(2,1)S(1)}) custom-call(s32[32]{0:T(128)} %shift_ref.3, f32[16,32]{1,0:T(8,128)S(1)} %pad_maximum_fusion.coef_ref, bf16[32,4,128,256]{3,2,1,0:T(8,128)(2,1)S(1)} %get-tuple-element.25.mixed_ref, ...), custom_call_target="tpu_custom_call" | custom-call | flops 1073741824 | bytes 6291456 | tf_op jit(solution)/shard_map/pallas_call | solution.py:167
  15.0 1.6 %collective-permute-start.3 = (bf16[4,128,128]{2,1,0:T(8,128)(2,1)S(1)}, bf16[4,128,128]{2,1,0:T(8,128)(2,1)S(1)}, u32[]{:S(2)}, u32[]{:S(2)}) collective-permute-start(bf16[4,128,128]{2,1,0:T(8,128)(2,1)S(1)} %get-tuple-element.27), channel_id=1, source_target_pairs={{0,2},{2,0},{1,3},{3,1},{4,6},{6,4},{5,7},{7,5},{8,10},{10,8},{9,1... | collective-permute-start | bytes 393224 | tf_op jit(solution)/shard_map/ppermute | solution.py:190
  16.6 3.8 %shard_map.66 = (f32[16,128,128]{2,1,0:T(8,128)S(1)}, f32[16,128,128]{2,1,0:T(8,128)S(1)}, f32[4,128,128]{2,1,0:T(8,128)S(1)}, bf16[4,128,128]{2,1,0:T(8,128)(2,...) custom-call(s32[32]{0:T(128)} %shift_ref.3, ...), custom_call_target="tpu_custom_call", output_to_operand_aliasing={{0}: (4, {}), {1}: (5, {})} | custom-call | flops 1073741824 | bytes 6291456 | tf_op jit(solution)/shard_map/pallas_call | solution.py:167
  20.3 0.0 collective-permute-done.3
  20.4 1.2 %collective-permute-start.4 = (bf16[4,128,128]{2,1,0:T(8,128)(2,1)S(1)}, bf16[4,128,128]{2,1,0:T(8,128)(2,1)S(1)}, u32[]{:S(2)}, u32[]{:S(2)}) collective-permute-start(bf16[4,128,128]{2,1,0:T(8,128)(2,1)S(1)} %get-tuple-element.37), channel_id=1, source_target_pairs={{0,2},{2,0},{1,3},{3,1},{4,6},{6,4},{5,7},{7,5},{8,10},{10,8},{9,1... | collective-permute-start | bytes 393224 | tf_op jit(solution)/shard_map/ppermute | solution.py:190
  21.6 0.3 collective-permute-start.7
  22.0 0.9 %collective-permute-start.6 = (bf16[4,128,128]{2,1,0:T(8,128)(2,1)S(1)}, bf16[4,128,128]{2,1,0:T(8,128)(2,1)S(1)}, u32[]{:S(2)}, u32[]{:S(2)}) collective-permute-start(bf16[4,128,128]{2,1,0:T(8,128)(2,1)S(1)} %get-tuple-element.42), channel_id=1, source_target_pairs={{0,2},{2,0},{1,3},{3,1},{4,6},{6,4},{5,7},{7,5},{8,10},{10,8},{9,1... | collective-permute-start | bytes 393224 | tf_op jit(solution)/shard_map/ppermute | solution.py:190
  22.8 3.2 %collective-permute-done.4 = bf16[4,128,128]{2,1,0:T(8,128)(2,1)S(1)} collective-permute-done((bf16[4,128,128]{2,1,0:T(8,128)(2,1)S(1)}, bf16[4,128,128]{2,1,0:T(8,128)(2,1)S(1)}, u32[]{:S(2)}, u32[]{:S(2)}) %collective-permute-start.4) | collective-permute-done | bytes 131104 | tf_op jit(solution)/shard_map/ppermute | solution.py:190
  26.0 0.9 %collective-permute-start.8 = (bf16[4,128,128]{2,1,0:T(8,128)(2,1)S(1)}, bf16[4,128,128]{2,1,0:T(8,128)(2,1)S(1)}, u32[]{:S(2)}, u32[]{:S(2)}) collective-permute-start(bf16[4,128,128]{2,1,0:T(8,128)(2,1)S(1)} %add_convert_fusion.1), channel_id=1, source_target_pairs={{0,4},{4,8},{8,12},{12,0},{1,5},{5,9},{9,13},{13,1},{2,6},{6,10},{... | collective-permute-start | bytes 393224 | tf_op jit(solution)/shard_map/ppermute | solution.py:190
  26.9 0.8 %collective-permute-start.5 = (bf16[4,128,128]{2,1,0:T(8,128)(2,1)S(1)}, bf16[4,128,128]{2,1,0:T(8,128)(2,1)S(1)}, u32[]{:S(2)}, u32[]{:S(2)}) collective-permute-start(bf16[4,128,128]{2,1,0:T(8,128)(2,1)S(1)} %get-tuple-element.39), channel_id=1, source_target_pairs={{0,2},{2,0},{1,3},{3,1},{4,6},{6,4},{5,7},{7,5},{8,10},{10,8},{9,1... | collective-permute-start | bytes 393224 | tf_op jit(solution)/shard_map/ppermute | solution.py:190
  27.7 1.0 %collective-permute-done.6 = bf16[4,128,128]{2,1,0:T(8,128)(2,1)S(1)} collective-permute-done((bf16[4,128,128]{2,1,0:T(8,128)(2,1)S(1)}, bf16[4,128,128]{2,1,0:T(8,128)(2,1)S(1)}, u32[]{:S(2)}, u32[]{:S(2)}) %collective-permute-start.6) | collective-permute-done | bytes 131104 | tf_op jit(solution)/shard_map/ppermute | solution.py:190
  28.7 1.9 %collective-permute-start.9 = (bf16[4,128,128]{2,1,0:T(8,128)(2,1)S(1)}, bf16[4,128,128]{2,1,0:T(8,128)(2,1)S(1)}, u32[]{:S(2)}, u32[]{:S(2)}) collective-permute-start(bf16[4,128,128]{2,1,0:T(8,128)(2,1)S(1)} %add_convert_fusion), channel_id=1, source_target_pairs={{0,12},{4,0},{8,4},{12,8},{1,13},{5,1},{9,5},{13,9},{2,14},{6,2},{... | collective-permute-start | bytes 393224 | tf_op jit(solution)/shard_map/ppermute | solution.py:190
  30.6 1.3 %collective-permute-done.5 = bf16[4,128,128]{2,1,0:T(8,128)(2,1)S(1)} collective-permute-done((bf16[4,128,128]{2,1,0:T(8,128)(2,1)S(1)}, bf16[4,128,128]{2,1,0:T(8,128)(2,1)S(1)}, u32[]{:S(2)}, u32[]{:S(2)}) %collective-permute-start.5) | collective-permute-done | bytes 131104 | tf_op jit(solution)/shard_map/ppermute | solution.py:190
  31.9 0.0 collective-permute-done.7
  31.9 1.1 %collective-permute-done.8 = bf16[4,128,128]{2,1,0:T(8,128)(2,1)S(1)} collective-permute-done((bf16[4,128,128]{2,1,0:T(8,128)(2,1)S(1)}, bf16[4,128,128]{2,1,0:T(8,128)(2,1)S(1)}, u32[]{:S(2)}, u32[]{:S(2)}) %collective-permute-start.8) | collective-permute-done | bytes 131104 | tf_op jit(solution)/shard_map/ppermute | solution.py:190
  33.0 1.5 %collective-permute-done.9 = bf16[4,128,128]{2,1,0:T(8,128)(2,1)S(1)} collective-permute-done((bf16[4,128,128]{2,1,0:T(8,128)(2,1)S(1)}, bf16[4,128,128]{2,1,0:T(8,128)(2,1)S(1)}, u32[]{:S(2)}, u32[]{:S(2)}) %collective-permute-start.9) | collective-permute-done | bytes 131104 | tf_op jit(solution)/shard_map/ppermute | solution.py:190
  34.5 0.7 %convert_add_fusion = f32[4,128,128]{2,1,0:T(8,128)} fusion(f32[4,128,128]{2,1,0:T(8,128)S(1)} %convert_add_fusion.1, bf16[4,128,128]{2,1,0:T(8,128)(2,1)S(1)} %collective-permute-done.9), kind=kLoop, calls=%fused_computation | loop fusion | flops 131072 | bytes 655360 | tf_op jit(solution)/shard_map/add | solution.py:224
  (7 shorter events, 0.2 us)
Async XLA Ops:
  0.7 10.9 %collective-permute-start.2 = (f32[4,32]{1,0:T(4,128)S(1)}, f32[4,32]{1,0:T(4,128)S(1)}, u32[]{:S(2)}, u32[]{:S(2)}) collective-permute-start(f32[4,32]{1,0:T(4,128)S(1)} %select_bitcast_fusion), channel_id=1, source_target_pairs={{0,4},{4,8},{8,12},{12,0},{1,5},{5,9},{9,13},{13,1},{2,6},{6,10},{... | collective-permute-start | bytes 1544 | tf_op jit(solution)/shard_map/ppermute | solution.py:190
  3.7 7.9 %collective-permute-start.1 = (f32[4,32]{1,0:T(4,128)S(1)}, f32[4,32]{1,0:T(4,128)S(1)}, u32[]{:S(2)}, u32[]{:S(2)}) collective-permute-start(f32[4,32]{1,0:T(4,128)S(1)} %select_bitcast_fusion), channel_id=1, source_target_pairs={{0,8},{4,12},{8,0},{12,4},{1,9},{5,13},{9,1},{13,5},{2,10},{6,14},... | collective-permute-start | bytes 1544 | tf_op jit(solution)/shard_map/ppermute | solution.py:190
  6.3 5.3 %collective-permute-start = (f32[4,32]{1,0:T(4,128)S(1)}, f32[4,32]{1,0:T(4,128)S(1)}, u32[]{:S(2)}, u32[]{:S(2)}) collective-permute-start(f32[4,32]{1,0:T(4,128)S(1)} %select_bitcast_fusion), channel_id=1, source_target_pairs={{0,12},{4,0},{8,4},{12,8},{1,13},{5,1},{9,5},{13,9},{2,14},{6,2},{... | collective-permute-start | bytes 1544 | tf_op jit(solution)/shard_map/ppermute | solution.py:190
  15.0 5.3 %collective-permute-start.3 = (bf16[4,128,128]{2,1,0:T(8,128)(2,1)S(1)}, bf16[4,128,128]{2,1,0:T(8,128)(2,1)S(1)}, u32[]{:S(2)}, u32[]{:S(2)}) collective-permute-start(bf16[4,128,128]{2,1,0:T(8,128)(2,1)S(1)} %get-tuple-element.27), channel_id=1, source_target_pairs={{0,2},{2,0},{1,3},{3,1},{4,6},{6,4},{5,7},{7,5},{8,10},{10,8},{9,1... | collective-permute-start | bytes 393224 | tf_op jit(solution)/shard_map/ppermute | solution.py:190
  20.4 5.6 %collective-permute-start.4 = (bf16[4,128,128]{2,1,0:T(8,128)(2,1)S(1)}, bf16[4,128,128]{2,1,0:T(8,128)(2,1)S(1)}, u32[]{:S(2)}, u32[]{:S(2)}) collective-permute-start(bf16[4,128,128]{2,1,0:T(8,128)(2,1)S(1)} %get-tuple-element.37), channel_id=1, source_target_pairs={{0,2},{2,0},{1,3},{3,1},{4,6},{6,4},{5,7},{7,5},{8,10},{10,8},{9,1... | collective-permute-start | bytes 393224 | tf_op jit(solution)/shard_map/ppermute | solution.py:190
  21.6 10.3 %collective-permute-start.7 = (bf16[4,128,128]{2,1,0:T(8,128)(2,1)S(1)}, bf16[4,128,128]{2,1,0:T(8,128)(2,1)S(1)}, u32[]{:S(2)}, u32[]{:S(2)}) collective-permute-start(bf16[4,128,128]{2,1,0:T(8,128)(2,1)S(1)} %add_convert_fusion.2), channel_id=1, source_target_pairs={{0,8},{4,12},{8,0},{12,4},{1,9},{5,13},{9,1},{13,5},{2,10},{6,14},... | collective-permute-start | bytes 393224 | tf_op jit(solution)/shard_map/ppermute | solution.py:190
  22.0 6.7 %collective-permute-start.6 = (bf16[4,128,128]{2,1,0:T(8,128)(2,1)S(1)}, bf16[4,128,128]{2,1,0:T(8,128)(2,1)S(1)}, u32[]{:S(2)}, u32[]{:S(2)}) collective-permute-start(bf16[4,128,128]{2,1,0:T(8,128)(2,1)S(1)} %get-tuple-element.42), channel_id=1, source_target_pairs={{0,2},{2,0},{1,3},{3,1},{4,6},{6,4},{5,7},{7,5},{8,10},{10,8},{9,1... | collective-permute-start | bytes 393224 | tf_op jit(solution)/shard_map/ppermute | solution.py:190
  26.0 7.0 %collective-permute-start.8 = (bf16[4,128,128]{2,1,0:T(8,128)(2,1)S(1)}, bf16[4,128,128]{2,1,0:T(8,128)(2,1)S(1)}, u32[]{:S(2)}, u32[]{:S(2)}) collective-permute-start(bf16[4,128,128]{2,1,0:T(8,128)(2,1)S(1)} %add_convert_fusion.1), channel_id=1, source_target_pairs={{0,4},{4,8},{8,12},{12,0},{1,5},{5,9},{9,13},{13,1},{2,6},{6,10},{... | collective-permute-start | bytes 393224 | tf_op jit(solution)/shard_map/ppermute | solution.py:190
  26.9 5.0 %collective-permute-start.5 = (bf16[4,128,128]{2,1,0:T(8,128)(2,1)S(1)}, bf16[4,128,128]{2,1,0:T(8,128)(2,1)S(1)}, u32[]{:S(2)}, u32[]{:S(2)}) collective-permute-start(bf16[4,128,128]{2,1,0:T(8,128)(2,1)S(1)} %get-tuple-element.39), channel_id=1, source_target_pairs={{0,2},{2,0},{1,3},{3,1},{4,6},{6,4},{5,7},{7,5},{8,10},{10,8},{9,1... | collective-permute-start | bytes 393224 | tf_op jit(solution)/shard_map/ppermute | solution.py:190
  28.7 5.8 %collective-permute-start.9 = (bf16[4,128,128]{2,1,0:T(8,128)(2,1)S(1)}, bf16[4,128,128]{2,1,0:T(8,128)(2,1)S(1)}, u32[]{:S(2)}, u32[]{:S(2)}) collective-permute-start(bf16[4,128,128]{2,1,0:T(8,128)(2,1)S(1)} %add_convert_fusion), channel_id=1, source_target_pairs={{0,12},{4,0},{8,4},{12,8},{1,13},{5,1},{9,5},{13,9},{2,14},{6,2},{... | collective-permute-start | bytes 393224 | tf_op jit(solution)/shard_map/ppermute | solution.py:190

commit v15 on v13

--- a/solution.py
+++ b/solution.py
@@ -88,27 +88,23 @@
     )(*(pltpu.with_memory_space_constraint(x, pltpu.HBM) for x in (wavefunction, left_ops, right_ops)))
 
 
-def reaches(shift, group, sec_dev, targets):
-    return wrapped(-shift - group * sec_dev + sec_dev - 1, targets) < 2 * sec_dev - 1
-
-
 def sum_kernel(order, stage, shift_ref, coef_ref, mixed_ref, held_ref, *refs):
     terms, sec_dev, rows, width = mixed_ref.shape
     targets = coef_ref.shape[0]
     half = width // 2
     picked = refs[-1]
+    first = lax.axis_index("sector") * sec_dev
+
+    def reaches(k, group):
+        start = (first ^ (group * sec_dev)) - first
+        return wrapped(sec_dev - 1 - start - shift_ref[k], targets) < 2 * sec_dev - 1
 
     def pick(k, count):
         picked[count] = k
         if stage is None:
             return count + 1
-        wanted = True
-        for at, groups in enumerate(order[: stage + 1]):
-            if at < stage:
-                wanted &= ~reaches(shift_ref[k], groups[0], sec_dev, targets)
-            elif at < len(order) - 1:
-                wanted &= reaches(shift_ref[k], groups[0], sec_dev, targets)
-        return count + jnp.where(wanted, 1, 0)
+        wanted = functools.reduce(jnp.logical_or, [reaches(k, group) for group in order[0]])
+        return count + jnp.where(wanted == (stage == 0), 1, 0)
 
     count = lax.fori_loop(0, terms, pick, 0)
     for i in range(SUM_TERMS):
@@ -136,14 +132,16 @@
                 preferred_element_type=jnp.float32,
             )
             for s in range(sec_dev):
-                target = wrapped(s - shift_ref[k], targets)
-                weight = jnp.where(at < count, coef_ref[target, k], 0.0)
+                slot = wrapped(first + s - shift_ref[k], targets)
+                if stage is not None:
+                    slot ^= first
+                weight = jnp.where(at < count, coef_ref[slot, k], 0.0)
                 scaled = weight * product[s * rows : (s + 1) * rows]
                 if stage is None:
-                    sums[0][target] += scaled
+                    sums[0][slot] += scaled
                 else:
-                    sums[0][target] += scaled[:, half:]
-                    sums[1][target] += scaled[:, :half]
+                    sums[0][slot] += scaled[:, half:]
+                    sums[1][slot] += scaled[:, :half]
 
     if stage is not None:
         for at, g in enumerate(order[stage]):
@@ -185,9 +183,8 @@
     )
 
 
-def shift_by(value, axis, distance):
-    size = lax.axis_size(axis)
-    return lax.ppermute(value, axis, [(i, (i + distance) % size) for i in range(size)])
+def swap(value, axis, mask):
+    return lax.ppermute(value, axis, [(i, i ^ mask) for i in range(lax.axis_size(axis))])
 
 
 def after(value, other):
@@ -198,37 +195,39 @@
     sec_dev = wavefunction.shape[0]
     devices = lax.axis_size("sector")
     live = jnp.where(coupled.T > 0, site_coef.T, 0.0)
-    split = lax.axis_size("op") == 2 and devices == 4
+    split = lax.axis_size("op") == 2 and devices == 4 and sec_dev & (sec_dev - 1) == 0
     mixed, held = mix(wavefunction, left_ops, right_ops, split)
 
     if split:
-        coefs = [live] + [shift_by(live, "sector", -g) for g in range(1, devices)]
-        coef = jnp.concatenate(coefs, axis=0)
-        order = ((2,), (3,), (1, 0))
-        *sums, mine_2, theirs_2 = summed(sector_shift, coef, mixed, held, order, 0)
-        crossed_2 = shift_by(theirs_2, "op", 1)
-        *sums, mine_3, theirs_3 = summed(sector_shift, coef, mixed, held, order, 1, sums)
-        crossed_3 = shift_by(theirs_3, "op", 1)
-        both_2 = (mine_2 + after(crossed_2, mine_3).astype(jnp.float32)).astype(jnp.bfloat16)
-        arrived_2 = shift_by(both_2, "sector", 2)
+        pair = jnp.concatenate([live, swap(live, "sector", 1)], axis=0)
+        coef = jnp.concatenate([pair, swap(pair, "sector", 2)], axis=0)
+        order = ((3, 2), (1, 0))
+        *sums, mine_3, theirs_3, mine_2, theirs_2 = summed(
+            sector_shift, coef, mixed, held, order, 0
+        )
+        crossed_3 = swap(theirs_3, "op", 1)
+        crossed_2 = swap(theirs_2, "op", 1)
         _, _, mine_1, theirs_1, mine_0, theirs_0 = summed(
-            sector_shift, after(coef, both_2), mixed, held, order, 2, sums
+            sector_shift, after(coef, theirs_3), mixed, held, order, 1, sums
         )
-        crossed_1 = shift_by(theirs_1, "op", 1)
-        both_3 = (mine_3 + after(crossed_3, mine_1).astype(jnp.float32)).astype(jnp.bfloat16)
-        arrived_3 = shift_by(both_3, "sector", 3)
-        crossed_0 = shift_by(after(theirs_0, both_3), "op", 1)
-        both_1 = (mine_1 + after(crossed_1, both_3).astype(jnp.float32)).astype(jnp.bfloat16)
-        arrived_1 = shift_by(both_1, "sector", 1)
+        both_3 = mine_3 + after(crossed_3, mine_1).astype(jnp.float32)
+        both_3 = both_3.astype(jnp.bfloat16)
+        relayed = swap(both_3, "sector", 1)
+        crossed_1 = swap(after(theirs_1, both_3), "op", 1)
+        both_2 = lax.optimization_barrier(mine_2 + after(crossed_2, both_3).astype(jnp.float32))
+        crossed_0 = swap(after(theirs_0, both_2), "op", 1)
+        both_2 = (both_2 + relayed.astype(jnp.float32)).astype(jnp.bfloat16)
+        far = swap(both_2, "sector", 2)
+        both_1 = mine_1 + after(crossed_1, both_2).astype(jnp.float32)
+        both_1 = both_1.astype(jnp.bfloat16)
+        near = swap(both_1, "sector", 1)
         sigma = mine_0 + after(crossed_0, both_1).astype(jnp.float32)
-        for other in (arrived_2, arrived_3, arrived_1):
+        for other in (near, far):
             sigma = lax.optimization_barrier(sigma) + other.astype(jnp.float32)
         return sigma
 
-    first = lax.axis_index("sector") * sec_dev
-    coef = jnp.roll(lax.all_gather(live, "sector", axis=0, tiled=True), -first, axis=0)
+    coef = lax.all_gather(live, "sector", axis=0, tiled=True)
     (total,) = summed(sector_shift, coef, mixed, held, (), None)
-    total = jnp.roll(total, first, axis=0)
     total = lax.psum_scatter(total, "op", scatter_dimension=2, tiled=True)
     return lax.psum_scatter(total, "sector", scatter_dimension=0, tiled=True)
 

time: 36.7 us -> 37 us (level)
  waiting for transfers between devices: 7.15 us -> 9.91 us
  Pallas kernels: 12.6 us -> 11.2 us
  starting transfers between devices: 15.2 us -> 14 us
    ppermute x10 -> x9, waiting for transfers between devices: 7.15 us -> 9.91 us  [swap(): lax.ppermute(value, axis, [(i, i ^ mask) for i in range(lax.axis_size(axi...]
    pallas_call x3 -> x2, Pallas kernels: 8.61 us -> 7.24 us  [summed(): pl.pallas_call(functools.partial(sum_kernel, order, stage), out_shape=out...]
    ppermute x10 -> x9, starting transfers between devices: 15.2 us -> 14 us  [swap(): lax.ppermute(value, axis, [(i, i ^ mask) for i in range(lax.axis_size(axi...]
    add x3 -> x2, other arithmetic: 0.8 us -> 0.77 us  [per_device(): sigma = lax.optimization_barrier(sigma) + other.astype(jnp.float32)]
  transfers between devices with their start and end apart: 10 -> 9, of which waited for: 5 -> 5; matrix products, arithmetic and copies ran while one was open for 1% -> 1% of each run, Pallas kernels for 25% -> 18%
where the time goes in v15:
time: 37 us; the launch traced here: 36.8 us
  starting transfers between devices  14 us (38%)
  Pallas kernels  11.2 us (30%)
  waiting for transfers between devices  9.91 us (27%)
  other arithmetic  1.66 us (4%)
    ppermute x9, starting transfers between devices, swap(): lax.ppermute(value, axis, [(i, i ^ mask) for i in range(lax.axis_size(axi...  14 us
    ppermute x9, waiting for transfers between devices, swap(): lax.ppermute(value, axis, [(i, i ^ mask) for i in range(lax.axis_size(axi...  9.91 us
    pallas_call x2, Pallas kernels, summed(): pl.pallas_call(functools.partial(sum_kernel, order, stage), out_shape=out...  7.24 us
    pallas_call x1, Pallas kernels, mix(): pl.pallas_call(functools.partial(mix_kernel, split), out_shape=[pltpu.VME...  3.95 us
    add x2, other arithmetic, per_device(): sigma = lax.optimization_barrier(sigma) + other.astype(jnp.float32)  0.77 us
  transfers between devices with their start and end apart: 9, of which 5 were waited for; matrix products, arithmetic and copies ran while one was open for 1% of the time, Pallas kernels for 18%

profile of v15, /device:TPU:0, one launch (start us, length us, event | category | flops | bytes accessed | tf_op | source)
XLA Modules:
  0.0 36.8 jit_solution(10343504053380803108)
XLA Ops:
  0.0 0.7 %select_bitcast_fusion = f32[4,32]{1,0:T(4,128)S(1)} fusion(f32[32,4]{0,1:T(4,128)} %param.9, s32[32,4]{0,1:T(4,128)} %param.10), kind=kLoop, calls=%fused_computation.9 | loop fusion | flops 256 | bytes 1536 | tf_op jit(solution)/shard_map/jit(_where)/select_n | solution.py:197
  0.7 3.0 %collective-permute-start = (f32[4,32]{1,0:T(4,128)S(1)}, f32[4,32]{1,0:T(4,128)S(1)}, u32[]{:S(2)}, u32[]{:S(2)}) collective-permute-start(f32[4,32]{1,0:T(4,128)S(1)} %select_bitcast_fusion), channel_id=1, source_target_pairs={{0,4},{4,0},{8,12},{12,8},{1,5},{5,1},{9,13},{13,9},{2,6},{6,2},{1... | collective-permute-start | bytes 1544 | tf_op jit(solution)/shard_map/ppermute | solution.py:187
  3.7 1.6 %collective-permute-done = f32[4,32]{1,0:T(4,128)S(1)} collective-permute-done((f32[4,32]{1,0:T(4,128)S(1)}, f32[4,32]{1,0:T(4,128)S(1)}, u32[]{:S(2)}, u32[]{:S(2)}) %collective-permute-start) | collective-permute-done | bytes 544 | tf_op jit(solution)/shard_map/ppermute | solution.py:187
  5.3 3.1 %collective-permute-start.1 = (f32[8,32]{1,0:T(8,128)S(1)}, f32[8,32]{1,0:T(8,128)S(1)}, u32[]{:S(2)}, u32[]{:S(2)}) collective-permute-start(f32[8,32]{1,0:T(8,128)S(1)} %pad_maximum_fusion.1), channel_id=1, source_target_pairs={{0,8},{4,12},{8,0},{12,4},{1,9},{5,13},{9,1},{13,5},{2,10},{6,14},... | collective-permute-start | bytes 3080 | tf_op jit(solution)/shard_map/ppermute | solution.py:187
  8.4 4.0 %shard_map.64 = (bf16[32,4,128,256]{3,2,1,0:T(8,128)(2,1)S(1)}, bf16[32,256,256]{2,1,0:T(8,128)(2,1)S(1)}) custom-call(bf16[4,256,256]{2,1,0:T(8,128)(2,1)} %wave_ref.1, bf16[32,128,256]{2,1,0:T(8,128)(2,1)} %left_ref.1, bf16[32,256,256]{2,1,0:T(8,128)(2,1)} %right_ref.1), custom_call_target="tpu_custom_call" | custom-call | flops 2147483648 | bytes 6291456 | tf_op jit(solution)/shard_map/pallas_call | solution.py:69
  12.3 0.0 collective-permute-done.1
  12.4 4.5 %shard_map.65 = (f32[16,128,128]{2,1,0:T(8,128)S(1)}, f32[16,128,128]{2,1,0:T(8,128)S(1)}, f32[4,128,128]{2,1,0:T(8,128)S(1)}, bf16[4,128,128]{2,1,0:T(8,128)(2,...) custom-call(s32[32]{0:T(128)} %shift_ref.3, f32[16,32]{1,0:T(8,128)S(1)} %pad_maximum_fusion.coef_ref, ...), custom_call_target="tpu_custom_call" | custom-call | flops 1073741824 | bytes 6291456 | tf_op jit(solution)/shard_map/pallas_call | solution.py:165
  16.9 1.0 %collective-permute-start.3 = (bf16[4,128,128]{2,1,0:T(8,128)(2,1)S(1)}, bf16[4,128,128]{2,1,0:T(8,128)(2,1)S(1)}, u32[]{:S(2)}, u32[]{:S(2)}) collective-permute-start(bf16[4,128,128]{2,1,0:T(8,128)(2,1)S(1)} %get-tuple-element.26), channel_id=1, source_target_pairs={{0,2},{2,0},{1,3},{3,1},{4,6},{6,4},{5,7},{7,5},{8,10},{10,8},{9,1... | collective-permute-start | bytes 393224 | tf_op jit(solution)/shard_map/ppermute | solution.py:187
  17.9 1.1 %collective-permute-start.2 = (bf16[4,128,128]{2,1,0:T(8,128)(2,1)S(1)}, bf16[4,128,128]{2,1,0:T(8,128)(2,1)S(1)}, u32[]{:S(2)}, u32[]{:S(2)}) collective-permute-start(bf16[4,128,128]{2,1,0:T(8,128)(2,1)S(1)} %get-tuple-element.33), channel_id=1, source_target_pairs={{0,2},{2,0},{1,3},{3,1},{4,6},{6,4},{5,7},{7,5},{8,10},{10,8},{9,1... | collective-permute-start | bytes 393224 | tf_op jit(solution)/shard_map/ppermute | solution.py:187
  19.0 2.7 %shard_map.66 = (f32[16,128,128]{2,1,0:T(8,128)S(1)}, f32[16,128,128]{2,1,0:T(8,128)S(1)}, f32[4,128,128]{2,1,0:T(8,128)S(1)}, bf16[4,128,128]{2,1,0:T(8,128)(2,...) custom-call(s32[32]{0:T(128)} %shift_ref.3, ...), custom_call_target="tpu_custom_call", output_to_operand_aliasing={{0}: (4, {}), {1}: (5, {})} | custom-call | flops 1073741824 | bytes 6291456 | tf_op jit(solution)/shard_map/pallas_call | solution.py:165
  21.7 0.5 %collective-permute-done.3 = bf16[4,128,128]{2,1,0:T(8,128)(2,1)S(1)} collective-permute-done((bf16[4,128,128]{2,1,0:T(8,128)(2,1)S(1)}, bf16[4,128,128]{2,1,0:T(8,128)(2,1)S(1)}, u32[]{:S(2)}, u32[]{:S(2)}) %collective-permute-start.3) | collective-permute-done | bytes 131104 | tf_op jit(solution)/shard_map/ppermute | solution.py:187
  22.2 2.0 %collective-permute-start.6 = (bf16[4,128,128]{2,1,0:T(8,128)(2,1)S(1)}, bf16[4,128,128]{2,1,0:T(8,128)(2,1)S(1)}, u32[]{:S(2)}, u32[]{:S(2)}) collective-permute-start(bf16[4,128,128]{2,1,0:T(8,128)(2,1)S(1)} %add_convert_fusion.2), channel_id=1, source_target_pairs={{0,4},{4,0},{8,12},{12,8},{1,5},{5,1},{9,13},{13,9},{2,6},{6,2},{1... | collective-permute-start | bytes 393224 | tf_op jit(solution)/shard_map/ppermute | solution.py:187
  24.2 0.0 collective-permute-done.2
  24.3 1.7 %collective-permute-start.4 = (bf16[4,128,128]{2,1,0:T(8,128)(2,1)S(1)}, bf16[4,128,128]{2,1,0:T(8,128)(2,1)S(1)}, u32[]{:S(2)}, u32[]{:S(2)}) collective-permute-start(bf16[4,128,128]{2,1,0:T(8,128)(2,1)S(1)} %get-tuple-element.38), channel_id=1, source_target_pairs={{0,2},{2,0},{1,3},{3,1},{4,6},{6,4},{5,7},{7,5},{8,10},{10,8},{9,1... | collective-permute-start | bytes 393224 | tf_op jit(solution)/shard_map/ppermute | solution.py:187
  26.0 0.3 collective-permute-start.5
  26.4 0.9 %collective-permute-done.6 = bf16[4,128,128]{2,1,0:T(8,128)(2,1)S(1)} collective-permute-done((bf16[4,128,128]{2,1,0:T(8,128)(2,1)S(1)}, bf16[4,128,128]{2,1,0:T(8,128)(2,1)S(1)}, u32[]{:S(2)}, u32[]{:S(2)}) %collective-permute-start.6) | collective-permute-done | bytes 131104 | tf_op jit(solution)/shard_map/ppermute | solution.py:187
  27.3 0.4 collective-permute-start.8
  27.7 3.3 %collective-permute-done.5 = bf16[4,128,128]{2,1,0:T(8,128)(2,1)S(1)} collective-permute-done((bf16[4,128,128]{2,1,0:T(8,128)(2,1)S(1)}, bf16[4,128,128]{2,1,0:T(8,128)(2,1)S(1)}, u32[]{:S(2)}, u32[]{:S(2)}) %collective-permute-start.5) | collective-permute-done | bytes 131104 | tf_op jit(solution)/shard_map/ppermute | solution.py:187
  31.0 1.4 %collective-permute-start.7 = (bf16[4,128,128]{2,1,0:T(8,128)(2,1)S(1)}, bf16[4,128,128]{2,1,0:T(8,128)(2,1)S(1)}, u32[]{:S(2)}, u32[]{:S(2)}) collective-permute-start(bf16[4,128,128]{2,1,0:T(8,128)(2,1)S(1)} %add_convert_fusion), channel_id=1, source_target_pairs={{0,4},{4,0},{8,12},{12,8},{1,5},{5,1},{9,13},{13,9},{2,6},{6,2},{1... | collective-permute-start | bytes 393224 | tf_op jit(solution)/shard_map/ppermute | solution.py:187
  32.4 0.0 collective-permute-done.4
  32.4 3.6 %collective-permute-done.7 = bf16[4,128,128]{2,1,0:T(8,128)(2,1)S(1)} collective-permute-done((bf16[4,128,128]{2,1,0:T(8,128)(2,1)S(1)}, bf16[4,128,128]{2,1,0:T(8,128)(2,1)S(1)}, u32[]{:S(2)}, u32[]{:S(2)}) %collective-permute-start.7) | collective-permute-done | bytes 131104 | tf_op jit(solution)/shard_map/ppermute | solution.py:187
  36.1 0.0 collective-permute-done.8
  36.1 0.7 %convert_add_fusion = f32[4,128,128]{2,1,0:T(8,128)} fusion(f32[4,128,128]{2,1,0:T(8,128)S(1)} %convert_add_fusion.1, bf16[4,128,128]{2,1,0:T(8,128)(2,1)S(1)} %collective-permute-done.8), kind=kLoop, calls=%fused_computation | loop fusion | flops 131072 | bytes 655360 | tf_op jit(solution)/shard_map/add | solution.py:226
  (8 shorter events, 0.2 us)
Async XLA Ops:
  0.7 4.6 %collective-permute-start = (f32[4,32]{1,0:T(4,128)S(1)}, f32[4,32]{1,0:T(4,128)S(1)}, u32[]{:S(2)}, u32[]{:S(2)}) collective-permute-start(f32[4,32]{1,0:T(4,128)S(1)} %select_bitcast_fusion), channel_id=1, source_target_pairs={{0,4},{4,0},{8,12},{12,8},{1,5},{5,1},{9,13},{13,9},{2,6},{6,2},{1... | collective-permute-start | bytes 1544 | tf_op jit(solution)/shard_map/ppermute | solution.py:187
  5.3 7.1 %collective-permute-start.1 = (f32[8,32]{1,0:T(8,128)S(1)}, f32[8,32]{1,0:T(8,128)S(1)}, u32[]{:S(2)}, u32[]{:S(2)}) collective-permute-start(f32[8,32]{1,0:T(8,128)S(1)} %pad_maximum_fusion.1), channel_id=1, source_target_pairs={{0,8},{4,12},{8,0},{12,4},{1,9},{5,13},{9,1},{13,5},{2,10},{6,14},... | collective-permute-start | bytes 3080 | tf_op jit(solution)/shard_map/ppermute | solution.py:187
  16.9 5.3 %collective-permute-start.3 = (bf16[4,128,128]{2,1,0:T(8,128)(2,1)S(1)}, bf16[4,128,128]{2,1,0:T(8,128)(2,1)S(1)}, u32[]{:S(2)}, u32[]{:S(2)}) collective-permute-start(bf16[4,128,128]{2,1,0:T(8,128)(2,1)S(1)} %get-tuple-element.26), channel_id=1, source_target_pairs={{0,2},{2,0},{1,3},{3,1},{4,6},{6,4},{5,7},{7,5},{8,10},{10,8},{9,1... | collective-permute-start | bytes 393224 | tf_op jit(solution)/shard_map/ppermute | solution.py:187
  17.9 6.3 %collective-permute-start.2 = (bf16[4,128,128]{2,1,0:T(8,128)(2,1)S(1)}, bf16[4,128,128]{2,1,0:T(8,128)(2,1)S(1)}, u32[]{:S(2)}, u32[]{:S(2)}) collective-permute-start(bf16[4,128,128]{2,1,0:T(8,128)(2,1)S(1)} %get-tuple-element.33), channel_id=1, source_target_pairs={{0,2},{2,0},{1,3},{3,1},{4,6},{6,4},{5,7},{7,5},{8,10},{10,8},{9,1... | collective-permute-start | bytes 393224 | tf_op jit(solution)/shard_map/ppermute | solution.py:187
  22.2 5.0 %collective-permute-start.6 = (bf16[4,128,128]{2,1,0:T(8,128)(2,1)S(1)}, bf16[4,128,128]{2,1,0:T(8,128)(2,1)S(1)}, u32[]{:S(2)}, u32[]{:S(2)}) collective-permute-start(bf16[4,128,128]{2,1,0:T(8,128)(2,1)S(1)} %add_convert_fusion.2), channel_id=1, source_target_pairs={{0,4},{4,0},{8,12},{12,8},{1,5},{5,1},{9,13},{13,9},{2,6},{6,2},{1... | collective-permute-start | bytes 393224 | tf_op jit(solution)/shard_map/ppermute | solution.py:187
  24.3 8.1 %collective-permute-start.4 = (bf16[4,128,128]{2,1,0:T(8,128)(2,1)S(1)}, bf16[4,128,128]{2,1,0:T(8,128)(2,1)S(1)}, u32[]{:S(2)}, u32[]{:S(2)}) collective-permute-start(bf16[4,128,128]{2,1,0:T(8,128)(2,1)S(1)} %get-tuple-element.38), channel_id=1, source_target_pairs={{0,2},{2,0},{1,3},{3,1},{4,6},{6,4},{5,7},{7,5},{8,10},{10,8},{9,1... | collective-permute-start | bytes 393224 | tf_op jit(solution)/shard_map/ppermute | solution.py:187
  26.0 5.0 %collective-permute-start.5 = (bf16[4,128,128]{2,1,0:T(8,128)(2,1)S(1)}, bf16[4,128,128]{2,1,0:T(8,128)(2,1)S(1)}, u32[]{:S(2)}, u32[]{:S(2)}) collective-permute-start(bf16[4,128,128]{2,1,0:T(8,128)(2,1)S(1)} %get-tuple-element.40), channel_id=1, source_target_pairs={{0,2},{2,0},{1,3},{3,1},{4,6},{6,4},{5,7},{7,5},{8,10},{10,8},{9,1... | collective-permute-start | bytes 393224 | tf_op jit(solution)/shard_map/ppermute | solution.py:187
  27.3 8.8 %collective-permute-start.8 = (bf16[4,128,128]{2,1,0:T(8,128)(2,1)S(1)}, bf16[4,128,128]{2,1,0:T(8,128)(2,1)S(1)}, u32[]{:S(2)}, u32[]{:S(2)}) collective-permute-start(bf16[4,128,128]{2,1,0:T(8,128)(2,1)S(1)} %add_convert_fusion.1), channel_id=1, source_target_pairs={{0,8},{4,12},{8,0},{12,4},{1,9},{5,13},{9,1},{13,5},{2,10},{6,14},... | collective-permute-start | bytes 393224 | tf_op jit(solution)/shard_map/ppermute | solution.py:187
  31.0 5.0 %collective-permute-start.7 = (bf16[4,128,128]{2,1,0:T(8,128)(2,1)S(1)}, bf16[4,128,128]{2,1,0:T(8,128)(2,1)S(1)}, u32[]{:S(2)}, u32[]{:S(2)}) collective-permute-start(bf16[4,128,128]{2,1,0:T(8,128)(2,1)S(1)} %add_convert_fusion), channel_id=1, source_target_pairs={{0,4},{4,0},{8,12},{12,8},{1,5},{5,1},{9,13},{13,9},{2,6},{6,2},{1... | collective-permute-start | bytes 393224 | tf_op jit(solution)/shard_map/ppermute | solution.py:187

commit v16 on v14

--- a/solution.py
+++ b/solution.py
@@ -97,6 +97,7 @@
     targets = coef_ref.shape[0]
     half = width // 2
     picked = refs[-1]
+    first = lax.axis_index("sector") * sec_dev
 
     def pick(k, count):
         picked[count] = k
@@ -137,7 +138,8 @@
             )
             for s in range(sec_dev):
                 target = wrapped(s - shift_ref[k], targets)
-                weight = jnp.where(at < count, coef_ref[target, k], 0.0)
+                sector = wrapped(first + s - shift_ref[k], targets)
+                weight = jnp.where(at < count, coef_ref[sector, k], 0.0)
                 scaled = weight * product[s * rows : (s + 1) * rows]
                 if stage is None:
                     sums[0][target] += scaled
@@ -202,8 +204,7 @@
     mixed, held = mix(wavefunction, left_ops, right_ops, split)
 
     if split:
-        coefs = [live] + [shift_by(live, "sector", -g) for g in range(1, devices)]
-        coef = jnp.concatenate(coefs, axis=0)
+        coef = lax.all_to_all(jnp.tile(live, (devices, 1)), "sector", 0, 0, tiled=True)
         order = ((2,), (1, 3, 0))
         *sums, mine_2, theirs_2 = summed(sector_shift, coef, mixed, held, order, 0)
         crossed_2 = shift_by(theirs_2, "op", 1)
@@ -225,7 +226,7 @@
         return sigma
 
     first = lax.axis_index("sector") * sec_dev
-    coef = jnp.roll(lax.all_gather(live, "sector", axis=0, tiled=True), -first, axis=0)
+    coef = lax.all_gather(live, "sector", axis=0, tiled=True)
     (total,) = summed(sector_shift, coef, mixed, held, (), None)
     total = jnp.roll(total, first, axis=0)
     total = lax.psum_scatter(total, "op", scatter_dimension=2, tiled=True)

time: 35.3 us -> 48.8 us (1.38)
  local copies, waits for them, and re-layouts: 0 us -> 12 us
  starting transfers between devices: 14.5 us -> 19 us
  waiting for transfers between devices: 7.95 us -> 4.1 us
  other arithmetic: 1.64 us -> 2.28 us
    unnamed x0 -> x10, local copies, waits for them, and re-layouts: none -> 11.5 us
    all_to_all x0 -> x1, starting transfers between devices: none -> 6.32 us  [per_device(): lax.all_to_all(jnp.tile(live, (devices, 1)), 'sector', 0, 0, tiled=True)]
    ppermute x10 -> x7, waiting for transfers between devices: 7.95 us -> 4.09 us  [shift_by(): lax.ppermute(value, axis, [(i, (i + distance) % size) for i in range(size)])]
    ppermute x10 -> x7, starting transfers between devices: 14.5 us -> 12.6 us  [shift_by(): lax.ppermute(value, axis, [(i, (i + distance) % size) for i in range(size)])]
    all_to_all x0 -> x1, other arithmetic: none -> 0.66 us  [per_device(): lax.all_to_all(jnp.tile(live, (devices, 1)), 'sector', 0, 0, tiled=True)]
    all_to_all x0 -> x1, local copies, waits for them, and re-layouts: none -> 0.51 us  [per_device(): lax.all_to_all(jnp.tile(live, (devices, 1)), 'sector', 0, 0, tiled=True)]
  transfers between devices with their start and end apart: 10 -> 8, of which waited for: 5 -> 4; matrix products, arithmetic and copies ran while one was open for 0% -> 0% of each run, Pallas kernels for 22% -> 15%
where the time goes in v16:
time: 48.8 us; the launch traced here: 48.6 us
  starting transfers between devices  19 us (39%)
  local copies, waits for them, and re-layouts  12 us (25%)
  Pallas kernels  11.2 us (23%)
  waiting for transfers between devices  4.1 us (8%)
  other arithmetic  2.28 us (5%)
    ppermute x7, starting transfers between devices, shift_by(): lax.ppermute(value, axis, [(i, (i + distance) % size) for i in range(size)])  12.6 us
    unnamed x10, local copies, waits for them, and re-layouts  11.5 us
    pallas_call x2, Pallas kernels, summed(): pl.pallas_call(functools.partial(sum_kernel, order, stage), out_shape=out...  7.24 us
    all_to_all x1, starting transfers between devices, per_device(): lax.all_to_all(jnp.tile(live, (devices, 1)), 'sector', 0, 0, tiled=True)  6.32 us
    ppermute x7, waiting for transfers between devices, shift_by(): lax.ppermute(value, axis, [(i, (i + distance) % size) for i in range(size)])  4.09 us
    pallas_call x1, Pallas kernels, mix(): pl.pallas_call(functools.partial(mix_kernel, split), out_shape=[pltpu.VME...  3.95 us
  transfers between devices with their start and end apart: 8, of which 4 were waited for; matrix products, arithmetic and copies ran while one was open for 0% of the time, Pallas kernels for 15%

profile of v16, /device:TPU:0, one launch (start us, length us, event | category | flops | bytes accessed | tf_op | source)
XLA Modules:
  0.0 48.6 jit_solution(10866540814861918055)
XLA Ops:
  0.0 0.7 %select_bitcast_fusion = f32[4,32]{1,0:T(4,128)S(1)} fusion(f32[32,4]{0,1:T(4,128)} %param.9, s32[32,4]{0,1:T(4,128)} %param.10), kind=kLoop, calls=%fused_computation.7 | loop fusion | flops 256 | bytes 1536 | tf_op jit(solution)/shard_map/jit(_where)/select_n | solution.py:202
  0.7 0.7 %reshape.7 = f32[4,1,128]{2,1,0:T(1,128)} reshape(f32[4,4,32]{2,1,0:T(4,128)S(1)} %tile.2) | data formatting | bytes 4096
  1.4 6.3 %all-to-all-start = ((f32[4,1,128]{2,1,0:T(1,128)}), f32[4,1,128]{2,1,0:T(1,128)S(1)}, u32[]{:S(2)}, u32[]{:S(2)}) async-start(f32[4,1,128]{2,1,0:T(1,128)} %reshape.7), calls=%async_computation | async-start | bytes 4096 | tf_op jit(solution)/shard_map/all_to_all | solution.py:207
  7.7 4.0 %shard_map.64 = (bf16[32,4,128,256]{3,2,1,0:T(8,128)(2,1)S(1)}, bf16[32,256,256]{2,1,0:T(8,128)(2,1)S(1)}) custom-call(bf16[4,256,256]{2,1,0:T(8,128)(2,1)} %wave_ref.1, bf16[32,128,256]{2,1,0:T(8,128)(2,1)} %left_ref.1, bf16[32,256,256]{2,1,0:T(8,128)(2,1)} %right_ref.1), custom_call_target="tpu_custom_call" | custom-call | flops 2147483648 | bytes 6291456 | tf_op jit(solution)/shard_map/pallas_call | solution.py:69
  11.7 0.0 copy-start
  11.7 3.2 %copy-done = bf16[32,4,128,256]{3,2,1,0:T(8,128)(2,1)} copy-done((bf16[32,4,128,256]{3,2,1,0:T(8,128)(2,1)}, bf16[32,4,128,256]{3,2,1,0:T(8,128)(2,1)S(1)}, u32[]{:S(2)}) %copy-start) | copy-done | bytes 8388632
  14.9 0.0 copy-start.2
  14.9 2.0 %copy-done.2 = bf16[32,256,256]{2,1,0:T(8,128)(2,1)} copy-done((bf16[32,256,256]{2,1,0:T(8,128)(2,1)}, bf16[32,256,256]{2,1,0:T(8,128)(2,1)S(1)}, u32[]{:S(2)}) %copy-start.2) | copy-done | bytes 4194328
  16.9 0.0 all-to-all-done
  16.9 0.5 %broadcast.7 = f32[]{:T(128)} broadcast(f32[]{:T(128)} %constant.5), dimensions={} | broadcast | bytes 8 | tf_op jit(solution)/shard_map/all_to_all | solution.py:207
  17.4 0.7 %reduce = f32[4,128]{1,0:T(4,128)S(1)} reduce(f32[4,1,128]{2,1,0:T(1,128)S(1)} %all-to-all-done, f32[]{:T(128)} %broadcast.7), dimensions={1}, to_apply=%all_to_all.5.reduce_sub_computation | reduce | bytes 4100 | tf_op jit(solution)/shard_map/all_to_all | solution.py:207
  18.0 0.1 reshape.8
  18.1 0.0 copy-start.1
  18.1 3.4 %copy-done.1 = bf16[32,4,128,256]{3,2,1,0:T(8,128)(2,1)S(1)} copy-done((bf16[32,4,128,256]{3,2,1,0:T(8,128)(2,1)S(1)}, bf16[32,4,128,256]{3,2,1,0:T(8,128)(2,1)}, u32[]{:S(2)}) %copy-start.1) | copy-done | bytes 8388632
  21.5 2.2 %copy-done.3 = bf16[32,256,256]{2,1,0:T(8,128)(2,1)S(1)} copy-done((bf16[32,256,256]{2,1,0:T(8,128)(2,1)S(1)}, bf16[32,256,256]{2,1,0:T(8,128)(2,1)}, u32[]{:S(2)}) %copy-start.3) | copy-done | bytes 4194328
  23.7 3.9 %shard_map.65 = (f32[16,128,128]{2,1,0:T(8,128)S(1)}, f32[16,128,128]{2,1,0:T(8,128)S(1)}, f32[4,128,128]{2,1,0:T(8,128)S(1)}, bf16[4,128,128]{2,1,0:T(8,128)(2,1)S(1)}) custom-call(s32[32]{0:T(128)} %shift_ref.3, f32[16,32]{1,0:T(8,128)S(1)} %bitcast.3, bf16[32,4,128,256]{3,2,1,0:T(8,128)(2,1)S(1)} %copy-done.1, bf16[32,256,256]{2,1,0:T(8,128)(2,1)S(1)} %copy-done.3), custom_call_target="tpu_custom_call" | custom-call | flops 1073741824 | bytes 6291456 | tf_op jit(solution)/shard_map/pallas_call | solution.py:169
  27.6 0.1 collective-permute-start
  27.7 3.3 %shard_map.66 = (f32[16,128,128]{2,1,0:T(8,128)S(1)}, f32[16,128,128]{2,1,0:T(8,128)S(1)}, f32[4,128,128]{2,1,0:T(8,128)S(1)}, bf16[4,128,128]{2,1,0:T(8,128)(2,...) custom-call(s32[32]{0:T(128)} %shift_ref.3, ...), custom_call_target="tpu_custom_call", output_to_operand_aliasing={{0}: (4, {}), {1}: (5, {})} | custom-call | flops 1073741824 | bytes 6291456 | tf_op jit(solution)/shard_map/pallas_call | solution.py:169
  31.0 1.6 %collective-permute-done = bf16[4,128,128]{2,1,0:T(8,128)(2,1)S(1)} collective-permute-done((bf16[4,128,128]{2,1,0:T(8,128)(2,1)S(1)}, bf16[4,128,128]{2,1,0:T(8,128)(2,1)S(1)}, u32[]{:S(2)}, u32[]{:S(2)}) %collective-permute-start) | collective-permute-done | bytes 131104 | tf_op jit(solution)/shard_map/ppermute | solution.py:192
  32.7 1.6 %collective-permute-start.1 = (bf16[4,128,128]{2,1,0:T(8,128)(2,1)S(1)}, bf16[4,128,128]{2,1,0:T(8,128)(2,1)S(1)}, u32[]{:S(2)}, u32[]{:S(2)}) collective-permute-start(bf16[4,128,128]{2,1,0:T(8,128)(2,1)S(1)} %get-tuple-element.37), channel_id=1, source_target_pairs={{0,2},{2,0},{1,3},{3,1},{4,6},{6,4},{5,7},{7,5},{8,10},{10,8},{9,1... | collective-permute-start | bytes 393224 | tf_op jit(solution)/shard_map/ppermute | solution.py:192
  34.3 2.9 %collective-permute-start.4 = (bf16[4,128,128]{2,1,0:T(8,128)(2,1)S(1)}, bf16[4,128,128]{2,1,0:T(8,128)(2,1)S(1)}, u32[]{:S(2)}, u32[]{:S(2)}) collective-permute-start(bf16[4,128,128]{2,1,0:T(8,128)(2,1)S(1)} %add_convert_fusion.2), channel_id=1, source_target_pairs={{0,8},{4,12},{8,0},{12,4},{1,9},{5,13},{9,1},{13,5},{2,10},{6,14},... | collective-permute-start | bytes 393224 | tf_op jit(solution)/shard_map/ppermute | solution.py:192
  37.2 0.5 %collective-permute-start.3 = (bf16[4,128,128]{2,1,0:T(8,128)(2,1)S(1)}, bf16[4,128,128]{2,1,0:T(8,128)(2,1)S(1)}, u32[]{:S(2)}, u32[]{:S(2)}) collective-permute-start(bf16[4,128,128]{2,1,0:T(8,128)(2,1)S(1)} %get-tuple-element.42), channel_id=1, source_target_pairs={{0,2},{2,0},{1,3},{3,1},{4,6},{6,4},{5,7},{7,5},{8,10},{10,8},{9,1... | collective-permute-start | bytes 393224 | tf_op jit(solution)/shard_map/ppermute | solution.py:192
  37.7 0.0 collective-permute-done.1
  37.8 2.3 %collective-permute-start.5 = (bf16[4,128,128]{2,1,0:T(8,128)(2,1)S(1)}, bf16[4,128,128]{2,1,0:T(8,128)(2,1)S(1)}, u32[]{:S(2)}, u32[]{:S(2)}) collective-permute-start(bf16[4,128,128]{2,1,0:T(8,128)(2,1)S(1)} %add_convert_fusion.1), channel_id=1, source_target_pairs={{0,4},{4,8},{8,12},{12,0},{1,5},{5,9},{9,13},{13,1},{2,6},{6,10},{... | collective-permute-start | bytes 393224 | tf_op jit(solution)/shard_map/ppermute | solution.py:192
  40.1 2.5 %collective-permute-start.2 = (bf16[4,128,128]{2,1,0:T(8,128)(2,1)S(1)}, bf16[4,128,128]{2,1,0:T(8,128)(2,1)S(1)}, u32[]{:S(2)}, u32[]{:S(2)}) collective-permute-start(bf16[4,128,128]{2,1,0:T(8,128)(2,1)S(1)} %get-tuple-element.39), channel_id=1, source_target_pairs={{0,2},{2,0},{1,3},{3,1},{4,6},{6,4},{5,7},{7,5},{8,10},{10,8},{9,1... | collective-permute-start | bytes 393224 | tf_op jit(solution)/shard_map/ppermute | solution.py:192
  42.6 0.0 collective-permute-done.3
  42.6 2.8 %collective-permute-start.6 = (bf16[4,128,128]{2,1,0:T(8,128)(2,1)S(1)}, bf16[4,128,128]{2,1,0:T(8,128)(2,1)S(1)}, u32[]{:S(2)}, u32[]{:S(2)}) collective-permute-start(bf16[4,128,128]{2,1,0:T(8,128)(2,1)S(1)} %add_convert_fusion), channel_id=1, source_target_pairs={{0,12},{4,0},{8,4},{12,8},{1,13},{5,1},{9,5},{13,9},{2,14},{6,2},{... | collective-permute-start | bytes 393224 | tf_op jit(solution)/shard_map/ppermute | solution.py:192
  45.4 0.1 collective-permute-done.2
  45.5 0.0 collective-permute-done.4
  45.6 0.5 %collective-permute-done.5 = bf16[4,128,128]{2,1,0:T(8,128)(2,1)S(1)} collective-permute-done((bf16[4,128,128]{2,1,0:T(8,128)(2,1)S(1)}, bf16[4,128,128]{2,1,0:T(8,128)(2,1)S(1)}, u32[]{:S(2)}, u32[]{:S(2)}) %collective-permute-start.5) | collective-permute-done | bytes 131104 | tf_op jit(solution)/shard_map/ppermute | solution.py:192
  46.1 1.8 %collective-permute-done.6 = bf16[4,128,128]{2,1,0:T(8,128)(2,1)S(1)} collective-permute-done((bf16[4,128,128]{2,1,0:T(8,128)(2,1)S(1)}, bf16[4,128,128]{2,1,0:T(8,128)(2,1)S(1)}, u32[]{:S(2)}, u32[]{:S(2)}) %collective-permute-start.6) | collective-permute-done | bytes 131104 | tf_op jit(solution)/shard_map/ppermute | solution.py:192
  47.9 0.7 %convert_add_fusion = f32[4,128,128]{2,1,0:T(8,128)} fusion(f32[4,128,128]{2,1,0:T(8,128)S(1)} %convert_add_fusion.1, bf16[4,128,128]{2,1,0:T(8,128)(2,1)S(1)} %collective-permute-done.6), kind=kLoop, calls=%fused_computation | loop fusion | flops 131072 | bytes 655360 | tf_op jit(solution)/shard_map/add | solution.py:225
  (8 shorter events, 0.2 us)
Async XLA Ops:
  1.4 15.5 %all-to-all-start = ((f32[4,1,128]{2,1,0:T(1,128)}), f32[4,1,128]{2,1,0:T(1,128)S(1)}, u32[]{:S(2)}, u32[]{:S(2)}) async-start(f32[4,1,128]{2,1,0:T(1,128)} %reshape.7), calls=%async_computation | async-start | bytes 4096 | tf_op jit(solution)/shard_map/all_to_all | solution.py:207
  11.7 3.2 %copy-start = (bf16[32,4,128,256]{3,2,1,0:T(8,128)(2,1)}, bf16[32,4,128,256]{3,2,1,0:T(8,128)(2,1)S(1)}, u32[]{:S(2)}) copy-start(bf16[32,4,128,256]{3,2,1,0:T(8,128)(2,1)S(1)} %get-tuple-element.25.mixed_ref) | copy-start | bytes 25165828
  14.9 2.0 %copy-start.2 = (bf16[32,256,256]{2,1,0:T(8,128)(2,1)}, bf16[32,256,256]{2,1,0:T(8,128)(2,1)S(1)}, u32[]{:S(2)}) copy-start(bf16[32,256,256]{2,1,0:T(8,128)(2,1)S(1)} %get-tuple-element.26.held_ref) | copy-start | bytes 12582916
  18.1 3.4 %copy-start.1 = (bf16[32,4,128,256]{3,2,1,0:T(8,128)(2,1)S(1)}, bf16[32,4,128,256]{3,2,1,0:T(8,128)(2,1)}, u32[]{:S(2)}) copy-start(bf16[32,4,128,256]{3,2,1,0:T(8,128)(2,1)} %copy-done) | copy-start | bytes 25165828
  21.5 2.2 %copy-start.3 = (bf16[32,256,256]{2,1,0:T(8,128)(2,1)S(1)}, bf16[32,256,256]{2,1,0:T(8,128)(2,1)}, u32[]{:S(2)}) copy-start(bf16[32,256,256]{2,1,0:T(8,128)(2,1)} %copy-done.2) | copy-start | bytes 12582916
  27.6 5.0 %collective-permute-start = (bf16[4,128,128]{2,1,0:T(8,128)(2,1)S(1)}, bf16[4,128,128]{2,1,0:T(8,128)(2,1)S(1)}, u32[]{:S(2)}, u32[]{:S(2)}) collective-permute-start(bf16[4,128,128]{2,1,0:T(8,128)(2,1)S(1)} %get-tuple-element.27), channel_id=1, source_target_pairs={{0,2},{2,0},{1,3},{3,1},{4,6},{6,4},{5,7},{7,5},{8,10},{10,8},{9,1... | collective-permute-start | bytes 393224 | tf_op jit(solution)/shard_map/ppermute | solution.py:192
  32.7 5.0 %collective-permute-start.1 = (bf16[4,128,128]{2,1,0:T(8,128)(2,1)S(1)}, bf16[4,128,128]{2,1,0:T(8,128)(2,1)S(1)}, u32[]{:S(2)}, u32[]{:S(2)}) collective-permute-start(bf16[4,128,128]{2,1,0:T(8,128)(2,1)S(1)} %get-tuple-element.37), channel_id=1, source_target_pairs={{0,2},{2,0},{1,3},{3,1},{4,6},{6,4},{5,7},{7,5},{8,10},{10,8},{9,1... | collective-permute-start | bytes 393224 | tf_op jit(solution)/shard_map/ppermute | solution.py:192
  34.3 11.3 %collective-permute-start.4 = (bf16[4,128,128]{2,1,0:T(8,128)(2,1)S(1)}, bf16[4,128,128]{2,1,0:T(8,128)(2,1)S(1)}, u32[]{:S(2)}, u32[]{:S(2)}) collective-permute-start(bf16[4,128,128]{2,1,0:T(8,128)(2,1)S(1)} %add_convert_fusion.2), channel_id=1, source_target_pairs={{0,8},{4,12},{8,0},{12,4},{1,9},{5,13},{9,1},{13,5},{2,10},{6,14},... | collective-permute-start | bytes 393224 | tf_op jit(solution)/shard_map/ppermute | solution.py:192
  37.2 5.4 %collective-permute-start.3 = (bf16[4,128,128]{2,1,0:T(8,128)(2,1)S(1)}, bf16[4,128,128]{2,1,0:T(8,128)(2,1)S(1)}, u32[]{:S(2)}, u32[]{:S(2)}) collective-permute-start(bf16[4,128,128]{2,1,0:T(8,128)(2,1)S(1)} %get-tuple-element.42), channel_id=1, source_target_pairs={{0,2},{2,0},{1,3},{3,1},{4,6},{6,4},{5,7},{7,5},{8,10},{10,8},{9,1... | collective-permute-start | bytes 393224 | tf_op jit(solution)/shard_map/ppermute | solution.py:192
  37.8 8.3 %collective-permute-start.5 = (bf16[4,128,128]{2,1,0:T(8,128)(2,1)S(1)}, bf16[4,128,128]{2,1,0:T(8,128)(2,1)S(1)}, u32[]{:S(2)}, u32[]{:S(2)}) collective-permute-start(bf16[4,128,128]{2,1,0:T(8,128)(2,1)S(1)} %add_convert_fusion.1), channel_id=1, source_target_pairs={{0,4},{4,8},{8,12},{12,0},{1,5},{5,9},{9,13},{13,1},{2,6},{6,10},{... | collective-permute-start | bytes 393224 | tf_op jit(solution)/shard_map/ppermute | solution.py:192
  40.1 5.4 %collective-permute-start.2 = (bf16[4,128,128]{2,1,0:T(8,128)(2,1)S(1)}, bf16[4,128,128]{2,1,0:T(8,128)(2,1)S(1)}, u32[]{:S(2)}, u32[]{:S(2)}) collective-permute-start(bf16[4,128,128]{2,1,0:T(8,128)(2,1)S(1)} %get-tuple-element.39), channel_id=1, source_target_pairs={{0,2},{2,0},{1,3},{3,1},{4,6},{6,4},{5,7},{7,5},{8,10},{10,8},{9,1... | collective-permute-start | bytes 393224 | tf_op jit(solution)/shard_map/ppermute | solution.py:192
  42.6 5.3 %collective-permute-start.6 = (bf16[4,128,128]{2,1,0:T(8,128)(2,1)S(1)}, bf16[4,128,128]{2,1,0:T(8,128)(2,1)S(1)}, u32[]{:S(2)}, u32[]{:S(2)}) collective-permute-start(bf16[4,128,128]{2,1,0:T(8,128)(2,1)S(1)} %add_convert_fusion), channel_id=1, source_target_pairs={{0,12},{4,0},{8,4},{12,8},{1,13},{5,1},{9,5},{13,9},{2,14},{6,2},{... | collective-permute-start | bytes 393224 | tf_op jit(solution)/shard_map/ppermute | solution.py:192

commit v17 on v15

--- a/solution.py
+++ b/solution.py
@@ -199,30 +199,24 @@
     mixed, held = mix(wavefunction, left_ops, right_ops, split)
 
     if split:
-        pair = jnp.concatenate([live, swap(live, "sector", 1)], axis=0)
-        coef = jnp.concatenate([pair, swap(pair, "sector", 2)], axis=0)
-        order = ((3, 2), (1, 0))
-        *sums, mine_3, theirs_3, mine_2, theirs_2 = summed(
-            sector_shift, coef, mixed, held, order, 0
+        coef = jnp.concatenate([live] + [swap(live, "sector", g) for g in (1, 2, 3)], axis=0)
+        order = ((2,), (3, 1, 0))
+        *sums, mine_2, theirs_2 = summed(sector_shift, coef, mixed, held, order, 0)
+        crossed_2 = swap(theirs_2, "op", 1)
+        _, _, mine_3, theirs_3, mine_1, theirs_1, mine_0, theirs_0 = summed(
+            sector_shift, after(coef, theirs_2), mixed, held, order, 1, sums
         )
-        crossed_3 = swap(theirs_3, "op", 1)
-        crossed_2 = swap(theirs_2, "op", 1)
-        _, _, mine_1, theirs_1, mine_0, theirs_0 = summed(
-            sector_shift, after(coef, theirs_3), mixed, held, order, 1, sums
-        )
-        both_3 = mine_3 + after(crossed_3, mine_1).astype(jnp.float32)
-        both_3 = both_3.astype(jnp.bfloat16)
-        relayed = swap(both_3, "sector", 1)
-        crossed_1 = swap(after(theirs_1, both_3), "op", 1)
-        both_2 = lax.optimization_barrier(mine_2 + after(crossed_2, both_3).astype(jnp.float32))
-        crossed_0 = swap(after(theirs_0, both_2), "op", 1)
-        both_2 = (both_2 + relayed.astype(jnp.float32)).astype(jnp.bfloat16)
-        far = swap(both_2, "sector", 2)
-        both_1 = mine_1 + after(crossed_1, both_2).astype(jnp.float32)
-        both_1 = both_1.astype(jnp.bfloat16)
-        near = swap(both_1, "sector", 1)
+        both_2 = (mine_2 + after(crossed_2, mine_3).astype(jnp.float32)).astype(jnp.bfloat16)
+        arrived_2 = swap(both_2, "sector", 2)
+        crossed_3 = swap(after(theirs_3, both_2), "op", 1)
+        crossed_1 = swap(after(theirs_1, both_2), "op", 1)
+        both_3 = (mine_3 + after(crossed_3, both_2).astype(jnp.float32)).astype(jnp.bfloat16)
+        arrived_3 = swap(both_3, "sector", 3)
+        crossed_0 = swap(after(theirs_0, both_3), "op", 1)
+        both_1 = (mine_1 + after(crossed_1, both_3).astype(jnp.float32)).astype(jnp.bfloat16)
+        arrived_1 = swap(both_1, "sector", 1)
         sigma = mine_0 + after(crossed_0, both_1).astype(jnp.float32)
-        for other in (near, far):
+        for other in (arrived_2, arrived_3, arrived_1):
             sigma = lax.optimization_barrier(sigma) + other.astype(jnp.float32)
         return sigma
 

time: 37 us -> 35.8 us (0.968)
  waiting for transfers between devices: 9.91 us -> 6.58 us
  starting transfers between devices: 14 us -> 16.6 us
  Pallas kernels: 11.2 us -> 10.6 us
    ppermute x9 -> x10, waiting for transfers between devices: 9.91 us -> 6.58 us  [swap(): lax.ppermute(value, axis, [(i, i ^ mask) for i in range(lax.axis_size(axi...]
    ppermute x9 -> x10, starting transfers between devices: 14 us -> 16.6 us  [swap(): lax.ppermute(value, axis, [(i, i ^ mask) for i in range(lax.axis_size(axi...]
    pallas_call x2, Pallas kernels: 7.24 us -> 6.61 us  [summed(): pl.pallas_call(functools.partial(sum_kernel, order, stage), out_shape=out...]
    add x2 -> x3, other arithmetic: 0.77 us -> 0.78 us  [per_device(): sigma = lax.optimization_barrier(sigma) + other.astype(jnp.float32)]
  transfers between devices with their start and end apart: 9 -> 10, of which waited for: 5 -> 3; matrix products, arithmetic and copies ran while one was open for 1% -> 0% of each run, Pallas kernels for 18% -> 22%
where the time goes in v17:
time: 35.8 us; the launch traced here: 35.5 us
  starting transfers between devices  16.6 us (46%)
  Pallas kernels  10.6 us (30%)
  waiting for transfers between devices  6.58 us (18%)
  other arithmetic  1.64 us (5%)
    ppermute x10, starting transfers between devices, swap(): lax.ppermute(value, axis, [(i, i ^ mask) for i in range(lax.axis_size(axi...  16.6 us
    pallas_call x2, Pallas kernels, summed(): pl.pallas_call(functools.partial(sum_kernel, order, stage), out_shape=out...  6.61 us
    ppermute x10, waiting for transfers between devices, swap(): lax.ppermute(value, axis, [(i, i ^ mask) for i in range(lax.axis_size(axi...  6.58 us
    pallas_call x1, Pallas kernels, mix(): pl.pallas_call(functools.partial(mix_kernel, split), out_shape=[pltpu.VME...  3.95 us
    add x3, other arithmetic, per_device(): sigma = lax.optimization_barrier(sigma) + other.astype(jnp.float32)  0.78 us
  transfers between devices with their start and end apart: 10, of which 3 were waited for; matrix products, arithmetic and copies ran while one was open for 0% of the time, Pallas kernels for 22%

profile of v17, /device:TPU:0, one launch (start us, length us, event | category | flops | bytes accessed | tf_op | source)
XLA Modules:
  0.0 35.5 jit_solution(14114157443604430209)
XLA Ops:
  0.0 0.7 %select_bitcast_fusion = f32[4,32]{1,0:T(4,128)S(1)} fusion(f32[32,4]{0,1:T(4,128)} %param.9, s32[32,4]{0,1:T(4,128)} %param.10), kind=kLoop, calls=%fused_computation.8 | loop fusion | flops 256 | bytes 1536 | tf_op jit(solution)/shard_map/jit(_where)/select_n | solution.py:197
  0.7 5.0 %collective-permute-start.2 = (f32[4,32]{1,0:T(4,128)S(1)}, f32[4,32]{1,0:T(4,128)S(1)}, u32[]{:S(2)}, u32[]{:S(2)}) collective-permute-start(f32[4,32]{1,0:T(4,128)S(1)} %select_bitcast_fusion), channel_id=1, source_target_pairs={{0,12},{4,8},{8,4},{12,0},{1,13},{5,9},{9,5},{13,1},{2,14},{6,10},... | collective-permute-start | bytes 1544 | tf_op jit(solution)/shard_map/ppermute | solution.py:187
  5.8 0.0 collective-permute-start.1
  5.8 0.6 %collective-permute-start = (f32[4,32]{1,0:T(4,128)S(1)}, f32[4,32]{1,0:T(4,128)S(1)}, u32[]{:S(2)}, u32[]{:S(2)}) collective-permute-start(f32[4,32]{1,0:T(4,128)S(1)} %select_bitcast_fusion), channel_id=1, source_target_pairs={{0,4},{4,0},{8,12},{12,8},{1,5},{5,1},{9,13},{13,9},{2,6},{6,2},{1... | collective-permute-start | bytes 1544 | tf_op jit(solution)/shard_map/ppermute | solution.py:187
  6.3 4.0 %shard_map.64 = (bf16[32,4,128,256]{3,2,1,0:T(8,128)(2,1)S(1)}, bf16[32,256,256]{2,1,0:T(8,128)(2,1)S(1)}) custom-call(bf16[4,256,256]{2,1,0:T(8,128)(2,1)} %wave_ref.1, bf16[32,128,256]{2,1,0:T(8,128)(2,1)} %left_ref.1, bf16[32,256,256]{2,1,0:T(8,128)(2,1)} %right_ref.1), custom_call_target="tpu_custom_call" | custom-call | flops 2147483648 | bytes 6291456 | tf_op jit(solution)/shard_map/pallas_call | solution.py:69
  10.3 0.0 collective-permute-done.2
  10.3 0.0 collective-permute-done.1
  10.3 0.0 collective-permute-done
  10.3 2.8 %shard_map.65 = (f32[16,128,128]{2,1,0:T(8,128)S(1)}, f32[16,128,128]{2,1,0:T(8,128)S(1)}, f32[4,128,128]{2,1,0:T(8,128)S(1)}, bf16[4,128,128]{2,1,0:T(8,128)(2,1)S(1)}) custom-call(s32[32]{0:T(128)} %shift_ref.3, f32[16,32]{1,0:T(8,128)S(1)} %pad_maximum_fusion.coef_ref, bf16[32,4,128,256]{3,2,1,0:T(8,128)(2,1)S(1)} %get-tuple-element.25.mixed_ref, ...), custom_call_target="tpu_custom_call" | custom-call | flops 1073741824 | bytes 6291456 | tf_op jit(solution)/shard_map/pallas_call | solution.py:165
  13.1 2.3 %collective-permute-start.3 = (bf16[4,128,128]{2,1,0:T(8,128)(2,1)S(1)}, bf16[4,128,128]{2,1,0:T(8,128)(2,1)S(1)}, u32[]{:S(2)}, u32[]{:S(2)}) collective-permute-start(bf16[4,128,128]{2,1,0:T(8,128)(2,1)S(1)} %get-tuple-element.27), channel_id=1, source_target_pairs={{0,2},{2,0},{1,3},{3,1},{4,6},{6,4},{5,7},{7,5},{8,10},{10,8},{9,1... | collective-permute-start | bytes 393224 | tf_op jit(solution)/shard_map/ppermute | solution.py:187
  15.5 3.8 %shard_map.66 = (f32[16,128,128]{2,1,0:T(8,128)S(1)}, f32[16,128,128]{2,1,0:T(8,128)S(1)}, f32[4,128,128]{2,1,0:T(8,128)S(1)}, bf16[4,128,128]{2,1,0:T(8,128)(2,...) custom-call(s32[32]{0:T(128)} %shift_ref.3, ...), custom_call_target="tpu_custom_call", output_to_operand_aliasing={{0}: (4, {}), {1}: (5, {})} | custom-call | flops 1073741824 | bytes 6291456 | tf_op jit(solution)/shard_map/pallas_call | solution.py:165
  19.3 0.0 collective-permute-done.3
  19.3 1.2 %collective-permute-start.4 = (bf16[4,128,128]{2,1,0:T(8,128)(2,1)S(1)}, bf16[4,128,128]{2,1,0:T(8,128)(2,1)S(1)}, u32[]{:S(2)}, u32[]{:S(2)}) collective-permute-start(bf16[4,128,128]{2,1,0:T(8,128)(2,1)S(1)} %get-tuple-element.37), channel_id=1, source_target_pairs={{0,2},{2,0},{1,3},{3,1},{4,6},{6,4},{5,7},{7,5},{8,10},{10,8},{9,1... | collective-permute-start | bytes 393224 | tf_op jit(solution)/shard_map/ppermute | solution.py:187
  20.5 2.1 %collective-permute-start.7 = (bf16[4,128,128]{2,1,0:T(8,128)(2,1)S(1)}, bf16[4,128,128]{2,1,0:T(8,128)(2,1)S(1)}, u32[]{:S(2)}, u32[]{:S(2)}) collective-permute-start(bf16[4,128,128]{2,1,0:T(8,128)(2,1)S(1)} %add_convert_fusion.2), channel_id=1, source_target_pairs={{0,8},{4,12},{8,0},{12,4},{1,9},{5,13},{9,1},{13,5},{2,10},{6,14},... | collective-permute-start | bytes 393224 | tf_op jit(solution)/shard_map/ppermute | solution.py:187
  22.7 0.9 %collective-permute-start.6 = (bf16[4,128,128]{2,1,0:T(8,128)(2,1)S(1)}, bf16[4,128,128]{2,1,0:T(8,128)(2,1)S(1)}, u32[]{:S(2)}, u32[]{:S(2)}) collective-permute-start(bf16[4,128,128]{2,1,0:T(8,128)(2,1)S(1)} %get-tuple-element.42), channel_id=1, source_target_pairs={{0,2},{2,0},{1,3},{3,1},{4,6},{6,4},{5,7},{7,5},{8,10},{10,8},{9,1... | collective-permute-start | bytes 393224 | tf_op jit(solution)/shard_map/ppermute | solution.py:187
  23.6 2.2 %collective-permute-done.4 = bf16[4,128,128]{2,1,0:T(8,128)(2,1)S(1)} collective-permute-done((bf16[4,128,128]{2,1,0:T(8,128)(2,1)S(1)}, bf16[4,128,128]{2,1,0:T(8,128)(2,1)S(1)}, u32[]{:S(2)}, u32[]{:S(2)}) %collective-permute-start.4) | collective-permute-done | bytes 131104 | tf_op jit(solution)/shard_map/ppermute | solution.py:187
  25.8 3.0 %collective-permute-start.8 = (bf16[4,128,128]{2,1,0:T(8,128)(2,1)S(1)}, bf16[4,128,128]{2,1,0:T(8,128)(2,1)S(1)}, u32[]{:S(2)}, u32[]{:S(2)}) collective-permute-start(bf16[4,128,128]{2,1,0:T(8,128)(2,1)S(1)} %add_convert_fusion.1), channel_id=1, source_target_pairs={{0,12},{4,8},{8,4},{12,0},{1,13},{5,9},{9,5},{13,1},{2,14},{6,10},... | collective-permute-start | bytes 393224 | tf_op jit(solution)/shard_map/ppermute | solution.py:187
  28.8 0.9 %collective-permute-start.5 = (bf16[4,128,128]{2,1,0:T(8,128)(2,1)S(1)}, bf16[4,128,128]{2,1,0:T(8,128)(2,1)S(1)}, u32[]{:S(2)}, u32[]{:S(2)}) collective-permute-start(bf16[4,128,128]{2,1,0:T(8,128)(2,1)S(1)} %get-tuple-element.39), channel_id=1, source_target_pairs={{0,2},{2,0},{1,3},{3,1},{4,6},{6,4},{5,7},{7,5},{8,10},{10,8},{9,1... | collective-permute-start | bytes 393224 | tf_op jit(solution)/shard_map/ppermute | solution.py:187
  29.7 0.0 collective-permute-done.6
  29.7 0.5 %collective-permute-start.9 = (bf16[4,128,128]{2,1,0:T(8,128)(2,1)S(1)}, bf16[4,128,128]{2,1,0:T(8,128)(2,1)S(1)}, u32[]{:S(2)}, u32[]{:S(2)}) collective-permute-start(bf16[4,128,128]{2,1,0:T(8,128)(2,1)S(1)} %add_convert_fusion), channel_id=1, source_target_pairs={{0,4},{4,0},{8,12},{12,8},{1,5},{5,1},{9,13},{13,9},{2,6},{6,2},{1... | collective-permute-start | bytes 393224 | tf_op jit(solution)/shard_map/ppermute | solution.py:187
  30.3 3.5 %collective-permute-done.5 = bf16[4,128,128]{2,1,0:T(8,128)(2,1)S(1)} collective-permute-done((bf16[4,128,128]{2,1,0:T(8,128)(2,1)S(1)}, bf16[4,128,128]{2,1,0:T(8,128)(2,1)S(1)}, u32[]{:S(2)}, u32[]{:S(2)}) %collective-permute-start.5) | collective-permute-done | bytes 131104 | tf_op jit(solution)/shard_map/ppermute | solution.py:187
  33.8 0.0 collective-permute-done.7
  33.8 0.0 collective-permute-done.8
  33.9 0.9 %collective-permute-done.9 = bf16[4,128,128]{2,1,0:T(8,128)(2,1)S(1)} collective-permute-done((bf16[4,128,128]{2,1,0:T(8,128)(2,1)S(1)}, bf16[4,128,128]{2,1,0:T(8,128)(2,1)S(1)}, u32[]{:S(2)}, u32[]{:S(2)}) %collective-permute-start.9) | collective-permute-done | bytes 131104 | tf_op jit(solution)/shard_map/ppermute | solution.py:187
  34.8 0.7 %convert_add_fusion = f32[4,128,128]{2,1,0:T(8,128)} fusion(f32[4,128,128]{2,1,0:T(8,128)S(1)} %convert_add_fusion.1, bf16[4,128,128]{2,1,0:T(8,128)(2,1)S(1)} %collective-permute-done.9), kind=kLoop, calls=%fused_computation | loop fusion | flops 131072 | bytes 655360 | tf_op jit(solution)/shard_map/add | solution.py:220
  (7 shorter events, 0.2 us)
Async XLA Ops:
  0.7 9.6 %collective-permute-start.2 = (f32[4,32]{1,0:T(4,128)S(1)}, f32[4,32]{1,0:T(4,128)S(1)}, u32[]{:S(2)}, u32[]{:S(2)}) collective-permute-start(f32[4,32]{1,0:T(4,128)S(1)} %select_bitcast_fusion), channel_id=1, source_target_pairs={{0,12},{4,8},{8,4},{12,0},{1,13},{5,9},{9,5},{13,1},{2,14},{6,10},... | collective-permute-start | bytes 1544 | tf_op jit(solution)/shard_map/ppermute | solution.py:187
  5.8 4.5 %collective-permute-start.1 = (f32[4,32]{1,0:T(4,128)S(1)}, f32[4,32]{1,0:T(4,128)S(1)}, u32[]{:S(2)}, u32[]{:S(2)}) collective-permute-start(f32[4,32]{1,0:T(4,128)S(1)} %select_bitcast_fusion), channel_id=1, source_target_pairs={{0,8},{4,12},{8,0},{12,4},{1,9},{5,13},{9,1},{13,5},{2,10},{6,14},... | collective-permute-start | bytes 1544 | tf_op jit(solution)/shard_map/ppermute | solution.py:187
  5.8 4.5 %collective-permute-start = (f32[4,32]{1,0:T(4,128)S(1)}, f32[4,32]{1,0:T(4,128)S(1)}, u32[]{:S(2)}, u32[]{:S(2)}) collective-permute-start(f32[4,32]{1,0:T(4,128)S(1)} %select_bitcast_fusion), channel_id=1, source_target_pairs={{0,4},{4,0},{8,12},{12,8},{1,5},{5,1},{9,13},{13,9},{2,6},{6,2},{1... | collective-permute-start | bytes 1544 | tf_op jit(solution)/shard_map/ppermute | solution.py:187
  13.1 6.2 %collective-permute-start.3 = (bf16[4,128,128]{2,1,0:T(8,128)(2,1)S(1)}, bf16[4,128,128]{2,1,0:T(8,128)(2,1)S(1)}, u32[]{:S(2)}, u32[]{:S(2)}) collective-permute-start(bf16[4,128,128]{2,1,0:T(8,128)(2,1)S(1)} %get-tuple-element.27), channel_id=1, source_target_pairs={{0,2},{2,0},{1,3},{3,1},{4,6},{6,4},{5,7},{7,5},{8,10},{10,8},{9,1... | collective-permute-start | bytes 393224 | tf_op jit(solution)/shard_map/ppermute | solution.py:187
  19.3 6.4 %collective-permute-start.4 = (bf16[4,128,128]{2,1,0:T(8,128)(2,1)S(1)}, bf16[4,128,128]{2,1,0:T(8,128)(2,1)S(1)}, u32[]{:S(2)}, u32[]{:S(2)}) collective-permute-start(bf16[4,128,128]{2,1,0:T(8,128)(2,1)S(1)} %get-tuple-element.37), channel_id=1, source_target_pairs={{0,2},{2,0},{1,3},{3,1},{4,6},{6,4},{5,7},{7,5},{8,10},{10,8},{9,1... | collective-permute-start | bytes 393224 | tf_op jit(solution)/shard_map/ppermute | solution.py:187
  20.5 13.2 %collective-permute-start.7 = (bf16[4,128,128]{2,1,0:T(8,128)(2,1)S(1)}, bf16[4,128,128]{2,1,0:T(8,128)(2,1)S(1)}, u32[]{:S(2)}, u32[]{:S(2)}) collective-permute-start(bf16[4,128,128]{2,1,0:T(8,128)(2,1)S(1)} %add_convert_fusion.2), channel_id=1, source_target_pairs={{0,8},{4,12},{8,0},{12,4},{1,9},{5,13},{9,1},{13,5},{2,10},{6,14},... | collective-permute-start | bytes 393224 | tf_op jit(solution)/shard_map/ppermute | solution.py:187
  22.7 7.0 %collective-permute-start.6 = (bf16[4,128,128]{2,1,0:T(8,128)(2,1)S(1)}, bf16[4,128,128]{2,1,0:T(8,128)(2,1)S(1)}, u32[]{:S(2)}, u32[]{:S(2)}) collective-permute-start(bf16[4,128,128]{2,1,0:T(8,128)(2,1)S(1)} %get-tuple-element.42), channel_id=1, source_target_pairs={{0,2},{2,0},{1,3},{3,1},{4,6},{6,4},{5,7},{7,5},{8,10},{10,8},{9,1... | collective-permute-start | bytes 393224 | tf_op jit(solution)/shard_map/ppermute | solution.py:187
  25.8 8.0 %collective-permute-start.8 = (bf16[4,128,128]{2,1,0:T(8,128)(2,1)S(1)}, bf16[4,128,128]{2,1,0:T(8,128)(2,1)S(1)}, u32[]{:S(2)}, u32[]{:S(2)}) collective-permute-start(bf16[4,128,128]{2,1,0:T(8,128)(2,1)S(1)} %add_convert_fusion.1), channel_id=1, source_target_pairs={{0,12},{4,8},{8,4},{12,0},{1,13},{5,9},{9,5},{13,1},{2,14},{6,10},... | collective-permute-start | bytes 393224 | tf_op jit(solution)/shard_map/ppermute | solution.py:187
  28.8 5.0 %collective-permute-start.5 = (bf16[4,128,128]{2,1,0:T(8,128)(2,1)S(1)}, bf16[4,128,128]{2,1,0:T(8,128)(2,1)S(1)}, u32[]{:S(2)}, u32[]{:S(2)}) collective-permute-start(bf16[4,128,128]{2,1,0:T(8,128)(2,1)S(1)} %get-tuple-element.39), channel_id=1, source_target_pairs={{0,2},{2,0},{1,3},{3,1},{4,6},{6,4},{5,7},{7,5},{8,10},{10,8},{9,1... | collective-permute-start | bytes 393224 | tf_op jit(solution)/shard_map/ppermute | solution.py:187
  29.7 5.0 %collective-permute-start.9 = (bf16[4,128,128]{2,1,0:T(8,128)(2,1)S(1)}, bf16[4,128,128]{2,1,0:T(8,128)(2,1)S(1)}, u32[]{:S(2)}, u32[]{:S(2)}) collective-permute-start(bf16[4,128,128]{2,1,0:T(8,128)(2,1)S(1)} %add_convert_fusion), channel_id=1, source_target_pairs={{0,4},{4,0},{8,12},{12,8},{1,5},{5,1},{9,13},{13,9},{2,6},{6,2},{1... | collective-permute-start | bytes 393224 | tf_op jit(solution)/shard_map/ppermute | solution.py:187

commit v18 on v16

--- a/solution.py
+++ b/solution.py
@@ -204,7 +204,7 @@
     mixed, held = mix(wavefunction, left_ops, right_ops, split)
 
     if split:
-        coef = lax.all_to_all(jnp.tile(live, (devices, 1)), "sector", 0, 0, tiled=True)
+        coef = lax.all_gather(live, "sector", axis=0, tiled=True)
         order = ((2,), (1, 3, 0))
         *sums, mine_2, theirs_2 = summed(sector_shift, coef, mixed, held, order, 0)
         crossed_2 = shift_by(theirs_2, "op", 1)

time: 48.8 us -> 42.3 us (0.87)
  blocking collectives: 0 us -> 13.5 us
  local copies, waits for them, and re-layouts: 12 us -> 0 us
  starting transfers between devices: 19 us -> 10.8 us
  waiting for transfers between devices: 4.1 us -> 5.21 us
  other arithmetic: 2.28 us -> 1.63 us
    all_gather x0 -> x1, blocking collectives: none -> 13.5 us  [per_device(): coef = lax.all_gather(live, 'sector', axis=0, tiled=True)]
    unnamed x10 -> x0, local copies, waits for them, and re-layouts: 11.5 us -> none
    all_to_all x1 -> x0, starting transfers between devices: 6.32 us -> none  [per_device(): lax.all_to_all(jnp.tile(live, (devices, 1)), 'sector', 0, 0, tiled=True)]
    ppermute x7, starting transfers between devices: 12.6 us -> 10.8 us  [shift_by(): lax.ppermute(value, axis, [(i, (i + distance) % size) for i in range(size)])]
    ppermute x7, waiting for transfers between devices: 4.09 us -> 5.21 us  [shift_by(): lax.ppermute(value, axis, [(i, (i + distance) % size) for i in range(size)])]
    select_n x1 -> x0, other arithmetic: 0.7 us -> none  [per_device(): live = jnp.where(coupled.T > 0, site_coef.T, 0.0)]
    unnamed x0 -> x1, other arithmetic: none -> 0.7 us
    all_to_all x1 -> x0, other arithmetic: 0.66 us -> none  [per_device(): lax.all_to_all(jnp.tile(live, (devices, 1)), 'sector', 0, 0, tiled=True)]
  transfers between devices with their start and end apart: 8 -> 7, of which waited for: 4 -> 3; matrix products, arithmetic and copies ran while one was open for 0% -> 0% of each run, Pallas kernels for 15% -> 10%
where the time goes in v18:
time: 42.3 us
  blocking collectives  13.5 us (32%)
  Pallas kernels  11 us (26%)
  starting transfers between devices  10.8 us (26%)
  waiting for transfers between devices  5.21 us (12%)
  other arithmetic  1.63 us (4%)
    all_gather x1, blocking collectives, per_device(): coef = lax.all_gather(live, 'sector', axis=0, tiled=True)  13.5 us
    ppermute x7, starting transfers between devices, shift_by(): lax.ppermute(value, axis, [(i, (i + distance) % size) for i in range(size)])  10.8 us
    pallas_call x2, Pallas kernels, summed(): pl.pallas_call(functools.partial(sum_kernel, order, stage), out_shape=out...  7.09 us
    ppermute x7, waiting for transfers between devices, shift_by(): lax.ppermute(value, axis, [(i, (i + distance) % size) for i in range(size)])  5.21 us
    pallas_call x1, Pallas kernels, mix(): pl.pallas_call(functools.partial(mix_kernel, split), out_shape=[pltpu.VME...  3.95 us
  transfers between devices with their start and end apart: 7, of which 3 were waited for; matrix products, arithmetic and copies ran while one was open for 0% of the time, Pallas kernels for 10%

profile of v18, /device:TPU:0, one launch (start us, length us, event | category | flops | bytes accessed | tf_op | source)
XLA Modules:
  0.0 42.3 jit_solution(1786143288713393708)
XLA Ops:
  0.0 0.7 %select_bitcast_fusion = f32[1,4,32]{2,1,0:T(4,128)S(1)} fusion(f32[32,4]{0,1:T(4,128)} %param.9, s32[32,4]{0,1:T(4,128)} %param.10), kind=kLoop, calls=%fused_computation.7 | loop fusion | flops 256 | bytes 1536
  0.7 13.5 %all-gather = f32[4,4,32]{2,1,0:T(4,128)S(1)} all-gather(f32[1,4,32]{2,1,0:T(4,128)S(1)} %select_bitcast_fusion), channel_id=1, replica_groups=mesh['groups'=2,'sector'=4,'op'=2,'rep'=2] {'sector'}, dimensions={0}, use_global_device_ids=true | all-gather | bytes 2560 | tf_op jit(solution)/shard_map/all_gather | solution.py:207
  14.2 4.0 %shard_map.64 = (bf16[32,4,128,256]{3,2,1,0:T(8,128)(2,1)S(1)}, bf16[32,256,256]{2,1,0:T(8,128)(2,1)S(1)}) custom-call(bf16[4,256,256]{2,1,0:T(8,128)(2,1)} %wave_ref.1, bf16[32,128,256]{2,1,0:T(8,128)(2,1)} %left_ref.1, bf16[32,256,256]{2,1,0:T(8,128)(2,1)} %right_ref.1), custom_call_target="tpu_custom_call" | custom-call | flops 2147483648 | bytes 6291456 | tf_op jit(solution)/shard_map/pallas_call | solution.py:69
  18.2 2.8 %shard_map.65 = (f32[16,128,128]{2,1,0:T(8,128)S(1)}, f32[16,128,128]{2,1,0:T(8,128)S(1)}, f32[4,128,128]{2,1,0:T(8,128)S(1)}, bf16[4,128,128]{2,1,0:T(8,128)(2,1)S(1)}) custom-call(s32[32]{0:T(128)} %shift_ref.3, f32[16,32]{1,0:T(8,128)S(1)} %bitcast.5, bf16[32,4,128,256]{3,2,1,0:T(8,128)(2,1)S(1)} %get-tuple-element.25.mixed_ref, ...), custom_call_target="tpu_custom_call" | custom-call | flops 1073741824 | bytes 6291456 | tf_op jit(solution)/shard_map/pallas_call | solution.py:169
  21.0 2.1 %collective-permute-start = (bf16[4,128,128]{2,1,0:T(8,128)(2,1)S(1)}, bf16[4,128,128]{2,1,0:T(8,128)(2,1)S(1)}, u32[]{:S(2)}, u32[]{:S(2)}) collective-permute-start(bf16[4,128,128]{2,1,0:T(8,128)(2,1)S(1)} %get-tuple-element.27), channel_id=1, source_target_pairs={{0,2},{2,0},{1,3},{3,1},{4,6},{6,4},{5,7},{7,5},{8,10},{10,8},{9,1... | collective-permute-start | bytes 393224 | tf_op jit(solution)/shard_map/ppermute | solution.py:192
  23.1 4.3 %shard_map.66 = (f32[16,128,128]{2,1,0:T(8,128)S(1)}, f32[16,128,128]{2,1,0:T(8,128)S(1)}, f32[4,128,128]{2,1,0:T(8,128)S(1)}, bf16[4,128,128]{2,1,0:T(8,128)(2,...) custom-call(s32[32]{0:T(128)} %shift_ref.3, ...), custom_call_target="tpu_custom_call", output_to_operand_aliasing={{0}: (4, {}), {1}: (5, {})} | custom-call | flops 1073741824 | bytes 6291456 | tf_op jit(solution)/shard_map/pallas_call | solution.py:169
  27.4 0.0 collective-permute-done
  27.5 1.4 %collective-permute-start.1 = (bf16[4,128,128]{2,1,0:T(8,128)(2,1)S(1)}, bf16[4,128,128]{2,1,0:T(8,128)(2,1)S(1)}, u32[]{:S(2)}, u32[]{:S(2)}) collective-permute-start(bf16[4,128,128]{2,1,0:T(8,128)(2,1)S(1)} %get-tuple-element.37), channel_id=1, source_target_pairs={{0,2},{2,0},{1,3},{3,1},{4,6},{6,4},{5,7},{7,5},{8,10},{10,8},{9,1... | collective-permute-start | bytes 393224 | tf_op jit(solution)/shard_map/ppermute | solution.py:192
  28.9 1.3 %collective-permute-start.4 = (bf16[4,128,128]{2,1,0:T(8,128)(2,1)S(1)}, bf16[4,128,128]{2,1,0:T(8,128)(2,1)S(1)}, u32[]{:S(2)}, u32[]{:S(2)}) collective-permute-start(bf16[4,128,128]{2,1,0:T(8,128)(2,1)S(1)} %add_convert_fusion.2), channel_id=1, source_target_pairs={{0,8},{4,12},{8,0},{12,4},{1,9},{5,13},{9,1},{13,5},{2,10},{6,14},... | collective-permute-start | bytes 393224 | tf_op jit(solution)/shard_map/ppermute | solution.py:192
  30.1 0.3 collective-permute-start.3
  30.5 2.2 %collective-permute-done.1 = bf16[4,128,128]{2,1,0:T(8,128)(2,1)S(1)} collective-permute-done((bf16[4,128,128]{2,1,0:T(8,128)(2,1)S(1)}, bf16[4,128,128]{2,1,0:T(8,128)(2,1)S(1)}, u32[]{:S(2)}, u32[]{:S(2)}) %collective-permute-start.1) | collective-permute-done | bytes 131104 | tf_op jit(solution)/shard_map/ppermute | solution.py:192
  32.7 2.8 %collective-permute-start.5 = (bf16[4,128,128]{2,1,0:T(8,128)(2,1)S(1)}, bf16[4,128,128]{2,1,0:T(8,128)(2,1)S(1)}, u32[]{:S(2)}, u32[]{:S(2)}) collective-permute-start(bf16[4,128,128]{2,1,0:T(8,128)(2,1)S(1)} %add_convert_fusion.1), channel_id=1, source_target_pairs={{0,4},{4,8},{8,12},{12,0},{1,5},{5,9},{9,13},{13,1},{2,6},{6,10},{... | collective-permute-start | bytes 393224 | tf_op jit(solution)/shard_map/ppermute | solution.py:192
  35.5 1.0 %collective-permute-start.2 = (bf16[4,128,128]{2,1,0:T(8,128)(2,1)S(1)}, bf16[4,128,128]{2,1,0:T(8,128)(2,1)S(1)}, u32[]{:S(2)}, u32[]{:S(2)}) collective-permute-start(bf16[4,128,128]{2,1,0:T(8,128)(2,1)S(1)} %get-tuple-element.39), channel_id=1, source_target_pairs={{0,2},{2,0},{1,3},{3,1},{4,6},{6,4},{5,7},{7,5},{8,10},{10,8},{9,1... | collective-permute-start | bytes 393224 | tf_op jit(solution)/shard_map/ppermute | solution.py:192
  36.5 0.0 collective-permute-done.3
  36.5 1.9 %collective-permute-start.6 = (bf16[4,128,128]{2,1,0:T(8,128)(2,1)S(1)}, bf16[4,128,128]{2,1,0:T(8,128)(2,1)S(1)}, u32[]{:S(2)}, u32[]{:S(2)}) collective-permute-start(bf16[4,128,128]{2,1,0:T(8,128)(2,1)S(1)} %add_convert_fusion), channel_id=1, source_target_pairs={{0,12},{4,0},{8,4},{12,8},{1,13},{5,1},{9,5},{13,9},{2,14},{6,2},{... | collective-permute-start | bytes 393224 | tf_op jit(solution)/shard_map/ppermute | solution.py:192
  38.5 2.0 %collective-permute-done.2 = bf16[4,128,128]{2,1,0:T(8,128)(2,1)S(1)} collective-permute-done((bf16[4,128,128]{2,1,0:T(8,128)(2,1)S(1)}, bf16[4,128,128]{2,1,0:T(8,128)(2,1)S(1)}, u32[]{:S(2)}, u32[]{:S(2)}) %collective-permute-start.2) | collective-permute-done | bytes 131104 | tf_op jit(solution)/shard_map/ppermute | solution.py:192
  40.5 0.0 collective-permute-done.4
  40.6 0.0 collective-permute-done.5
  40.6 0.9 %collective-permute-done.6 = bf16[4,128,128]{2,1,0:T(8,128)(2,1)S(1)} collective-permute-done((bf16[4,128,128]{2,1,0:T(8,128)(2,1)S(1)}, bf16[4,128,128]{2,1,0:T(8,128)(2,1)S(1)}, u32[]{:S(2)}, u32[]{:S(2)}) %collective-permute-start.6) | collective-permute-done | bytes 131104 | tf_op jit(solution)/shard_map/ppermute | solution.py:192
  41.6 0.7 %convert_add_fusion = f32[4,128,128]{2,1,0:T(8,128)} fusion(f32[4,128,128]{2,1,0:T(8,128)S(1)} %convert_add_fusion.1, bf16[4,128,128]{2,1,0:T(8,128)(2,1)S(1)} %collective-permute-done.6), kind=kLoop, calls=%fused_computation | loop fusion | flops 131072 | bytes 655360 | tf_op jit(solution)/shard_map/add | solution.py:225
  (6 shorter events, 0.2 us)
Async XLA Ops:
  21.0 6.4 %collective-permute-start = (bf16[4,128,128]{2,1,0:T(8,128)(2,1)S(1)}, bf16[4,128,128]{2,1,0:T(8,128)(2,1)S(1)}, u32[]{:S(2)}, u32[]{:S(2)}) collective-permute-start(bf16[4,128,128]{2,1,0:T(8,128)(2,1)S(1)} %get-tuple-element.27), channel_id=1, source_target_pairs={{0,2},{2,0},{1,3},{3,1},{4,6},{6,4},{5,7},{7,5},{8,10},{10,8},{9,1... | collective-permute-start | bytes 393224 | tf_op jit(solution)/shard_map/ppermute | solution.py:192
  27.5 5.2 %collective-permute-start.1 = (bf16[4,128,128]{2,1,0:T(8,128)(2,1)S(1)}, bf16[4,128,128]{2,1,0:T(8,128)(2,1)S(1)}, u32[]{:S(2)}, u32[]{:S(2)}) collective-permute-start(bf16[4,128,128]{2,1,0:T(8,128)(2,1)S(1)} %get-tuple-element.37), channel_id=1, source_target_pairs={{0,2},{2,0},{1,3},{3,1},{4,6},{6,4},{5,7},{7,5},{8,10},{10,8},{9,1... | collective-permute-start | bytes 393224 | tf_op jit(solution)/shard_map/ppermute | solution.py:192
  28.9 11.7 %collective-permute-start.4 = (bf16[4,128,128]{2,1,0:T(8,128)(2,1)S(1)}, bf16[4,128,128]{2,1,0:T(8,128)(2,1)S(1)}, u32[]{:S(2)}, u32[]{:S(2)}) collective-permute-start(bf16[4,128,128]{2,1,0:T(8,128)(2,1)S(1)} %add_convert_fusion.2), channel_id=1, source_target_pairs={{0,8},{4,12},{8,0},{12,4},{1,9},{5,13},{9,1},{13,5},{2,10},{6,14},... | collective-permute-start | bytes 393224 | tf_op jit(solution)/shard_map/ppermute | solution.py:192
  30.1 6.4 %collective-permute-start.3 = (bf16[4,128,128]{2,1,0:T(8,128)(2,1)S(1)}, bf16[4,128,128]{2,1,0:T(8,128)(2,1)S(1)}, u32[]{:S(2)}, u32[]{:S(2)}) collective-permute-start(bf16[4,128,128]{2,1,0:T(8,128)(2,1)S(1)} %get-tuple-element.42), channel_id=1, source_target_pairs={{0,2},{2,0},{1,3},{3,1},{4,6},{6,4},{5,7},{7,5},{8,10},{10,8},{9,1... | collective-permute-start | bytes 393224 | tf_op jit(solution)/shard_map/ppermute | solution.py:192
  32.7 7.9 %collective-permute-start.5 = (bf16[4,128,128]{2,1,0:T(8,128)(2,1)S(1)}, bf16[4,128,128]{2,1,0:T(8,128)(2,1)S(1)}, u32[]{:S(2)}, u32[]{:S(2)}) collective-permute-start(bf16[4,128,128]{2,1,0:T(8,128)(2,1)S(1)} %add_convert_fusion.1), channel_id=1, source_target_pairs={{0,4},{4,8},{8,12},{12,0},{1,5},{5,9},{9,13},{13,1},{2,6},{6,10},{... | collective-permute-start | bytes 393224 | tf_op jit(solution)/shard_map/ppermute | solution.py:192
  35.5 5.0 %collective-permute-start.2 = (bf16[4,128,128]{2,1,0:T(8,128)(2,1)S(1)}, bf16[4,128,128]{2,1,0:T(8,128)(2,1)S(1)}, u32[]{:S(2)}, u32[]{:S(2)}) collective-permute-start(bf16[4,128,128]{2,1,0:T(8,128)(2,1)S(1)} %get-tuple-element.39), channel_id=1, source_target_pairs={{0,2},{2,0},{1,3},{3,1},{4,6},{6,4},{5,7},{7,5},{8,10},{10,8},{9,1... | collective-permute-start | bytes 393224 | tf_op jit(solution)/shard_map/ppermute | solution.py:192
  36.5 5.0 %collective-permute-start.6 = (bf16[4,128,128]{2,1,0:T(8,128)(2,1)S(1)}, bf16[4,128,128]{2,1,0:T(8,128)(2,1)S(1)}, u32[]{:S(2)}, u32[]{:S(2)}) collective-permute-start(bf16[4,128,128]{2,1,0:T(8,128)(2,1)S(1)} %add_convert_fusion), channel_id=1, source_target_pairs={{0,12},{4,0},{8,4},{12,8},{1,13},{5,1},{9,5},{13,9},{2,14},{6,2},{... | collective-permute-start | bytes 393224 | tf_op jit(solution)/shard_map/ppermute | solution.py:192

commit v19 on v17

--- a/solution.py
+++ b/solution.py
@@ -99,16 +99,21 @@
         start = (first ^ (group * sec_dev)) - first
         return wrapped(sec_dev - 1 - start - shift_ref[k], targets) < 2 * sec_dev - 1
 
-    def pick(k, count):
-        picked[count] = k
-        if stage is None:
-            return count + 1
-        wanted = functools.reduce(jnp.logical_or, [reaches(k, group) for group in order[0]])
-        return count + jnp.where(wanted == (stage == 0), 1, 0)
-
-    count = lax.fori_loop(0, terms, pick, 0)
-    for i in range(SUM_TERMS):
-        picked[count + i] = 0
+    def pick(wanted):
+        def body(k, count):
+            picked[count] = k
+            found = functools.reduce(jnp.logical_or, [reaches(k, group) for group in order[0]])
+            return count + jnp.where(found == wanted, 1, 0)
+
+        return body
+
+    if stage is None:
+        low, high = 0, terms // SUM_TERMS
+    else:
+        count = lax.fori_loop(0, terms, pick(True), 0)
+        lax.fori_loop(0, terms, pick(False), count)
+        steps = lax.div(jnp.maximum(count, terms // 2) + SUM_TERMS - 1, SUM_TERMS)
+        low, high = (0, steps) if stage == 0 else (steps, terms // SUM_TERMS)
 
     if stage is None:
         sums = refs[:1]
@@ -120,11 +125,12 @@
         for total in sums:
             total[...] = jnp.zeros_like(total)
 
-    @pl.loop(0, lax.div(count + SUM_TERMS - 1, SUM_TERMS))
+    @pl.loop(low, high)
     def _(step):
         for t in range(SUM_TERMS):
-            at = step * SUM_TERMS + t
-            k = picked[at]
+            k = step * SUM_TERMS + t
+            if stage is not None:
+                k = picked[k]
             product = lax.dot_general(
                 mixed_ref[k].reshape(sec_dev * rows, width),
                 held_ref[k],
@@ -135,8 +141,7 @@
                 slot = wrapped(first + s - shift_ref[k], targets)
                 if stage is not None:
                     slot ^= first
-                weight = jnp.where(at < count, coef_ref[slot, k], 0.0)
-                scaled = weight * product[s * rows : (s + 1) * rows]
+                scaled = coef_ref[slot, k] * product[s * rows : (s + 1) * rows]
                 if stage is None:
                     sums[0][slot] += scaled
                 else:

time: 35.8 us -> 36.5 us (1.020)
  Pallas kernels: 10.6 us -> 11 us
    pallas_call x2, Pallas kernels: 6.61 us -> 7.02 us  [summed(): pl.pallas_call(functools.partial(sum_kernel, order, stage), out_shape=out...]
  transfers between devices with their start and end apart: 10 -> 10, of which waited for: 3 -> 3; matrix products, arithmetic and copies ran while one was open for 0% -> 0% of each run, Pallas kernels for 22% -> 20%
where the time goes in v19:
time: 36.5 us; the launch traced here: 36.3 us
  starting transfers between devices  16.8 us (46%)
  Pallas kernels  11 us (30%)
  waiting for transfers between devices  6.81 us (19%)
  other arithmetic  1.64 us (4%)
    ppermute x10, starting transfers between devices, swap(): lax.ppermute(value, axis, [(i, i ^ mask) for i in range(lax.axis_size(axi...  16.8 us
    pallas_call x2, Pallas kernels, summed(): pl.pallas_call(functools.partial(sum_kernel, order, stage), out_shape=out...  7.02 us
    ppermute x10, waiting for transfers between devices, swap(): lax.ppermute(value, axis, [(i, i ^ mask) for i in range(lax.axis_size(axi...  6.81 us
    pallas_call x1, Pallas kernels, mix(): pl.pallas_call(functools.partial(mix_kernel, split), out_shape=[pltpu.VME...  3.95 us
    add x3, other arithmetic, per_device(): sigma = lax.optimization_barrier(sigma) + other.astype(jnp.float32)  0.78 us
  transfers between devices with their start and end apart: 10, of which 3 were waited for; matrix products, arithmetic and copies ran while one was open for 0% of the time, Pallas kernels for 20%

profile of v19, /device:TPU:0, one launch (start us, length us, event | category | flops | bytes accessed | tf_op | source)
XLA Modules:
  0.0 36.3 jit_solution(13863045530589474268)
XLA Ops:
  0.0 0.7 %select_bitcast_fusion = f32[4,32]{1,0:T(4,128)S(1)} fusion(f32[32,4]{0,1:T(4,128)} %param.9, s32[32,4]{0,1:T(4,128)} %param.10), kind=kLoop, calls=%fused_computation.8 | loop fusion | flops 256 | bytes 1536 | tf_op jit(solution)/shard_map/jit(_where)/select_n | solution.py:202
  0.7 5.0 %collective-permute-start.2 = (f32[4,32]{1,0:T(4,128)S(1)}, f32[4,32]{1,0:T(4,128)S(1)}, u32[]{:S(2)}, u32[]{:S(2)}) collective-permute-start(f32[4,32]{1,0:T(4,128)S(1)} %select_bitcast_fusion), channel_id=1, source_target_pairs={{0,12},{4,8},{8,4},{12,0},{1,13},{5,9},{9,5},{13,1},{2,14},{6,10},... | collective-permute-start | bytes 1544 | tf_op jit(solution)/shard_map/ppermute | solution.py:192
  5.8 0.0 collective-permute-start.1
  5.8 0.6 %collective-permute-start = (f32[4,32]{1,0:T(4,128)S(1)}, f32[4,32]{1,0:T(4,128)S(1)}, u32[]{:S(2)}, u32[]{:S(2)}) collective-permute-start(f32[4,32]{1,0:T(4,128)S(1)} %select_bitcast_fusion), channel_id=1, source_target_pairs={{0,4},{4,0},{8,12},{12,8},{1,5},{5,1},{9,13},{13,9},{2,6},{6,2},{1... | collective-permute-start | bytes 1544 | tf_op jit(solution)/shard_map/ppermute | solution.py:192
  6.3 4.0 %shard_map.64 = (bf16[32,4,128,256]{3,2,1,0:T(8,128)(2,1)S(1)}, bf16[32,256,256]{2,1,0:T(8,128)(2,1)S(1)}) custom-call(bf16[4,256,256]{2,1,0:T(8,128)(2,1)} %wave_ref.1, bf16[32,128,256]{2,1,0:T(8,128)(2,1)} %left_ref.1, bf16[32,256,256]{2,1,0:T(8,128)(2,1)} %right_ref.1), custom_call_target="tpu_custom_call" | custom-call | flops 2147483648 | bytes 6291456 | tf_op jit(solution)/shard_map/pallas_call | solution.py:69
  10.3 0.0 collective-permute-done.2
  10.3 0.0 collective-permute-done.1
  10.3 0.0 collective-permute-done
  10.3 3.6 %shard_map.65 = (f32[16,128,128]{2,1,0:T(8,128)S(1)}, f32[16,128,128]{2,1,0:T(8,128)S(1)}, f32[4,128,128]{2,1,0:T(8,128)S(1)}, bf16[4,128,128]{2,1,0:T(8,128)(2,1)S(1)}) custom-call(s32[32]{0:T(128)} %shift_ref.3, f32[16,32]{1,0:T(8,128)S(1)} %pad_maximum_fusion.coef_ref, bf16[32,4,128,256]{3,2,1,0:T(8,128)(2,1)S(1)} %get-tuple-element.25.mixed_ref, ...), custom_call_target="tpu_custom_call" | custom-call | flops 1073741824 | bytes 6291456 | tf_op jit(solution)/shard_map/pallas_call | solution.py:170
  13.9 2.3 %collective-permute-start.3 = (bf16[4,128,128]{2,1,0:T(8,128)(2,1)S(1)}, bf16[4,128,128]{2,1,0:T(8,128)(2,1)S(1)}, u32[]{:S(2)}, u32[]{:S(2)}) collective-permute-start(bf16[4,128,128]{2,1,0:T(8,128)(2,1)S(1)} %get-tuple-element.27), channel_id=1, source_target_pairs={{0,2},{2,0},{1,3},{3,1},{4,6},{6,4},{5,7},{7,5},{8,10},{10,8},{9,1... | collective-permute-start | bytes 393224 | tf_op jit(solution)/shard_map/ppermute | solution.py:192
  16.2 3.5 %shard_map.66 = (f32[16,128,128]{2,1,0:T(8,128)S(1)}, f32[16,128,128]{2,1,0:T(8,128)S(1)}, f32[4,128,128]{2,1,0:T(8,128)S(1)}, bf16[4,128,128]{2,1,0:T(8,128)(2,...) custom-call(s32[32]{0:T(128)} %shift_ref.3, ...), custom_call_target="tpu_custom_call", output_to_operand_aliasing={{0}: (4, {}), {1}: (5, {})} | custom-call | flops 1073741824 | bytes 6291456 | tf_op jit(solution)/shard_map/pallas_call | solution.py:170
  19.7 0.0 collective-permute-done.3
  19.7 1.6 %collective-permute-start.4 = (bf16[4,128,128]{2,1,0:T(8,128)(2,1)S(1)}, bf16[4,128,128]{2,1,0:T(8,128)(2,1)S(1)}, u32[]{:S(2)}, u32[]{:S(2)}) collective-permute-start(bf16[4,128,128]{2,1,0:T(8,128)(2,1)S(1)} %get-tuple-element.37), channel_id=1, source_target_pairs={{0,2},{2,0},{1,3},{3,1},{4,6},{6,4},{5,7},{7,5},{8,10},{10,8},{9,1... | collective-permute-start | bytes 393224 | tf_op jit(solution)/shard_map/ppermute | solution.py:192
  21.3 2.1 %collective-permute-start.7 = (bf16[4,128,128]{2,1,0:T(8,128)(2,1)S(1)}, bf16[4,128,128]{2,1,0:T(8,128)(2,1)S(1)}, u32[]{:S(2)}, u32[]{:S(2)}) collective-permute-start(bf16[4,128,128]{2,1,0:T(8,128)(2,1)S(1)} %add_convert_fusion.2), channel_id=1, source_target_pairs={{0,8},{4,12},{8,0},{12,4},{1,9},{5,13},{9,1},{13,5},{2,10},{6,14},... | collective-permute-start | bytes 393224 | tf_op jit(solution)/shard_map/ppermute | solution.py:192
  23.4 0.5 %collective-permute-start.6 = (bf16[4,128,128]{2,1,0:T(8,128)(2,1)S(1)}, bf16[4,128,128]{2,1,0:T(8,128)(2,1)S(1)}, u32[]{:S(2)}, u32[]{:S(2)}) collective-permute-start(bf16[4,128,128]{2,1,0:T(8,128)(2,1)S(1)} %get-tuple-element.42), channel_id=1, source_target_pairs={{0,2},{2,0},{1,3},{3,1},{4,6},{6,4},{5,7},{7,5},{8,10},{10,8},{9,1... | collective-permute-start | bytes 393224 | tf_op jit(solution)/shard_map/ppermute | solution.py:192
  24.0 2.0 %collective-permute-done.4 = bf16[4,128,128]{2,1,0:T(8,128)(2,1)S(1)} collective-permute-done((bf16[4,128,128]{2,1,0:T(8,128)(2,1)S(1)}, bf16[4,128,128]{2,1,0:T(8,128)(2,1)S(1)}, u32[]{:S(2)}, u32[]{:S(2)}) %collective-permute-start.4) | collective-permute-done | bytes 131104 | tf_op jit(solution)/shard_map/ppermute | solution.py:192
  26.0 3.2 %collective-permute-start.8 = (bf16[4,128,128]{2,1,0:T(8,128)(2,1)S(1)}, bf16[4,128,128]{2,1,0:T(8,128)(2,1)S(1)}, u32[]{:S(2)}, u32[]{:S(2)}) collective-permute-start(bf16[4,128,128]{2,1,0:T(8,128)(2,1)S(1)} %add_convert_fusion.1), channel_id=1, source_target_pairs={{0,12},{4,8},{8,4},{12,0},{1,13},{5,9},{9,5},{13,1},{2,14},{6,10},... | collective-permute-start | bytes 393224 | tf_op jit(solution)/shard_map/ppermute | solution.py:192
  29.2 1.4 %collective-permute-start.5 = (bf16[4,128,128]{2,1,0:T(8,128)(2,1)S(1)}, bf16[4,128,128]{2,1,0:T(8,128)(2,1)S(1)}, u32[]{:S(2)}, u32[]{:S(2)}) collective-permute-start(bf16[4,128,128]{2,1,0:T(8,128)(2,1)S(1)} %get-tuple-element.39), channel_id=1, source_target_pairs={{0,2},{2,0},{1,3},{3,1},{4,6},{6,4},{5,7},{7,5},{8,10},{10,8},{9,1... | collective-permute-start | bytes 393224 | tf_op jit(solution)/shard_map/ppermute | solution.py:192
  30.5 0.0 collective-permute-done.6
  30.6 0.1 collective-permute-start.9
  30.6 3.5 %collective-permute-done.5 = bf16[4,128,128]{2,1,0:T(8,128)(2,1)S(1)} collective-permute-done((bf16[4,128,128]{2,1,0:T(8,128)(2,1)S(1)}, bf16[4,128,128]{2,1,0:T(8,128)(2,1)S(1)}, u32[]{:S(2)}, u32[]{:S(2)}) %collective-permute-start.5) | collective-permute-done | bytes 131104 | tf_op jit(solution)/shard_map/ppermute | solution.py:192
  34.2 0.0 collective-permute-done.7
  34.2 0.0 collective-permute-done.8
  34.3 1.3 %collective-permute-done.9 = bf16[4,128,128]{2,1,0:T(8,128)(2,1)S(1)} collective-permute-done((bf16[4,128,128]{2,1,0:T(8,128)(2,1)S(1)}, bf16[4,128,128]{2,1,0:T(8,128)(2,1)S(1)}, u32[]{:S(2)}, u32[]{:S(2)}) %collective-permute-start.9) | collective-permute-done | bytes 131104 | tf_op jit(solution)/shard_map/ppermute | solution.py:192
  35.6 0.7 %convert_add_fusion = f32[4,128,128]{2,1,0:T(8,128)} fusion(f32[4,128,128]{2,1,0:T(8,128)S(1)} %convert_add_fusion.1, bf16[4,128,128]{2,1,0:T(8,128)(2,1)S(1)} %collective-permute-done.9), kind=kLoop, calls=%fused_computation | loop fusion | flops 131072 | bytes 655360 | tf_op jit(solution)/shard_map/add | solution.py:225
  (7 shorter events, 0.2 us)
Async XLA Ops:
  0.7 9.6 %collective-permute-start.2 = (f32[4,32]{1,0:T(4,128)S(1)}, f32[4,32]{1,0:T(4,128)S(1)}, u32[]{:S(2)}, u32[]{:S(2)}) collective-permute-start(f32[4,32]{1,0:T(4,128)S(1)} %select_bitcast_fusion), channel_id=1, source_target_pairs={{0,12},{4,8},{8,4},{12,0},{1,13},{5,9},{9,5},{13,1},{2,14},{6,10},... | collective-permute-start | bytes 1544 | tf_op jit(solution)/shard_map/ppermute | solution.py:192
  5.8 4.5 %collective-permute-start.1 = (f32[4,32]{1,0:T(4,128)S(1)}, f32[4,32]{1,0:T(4,128)S(1)}, u32[]{:S(2)}, u32[]{:S(2)}) collective-permute-start(f32[4,32]{1,0:T(4,128)S(1)} %select_bitcast_fusion), channel_id=1, source_target_pairs={{0,8},{4,12},{8,0},{12,4},{1,9},{5,13},{9,1},{13,5},{2,10},{6,14},... | collective-permute-start | bytes 1544 | tf_op jit(solution)/shard_map/ppermute | solution.py:192
  5.8 4.5 %collective-permute-start = (f32[4,32]{1,0:T(4,128)S(1)}, f32[4,32]{1,0:T(4,128)S(1)}, u32[]{:S(2)}, u32[]{:S(2)}) collective-permute-start(f32[4,32]{1,0:T(4,128)S(1)} %select_bitcast_fusion), channel_id=1, source_target_pairs={{0,4},{4,0},{8,12},{12,8},{1,5},{5,1},{9,13},{13,9},{2,6},{6,2},{1... | collective-permute-start | bytes 1544 | tf_op jit(solution)/shard_map/ppermute | solution.py:192
  13.9 5.8 %collective-permute-start.3 = (bf16[4,128,128]{2,1,0:T(8,128)(2,1)S(1)}, bf16[4,128,128]{2,1,0:T(8,128)(2,1)S(1)}, u32[]{:S(2)}, u32[]{:S(2)}) collective-permute-start(bf16[4,128,128]{2,1,0:T(8,128)(2,1)S(1)} %get-tuple-element.27), channel_id=1, source_target_pairs={{0,2},{2,0},{1,3},{3,1},{4,6},{6,4},{5,7},{7,5},{8,10},{10,8},{9,1... | collective-permute-start | bytes 393224 | tf_op jit(solution)/shard_map/ppermute | solution.py:192
  19.7 6.2 %collective-permute-start.4 = (bf16[4,128,128]{2,1,0:T(8,128)(2,1)S(1)}, bf16[4,128,128]{2,1,0:T(8,128)(2,1)S(1)}, u32[]{:S(2)}, u32[]{:S(2)}) collective-permute-start(bf16[4,128,128]{2,1,0:T(8,128)(2,1)S(1)} %get-tuple-element.37), channel_id=1, source_target_pairs={{0,2},{2,0},{1,3},{3,1},{4,6},{6,4},{5,7},{7,5},{8,10},{10,8},{9,1... | collective-permute-start | bytes 393224 | tf_op jit(solution)/shard_map/ppermute | solution.py:192
  21.3 12.9 %collective-permute-start.7 = (bf16[4,128,128]{2,1,0:T(8,128)(2,1)S(1)}, bf16[4,128,128]{2,1,0:T(8,128)(2,1)S(1)}, u32[]{:S(2)}, u32[]{:S(2)}) collective-permute-start(bf16[4,128,128]{2,1,0:T(8,128)(2,1)S(1)} %add_convert_fusion.2), channel_id=1, source_target_pairs={{0,8},{4,12},{8,0},{12,4},{1,9},{5,13},{9,1},{13,5},{2,10},{6,14},... | collective-permute-start | bytes 393224 | tf_op jit(solution)/shard_map/ppermute | solution.py:192
  23.4 7.1 %collective-permute-start.6 = (bf16[4,128,128]{2,1,0:T(8,128)(2,1)S(1)}, bf16[4,128,128]{2,1,0:T(8,128)(2,1)S(1)}, u32[]{:S(2)}, u32[]{:S(2)}) collective-permute-start(bf16[4,128,128]{2,1,0:T(8,128)(2,1)S(1)} %get-tuple-element.42), channel_id=1, source_target_pairs={{0,2},{2,0},{1,3},{3,1},{4,6},{6,4},{5,7},{7,5},{8,10},{10,8},{9,1... | collective-permute-start | bytes 393224 | tf_op jit(solution)/shard_map/ppermute | solution.py:192
  26.0 8.2 %collective-permute-start.8 = (bf16[4,128,128]{2,1,0:T(8,128)(2,1)S(1)}, bf16[4,128,128]{2,1,0:T(8,128)(2,1)S(1)}, u32[]{:S(2)}, u32[]{:S(2)}) collective-permute-start(bf16[4,128,128]{2,1,0:T(8,128)(2,1)S(1)} %add_convert_fusion.1), channel_id=1, source_target_pairs={{0,12},{4,8},{8,4},{12,0},{1,13},{5,9},{9,5},{13,1},{2,14},{6,10},... | collective-permute-start | bytes 393224 | tf_op jit(solution)/shard_map/ppermute | solution.py:192
  29.2 5.0 %collective-permute-start.5 = (bf16[4,128,128]{2,1,0:T(8,128)(2,1)S(1)}, bf16[4,128,128]{2,1,0:T(8,128)(2,1)S(1)}, u32[]{:S(2)}, u32[]{:S(2)}) collective-permute-start(bf16[4,128,128]{2,1,0:T(8,128)(2,1)S(1)} %get-tuple-element.39), channel_id=1, source_target_pairs={{0,2},{2,0},{1,3},{3,1},{4,6},{6,4},{5,7},{7,5},{8,10},{10,8},{9,1... | collective-permute-start | bytes 393224 | tf_op jit(solution)/shard_map/ppermute | solution.py:192
  30.6 5.0 %collective-permute-start.9 = (bf16[4,128,128]{2,1,0:T(8,128)(2,1)S(1)}, bf16[4,128,128]{2,1,0:T(8,128)(2,1)S(1)}, u32[]{:S(2)}, u32[]{:S(2)}) collective-permute-start(bf16[4,128,128]{2,1,0:T(8,128)(2,1)S(1)} %add_convert_fusion), channel_id=1, source_target_pairs={{0,4},{4,0},{8,12},{12,8},{1,5},{5,1},{9,13},{13,9},{2,6},{6,2},{1... | collective-permute-start | bytes 393224 | tf_op jit(solution)/shard_map/ppermute | solution.py:192

commit v20 on v19

--- a/solution.py
+++ b/solution.py
@@ -205,23 +205,24 @@
 
     if split:
         coef = jnp.concatenate([live] + [swap(live, "sector", g) for g in (1, 2, 3)], axis=0)
-        order = ((2,), (3, 1, 0))
-        *sums, mine_2, theirs_2 = summed(sector_shift, coef, mixed, held, order, 0)
-        crossed_2 = swap(theirs_2, "op", 1)
-        _, _, mine_3, theirs_3, mine_1, theirs_1, mine_0, theirs_0 = summed(
-            sector_shift, after(coef, theirs_2), mixed, held, order, 1, sums
+        order = ((3,), (2, 1, 0))
+        *sums, mine_3, theirs_3 = summed(sector_shift, coef, mixed, held, order, 0)
+        crossed_3 = swap(theirs_3, "op", 1)
+        _, _, mine_2, theirs_2, mine_1, theirs_1, mine_0, theirs_0 = summed(
+            sector_shift, after(coef, theirs_3), mixed, held, order, 1, sums
         )
-        both_2 = (mine_2 + after(crossed_2, mine_3).astype(jnp.float32)).astype(jnp.bfloat16)
-        arrived_2 = swap(both_2, "sector", 2)
-        crossed_3 = swap(after(theirs_3, both_2), "op", 1)
-        crossed_1 = swap(after(theirs_1, both_2), "op", 1)
-        both_3 = (mine_3 + after(crossed_3, both_2).astype(jnp.float32)).astype(jnp.bfloat16)
-        arrived_3 = swap(both_3, "sector", 3)
-        crossed_0 = swap(after(theirs_0, both_3), "op", 1)
-        both_1 = (mine_1 + after(crossed_1, both_3).astype(jnp.float32)).astype(jnp.bfloat16)
-        arrived_1 = swap(both_1, "sector", 1)
-        sigma = mine_0 + after(crossed_0, both_1).astype(jnp.float32)
-        for other in (arrived_2, arrived_3, arrived_1):
+        both_3 = (mine_3 + after(crossed_3, mine_2).astype(jnp.float32)).astype(jnp.bfloat16)
+        relayed = swap(both_3, "sector", 1)
+        crossed_2 = swap(after(theirs_2, both_3), "op", 1)
+        crossed_1 = swap(after(theirs_1, both_3), "op", 1)
+        halfway = lax.optimization_barrier(mine_2 + after(crossed_2, both_3).astype(jnp.float32))
+        both_2 = (halfway + relayed.astype(jnp.float32)).astype(jnp.bfloat16)
+        far = swap(both_2, "sector", 2)
+        both_1 = (mine_1 + after(crossed_1, halfway).astype(jnp.float32)).astype(jnp.bfloat16)
+        near = swap(both_1, "sector", 1)
+        crossed_0 = swap(after(theirs_0, both_2), "op", 1)
+        sigma = mine_0 + after(near, both_1).astype(jnp.float32)
+        for other in (crossed_0, far):
             sigma = lax.optimization_barrier(sigma) + other.astype(jnp.float32)
         return sigma
 

time: 36.5 us -> 36.5 us (level)
  starting transfers between devices: 16.8 us -> 15.2 us
  waiting for transfers between devices: 6.81 us -> 8.41 us
    ppermute x10, starting transfers between devices: 16.8 us -> 15.2 us  [swap(): lax.ppermute(value, axis, [(i, i ^ mask) for i in range(lax.axis_size(axi...]
    ppermute x10, waiting for transfers between devices: 6.81 us -> 8.41 us  [swap(): lax.ppermute(value, axis, [(i, i ^ mask) for i in range(lax.axis_size(axi...]
    add x3 -> x2, other arithmetic: 0.78 us -> 0.75 us  [per_device(): sigma = lax.optimization_barrier(sigma) + other.astype(jnp.float32)]
  transfers between devices with their start and end apart: 10 -> 10, of which waited for: 3 -> 4; matrix products, arithmetic and copies ran while one was open for 0% -> 0% of each run, Pallas kernels for 20% -> 20%
where the time goes in v20:
time: 36.5 us; the launch traced here: 36.3 us
  starting transfers between devices  15.2 us (42%)
  Pallas kernels  11 us (30%)
  waiting for transfers between devices  8.41 us (23%)
  other arithmetic  1.64 us (4%)
    ppermute x10, starting transfers between devices, swap(): lax.ppermute(value, axis, [(i, i ^ mask) for i in range(lax.axis_size(axi...  15.2 us
    ppermute x10, waiting for transfers between devices, swap(): lax.ppermute(value, axis, [(i, i ^ mask) for i in range(lax.axis_size(axi...  8.41 us
    pallas_call x2, Pallas kernels, summed(): pl.pallas_call(functools.partial(sum_kernel, order, stage), out_shape=out...  7.01 us
    pallas_call x1, Pallas kernels, mix(): pl.pallas_call(functools.partial(mix_kernel, split), out_shape=[pltpu.VME...  3.95 us
    add x2, other arithmetic, per_device(): sigma = lax.optimization_barrier(sigma) + other.astype(jnp.float32)  0.75 us
  transfers between devices with their start and end apart: 10, of which 4 were waited for; matrix products, arithmetic and copies ran while one was open for 0% of the time, Pallas kernels for 20%

profile of v20, /device:TPU:0, one launch (start us, length us, event | category | flops | bytes accessed | tf_op | source)
XLA Modules:
  0.0 36.3 jit_solution(11687041007716427798)
XLA Ops:
  0.0 0.7 %select_bitcast_fusion = f32[4,32]{1,0:T(4,128)S(1)} fusion(f32[32,4]{0,1:T(4,128)} %param.9, s32[32,4]{0,1:T(4,128)} %param.10), kind=kLoop, calls=%fused_computation.8 | loop fusion | flops 256 | bytes 1536 | tf_op jit(solution)/shard_map/jit(_where)/select_n | solution.py:202
  0.7 5.0 %collective-permute-start.2 = (f32[4,32]{1,0:T(4,128)S(1)}, f32[4,32]{1,0:T(4,128)S(1)}, u32[]{:S(2)}, u32[]{:S(2)}) collective-permute-start(f32[4,32]{1,0:T(4,128)S(1)} %select_bitcast_fusion), channel_id=1, source_target_pairs={{0,12},{4,8},{8,4},{12,0},{1,13},{5,9},{9,5},{13,1},{2,14},{6,10},... | collective-permute-start | bytes 1544 | tf_op jit(solution)/shard_map/ppermute | solution.py:192
  5.8 0.0 collective-permute-start.1
  5.8 0.6 %collective-permute-start = (f32[4,32]{1,0:T(4,128)S(1)}, f32[4,32]{1,0:T(4,128)S(1)}, u32[]{:S(2)}, u32[]{:S(2)}) collective-permute-start(f32[4,32]{1,0:T(4,128)S(1)} %select_bitcast_fusion), channel_id=1, source_target_pairs={{0,4},{4,0},{8,12},{12,8},{1,5},{5,1},{9,13},{13,9},{2,6},{6,2},{1... | collective-permute-start | bytes 1544 | tf_op jit(solution)/shard_map/ppermute | solution.py:192
  6.3 4.0 %shard_map.64 = (bf16[32,4,128,256]{3,2,1,0:T(8,128)(2,1)S(1)}, bf16[32,256,256]{2,1,0:T(8,128)(2,1)S(1)}) custom-call(bf16[4,256,256]{2,1,0:T(8,128)(2,1)} %wave_ref.1, bf16[32,128,256]{2,1,0:T(8,128)(2,1)} %left_ref.1, bf16[32,256,256]{2,1,0:T(8,128)(2,1)} %right_ref.1), custom_call_target="tpu_custom_call" | custom-call | flops 2147483648 | bytes 6291456 | tf_op jit(solution)/shard_map/pallas_call | solution.py:69
  10.3 0.0 collective-permute-done.2
  10.3 0.0 collective-permute-done.1
  10.3 0.0 collective-permute-done
  10.3 3.6 %shard_map.65 = (f32[16,128,128]{2,1,0:T(8,128)S(1)}, f32[16,128,128]{2,1,0:T(8,128)S(1)}, f32[4,128,128]{2,1,0:T(8,128)S(1)}, bf16[4,128,128]{2,1,0:T(8,128)(2,1)S(1)}) custom-call(s32[32]{0:T(128)} %shift_ref.3, f32[16,32]{1,0:T(8,128)S(1)} %pad_maximum_fusion.coef_ref, bf16[32,4,128,256]{3,2,1,0:T(8,128)(2,1)S(1)} %get-tuple-element.25.mixed_ref, ...), custom_call_target="tpu_custom_call" | custom-call | flops 1073741824 | bytes 6291456 | tf_op jit(solution)/shard_map/pallas_call | solution.py:170
  13.9 1.8 %collective-permute-start.3 = (bf16[4,128,128]{2,1,0:T(8,128)(2,1)S(1)}, bf16[4,128,128]{2,1,0:T(8,128)(2,1)S(1)}, u32[]{:S(2)}, u32[]{:S(2)}) collective-permute-start(bf16[4,128,128]{2,1,0:T(8,128)(2,1)S(1)} %get-tuple-element.27), channel_id=1, source_target_pairs={{0,2},{2,0},{1,3},{3,1},{4,6},{6,4},{5,7},{7,5},{8,10},{10,8},{9,1... | collective-permute-start | bytes 393224 | tf_op jit(solution)/shard_map/ppermute | solution.py:192
  15.7 3.5 %shard_map.66 = (f32[16,128,128]{2,1,0:T(8,128)S(1)}, f32[16,128,128]{2,1,0:T(8,128)S(1)}, f32[4,128,128]{2,1,0:T(8,128)S(1)}, bf16[4,128,128]{2,1,0:T(8,128)(2,...) custom-call(s32[32]{0:T(128)} %shift_ref.3, ...), custom_call_target="tpu_custom_call", output_to_operand_aliasing={{0}: (4, {}), {1}: (5, {})} | custom-call | flops 1073741824 | bytes 6291456 | tf_op jit(solution)/shard_map/pallas_call | solution.py:170
  19.1 0.0 collective-permute-done.3
  19.2 1.6 %collective-permute-start.5 = (bf16[4,128,128]{2,1,0:T(8,128)(2,1)S(1)}, bf16[4,128,128]{2,1,0:T(8,128)(2,1)S(1)}, u32[]{:S(2)}, u32[]{:S(2)}) collective-permute-start(bf16[4,128,128]{2,1,0:T(8,128)(2,1)S(1)} %get-tuple-element.39), channel_id=1, source_target_pairs={{0,2},{2,0},{1,3},{3,1},{4,6},{6,4},{5,7},{7,5},{8,10},{10,8},{9,1... | collective-permute-start | bytes 393224 | tf_op jit(solution)/shard_map/ppermute | solution.py:192
  20.7 1.2 %collective-permute-start.7 = (bf16[4,128,128]{2,1,0:T(8,128)(2,1)S(1)}, bf16[4,128,128]{2,1,0:T(8,128)(2,1)S(1)}, u32[]{:S(2)}, u32[]{:S(2)}) collective-permute-start(bf16[4,128,128]{2,1,0:T(8,128)(2,1)S(1)} %add_convert_fusion.2), channel_id=1, source_target_pairs={{0,4},{4,0},{8,12},{12,8},{1,5},{5,1},{9,13},{13,9},{2,6},{6,2},{1... | collective-permute-start | bytes 393224 | tf_op jit(solution)/shard_map/ppermute | solution.py:192
  22.0 0.5 %collective-permute-start.4 = (bf16[4,128,128]{2,1,0:T(8,128)(2,1)S(1)}, bf16[4,128,128]{2,1,0:T(8,128)(2,1)S(1)}, u32[]{:S(2)}, u32[]{:S(2)}) collective-permute-start(bf16[4,128,128]{2,1,0:T(8,128)(2,1)S(1)} %get-tuple-element.37), channel_id=1, source_target_pairs={{0,2},{2,0},{1,3},{3,1},{4,6},{6,4},{5,7},{7,5},{8,10},{10,8},{9,1... | collective-permute-start | bytes 393224 | tf_op jit(solution)/shard_map/ppermute | solution.py:192
  22.5 2.4 %collective-permute-done.5 = bf16[4,128,128]{2,1,0:T(8,128)(2,1)S(1)} collective-permute-done((bf16[4,128,128]{2,1,0:T(8,128)(2,1)S(1)}, bf16[4,128,128]{2,1,0:T(8,128)(2,1)S(1)}, u32[]{:S(2)}, u32[]{:S(2)}) %collective-permute-start.5) | collective-permute-done | bytes 131104 | tf_op jit(solution)/shard_map/ppermute | solution.py:192
  25.0 2.0 %collective-permute-done.4 = bf16[4,128,128]{2,1,0:T(8,128)(2,1)S(1)} collective-permute-done((bf16[4,128,128]{2,1,0:T(8,128)(2,1)S(1)}, bf16[4,128,128]{2,1,0:T(8,128)(2,1)S(1)}, u32[]{:S(2)}, u32[]{:S(2)}) %collective-permute-start.4) | collective-permute-done | bytes 131104 | tf_op jit(solution)/shard_map/ppermute | solution.py:192
  27.0 0.8 %collective-permute-start.6 = (bf16[4,128,128]{2,1,0:T(8,128)(2,1)S(1)}, bf16[4,128,128]{2,1,0:T(8,128)(2,1)S(1)}, u32[]{:S(2)}, u32[]{:S(2)}) collective-permute-start(bf16[4,128,128]{2,1,0:T(8,128)(2,1)S(1)} %add_convert_fusion.1), channel_id=1, source_target_pairs={{0,4},{4,0},{8,12},{12,8},{1,5},{5,1},{9,13},{13,9},{2,6},{6,2},{1... | collective-permute-start | bytes 393224 | tf_op jit(solution)/shard_map/ppermute | solution.py:192
  27.8 0.0 collective-permute-done.7
  27.9 2.7 %collective-permute-start.9 = (bf16[4,128,128]{2,1,0:T(8,128)(2,1)S(1)}, bf16[4,128,128]{2,1,0:T(8,128)(2,1)S(1)}, u32[]{:S(2)}, u32[]{:S(2)}) collective-permute-start(bf16[4,128,128]{2,1,0:T(8,128)(2,1)S(1)} %add_convert_fusion), channel_id=1, source_target_pairs={{0,8},{4,12},{8,0},{12,4},{1,9},{5,13},{9,1},{13,5},{2,10},{6,14},... | collective-permute-start | bytes 393224 | tf_op jit(solution)/shard_map/ppermute | solution.py:192
  30.6 0.9 %collective-permute-start.8 = (bf16[4,128,128]{2,1,0:T(8,128)(2,1)S(1)}, bf16[4,128,128]{2,1,0:T(8,128)(2,1)S(1)}, u32[]{:S(2)}, u32[]{:S(2)}) collective-permute-start(bf16[4,128,128]{2,1,0:T(8,128)(2,1)S(1)} %get-tuple-element.44), channel_id=1, source_target_pairs={{0,2},{2,0},{1,3},{3,1},{4,6},{6,4},{5,7},{7,5},{8,10},{10,8},{9,1... | collective-permute-start | bytes 393224 | tf_op jit(solution)/shard_map/ppermute | solution.py:192
  31.5 0.5 %collective-permute-done.6 = bf16[4,128,128]{2,1,0:T(8,128)(2,1)S(1)} collective-permute-done((bf16[4,128,128]{2,1,0:T(8,128)(2,1)S(1)}, bf16[4,128,128]{2,1,0:T(8,128)(2,1)S(1)}, u32[]{:S(2)}, u32[]{:S(2)}) %collective-permute-start.6) | collective-permute-done | bytes 131104 | tf_op jit(solution)/shard_map/ppermute | solution.py:192
  32.1 3.5 %collective-permute-done.8 = bf16[4,128,128]{2,1,0:T(8,128)(2,1)S(1)} collective-permute-done((bf16[4,128,128]{2,1,0:T(8,128)(2,1)S(1)}, bf16[4,128,128]{2,1,0:T(8,128)(2,1)S(1)}, u32[]{:S(2)}, u32[]{:S(2)}) %collective-permute-start.8) | collective-permute-done | bytes 131104 | tf_op jit(solution)/shard_map/ppermute | solution.py:192
  35.6 0.0 collective-permute-done.9
  35.6 0.7 %convert_add_fusion = f32[4,128,128]{2,1,0:T(8,128)} fusion(f32[4,128,128]{2,1,0:T(8,128)S(1)} %convert_add_fusion.1, bf16[4,128,128]{2,1,0:T(8,128)(2,1)S(1)} %collective-permute-done.9), kind=kLoop, calls=%fused_computation | loop fusion | flops 131072 | bytes 655360 | tf_op jit(solution)/shard_map/add | solution.py:226
  (7 shorter events, 0.2 us)
Async XLA Ops:
  0.7 9.6 %collective-permute-start.2 = (f32[4,32]{1,0:T(4,128)S(1)}, f32[4,32]{1,0:T(4,128)S(1)}, u32[]{:S(2)}, u32[]{:S(2)}) collective-permute-start(f32[4,32]{1,0:T(4,128)S(1)} %select_bitcast_fusion), channel_id=1, source_target_pairs={{0,12},{4,8},{8,4},{12,0},{1,13},{5,9},{9,5},{13,1},{2,14},{6,10},... | collective-permute-start | bytes 1544 | tf_op jit(solution)/shard_map/ppermute | solution.py:192
  5.8 4.5 %collective-permute-start.1 = (f32[4,32]{1,0:T(4,128)S(1)}, f32[4,32]{1,0:T(4,128)S(1)}, u32[]{:S(2)}, u32[]{:S(2)}) collective-permute-start(f32[4,32]{1,0:T(4,128)S(1)} %select_bitcast_fusion), channel_id=1, source_target_pairs={{0,8},{4,12},{8,0},{12,4},{1,9},{5,13},{9,1},{13,5},{2,10},{6,14},... | collective-permute-start | bytes 1544 | tf_op jit(solution)/shard_map/ppermute | solution.py:192
  5.8 4.5 %collective-permute-start = (f32[4,32]{1,0:T(4,128)S(1)}, f32[4,32]{1,0:T(4,128)S(1)}, u32[]{:S(2)}, u32[]{:S(2)}) collective-permute-start(f32[4,32]{1,0:T(4,128)S(1)} %select_bitcast_fusion), channel_id=1, source_target_pairs={{0,4},{4,0},{8,12},{12,8},{1,5},{5,1},{9,13},{13,9},{2,6},{6,2},{1... | collective-permute-start | bytes 1544 | tf_op jit(solution)/shard_map/ppermute | solution.py:192
  13.9 5.2 %collective-permute-start.3 = (bf16[4,128,128]{2,1,0:T(8,128)(2,1)S(1)}, bf16[4,128,128]{2,1,0:T(8,128)(2,1)S(1)}, u32[]{:S(2)}, u32[]{:S(2)}) collective-permute-start(bf16[4,128,128]{2,1,0:T(8,128)(2,1)S(1)} %get-tuple-element.27), channel_id=1, source_target_pairs={{0,2},{2,0},{1,3},{3,1},{4,6},{6,4},{5,7},{7,5},{8,10},{10,8},{9,1... | collective-permute-start | bytes 393224 | tf_op jit(solution)/shard_map/ppermute | solution.py:192
  19.2 5.8 %collective-permute-start.5 = (bf16[4,128,128]{2,1,0:T(8,128)(2,1)S(1)}, bf16[4,128,128]{2,1,0:T(8,128)(2,1)S(1)}, u32[]{:S(2)}, u32[]{:S(2)}) collective-permute-start(bf16[4,128,128]{2,1,0:T(8,128)(2,1)S(1)} %get-tuple-element.39), channel_id=1, source_target_pairs={{0,2},{2,0},{1,3},{3,1},{4,6},{6,4},{5,7},{7,5},{8,10},{10,8},{9,1... | collective-permute-start | bytes 393224 | tf_op jit(solution)/shard_map/ppermute | solution.py:192
  20.7 7.1 %collective-permute-start.7 = (bf16[4,128,128]{2,1,0:T(8,128)(2,1)S(1)}, bf16[4,128,128]{2,1,0:T(8,128)(2,1)S(1)}, u32[]{:S(2)}, u32[]{:S(2)}) collective-permute-start(bf16[4,128,128]{2,1,0:T(8,128)(2,1)S(1)} %add_convert_fusion.2), channel_id=1, source_target_pairs={{0,4},{4,0},{8,12},{12,8},{1,5},{5,1},{9,13},{13,9},{2,6},{6,2},{1... | collective-permute-start | bytes 393224 | tf_op jit(solution)/shard_map/ppermute | solution.py:192
  22.0 5.0 %collective-permute-start.4 = (bf16[4,128,128]{2,1,0:T(8,128)(2,1)S(1)}, bf16[4,128,128]{2,1,0:T(8,128)(2,1)S(1)}, u32[]{:S(2)}, u32[]{:S(2)}) collective-permute-start(bf16[4,128,128]{2,1,0:T(8,128)(2,1)S(1)} %get-tuple-element.37), channel_id=1, source_target_pairs={{0,2},{2,0},{1,3},{3,1},{4,6},{6,4},{5,7},{7,5},{8,10},{10,8},{9,1... | collective-permute-start | bytes 393224 | tf_op jit(solution)/shard_map/ppermute | solution.py:192
  27.0 5.0 %collective-permute-start.6 = (bf16[4,128,128]{2,1,0:T(8,128)(2,1)S(1)}, bf16[4,128,128]{2,1,0:T(8,128)(2,1)S(1)}, u32[]{:S(2)}, u32[]{:S(2)}) collective-permute-start(bf16[4,128,128]{2,1,0:T(8,128)(2,1)S(1)} %add_convert_fusion.1), channel_id=1, source_target_pairs={{0,4},{4,0},{8,12},{12,8},{1,5},{5,1},{9,13},{13,9},{2,6},{6,2},{1... | collective-permute-start | bytes 393224 | tf_op jit(solution)/shard_map/ppermute | solution.py:192
  27.9 7.7 %collective-permute-start.9 = (bf16[4,128,128]{2,1,0:T(8,128)(2,1)S(1)}, bf16[4,128,128]{2,1,0:T(8,128)(2,1)S(1)}, u32[]{:S(2)}, u32[]{:S(2)}) collective-permute-start(bf16[4,128,128]{2,1,0:T(8,128)(2,1)S(1)} %add_convert_fusion), channel_id=1, source_target_pairs={{0,8},{4,12},{8,0},{12,4},{1,9},{5,13},{9,1},{13,5},{2,10},{6,14},... | collective-permute-start | bytes 393224 | tf_op jit(solution)/shard_map/ppermute | solution.py:192
  30.6 5.0 %collective-permute-start.8 = (bf16[4,128,128]{2,1,0:T(8,128)(2,1)S(1)}, bf16[4,128,128]{2,1,0:T(8,128)(2,1)S(1)}, u32[]{:S(2)}, u32[]{:S(2)}) collective-permute-start(bf16[4,128,128]{2,1,0:T(8,128)(2,1)S(1)} %get-tuple-element.44), channel_id=1, source_target_pairs={{0,2},{2,0},{1,3},{3,1},{4,6},{6,4},{5,7},{7,5},{8,10},{10,8},{9,1... | collective-permute-start | bytes 393224 | tf_op jit(solution)/shard_map/ppermute | solution.py:192

commit v21 on v19

--- a/solution.py
+++ b/solution.py
@@ -18,17 +18,26 @@
     return lax.rem(value + size, size)
 
 
-def mix_kernel(split, wave_ref, left_ref, right_ref, mixed_ref, held_ref, wave, left, sems):
+def divided(value, size):
+    if size & (size - 1) == 0:
+        return value >> (size.bit_length() - 1)
+    return lax.div(value, size)
+
+
+def mix_kernel(split, group, targets, shift_ref, wave_ref, left_ref, right_ref, *refs):
+    mixed_ref, held_ref, plan, wave, left, shifts, sems = refs
     sec_dev = wave.shape[0]
     terms, rows, width = left.shape
     chunks = terms // MIX_TERMS
 
     def left_copy(c):
         part = pl.ds(c * MIX_TERMS, MIX_TERMS)
-        return pltpu.make_async_copy(left_ref.at[part], left.at[part], sems.at[3 + c])
+        return pltpu.make_async_copy(left_ref.at[part], left.at[part], sems.at[4 + c])
 
     wave_copy = pltpu.make_async_copy(wave_ref, wave, sems.at[0])
     wave_copy.start()
+    shift_copy = pltpu.make_async_copy(shift_ref, shifts, sems.at[3])
+    shift_copy.start()
     for c in range(chunks):
         left_copy(c).start()
     if split:
@@ -48,6 +57,24 @@
         right_copies = [pltpu.make_async_copy(right_ref, held_ref, sems.at[1])]
     for copy in right_copies:
         copy.start()
+
+    first = lax.axis_index("sector") * sec_dev
+    start = (first ^ (group * sec_dev)) - first
+    shift_copy.wait()
+
+    def pick(wanted):
+        def body(k, count):
+            shift = shifts[k]
+            plan[count] = k * targets + shift
+            reaches = wrapped(sec_dev - 1 - start - shift, targets) < 2 * sec_dev - 1
+            return count + jnp.where(reaches == wanted, 1, 0)
+
+        return body
+
+    count = lax.fori_loop(0, terms, pick(True), 0)
+    lax.fori_loop(0, terms, pick(False), count)
+    most = jnp.maximum(count, terms // 2)
+    plan[terms + 1] = lax.div(most + SUM_TERMS - 1, SUM_TERMS)
     wave_copy.wait()
 
     @pl.loop(0, chunks)
@@ -63,21 +90,24 @@
         copy.wait()
 
 
-def mix(wavefunction, left_ops, right_ops, split):
+def mix(shift, wavefunction, left_ops, right_ops, group, targets, split):
     k_dev, rows, width = left_ops.shape
     sec_dev = wavefunction.shape[0]
     return pl.pallas_call(
-        functools.partial(mix_kernel, split),
+        functools.partial(mix_kernel, split, group, targets),
         out_shape=[
             pltpu.VMEM((k_dev, sec_dev, rows, width), jnp.bfloat16),
             pltpu.VMEM(right_ops.shape, jnp.bfloat16),
+            jax.ShapeDtypeStruct((k_dev + 2,), jnp.int32),
         ],
-        in_specs=[pl.BlockSpec(memory_space=pltpu.HBM)] * 3,
-        out_specs=[pl.BlockSpec(memory_space=pltpu.VMEM)] * 2,
+        in_specs=[pl.BlockSpec(memory_space=pltpu.HBM)] * 4,
+        out_specs=[pl.BlockSpec(memory_space=pltpu.VMEM)] * 2
+        + [pl.BlockSpec(memory_space=pltpu.SMEM)],
         scratch_shapes=[
             pltpu.VMEM(wavefunction.shape, jnp.bfloat16),
             pltpu.VMEM(left_ops.shape, jnp.bfloat16),
-            pltpu.SemaphoreType.DMA((3 + k_dev // MIX_TERMS,)),
+            pltpu.SMEM(shift.shape, jnp.int32),
+            pltpu.SemaphoreType.DMA((4 + k_dev // MIX_TERMS,)),
         ],
         compiler_params=pltpu.CompilerParams(vmem_limit_bytes=24 * MIB),
         cost_estimate=pl.CostEstimate(
@@ -85,42 +115,28 @@
             bytes_accessed=2 * (left_ops.size + right_ops.size),
             transcendentals=0,
         ),
-    )(*(pltpu.with_memory_space_constraint(x, pltpu.HBM) for x in (wavefunction, left_ops, right_ops)))
-
-
-def sum_kernel(order, stage, shift_ref, coef_ref, mixed_ref, held_ref, *refs):
+    )(
+        *(
+            pltpu.with_memory_space_constraint(x, pltpu.HBM)
+            for x in (shift, wavefunction, left_ops, right_ops)
+        )
+    )
+
+
+def sum_kernel(order, stage, plan, coef_ref, mixed_ref, held_ref, *refs):
     terms, sec_dev, rows, width = mixed_ref.shape
     targets = coef_ref.shape[0]
     half = width // 2
-    picked = refs[-1]
     first = lax.axis_index("sector") * sec_dev
-
-    def reaches(k, group):
-        start = (first ^ (group * sec_dev)) - first
-        return wrapped(sec_dev - 1 - start - shift_ref[k], targets) < 2 * sec_dev - 1
-
-    def pick(wanted):
-        def body(k, count):
-            picked[count] = k
-            found = functools.reduce(jnp.logical_or, [reaches(k, group) for group in order[0]])
-            return count + jnp.where(found == wanted, 1, 0)
-
-        return body
-
-    if stage is None:
-        low, high = 0, terms // SUM_TERMS
-    else:
-        count = lax.fori_loop(0, terms, pick(True), 0)
-        lax.fori_loop(0, terms, pick(False), count)
-        steps = lax.div(jnp.maximum(count, terms // 2) + SUM_TERMS - 1, SUM_TERMS)
-        low, high = (0, steps) if stage == 0 else (steps, terms // SUM_TERMS)
+    low = plan[terms + 1] if stage == 1 else 0
+    high = plan[terms + 1] if stage == 0 else terms // SUM_TERMS
 
     if stage is None:
         sums = refs[:1]
     elif stage == 0:
-        sums, outs = refs[:2], refs[2:-1]
+        sums, outs = refs[:2], refs[2:]
     else:
-        sums, outs = refs[2:4], refs[4:-1]
+        sums, outs = refs[2:4], refs[4:]
     if not stage:
         for total in sums:
             total[...] = jnp.zeros_like(total)
@@ -128,9 +144,8 @@
     @pl.loop(low, high)
     def _(step):
         for t in range(SUM_TERMS):
-            k = step * SUM_TERMS + t
-            if stage is not None:
-                k = picked[k]
+            entry = plan[step * SUM_TERMS + t]
+            k, shift = divided(entry, targets), wrapped(entry, targets)
             product = lax.dot_general(
                 mixed_ref[k].reshape(sec_dev * rows, width),
                 held_ref[k],
@@ -138,7 +153,7 @@
                 preferred_element_type=jnp.float32,
             )
             for s in range(sec_dev):
-                slot = wrapped(first + s - shift_ref[k], targets)
+                slot = wrapped(first + s - shift, targets)
                 if stage is not None:
                     slot ^= first
                 scaled = coef_ref[slot, k] * product[s * rows : (s + 1) * rows]
@@ -155,7 +170,7 @@
             outs[2 * at + 1][...] = sums[1][part].astype(jnp.bfloat16)
 
 
-def summed(shift, coef, mixed, held, order, stage, sums=()):
+def summed(plan, coef, mixed, held, order, stage, sums=()):
     k_dev, sec_dev, rows, width = mixed.shape
     targets = coef.shape[0]
     columns = width if stage is None else width // 2
@@ -174,7 +189,6 @@
         + [pl.BlockSpec(memory_space=pltpu.VMEM)] * len(in_vmem),
         out_specs=[pl.BlockSpec(memory_space=pltpu.VMEM)] * len(out_shape),
         input_output_aliases={4 + i: i for i in range(len(sums))},
-        scratch_shapes=[pltpu.SMEM((k_dev + SUM_TERMS,), jnp.int32)],
         compiler_params=pltpu.CompilerParams(vmem_limit_bytes=24 * MIB),
         cost_estimate=pl.CostEstimate(
             flops=k_dev * sec_dev * rows * width * width,
@@ -182,7 +196,7 @@
             transcendentals=0,
         ),
     )(
-        pltpu.with_memory_space_constraint(shift, pltpu.HBM),
+        plan,
         coef,
         *(pltpu.with_memory_space_constraint(x, pltpu.VMEM) for x in in_vmem),
     )
@@ -201,15 +215,17 @@
     devices = lax.axis_size("sector")
     live = jnp.where(coupled.T > 0, site_coef.T, 0.0)
     split = lax.axis_size("op") == 2 and devices == 4 and sec_dev & (sec_dev - 1) == 0
-    mixed, held = mix(wavefunction, left_ops, right_ops, split)
+    order = ((2,), (3, 1, 0))
+    mixed, held, plan = mix(
+        sector_shift, wavefunction, left_ops, right_ops, order[0][0], devices * sec_dev, split
+    )
 
     if split:
         coef = jnp.concatenate([live] + [swap(live, "sector", g) for g in (1, 2, 3)], axis=0)
-        order = ((2,), (3, 1, 0))
-        *sums, mine_2, theirs_2 = summed(sector_shift, coef, mixed, held, order, 0)
+        *sums, mine_2, theirs_2 = summed(plan, coef, mixed, held, order, 0)
         crossed_2 = swap(theirs_2, "op", 1)
         _, _, mine_3, theirs_3, mine_1, theirs_1, mine_0, theirs_0 = summed(
-            sector_shift, after(coef, theirs_2), mixed, held, order, 1, sums
+            plan, after(coef, theirs_2), mixed, held, order, 1, sums
         )
         both_2 = (mine_2 + after(crossed_2, mine_3).astype(jnp.float32)).astype(jnp.bfloat16)
         arrived_2 = swap(both_2, "sector", 2)
@@ -226,7 +242,7 @@
         return sigma
 
     coef = lax.all_gather(live, "sector", axis=0, tiled=True)
-    (total,) = summed(sector_shift, coef, mixed, held, (), None)
+    (total,) = summed(plan, coef, mixed, held, (), None)
     total = lax.psum_scatter(total, "op", scatter_dimension=2, tiled=True)
     return lax.psum_scatter(total, "sector", scatter_dimension=0, tiled=True)
 

time: 36.5 us -> 36 us (0.986)
  Pallas kernels: 11 us -> 10.5 us
    pallas_call x2, Pallas kernels: 7.02 us -> 6 us  [summed(): pl.pallas_call(functools.partial(sum_kernel, order, stage), out_shape=out...]
    pallas_call x1, Pallas kernels: 3.95 us -> 4.55 us  [mix(): pl.pallas_call(functools.partial(mix_kernel, split, group, targets), out_...]
  transfers between devices with their start and end apart: 10 -> 10, of which waited for: 3 -> 4; matrix products, arithmetic and copies ran while one was open for 0% -> 0% of each run, Pallas kernels for 20% -> 21%
where the time goes in v21:
time: 36 us; the launch traced here: 35.8 us
  starting transfers between devices  16.8 us (47%)
  Pallas kernels  10.5 us (29%)
  waiting for transfers between devices  6.75 us (19%)
  other arithmetic  1.64 us (5%)
    ppermute x10, starting transfers between devices, swap(): lax.ppermute(value, axis, [(i, i ^ mask) for i in range(lax.axis_size(axi...  16.8 us
    ppermute x10, waiting for transfers between devices, swap(): lax.ppermute(value, axis, [(i, i ^ mask) for i in range(lax.axis_size(axi...  6.75 us
    pallas_call x2, Pallas kernels, summed(): pl.pallas_call(functools.partial(sum_kernel, order, stage), out_shape=out...  6 us
    pallas_call x1, Pallas kernels, mix(): pl.pallas_call(functools.partial(mix_kernel, split, group, targets), out_...  4.55 us
    add x3, other arithmetic, per_device(): sigma = lax.optimization_barrier(sigma) + other.astype(jnp.float32)  0.78 us
  transfers between devices with their start and end apart: 10, of which 4 were waited for; matrix products, arithmetic and copies ran while one was open for 0% of the time, Pallas kernels for 21%

profile of v21, /device:TPU:0, one launch (start us, length us, event | category | flops | bytes accessed | tf_op | source)
XLA Modules:
  0.0 35.8 jit_solution(13956121209084751681)
XLA Ops:
  0.0 0.7 %select_bitcast_fusion = f32[4,32]{1,0:T(4,128)S(1)} fusion(f32[32,4]{0,1:T(4,128)} %param.9, s32[32,4]{0,1:T(4,128)} %param.10), kind=kLoop, calls=%fused_computation.8 | loop fusion | flops 256 | bytes 1536 | tf_op jit(solution)/shard_map/jit(_where)/select_n | solution.py:216
  0.7 5.0 %collective-permute-start.2 = (f32[4,32]{1,0:T(4,128)S(1)}, f32[4,32]{1,0:T(4,128)S(1)}, u32[]{:S(2)}, u32[]{:S(2)}) collective-permute-start(f32[4,32]{1,0:T(4,128)S(1)} %select_bitcast_fusion), channel_id=1, source_target_pairs={{0,12},{4,8},{8,4},{12,0},{1,13},{5,9},{9,5},{13,1},{2,14},{6,10},... | collective-permute-start | bytes 1544 | tf_op jit(solution)/shard_map/ppermute | solution.py:206
  5.8 0.0 collective-permute-start.1
  5.8 0.6 %collective-permute-start = (f32[4,32]{1,0:T(4,128)S(1)}, f32[4,32]{1,0:T(4,128)S(1)}, u32[]{:S(2)}, u32[]{:S(2)}) collective-permute-start(f32[4,32]{1,0:T(4,128)S(1)} %select_bitcast_fusion), channel_id=1, source_target_pairs={{0,4},{4,0},{8,12},{12,8},{1,5},{5,1},{9,13},{13,9},{2,6},{6,2},{1... | collective-permute-start | bytes 1544 | tf_op jit(solution)/shard_map/ppermute | solution.py:206
  6.3 4.6 %shard_map.64 = (bf16[32,4,128,256]{3,2,1,0:T(8,128)(2,1)S(1)}, bf16[32,256,256]{2,1,0:T(8,128)(2,1)S(1)}, s32[34]{0:T(128)S(1)}) custom-call(s32[32]{0:T(128)} %shift_ref.1, bf16[4,256,256]{2,1,0:T(8,128)(2,1)} %wave_ref.1, bf16[32,128,256]{2,1,0:T(8,128)(2,1)} %left_ref.1, bf16[32,256,256]{2,1,0:T(8,128)(2,1)} %right_ref.1), custom_call_target="tpu_custom_call" | custom-call | flops 2147483648 | bytes 6291456 | tf_op jit(solution)/shard_map/pallas_call | solution.py:96
  10.9 0.0 collective-permute-done.2
  10.9 0.0 collective-permute-done.1
  10.9 0.0 collective-permute-done
  10.9 3.0 %shard_map.65 = (f32[16,128,128]{2,1,0:T(8,128)S(1)}, f32[16,128,128]{2,1,0:T(8,128)S(1)}, f32[4,128,128]{2,1,0:T(8,128)S(1)}, bf16[4,128,128]{2,1,0:T(8,128)(2,1)S(1)}) custom-call(s32[34]{0:T(128)S(1)} %get-tuple-element.26.plan, f32[16,32]{1,0:T(8,128)S(1)} %pad_maximum_fusion.coef_ref, bf16[32,4,128,256]{3,2,1,0:T(8,128)(2,1)S(1)} %get-tuple-element.27.mixed_ref, ...), custom_call_target="tpu_custom_call" | custom-call | flops 1073741824 | bytes 6291456 | tf_op jit(solution)/shard_map/pallas_call | solution.py:185
  14.0 1.8 %collective-permute-start.3 = (bf16[4,128,128]{2,1,0:T(8,128)(2,1)S(1)}, bf16[4,128,128]{2,1,0:T(8,128)(2,1)S(1)}, u32[]{:S(2)}, u32[]{:S(2)}) collective-permute-start(bf16[4,128,128]{2,1,0:T(8,128)(2,1)S(1)} %get-tuple-element.29), channel_id=1, source_target_pairs={{0,2},{2,0},{1,3},{3,1},{4,6},{6,4},{5,7},{7,5},{8,10},{10,8},{9,1... | collective-permute-start | bytes 393224 | tf_op jit(solution)/shard_map/ppermute | solution.py:206
  15.7 3.0 %shard_map.66 = (f32[16,128,128]{2,1,0:T(8,128)S(1)}, f32[16,128,128]{2,1,0:T(8,128)S(1)}, f32[4,128,128]{2,1,0:T(8,128)S(1)}, bf16[4,128,128]{2,1,0:T(8,128)(2,...) custom-call(s32[34]{0:T(128)S(1)} %get-tuple-element.26.plan, ...), custom_call_target="tpu_custom_call", output_to_operand_aliasing={{0}: (4, {}), {1}: (5, {})} | custom-call | flops 1073741824 | bytes 6291456 | tf_op jit(solution)/shard_map/pallas_call | solution.py:185
  18.7 0.3 collective-permute-done.3
  19.0 1.8 %collective-permute-start.4 = (bf16[4,128,128]{2,1,0:T(8,128)(2,1)S(1)}, bf16[4,128,128]{2,1,0:T(8,128)(2,1)S(1)}, u32[]{:S(2)}, u32[]{:S(2)}) collective-permute-start(bf16[4,128,128]{2,1,0:T(8,128)(2,1)S(1)} %get-tuple-element.39), channel_id=1, source_target_pairs={{0,2},{2,0},{1,3},{3,1},{4,6},{6,4},{5,7},{7,5},{8,10},{10,8},{9,1... | collective-permute-start | bytes 393224 | tf_op jit(solution)/shard_map/ppermute | solution.py:206
  20.8 2.1 %collective-permute-start.7 = (bf16[4,128,128]{2,1,0:T(8,128)(2,1)S(1)}, bf16[4,128,128]{2,1,0:T(8,128)(2,1)S(1)}, u32[]{:S(2)}, u32[]{:S(2)}) collective-permute-start(bf16[4,128,128]{2,1,0:T(8,128)(2,1)S(1)} %add_convert_fusion.2), channel_id=1, source_target_pairs={{0,8},{4,12},{8,0},{12,4},{1,9},{5,13},{9,1},{13,5},{2,10},{6,14},... | collective-permute-start | bytes 393224 | tf_op jit(solution)/shard_map/ppermute | solution.py:206
  23.0 0.5 %collective-permute-start.6 = (bf16[4,128,128]{2,1,0:T(8,128)(2,1)S(1)}, bf16[4,128,128]{2,1,0:T(8,128)(2,1)S(1)}, u32[]{:S(2)}, u32[]{:S(2)}) collective-permute-start(bf16[4,128,128]{2,1,0:T(8,128)(2,1)S(1)} %get-tuple-element.44), channel_id=1, source_target_pairs={{0,2},{2,0},{1,3},{3,1},{4,6},{6,4},{5,7},{7,5},{8,10},{10,8},{9,1... | collective-permute-start | bytes 393224 | tf_op jit(solution)/shard_map/ppermute | solution.py:206
  23.5 1.6 %collective-permute-done.4 = bf16[4,128,128]{2,1,0:T(8,128)(2,1)S(1)} collective-permute-done((bf16[4,128,128]{2,1,0:T(8,128)(2,1)S(1)}, bf16[4,128,128]{2,1,0:T(8,128)(2,1)S(1)}, u32[]{:S(2)}, u32[]{:S(2)}) %collective-permute-start.4) | collective-permute-done | bytes 131104 | tf_op jit(solution)/shard_map/ppermute | solution.py:206
  25.2 3.1 %collective-permute-start.8 = (bf16[4,128,128]{2,1,0:T(8,128)(2,1)S(1)}, bf16[4,128,128]{2,1,0:T(8,128)(2,1)S(1)}, u32[]{:S(2)}, u32[]{:S(2)}) collective-permute-start(bf16[4,128,128]{2,1,0:T(8,128)(2,1)S(1)} %add_convert_fusion.1), channel_id=1, source_target_pairs={{0,12},{4,8},{8,4},{12,0},{1,13},{5,9},{9,5},{13,1},{2,14},{6,10},... | collective-permute-start | bytes 393224 | tf_op jit(solution)/shard_map/ppermute | solution.py:206
  28.2 1.8 %collective-permute-start.5 = (bf16[4,128,128]{2,1,0:T(8,128)(2,1)S(1)}, bf16[4,128,128]{2,1,0:T(8,128)(2,1)S(1)}, u32[]{:S(2)}, u32[]{:S(2)}) collective-permute-start(bf16[4,128,128]{2,1,0:T(8,128)(2,1)S(1)} %get-tuple-element.41), channel_id=1, source_target_pairs={{0,2},{2,0},{1,3},{3,1},{4,6},{6,4},{5,7},{7,5},{8,10},{10,8},{9,1... | collective-permute-start | bytes 393224 | tf_op jit(solution)/shard_map/ppermute | solution.py:206
  30.0 0.0 collective-permute-done.6
  30.1 0.1 collective-permute-start.9
  30.2 3.0 %collective-permute-done.5 = bf16[4,128,128]{2,1,0:T(8,128)(2,1)S(1)} collective-permute-done((bf16[4,128,128]{2,1,0:T(8,128)(2,1)S(1)}, bf16[4,128,128]{2,1,0:T(8,128)(2,1)S(1)}, u32[]{:S(2)}, u32[]{:S(2)}) %collective-permute-start.5) | collective-permute-done | bytes 131104 | tf_op jit(solution)/shard_map/ppermute | solution.py:206
  33.2 0.0 collective-permute-done.7
  33.3 0.0 collective-permute-done.8
  33.3 1.8 %collective-permute-done.9 = bf16[4,128,128]{2,1,0:T(8,128)(2,1)S(1)} collective-permute-done((bf16[4,128,128]{2,1,0:T(8,128)(2,1)S(1)}, bf16[4,128,128]{2,1,0:T(8,128)(2,1)S(1)}, u32[]{:S(2)}, u32[]{:S(2)}) %collective-permute-start.9) | collective-permute-done | bytes 131104 | tf_op jit(solution)/shard_map/ppermute | solution.py:206
  35.1 0.7 %convert_add_fusion = f32[4,128,128]{2,1,0:T(8,128)} fusion(f32[4,128,128]{2,1,0:T(8,128)S(1)} %convert_add_fusion.1, bf16[4,128,128]{2,1,0:T(8,128)(2,1)S(1)} %collective-permute-done.9), kind=kLoop, calls=%fused_computation | loop fusion | flops 131072 | bytes 655360 | tf_op jit(solution)/shard_map/add | solution.py:241
  (7 shorter events, 0.2 us)
Async XLA Ops:
  0.7 10.2 %collective-permute-start.2 = (f32[4,32]{1,0:T(4,128)S(1)}, f32[4,32]{1,0:T(4,128)S(1)}, u32[]{:S(2)}, u32[]{:S(2)}) collective-permute-start(f32[4,32]{1,0:T(4,128)S(1)} %select_bitcast_fusion), channel_id=1, source_target_pairs={{0,12},{4,8},{8,4},{12,0},{1,13},{5,9},{9,5},{13,1},{2,14},{6,10},... | collective-permute-start | bytes 1544 | tf_op jit(solution)/shard_map/ppermute | solution.py:206
  5.8 5.1 %collective-permute-start.1 = (f32[4,32]{1,0:T(4,128)S(1)}, f32[4,32]{1,0:T(4,128)S(1)}, u32[]{:S(2)}, u32[]{:S(2)}) collective-permute-start(f32[4,32]{1,0:T(4,128)S(1)} %select_bitcast_fusion), channel_id=1, source_target_pairs={{0,8},{4,12},{8,0},{12,4},{1,9},{5,13},{9,1},{13,5},{2,10},{6,14},... | collective-permute-start | bytes 1544 | tf_op jit(solution)/shard_map/ppermute | solution.py:206
  5.8 5.1 %collective-permute-start = (f32[4,32]{1,0:T(4,128)S(1)}, f32[4,32]{1,0:T(4,128)S(1)}, u32[]{:S(2)}, u32[]{:S(2)}) collective-permute-start(f32[4,32]{1,0:T(4,128)S(1)} %select_bitcast_fusion), channel_id=1, source_target_pairs={{0,4},{4,0},{8,12},{12,8},{1,5},{5,1},{9,13},{13,9},{2,6},{6,2},{1... | collective-permute-start | bytes 1544 | tf_op jit(solution)/shard_map/ppermute | solution.py:206
  14.0 5.0 %collective-permute-start.3 = (bf16[4,128,128]{2,1,0:T(8,128)(2,1)S(1)}, bf16[4,128,128]{2,1,0:T(8,128)(2,1)S(1)}, u32[]{:S(2)}, u32[]{:S(2)}) collective-permute-start(bf16[4,128,128]{2,1,0:T(8,128)(2,1)S(1)} %get-tuple-element.29), channel_id=1, source_target_pairs={{0,2},{2,0},{1,3},{3,1},{4,6},{6,4},{5,7},{7,5},{8,10},{10,8},{9,1... | collective-permute-start | bytes 393224 | tf_op jit(solution)/shard_map/ppermute | solution.py:206
  19.0 6.1 %collective-permute-start.4 = (bf16[4,128,128]{2,1,0:T(8,128)(2,1)S(1)}, bf16[4,128,128]{2,1,0:T(8,128)(2,1)S(1)}, u32[]{:S(2)}, u32[]{:S(2)}) collective-permute-start(bf16[4,128,128]{2,1,0:T(8,128)(2,1)S(1)} %get-tuple-element.39), channel_id=1, source_target_pairs={{0,2},{2,0},{1,3},{3,1},{4,6},{6,4},{5,7},{7,5},{8,10},{10,8},{9,1... | collective-permute-start | bytes 393224 | tf_op jit(solution)/shard_map/ppermute | solution.py:206
  20.8 12.4 %collective-permute-start.7 = (bf16[4,128,128]{2,1,0:T(8,128)(2,1)S(1)}, bf16[4,128,128]{2,1,0:T(8,128)(2,1)S(1)}, u32[]{:S(2)}, u32[]{:S(2)}) collective-permute-start(bf16[4,128,128]{2,1,0:T(8,128)(2,1)S(1)} %add_convert_fusion.2), channel_id=1, source_target_pairs={{0,8},{4,12},{8,0},{12,4},{1,9},{5,13},{9,1},{13,5},{2,10},{6,14},... | collective-permute-start | bytes 393224 | tf_op jit(solution)/shard_map/ppermute | solution.py:206
  23.0 7.1 %collective-permute-start.6 = (bf16[4,128,128]{2,1,0:T(8,128)(2,1)S(1)}, bf16[4,128,128]{2,1,0:T(8,128)(2,1)S(1)}, u32[]{:S(2)}, u32[]{:S(2)}) collective-permute-start(bf16[4,128,128]{2,1,0:T(8,128)(2,1)S(1)} %get-tuple-element.44), channel_id=1, source_target_pairs={{0,2},{2,0},{1,3},{3,1},{4,6},{6,4},{5,7},{7,5},{8,10},{10,8},{9,1... | collective-permute-start | bytes 393224 | tf_op jit(solution)/shard_map/ppermute | solution.py:206
  25.2 8.1 %collective-permute-start.8 = (bf16[4,128,128]{2,1,0:T(8,128)(2,1)S(1)}, bf16[4,128,128]{2,1,0:T(8,128)(2,1)S(1)}, u32[]{:S(2)}, u32[]{:S(2)}) collective-permute-start(bf16[4,128,128]{2,1,0:T(8,128)(2,1)S(1)} %add_convert_fusion.1), channel_id=1, source_target_pairs={{0,12},{4,8},{8,4},{12,0},{1,13},{5,9},{9,5},{13,1},{2,14},{6,10},... | collective-permute-start | bytes 393224 | tf_op jit(solution)/shard_map/ppermute | solution.py:206
  28.2 5.0 %collective-permute-start.5 = (bf16[4,128,128]{2,1,0:T(8,128)(2,1)S(1)}, bf16[4,128,128]{2,1,0:T(8,128)(2,1)S(1)}, u32[]{:S(2)}, u32[]{:S(2)}) collective-permute-start(bf16[4,128,128]{2,1,0:T(8,128)(2,1)S(1)} %get-tuple-element.41), channel_id=1, source_target_pairs={{0,2},{2,0},{1,3},{3,1},{4,6},{6,4},{5,7},{7,5},{8,10},{10,8},{9,1... | collective-permute-start | bytes 393224 | tf_op jit(solution)/shard_map/ppermute | solution.py:206
  30.1 5.0 %collective-permute-start.9 = (bf16[4,128,128]{2,1,0:T(8,128)(2,1)S(1)}, bf16[4,128,128]{2,1,0:T(8,128)(2,1)S(1)}, u32[]{:S(2)}, u32[]{:S(2)}) collective-permute-start(bf16[4,128,128]{2,1,0:T(8,128)(2,1)S(1)} %add_convert_fusion), channel_id=1, source_target_pairs={{0,4},{4,0},{8,12},{12,8},{1,5},{5,1},{9,13},{13,9},{2,6},{6,2},{1... | collective-permute-start | bytes 393224 | tf_op jit(solution)/shard_map/ppermute | solution.py:206

commit v22 on v19

--- a/solution.py
+++ b/solution.py
@@ -211,17 +211,17 @@
         _, _, mine_3, theirs_3, mine_1, theirs_1, mine_0, theirs_0 = summed(
             sector_shift, after(coef, theirs_2), mixed, held, order, 1, sums
         )
+        crossed_3 = swap(theirs_3, "op", 1)
         both_2 = (mine_2 + after(crossed_2, mine_3).astype(jnp.float32)).astype(jnp.bfloat16)
         arrived_2 = swap(both_2, "sector", 2)
-        crossed_3 = swap(after(theirs_3, both_2), "op", 1)
         crossed_1 = swap(after(theirs_1, both_2), "op", 1)
         both_3 = (mine_3 + after(crossed_3, both_2).astype(jnp.float32)).astype(jnp.bfloat16)
         arrived_3 = swap(both_3, "sector", 3)
         crossed_0 = swap(after(theirs_0, both_3), "op", 1)
         both_1 = (mine_1 + after(crossed_1, both_3).astype(jnp.float32)).astype(jnp.bfloat16)
         arrived_1 = swap(both_1, "sector", 1)
-        sigma = mine_0 + after(crossed_0, both_1).astype(jnp.float32)
-        for other in (arrived_2, arrived_3, arrived_1):
+        sigma = mine_0 + after(arrived_2, both_1).astype(jnp.float32)
+        for other in (crossed_0, arrived_3, arrived_1):
             sigma = lax.optimization_barrier(sigma) + other.astype(jnp.float32)
         return sigma
 

time: 36.5 us -> 35.8 us (0.981); the launches traced: 36.3 us -> 36.1 us
  starting transfers between devices: 16.8 us -> 16.1 us
  waiting for transfers between devices: 6.81 us -> 7.28 us
    ppermute x10, starting transfers between devices: 16.8 us -> 16.1 us  [swap(): lax.ppermute(value, axis, [(i, i ^ mask) for i in range(lax.axis_size(axi...]
    ppermute x10, waiting for transfers between devices: 6.81 us -> 7.28 us  [swap(): lax.ppermute(value, axis, [(i, i ^ mask) for i in range(lax.axis_size(axi...]
  transfers between devices with their start and end apart: 10 -> 10, of which waited for: 3 -> 4; matrix products, arithmetic and copies ran while one was open for 0% -> 1% of each run, Pallas kernels for 20% -> 21%
where the time goes in v22:
time: 35.8 us; the launch traced here: 36.1 us
  starting transfers between devices  16.1 us (45%)
  Pallas kernels  11 us (31%)
  waiting for transfers between devices  7.28 us (20%)
  other arithmetic  1.64 us (5%)
    ppermute x10, starting transfers between devices, swap(): lax.ppermute(value, axis, [(i, i ^ mask) for i in range(lax.axis_size(axi...  16.1 us
    ppermute x10, waiting for transfers between devices, swap(): lax.ppermute(value, axis, [(i, i ^ mask) for i in range(lax.axis_size(axi...  7.28 us
    pallas_call x2, Pallas kernels, summed(): pl.pallas_call(functools.partial(sum_kernel, order, stage), out_shape=out...  7.01 us
    pallas_call x1, Pallas kernels, mix(): pl.pallas_call(functools.partial(mix_kernel, split), out_shape=[pltpu.VME...  3.95 us
    add x3, other arithmetic, per_device(): sigma = lax.optimization_barrier(sigma) + other.astype(jnp.float32)  0.78 us
  transfers between devices with their start and end apart: 10, of which 4 were waited for; matrix products, arithmetic and copies ran while one was open for 1% of the time, Pallas kernels for 21%

profile of v22, /device:TPU:0, one launch (start us, length us, event | category | flops | bytes accessed | tf_op | source)
XLA Modules:
  0.0 36.1 jit_solution(12933214979336371009)
XLA Ops:
  0.0 0.7 %select_bitcast_fusion = f32[4,32]{1,0:T(4,128)S(1)} fusion(f32[32,4]{0,1:T(4,128)} %param.9, s32[32,4]{0,1:T(4,128)} %param.10), kind=kLoop, calls=%fused_computation.8 | loop fusion | flops 256 | bytes 1536 | tf_op jit(solution)/shard_map/jit(_where)/select_n | solution.py:202
  0.7 5.0 %collective-permute-start.2 = (f32[4,32]{1,0:T(4,128)S(1)}, f32[4,32]{1,0:T(4,128)S(1)}, u32[]{:S(2)}, u32[]{:S(2)}) collective-permute-start(f32[4,32]{1,0:T(4,128)S(1)} %select_bitcast_fusion), channel_id=1, source_target_pairs={{0,12},{4,8},{8,4},{12,0},{1,13},{5,9},{9,5},{13,1},{2,14},{6,10},... | collective-permute-start | bytes 1544 | tf_op jit(solution)/shard_map/ppermute | solution.py:192
  5.8 0.0 collective-permute-start.1
  5.8 0.6 %collective-permute-start = (f32[4,32]{1,0:T(4,128)S(1)}, f32[4,32]{1,0:T(4,128)S(1)}, u32[]{:S(2)}, u32[]{:S(2)}) collective-permute-start(f32[4,32]{1,0:T(4,128)S(1)} %select_bitcast_fusion), channel_id=1, source_target_pairs={{0,4},{4,0},{8,12},{12,8},{1,5},{5,1},{9,13},{13,9},{2,6},{6,2},{1... | collective-permute-start | bytes 1544 | tf_op jit(solution)/shard_map/ppermute | solution.py:192
  6.3 4.0 %shard_map.64 = (bf16[32,4,128,256]{3,2,1,0:T(8,128)(2,1)S(1)}, bf16[32,256,256]{2,1,0:T(8,128)(2,1)S(1)}) custom-call(bf16[4,256,256]{2,1,0:T(8,128)(2,1)} %wave_ref.1, bf16[32,128,256]{2,1,0:T(8,128)(2,1)} %left_ref.1, bf16[32,256,256]{2,1,0:T(8,128)(2,1)} %right_ref.1), custom_call_target="tpu_custom_call" | custom-call | flops 2147483648 | bytes 6291456 | tf_op jit(solution)/shard_map/pallas_call | solution.py:69
  10.3 0.0 collective-permute-done.2
  10.3 0.0 collective-permute-done.1
  10.3 0.0 collective-permute-done
  10.3 3.6 %shard_map.65 = (f32[16,128,128]{2,1,0:T(8,128)S(1)}, f32[16,128,128]{2,1,0:T(8,128)S(1)}, f32[4,128,128]{2,1,0:T(8,128)S(1)}, bf16[4,128,128]{2,1,0:T(8,128)(2,1)S(1)}) custom-call(s32[32]{0:T(128)} %shift_ref.3, f32[16,32]{1,0:T(8,128)S(1)} %pad_maximum_fusion.coef_ref, bf16[32,4,128,256]{3,2,1,0:T(8,128)(2,1)S(1)} %get-tuple-element.24.mixed_ref, ...), custom_call_target="tpu_custom_call" | custom-call | flops 1073741824 | bytes 6291456 | tf_op jit(solution)/shard_map/pallas_call | solution.py:170
  13.9 1.8 %collective-permute-start.3 = (bf16[4,128,128]{2,1,0:T(8,128)(2,1)S(1)}, bf16[4,128,128]{2,1,0:T(8,128)(2,1)S(1)}, u32[]{:S(2)}, u32[]{:S(2)}) collective-permute-start(bf16[4,128,128]{2,1,0:T(8,128)(2,1)S(1)} %get-tuple-element.26), channel_id=1, source_target_pairs={{0,2},{2,0},{1,3},{3,1},{4,6},{6,4},{5,7},{7,5},{8,10},{10,8},{9,1... | collective-permute-start | bytes 393224 | tf_op jit(solution)/shard_map/ppermute | solution.py:192
  15.7 3.5 %shard_map.66 = (f32[16,128,128]{2,1,0:T(8,128)S(1)}, f32[16,128,128]{2,1,0:T(8,128)S(1)}, f32[4,128,128]{2,1,0:T(8,128)S(1)}, bf16[4,128,128]{2,1,0:T(8,128)(2,...) custom-call(s32[32]{0:T(128)} %shift_ref.3, ...), custom_call_target="tpu_custom_call", output_to_operand_aliasing={{0}: (4, {}), {1}: (5, {})} | custom-call | flops 1073741824 | bytes 6291456 | tf_op jit(solution)/shard_map/pallas_call | solution.py:170
  19.1 0.4 %collective-permute-start.6 = (bf16[4,128,128]{2,1,0:T(8,128)(2,1)S(1)}, bf16[4,128,128]{2,1,0:T(8,128)(2,1)S(1)}, u32[]{:S(2)}, u32[]{:S(2)}) collective-permute-start(bf16[4,128,128]{2,1,0:T(8,128)(2,1)S(1)} %get-tuple-element.37), channel_id=1, source_target_pairs={{0,2},{2,0},{1,3},{3,1},{4,6},{6,4},{5,7},{7,5},{8,10},{10,8},{9,1... | collective-permute-start | bytes 393224 | tf_op jit(solution)/shard_map/ppermute | solution.py:192
  19.5 0.0 collective-permute-done.3
  19.6 2.4 %collective-permute-start.4 = (bf16[4,128,128]{2,1,0:T(8,128)(2,1)S(1)}, bf16[4,128,128]{2,1,0:T(8,128)(2,1)S(1)}, u32[]{:S(2)}, u32[]{:S(2)}) collective-permute-start(bf16[4,128,128]{2,1,0:T(8,128)(2,1)S(1)} %add_convert_fusion.2), channel_id=1, source_target_pairs={{0,8},{4,12},{8,0},{12,4},{1,9},{5,13},{9,1},{13,5},{2,10},{6,14},... | collective-permute-start | bytes 393224 | tf_op jit(solution)/shard_map/ppermute | solution.py:192
  22.0 2.2 %collective-permute-done.6 = bf16[4,128,128]{2,1,0:T(8,128)(2,1)S(1)} collective-permute-done((bf16[4,128,128]{2,1,0:T(8,128)(2,1)S(1)}, bf16[4,128,128]{2,1,0:T(8,128)(2,1)S(1)}, u32[]{:S(2)}, u32[]{:S(2)}) %collective-permute-start.6) | collective-permute-done | bytes 131104 | tf_op jit(solution)/shard_map/ppermute | solution.py:192
  24.2 0.3 collective-permute-start.5
  24.5 3.9 %collective-permute-start.8 = (bf16[4,128,128]{2,1,0:T(8,128)(2,1)S(1)}, bf16[4,128,128]{2,1,0:T(8,128)(2,1)S(1)}, u32[]{:S(2)}, u32[]{:S(2)}) collective-permute-start(bf16[4,128,128]{2,1,0:T(8,128)(2,1)S(1)} %add_convert_fusion.1), channel_id=1, source_target_pairs={{0,12},{4,8},{8,4},{12,0},{1,13},{5,9},{9,5},{13,1},{2,14},{6,10},... | collective-permute-start | bytes 393224 | tf_op jit(solution)/shard_map/ppermute | solution.py:192
  28.4 1.5 %collective-permute-start.7 = (bf16[4,128,128]{2,1,0:T(8,128)(2,1)S(1)}, bf16[4,128,128]{2,1,0:T(8,128)(2,1)S(1)}, u32[]{:S(2)}, u32[]{:S(2)}) collective-permute-start(bf16[4,128,128]{2,1,0:T(8,128)(2,1)S(1)} %get-tuple-element.42), channel_id=1, source_target_pairs={{0,2},{2,0},{1,3},{3,1},{4,6},{6,4},{5,7},{7,5},{8,10},{10,8},{9,1... | collective-permute-start | bytes 393224 | tf_op jit(solution)/shard_map/ppermute | solution.py:192
  29.9 0.4 collective-permute-done.5
  30.3 0.2 collective-permute-start.9
  30.5 0.0 collective-permute-done.4
  30.5 2.8 %collective-permute-done.7 = bf16[4,128,128]{2,1,0:T(8,128)(2,1)S(1)} collective-permute-done((bf16[4,128,128]{2,1,0:T(8,128)(2,1)S(1)}, bf16[4,128,128]{2,1,0:T(8,128)(2,1)S(1)}, u32[]{:S(2)}, u32[]{:S(2)}) %collective-permute-start.7) | collective-permute-done | bytes 131104 | tf_op jit(solution)/shard_map/ppermute | solution.py:192
  33.4 0.0 collective-permute-done.8
  33.4 1.9 %collective-permute-done.9 = bf16[4,128,128]{2,1,0:T(8,128)(2,1)S(1)} collective-permute-done((bf16[4,128,128]{2,1,0:T(8,128)(2,1)S(1)}, bf16[4,128,128]{2,1,0:T(8,128)(2,1)S(1)}, u32[]{:S(2)}, u32[]{:S(2)}) %collective-permute-start.9) | collective-permute-done | bytes 131104 | tf_op jit(solution)/shard_map/ppermute | solution.py:192
  35.3 0.7 %convert_add_fusion = f32[4,128,128]{2,1,0:T(8,128)} fusion(f32[4,128,128]{2,1,0:T(8,128)S(1)} %convert_add_fusion.1, bf16[4,128,128]{2,1,0:T(8,128)(2,1)S(1)} %collective-permute-done.9), kind=kLoop, calls=%fused_computation | loop fusion | flops 131072 | bytes 655360 | tf_op jit(solution)/shard_map/add | solution.py:225
  (7 shorter events, 0.2 us)
Async XLA Ops:
  0.7 9.6 %collective-permute-start.2 = (f32[4,32]{1,0:T(4,128)S(1)}, f32[4,32]{1,0:T(4,128)S(1)}, u32[]{:S(2)}, u32[]{:S(2)}) collective-permute-start(f32[4,32]{1,0:T(4,128)S(1)} %select_bitcast_fusion), channel_id=1, source_target_pairs={{0,12},{4,8},{8,4},{12,0},{1,13},{5,9},{9,5},{13,1},{2,14},{6,10},... | collective-permute-start | bytes 1544 | tf_op jit(solution)/shard_map/ppermute | solution.py:192
  5.8 4.5 %collective-permute-start.1 = (f32[4,32]{1,0:T(4,128)S(1)}, f32[4,32]{1,0:T(4,128)S(1)}, u32[]{:S(2)}, u32[]{:S(2)}) collective-permute-start(f32[4,32]{1,0:T(4,128)S(1)} %select_bitcast_fusion), channel_id=1, source_target_pairs={{0,8},{4,12},{8,0},{12,4},{1,9},{5,13},{9,1},{13,5},{2,10},{6,14},... | collective-permute-start | bytes 1544 | tf_op jit(solution)/shard_map/ppermute | solution.py:192
  5.8 4.5 %collective-permute-start = (f32[4,32]{1,0:T(4,128)S(1)}, f32[4,32]{1,0:T(4,128)S(1)}, u32[]{:S(2)}, u32[]{:S(2)}) collective-permute-start(f32[4,32]{1,0:T(4,128)S(1)} %select_bitcast_fusion), channel_id=1, source_target_pairs={{0,4},{4,0},{8,12},{12,8},{1,5},{5,1},{9,13},{13,9},{2,6},{6,2},{1... | collective-permute-start | bytes 1544 | tf_op jit(solution)/shard_map/ppermute | solution.py:192
  13.9 5.6 %collective-permute-start.3 = (bf16[4,128,128]{2,1,0:T(8,128)(2,1)S(1)}, bf16[4,128,128]{2,1,0:T(8,128)(2,1)S(1)}, u32[]{:S(2)}, u32[]{:S(2)}) collective-permute-start(bf16[4,128,128]{2,1,0:T(8,128)(2,1)S(1)} %get-tuple-element.26), channel_id=1, source_target_pairs={{0,2},{2,0},{1,3},{3,1},{4,6},{6,4},{5,7},{7,5},{8,10},{10,8},{9,1... | collective-permute-start | bytes 393224 | tf_op jit(solution)/shard_map/ppermute | solution.py:192
  19.1 5.0 %collective-permute-start.6 = (bf16[4,128,128]{2,1,0:T(8,128)(2,1)S(1)}, bf16[4,128,128]{2,1,0:T(8,128)(2,1)S(1)}, u32[]{:S(2)}, u32[]{:S(2)}) collective-permute-start(bf16[4,128,128]{2,1,0:T(8,128)(2,1)S(1)} %get-tuple-element.37), channel_id=1, source_target_pairs={{0,2},{2,0},{1,3},{3,1},{4,6},{6,4},{5,7},{7,5},{8,10},{10,8},{9,1... | collective-permute-start | bytes 393224 | tf_op jit(solution)/shard_map/ppermute | solution.py:192
  19.6 10.9 %collective-permute-start.4 = (bf16[4,128,128]{2,1,0:T(8,128)(2,1)S(1)}, bf16[4,128,128]{2,1,0:T(8,128)(2,1)S(1)}, u32[]{:S(2)}, u32[]{:S(2)}) collective-permute-start(bf16[4,128,128]{2,1,0:T(8,128)(2,1)S(1)} %add_convert_fusion.2), channel_id=1, source_target_pairs={{0,8},{4,12},{8,0},{12,4},{1,9},{5,13},{9,1},{13,5},{2,10},{6,14},... | collective-permute-start | bytes 393224 | tf_op jit(solution)/shard_map/ppermute | solution.py:192
  24.2 6.1 %collective-permute-start.5 = (bf16[4,128,128]{2,1,0:T(8,128)(2,1)S(1)}, bf16[4,128,128]{2,1,0:T(8,128)(2,1)S(1)}, u32[]{:S(2)}, u32[]{:S(2)}) collective-permute-start(bf16[4,128,128]{2,1,0:T(8,128)(2,1)S(1)} %get-tuple-element.36), channel_id=1, source_target_pairs={{0,2},{2,0},{1,3},{3,1},{4,6},{6,4},{5,7},{7,5},{8,10},{10,8},{9,1... | collective-permute-start | bytes 393224 | tf_op jit(solution)/shard_map/ppermute | solution.py:192
  24.5 8.9 %collective-permute-start.8 = (bf16[4,128,128]{2,1,0:T(8,128)(2,1)S(1)}, bf16[4,128,128]{2,1,0:T(8,128)(2,1)S(1)}, u32[]{:S(2)}, u32[]{:S(2)}) collective-permute-start(bf16[4,128,128]{2,1,0:T(8,128)(2,1)S(1)} %add_convert_fusion.1), channel_id=1, source_target_pairs={{0,12},{4,8},{8,4},{12,0},{1,13},{5,9},{9,5},{13,1},{2,14},{6,10},... | collective-permute-start | bytes 393224 | tf_op jit(solution)/shard_map/ppermute | solution.py:192
  28.4 5.0 %collective-permute-start.7 = (bf16[4,128,128]{2,1,0:T(8,128)(2,1)S(1)}, bf16[4,128,128]{2,1,0:T(8,128)(2,1)S(1)}, u32[]{:S(2)}, u32[]{:S(2)}) collective-permute-start(bf16[4,128,128]{2,1,0:T(8,128)(2,1)S(1)} %get-tuple-element.42), channel_id=1, source_target_pairs={{0,2},{2,0},{1,3},{3,1},{4,6},{6,4},{5,7},{7,5},{8,10},{10,8},{9,1... | collective-permute-start | bytes 393224 | tf_op jit(solution)/shard_map/ppermute | solution.py:192
  30.3 5.0 %collective-permute-start.9 = (bf16[4,128,128]{2,1,0:T(8,128)(2,1)S(1)}, bf16[4,128,128]{2,1,0:T(8,128)(2,1)S(1)}, u32[]{:S(2)}, u32[]{:S(2)}) collective-permute-start(bf16[4,128,128]{2,1,0:T(8,128)(2,1)S(1)} %add_convert_fusion), channel_id=1, source_target_pairs={{0,4},{4,0},{8,12},{12,8},{1,5},{5,1},{9,13},{13,9},{2,6},{6,2},{1... | collective-permute-start | bytes 393224 | tf_op jit(solution)/shard_map/ppermute | solution.py:192

commit v23 on v14

--- a/solution.py
+++ b/solution.py
@@ -212,15 +212,14 @@
         )
         both_2 = (mine_2 + after(crossed_2, mine_1).astype(jnp.float32)).astype(jnp.bfloat16)
         arrived_2 = shift_by(both_2, "sector", 2)
-        crossed_1 = shift_by(after(theirs_1, both_2), "op", 1)
-        crossed_3 = shift_by(after(theirs_3, both_2), "op", 1)
-        both_1 = (mine_1 + after(crossed_1, both_2).astype(jnp.float32)).astype(jnp.bfloat16)
+        crossed = shift_by(jnp.concatenate([theirs_1, theirs_3], axis=0), "op", 1)
+        both_1 = (mine_1 + after(crossed, both_2)[:sec_dev].astype(jnp.float32)).astype(jnp.bfloat16)
         arrived_1 = shift_by(both_1, "sector", 1)
-        crossed_0 = shift_by(after(theirs_0, both_1), "op", 1)
-        both_3 = (mine_3 + after(crossed_3, both_1).astype(jnp.float32)).astype(jnp.bfloat16)
+        both_3 = (mine_3 + after(crossed, both_1)[sec_dev:].astype(jnp.float32)).astype(jnp.bfloat16)
+        crossed_0 = shift_by(after(theirs_0, both_3), "op", 1)
         arrived_3 = shift_by(both_3, "sector", 3)
-        sigma = mine_0 + after(crossed_0, both_3).astype(jnp.float32)
-        for other in (arrived_2, arrived_1, arrived_3):
+        sigma = mine_0 + after(arrived_2, both_3).astype(jnp.float32)
+        for other in (arrived_1, crossed_0, arrived_3):
             sigma = lax.optimization_barrier(sigma) + other.astype(jnp.float32)
         return sigma
 

time: 35.3 us -> 37.7 us (1.068)
  waiting for transfers between devices: 7.95 us -> 10.1 us
  starting transfers between devices: 14.5 us -> 14.9 us
    ppermute x10 -> x9, waiting for transfers between devices: 7.95 us -> 10.1 us  [shift_by(): lax.ppermute(value, axis, [(i, (i + distance) % size) for i in range(size)])]
    ppermute x10 -> x9, starting transfers between devices: 14.5 us -> 14.9 us  [shift_by(): lax.ppermute(value, axis, [(i, (i + distance) % size) for i in range(size)])]
  transfers between devices with their start and end apart: 10 -> 9, of which waited for: 5 -> 3; matrix products, arithmetic and copies ran while one was open for 0% -> 1% of each run, Pallas kernels for 22% -> 22%
where the time goes in v23:
time: 37.7 us
  starting transfers between devices  14.9 us (40%)
  Pallas kernels  11 us (29%)
  waiting for transfers between devices  10.1 us (27%)
  other arithmetic  1.65 us (4%)
    ppermute x9, starting transfers between devices, shift_by(): lax.ppermute(value, axis, [(i, (i + distance) % size) for i in range(size)])  14.9 us
    ppermute x9, waiting for transfers between devices, shift_by(): lax.ppermute(value, axis, [(i, (i + distance) % size) for i in range(size)])  10.1 us
    pallas_call x2, Pallas kernels, summed(): pl.pallas_call(functools.partial(sum_kernel, order, stage), out_shape=out...  7.09 us
    pallas_call x1, Pallas kernels, mix(): pl.pallas_call(functools.partial(mix_kernel, split), out_shape=[pltpu.VME...  3.95 us
    add x3, other arithmetic, per_device(): sigma = lax.optimization_barrier(sigma) + other.astype(jnp.float32)  0.79 us
  transfers between devices with their start and end apart: 9, of which 3 were waited for; matrix products, arithmetic and copies ran while one was open for 1% of the time, Pallas kernels for 22%

profile of v23, /device:TPU:0, one launch (start us, length us, event | category | flops | bytes accessed | tf_op | source)
XLA Modules:
  0.0 37.7 jit_solution(10760336020433555966)
XLA Ops:
  0.0 0.7 %select_bitcast_fusion = f32[4,32]{1,0:T(4,128)S(1)} fusion(f32[32,4]{0,1:T(4,128)} %param.9, s32[32,4]{0,1:T(4,128)} %param.10), kind=kLoop, calls=%fused_computation.9 | loop fusion | flops 256 | bytes 1536 | tf_op jit(solution)/shard_map/jit(_where)/select_n | solution.py:200
  0.7 3.0 %collective-permute-start.2 = (f32[4,32]{1,0:T(4,128)S(1)}, f32[4,32]{1,0:T(4,128)S(1)}, u32[]{:S(2)}, u32[]{:S(2)}) collective-permute-start(f32[4,32]{1,0:T(4,128)S(1)} %select_bitcast_fusion), channel_id=1, source_target_pairs={{0,4},{4,8},{8,12},{12,0},{1,5},{5,9},{9,13},{13,1},{2,6},{6,10},{... | collective-permute-start | bytes 1544 | tf_op jit(solution)/shard_map/ppermute | solution.py:190
  3.7 2.6 %collective-permute-start.1 = (f32[4,32]{1,0:T(4,128)S(1)}, f32[4,32]{1,0:T(4,128)S(1)}, u32[]{:S(2)}, u32[]{:S(2)}) collective-permute-start(f32[4,32]{1,0:T(4,128)S(1)} %select_bitcast_fusion), channel_id=1, source_target_pairs={{0,8},{4,12},{8,0},{12,4},{1,9},{5,13},{9,1},{13,5},{2,10},{6,14},... | collective-permute-start | bytes 1544 | tf_op jit(solution)/shard_map/ppermute | solution.py:190
  6.3 1.3 %collective-permute-start = (f32[4,32]{1,0:T(4,128)S(1)}, f32[4,32]{1,0:T(4,128)S(1)}, u32[]{:S(2)}, u32[]{:S(2)}) collective-permute-start(f32[4,32]{1,0:T(4,128)S(1)} %select_bitcast_fusion), channel_id=1, source_target_pairs={{0,12},{4,0},{8,4},{12,8},{1,13},{5,1},{9,5},{13,9},{2,14},{6,2},{... | collective-permute-start | bytes 1544 | tf_op jit(solution)/shard_map/ppermute | solution.py:190
  7.7 4.0 %shard_map.64 = (bf16[32,4,128,256]{3,2,1,0:T(8,128)(2,1)S(1)}, bf16[32,256,256]{2,1,0:T(8,128)(2,1)S(1)}) custom-call(bf16[4,256,256]{2,1,0:T(8,128)(2,1)} %wave_ref.1, bf16[32,128,256]{2,1,0:T(8,128)(2,1)} %left_ref.1, bf16[32,256,256]{2,1,0:T(8,128)(2,1)} %right_ref.1), custom_call_target="tpu_custom_call" | custom-call | flops 2147483648 | bytes 6291456 | tf_op jit(solution)/shard_map/pallas_call | solution.py:69
  11.6 0.0 collective-permute-done.2
  11.6 0.0 collective-permute-done.1
  11.6 0.0 collective-permute-done
  11.7 2.8 %shard_map.65 = (f32[16,128,128]{2,1,0:T(8,128)S(1)}, f32[16,128,128]{2,1,0:T(8,128)S(1)}, f32[4,128,128]{2,1,0:T(8,128)S(1)}, bf16[4,128,128]{2,1,0:T(8,128)(2,1)S(1)}) custom-call(s32[32]{0:T(128)} %shift_ref.3, f32[16,32]{1,0:T(8,128)S(1)} %pad_maximum_fusion.1.coef_ref, bf16[32,4,128,256]{3,2,1,0:T(8,128)(2,1)S(1)} %get-tuple-element.23.mixed_ref, ...), custom_call_target="tpu_custom_call" | custom-call | flops 1073741824 | bytes 6291456 | tf_op jit(solution)/shard_map/pallas_call | solution.py:167
  14.4 2.1 %collective-permute-start.3 = (bf16[4,128,128]{2,1,0:T(8,128)(2,1)S(1)}, bf16[4,128,128]{2,1,0:T(8,128)(2,1)S(1)}, u32[]{:S(2)}, u32[]{:S(2)}) collective-permute-start(bf16[4,128,128]{2,1,0:T(8,128)(2,1)S(1)} %get-tuple-element.25), channel_id=1, source_target_pairs={{0,2},{2,0},{1,3},{3,1},{4,6},{6,4},{5,7},{7,5},{8,10},{10,8},{9,1... | collective-permute-start | bytes 393224 | tf_op jit(solution)/shard_map/ppermute | solution.py:190
  16.6 4.3 %shard_map.66 = (f32[16,128,128]{2,1,0:T(8,128)S(1)}, f32[16,128,128]{2,1,0:T(8,128)S(1)}, f32[4,128,128]{2,1,0:T(8,128)S(1)}, bf16[4,128,128]{2,1,0:T(8,128)(2,...) custom-call(s32[32]{0:T(128)} %shift_ref.3, ...), custom_call_target="tpu_custom_call", output_to_operand_aliasing={{0}: (4, {}), {1}: (5, {})} | custom-call | flops 1073741824 | bytes 6291456 | tf_op jit(solution)/shard_map/pallas_call | solution.py:167
  20.9 0.1 collective-permute-start.5
  21.0 0.0 collective-permute-done.3
  21.1 0.4 %collective-permute-start.4 = (bf16[4,128,128]{2,1,0:T(8,128)(2,1)S(1)}, bf16[4,128,128]{2,1,0:T(8,128)(2,1)S(1)}, u32[]{:S(2)}, u32[]{:S(2)}) collective-permute-start(bf16[4,128,128]{2,1,0:T(8,128)(2,1)S(1)} %add_convert_fusion.2), channel_id=1, source_target_pairs={{0,8},{4,12},{8,0},{12,4},{1,9},{5,13},{9,1},{13,5},{2,10},{6,14},... | collective-permute-start | bytes 393224 | tf_op jit(solution)/shard_map/ppermute | solution.py:190
  21.5 6.5 %collective-permute-done.5 = bf16[8,128,128]{2,1,0:T(8,128)(2,1)S(1)} collective-permute-done((bf16[8,128,128]{2,1,0:T(8,128)(2,1)S(1)}, bf16[8,128,128]{2,1,0:T(8,128)(2,1)S(1)}, u32[]{:S(2)}, u32[]{:S(2)}) %collective-permute-start.5) | collective-permute-done | bytes 262176 | tf_op jit(solution)/shard_map/ppermute | solution.py:190
  27.9 0.7 %collective-permute-start.6 = (bf16[4,128,128]{2,1,0:T(8,128)(2,1)S(1)}, bf16[4,128,128]{2,1,0:T(8,128)(2,1)S(1)}, u32[]{:S(2)}, u32[]{:S(2)}) collective-permute-start(bf16[4,128,128]{2,1,0:T(8,128)(2,1)S(1)} %add_convert_fusion.1), channel_id=1, source_target_pairs={{0,4},{4,8},{8,12},{12,0},{1,5},{5,9},{9,13},{13,1},{2,6},{6,10},{... | collective-permute-start | bytes 393224 | tf_op jit(solution)/shard_map/ppermute | solution.py:190
  28.7 3.2 %collective-permute-start.8 = (bf16[4,128,128]{2,1,0:T(8,128)(2,1)S(1)}, bf16[4,128,128]{2,1,0:T(8,128)(2,1)S(1)}, u32[]{:S(2)}, u32[]{:S(2)}) collective-permute-start(bf16[4,128,128]{2,1,0:T(8,128)(2,1)S(1)} %add_convert_fusion), channel_id=1, source_target_pairs={{0,12},{4,0},{8,4},{12,8},{1,13},{5,1},{9,5},{13,9},{2,14},{6,2},{... | collective-permute-start | bytes 393224 | tf_op jit(solution)/shard_map/ppermute | solution.py:190
  31.9 0.0 collective-permute-done.4
  31.9 1.4 %collective-permute-start.7 = (bf16[4,128,128]{2,1,0:T(8,128)(2,1)S(1)}, bf16[4,128,128]{2,1,0:T(8,128)(2,1)S(1)}, u32[]{:S(2)}, u32[]{:S(2)}) collective-permute-start(bf16[4,128,128]{2,1,0:T(8,128)(2,1)S(1)} %get-tuple-element.40), channel_id=1, source_target_pairs={{0,2},{2,0},{1,3},{3,1},{4,6},{6,4},{5,7},{7,5},{8,10},{10,8},{9,1... | collective-permute-start | bytes 393224 | tf_op jit(solution)/shard_map/ppermute | solution.py:190
  33.4 1.5 %collective-permute-done.6 = bf16[4,128,128]{2,1,0:T(8,128)(2,1)S(1)} collective-permute-done((bf16[4,128,128]{2,1,0:T(8,128)(2,1)S(1)}, bf16[4,128,128]{2,1,0:T(8,128)(2,1)S(1)}, u32[]{:S(2)}, u32[]{:S(2)}) %collective-permute-start.6) | collective-permute-done | bytes 131104 | tf_op jit(solution)/shard_map/ppermute | solution.py:190
  34.9 2.0 %collective-permute-done.7 = bf16[4,128,128]{2,1,0:T(8,128)(2,1)S(1)} collective-permute-done((bf16[4,128,128]{2,1,0:T(8,128)(2,1)S(1)}, bf16[4,128,128]{2,1,0:T(8,128)(2,1)S(1)}, u32[]{:S(2)}, u32[]{:S(2)}) %collective-permute-start.7) | collective-permute-done | bytes 131104 | tf_op jit(solution)/shard_map/ppermute | solution.py:190
  37.0 0.0 collective-permute-done.8
  37.0 0.7 %convert_add_fusion = f32[4,128,128]{2,1,0:T(8,128)} fusion(f32[4,128,128]{2,1,0:T(8,128)S(1)} %convert_add_fusion.1, bf16[4,128,128]{2,1,0:T(8,128)(2,1)S(1)} %collective-permute-done.8), kind=kLoop, calls=%fused_computation.1 | loop fusion | flops 131072 | bytes 655360 | tf_op jit(solution)/shard_map/add | solution.py:223
  (8 shorter events, 0.2 us)
Async XLA Ops:
  0.7 10.9 %collective-permute-start.2 = (f32[4,32]{1,0:T(4,128)S(1)}, f32[4,32]{1,0:T(4,128)S(1)}, u32[]{:S(2)}, u32[]{:S(2)}) collective-permute-start(f32[4,32]{1,0:T(4,128)S(1)} %select_bitcast_fusion), channel_id=1, source_target_pairs={{0,4},{4,8},{8,12},{12,0},{1,5},{5,9},{9,13},{13,1},{2,6},{6,10},{... | collective-permute-start | bytes 1544 | tf_op jit(solution)/shard_map/ppermute | solution.py:190
  3.7 7.9 %collective-permute-start.1 = (f32[4,32]{1,0:T(4,128)S(1)}, f32[4,32]{1,0:T(4,128)S(1)}, u32[]{:S(2)}, u32[]{:S(2)}) collective-permute-start(f32[4,32]{1,0:T(4,128)S(1)} %select_bitcast_fusion), channel_id=1, source_target_pairs={{0,8},{4,12},{8,0},{12,4},{1,9},{5,13},{9,1},{13,5},{2,10},{6,14},... | collective-permute-start | bytes 1544 | tf_op jit(solution)/shard_map/ppermute | solution.py:190
  6.3 5.3 %collective-permute-start = (f32[4,32]{1,0:T(4,128)S(1)}, f32[4,32]{1,0:T(4,128)S(1)}, u32[]{:S(2)}, u32[]{:S(2)}) collective-permute-start(f32[4,32]{1,0:T(4,128)S(1)} %select_bitcast_fusion), channel_id=1, source_target_pairs={{0,12},{4,0},{8,4},{12,8},{1,13},{5,1},{9,5},{13,9},{2,14},{6,2},{... | collective-permute-start | bytes 1544 | tf_op jit(solution)/shard_map/ppermute | solution.py:190
  14.4 6.6 %collective-permute-start.3 = (bf16[4,128,128]{2,1,0:T(8,128)(2,1)S(1)}, bf16[4,128,128]{2,1,0:T(8,128)(2,1)S(1)}, u32[]{:S(2)}, u32[]{:S(2)}) collective-permute-start(bf16[4,128,128]{2,1,0:T(8,128)(2,1)S(1)} %get-tuple-element.25), channel_id=1, source_target_pairs={{0,2},{2,0},{1,3},{3,1},{4,6},{6,4},{5,7},{7,5},{8,10},{10,8},{9,1... | collective-permute-start | bytes 393224 | tf_op jit(solution)/shard_map/ppermute | solution.py:190
  20.9 7.0 %collective-permute-start.5 = (bf16[8,128,128]{2,1,0:T(8,128)(2,1)S(1)}, bf16[8,128,128]{2,1,0:T(8,128)(2,1)S(1)}, u32[]{:S(2)}, u32[]{:S(2)}) collective-permute-start(bf16[8,128,128]{2,1,0:T(8,128)(2,1)S(1)} %pad_maximum_fusion), channel_id=1, source_target_pairs={{0,2},{2,0},{1,3},{3,1},{4,6},{6,4},{5,7},{7,5},{8,10},{10,8},{9,1... | collective-permute-start | bytes 786440 | tf_op jit(solution)/shard_map/ppermute | solution.py:190
  21.1 10.9 %collective-permute-start.4 = (bf16[4,128,128]{2,1,0:T(8,128)(2,1)S(1)}, bf16[4,128,128]{2,1,0:T(8,128)(2,1)S(1)}, u32[]{:S(2)}, u32[]{:S(2)}) collective-permute-start(bf16[4,128,128]{2,1,0:T(8,128)(2,1)S(1)} %add_convert_fusion.2), channel_id=1, source_target_pairs={{0,8},{4,12},{8,0},{12,4},{1,9},{5,13},{9,1},{13,5},{2,10},{6,14},... | collective-permute-start | bytes 393224 | tf_op jit(solution)/shard_map/ppermute | solution.py:190
  27.9 6.9 %collective-permute-start.6 = (bf16[4,128,128]{2,1,0:T(8,128)(2,1)S(1)}, bf16[4,128,128]{2,1,0:T(8,128)(2,1)S(1)}, u32[]{:S(2)}, u32[]{:S(2)}) collective-permute-start(bf16[4,128,128]{2,1,0:T(8,128)(2,1)S(1)} %add_convert_fusion.1), channel_id=1, source_target_pairs={{0,4},{4,8},{8,12},{12,0},{1,5},{5,9},{9,13},{13,1},{2,6},{6,10},{... | collective-permute-start | bytes 393224 | tf_op jit(solution)/shard_map/ppermute | solution.py:190
  28.7 8.3 %collective-permute-start.8 = (bf16[4,128,128]{2,1,0:T(8,128)(2,1)S(1)}, bf16[4,128,128]{2,1,0:T(8,128)(2,1)S(1)}, u32[]{:S(2)}, u32[]{:S(2)}) collective-permute-start(bf16[4,128,128]{2,1,0:T(8,128)(2,1)S(1)} %add_convert_fusion), channel_id=1, source_target_pairs={{0,12},{4,0},{8,4},{12,8},{1,13},{5,1},{9,5},{13,9},{2,14},{6,2},{... | collective-permute-start | bytes 393224 | tf_op jit(solution)/shard_map/ppermute | solution.py:190
  31.9 5.0 %collective-permute-start.7 = (bf16[4,128,128]{2,1,0:T(8,128)(2,1)S(1)}, bf16[4,128,128]{2,1,0:T(8,128)(2,1)S(1)}, u32[]{:S(2)}, u32[]{:S(2)}) collective-permute-start(bf16[4,128,128]{2,1,0:T(8,128)(2,1)S(1)} %get-tuple-element.40), channel_id=1, source_target_pairs={{0,2},{2,0},{1,3},{3,1},{4,6},{6,4},{5,7},{7,5},{8,10},{10,8},{9,1... | collective-permute-start | bytes 393224 | tf_op jit(solution)/shard_map/ppermute | solution.py:190

commit v24 on v20

--- a/solution.py
+++ b/solution.py
@@ -212,17 +212,16 @@
             sector_shift, after(coef, theirs_3), mixed, held, order, 1, sums
         )
         both_3 = (mine_3 + after(crossed_3, mine_2).astype(jnp.float32)).astype(jnp.bfloat16)
-        relayed = swap(both_3, "sector", 1)
+        arrived_3 = swap(both_3, "sector", 3)
         crossed_2 = swap(after(theirs_2, both_3), "op", 1)
         crossed_1 = swap(after(theirs_1, both_3), "op", 1)
-        halfway = lax.optimization_barrier(mine_2 + after(crossed_2, both_3).astype(jnp.float32))
-        both_2 = (halfway + relayed.astype(jnp.float32)).astype(jnp.bfloat16)
-        far = swap(both_2, "sector", 2)
-        both_1 = (mine_1 + after(crossed_1, halfway).astype(jnp.float32)).astype(jnp.bfloat16)
-        near = swap(both_1, "sector", 1)
+        both_2 = (mine_2 + after(crossed_2, both_3).astype(jnp.float32)).astype(jnp.bfloat16)
+        arrived_2 = swap(both_2, "sector", 2)
         crossed_0 = swap(after(theirs_0, both_2), "op", 1)
-        sigma = mine_0 + after(near, both_1).astype(jnp.float32)
-        for other in (crossed_0, far):
+        both_1 = (mine_1 + after(crossed_1, both_2).astype(jnp.float32)).astype(jnp.bfloat16)
+        arrived_1 = swap(both_1, "sector", 1)
+        sigma = mine_0 + after(crossed_0, both_1).astype(jnp.float32)
+        for other in (arrived_3, arrived_2, arrived_1):
             sigma = lax.optimization_barrier(sigma) + other.astype(jnp.float32)
         return sigma
 

time: 36.5 us -> 35.8 us (0.981)
  waiting for transfers between devices: 8.41 us -> 5.96 us
  starting transfers between devices: 15.2 us -> 16.9 us
    ppermute x10, waiting for transfers between devices: 8.41 us -> 5.96 us  [swap(): lax.ppermute(value, axis, [(i, i ^ mask) for i in range(lax.axis_size(axi...]
    ppermute x10, starting transfers between devices: 15.2 us -> 16.9 us  [swap(): lax.ppermute(value, axis, [(i, i ^ mask) for i in range(lax.axis_size(axi...]
    add x2 -> x3, other arithmetic: 0.75 us -> 0.78 us  [per_device(): sigma = lax.optimization_barrier(sigma) + other.astype(jnp.float32)]
  transfers between devices with their start and end apart: 10 -> 10, of which waited for: 4 -> 5; matrix products, arithmetic and copies ran while one was open for 0% -> 0% of each run, Pallas kernels for 20% -> 19%
where the time goes in v24:
time: 35.8 us; the launch traced here: 35.6 us
  starting transfers between devices  16.9 us (47%)
  Pallas kernels  11 us (31%)
  waiting for transfers between devices  5.96 us (17%)
  other arithmetic  1.64 us (5%)
    ppermute x10, starting transfers between devices, swap(): lax.ppermute(value, axis, [(i, i ^ mask) for i in range(lax.axis_size(axi...  16.9 us
    pallas_call x2, Pallas kernels, summed(): pl.pallas_call(functools.partial(sum_kernel, order, stage), out_shape=out...  7.02 us
    ppermute x10, waiting for transfers between devices, swap(): lax.ppermute(value, axis, [(i, i ^ mask) for i in range(lax.axis_size(axi...  5.96 us
    pallas_call x1, Pallas kernels, mix(): pl.pallas_call(functools.partial(mix_kernel, split), out_shape=[pltpu.VME...  3.95 us
    add x3, other arithmetic, per_device(): sigma = lax.optimization_barrier(sigma) + other.astype(jnp.float32)  0.78 us
  transfers between devices with their start and end apart: 10, of which 5 were waited for; matrix products, arithmetic and copies ran while one was open for 0% of the time, Pallas kernels for 19%

profile of v24, /device:TPU:0, one launch (start us, length us, event | category | flops | bytes accessed | tf_op | source)
XLA Modules:
  0.0 35.6 jit_solution(2727254562576195507)
XLA Ops:
  0.0 0.7 %select_bitcast_fusion = f32[4,32]{1,0:T(4,128)S(1)} fusion(f32[32,4]{0,1:T(4,128)} %param.9, s32[32,4]{0,1:T(4,128)} %param.10), kind=kLoop, calls=%fused_computation.8 | loop fusion | flops 256 | bytes 1536 | tf_op jit(solution)/shard_map/jit(_where)/select_n | solution.py:202
  0.7 5.0 %collective-permute-start.2 = (f32[4,32]{1,0:T(4,128)S(1)}, f32[4,32]{1,0:T(4,128)S(1)}, u32[]{:S(2)}, u32[]{:S(2)}) collective-permute-start(f32[4,32]{1,0:T(4,128)S(1)} %select_bitcast_fusion), channel_id=1, source_target_pairs={{0,12},{4,8},{8,4},{12,0},{1,13},{5,9},{9,5},{13,1},{2,14},{6,10},... | collective-permute-start | bytes 1544 | tf_op jit(solution)/shard_map/ppermute | solution.py:192
  5.8 0.0 collective-permute-start.1
  5.8 0.6 %collective-permute-start = (f32[4,32]{1,0:T(4,128)S(1)}, f32[4,32]{1,0:T(4,128)S(1)}, u32[]{:S(2)}, u32[]{:S(2)}) collective-permute-start(f32[4,32]{1,0:T(4,128)S(1)} %select_bitcast_fusion), channel_id=1, source_target_pairs={{0,4},{4,0},{8,12},{12,8},{1,5},{5,1},{9,13},{13,9},{2,6},{6,2},{1... | collective-permute-start | bytes 1544 | tf_op jit(solution)/shard_map/ppermute | solution.py:192
  6.3 4.0 %shard_map.64 = (bf16[32,4,128,256]{3,2,1,0:T(8,128)(2,1)S(1)}, bf16[32,256,256]{2,1,0:T(8,128)(2,1)S(1)}) custom-call(bf16[4,256,256]{2,1,0:T(8,128)(2,1)} %wave_ref.1, bf16[32,128,256]{2,1,0:T(8,128)(2,1)} %left_ref.1, bf16[32,256,256]{2,1,0:T(8,128)(2,1)} %right_ref.1), custom_call_target="tpu_custom_call" | custom-call | flops 2147483648 | bytes 6291456 | tf_op jit(solution)/shard_map/pallas_call | solution.py:69
  10.3 0.0 collective-permute-done.2
  10.3 0.0 collective-permute-done.1
  10.3 0.0 collective-permute-done
  10.3 4.1 %shard_map.65 = (f32[16,128,128]{2,1,0:T(8,128)S(1)}, f32[16,128,128]{2,1,0:T(8,128)S(1)}, f32[4,128,128]{2,1,0:T(8,128)S(1)}, bf16[4,128,128]{2,1,0:T(8,128)(2,1)S(1)}) custom-call(s32[32]{0:T(128)} %shift_ref.3, f32[16,32]{1,0:T(8,128)S(1)} %pad_maximum_fusion.coef_ref, bf16[32,4,128,256]{3,2,1,0:T(8,128)(2,1)S(1)} %get-tuple-element.25.mixed_ref, ...), custom_call_target="tpu_custom_call" | custom-call | flops 1073741824 | bytes 6291456 | tf_op jit(solution)/shard_map/pallas_call | solution.py:170
  14.4 1.2 %collective-permute-start.3 = (bf16[4,128,128]{2,1,0:T(8,128)(2,1)S(1)}, bf16[4,128,128]{2,1,0:T(8,128)(2,1)S(1)}, u32[]{:S(2)}, u32[]{:S(2)}) collective-permute-start(bf16[4,128,128]{2,1,0:T(8,128)(2,1)S(1)} %get-tuple-element.27), channel_id=1, source_target_pairs={{0,2},{2,0},{1,3},{3,1},{4,6},{6,4},{5,7},{7,5},{8,10},{10,8},{9,1... | collective-permute-start | bytes 393224 | tf_op jit(solution)/shard_map/ppermute | solution.py:192
  15.7 2.9 %shard_map.66 = (f32[16,128,128]{2,1,0:T(8,128)S(1)}, f32[16,128,128]{2,1,0:T(8,128)S(1)}, f32[4,128,128]{2,1,0:T(8,128)S(1)}, bf16[4,128,128]{2,1,0:T(8,128)(2,...) custom-call(s32[32]{0:T(128)} %shift_ref.3, ...), custom_call_target="tpu_custom_call", output_to_operand_aliasing={{0}: (4, {}), {1}: (5, {})} | custom-call | flops 1073741824 | bytes 6291456 | tf_op jit(solution)/shard_map/pallas_call | solution.py:170
  18.6 0.9 %collective-permute-done.3 = bf16[4,128,128]{2,1,0:T(8,128)(2,1)S(1)} collective-permute-done((bf16[4,128,128]{2,1,0:T(8,128)(2,1)S(1)}, bf16[4,128,128]{2,1,0:T(8,128)(2,1)S(1)}, u32[]{:S(2)}, u32[]{:S(2)}) %collective-permute-start.3) | collective-permute-done | bytes 131104 | tf_op jit(solution)/shard_map/ppermute | solution.py:192
  19.5 1.2 %collective-permute-start.4 = (bf16[4,128,128]{2,1,0:T(8,128)(2,1)S(1)}, bf16[4,128,128]{2,1,0:T(8,128)(2,1)S(1)}, u32[]{:S(2)}, u32[]{:S(2)}) collective-permute-start(bf16[4,128,128]{2,1,0:T(8,128)(2,1)S(1)} %get-tuple-element.37), channel_id=1, source_target_pairs={{0,2},{2,0},{1,3},{3,1},{4,6},{6,4},{5,7},{7,5},{8,10},{10,8},{9,1... | collective-permute-start | bytes 393224 | tf_op jit(solution)/shard_map/ppermute | solution.py:192
  20.7 3.6 %collective-permute-start.7 = (bf16[4,128,128]{2,1,0:T(8,128)(2,1)S(1)}, bf16[4,128,128]{2,1,0:T(8,128)(2,1)S(1)}, u32[]{:S(2)}, u32[]{:S(2)}) collective-permute-start(bf16[4,128,128]{2,1,0:T(8,128)(2,1)S(1)} %add_convert_fusion.2), channel_id=1, source_target_pairs={{0,12},{4,8},{8,4},{12,0},{1,13},{5,9},{9,5},{13,1},{2,14},{6,10},... | collective-permute-start | bytes 393224 | tf_op jit(solution)/shard_map/ppermute | solution.py:192
  24.3 0.5 %collective-permute-start.6 = (bf16[4,128,128]{2,1,0:T(8,128)(2,1)S(1)}, bf16[4,128,128]{2,1,0:T(8,128)(2,1)S(1)}, u32[]{:S(2)}, u32[]{:S(2)}) collective-permute-start(bf16[4,128,128]{2,1,0:T(8,128)(2,1)S(1)} %get-tuple-element.42), channel_id=1, source_target_pairs={{0,2},{2,0},{1,3},{3,1},{4,6},{6,4},{5,7},{7,5},{8,10},{10,8},{9,1... | collective-permute-start | bytes 393224 | tf_op jit(solution)/shard_map/ppermute | solution.py:192
  24.9 0.0 collective-permute-done.4
  24.9 2.1 %collective-permute-start.8 = (bf16[4,128,128]{2,1,0:T(8,128)(2,1)S(1)}, bf16[4,128,128]{2,1,0:T(8,128)(2,1)S(1)}, u32[]{:S(2)}, u32[]{:S(2)}) collective-permute-start(bf16[4,128,128]{2,1,0:T(8,128)(2,1)S(1)} %add_convert_fusion.1), channel_id=1, source_target_pairs={{0,8},{4,12},{8,0},{12,4},{1,9},{5,13},{9,1},{13,5},{2,10},{6,14},... | collective-permute-start | bytes 393224 | tf_op jit(solution)/shard_map/ppermute | solution.py:192
  27.0 1.4 %collective-permute-start.5 = (bf16[4,128,128]{2,1,0:T(8,128)(2,1)S(1)}, bf16[4,128,128]{2,1,0:T(8,128)(2,1)S(1)}, u32[]{:S(2)}, u32[]{:S(2)}) collective-permute-start(bf16[4,128,128]{2,1,0:T(8,128)(2,1)S(1)} %get-tuple-element.39), channel_id=1, source_target_pairs={{0,2},{2,0},{1,3},{3,1},{4,6},{6,4},{5,7},{7,5},{8,10},{10,8},{9,1... | collective-permute-start | bytes 393224 | tf_op jit(solution)/shard_map/ppermute | solution.py:192
  28.4 0.9 %collective-permute-done.6 = bf16[4,128,128]{2,1,0:T(8,128)(2,1)S(1)} collective-permute-done((bf16[4,128,128]{2,1,0:T(8,128)(2,1)S(1)}, bf16[4,128,128]{2,1,0:T(8,128)(2,1)S(1)}, u32[]{:S(2)}, u32[]{:S(2)}) %collective-permute-start.6) | collective-permute-done | bytes 131104 | tf_op jit(solution)/shard_map/ppermute | solution.py:192
  29.4 1.3 %collective-permute-start.9 = (bf16[4,128,128]{2,1,0:T(8,128)(2,1)S(1)}, bf16[4,128,128]{2,1,0:T(8,128)(2,1)S(1)}, u32[]{:S(2)}, u32[]{:S(2)}) collective-permute-start(bf16[4,128,128]{2,1,0:T(8,128)(2,1)S(1)} %add_convert_fusion), channel_id=1, source_target_pairs={{0,4},{4,0},{8,12},{12,8},{1,5},{5,1},{9,13},{13,9},{2,6},{6,2},{1... | collective-permute-start | bytes 393224 | tf_op jit(solution)/shard_map/ppermute | solution.py:192
  30.6 1.4 %collective-permute-done.5 = bf16[4,128,128]{2,1,0:T(8,128)(2,1)S(1)} collective-permute-done((bf16[4,128,128]{2,1,0:T(8,128)(2,1)S(1)}, bf16[4,128,128]{2,1,0:T(8,128)(2,1)S(1)}, u32[]{:S(2)}, u32[]{:S(2)}) %collective-permute-start.5) | collective-permute-done | bytes 131104 | tf_op jit(solution)/shard_map/ppermute | solution.py:192
  32.0 0.0 collective-permute-done.7
  32.1 1.4 %collective-permute-done.8 = bf16[4,128,128]{2,1,0:T(8,128)(2,1)S(1)} collective-permute-done((bf16[4,128,128]{2,1,0:T(8,128)(2,1)S(1)}, bf16[4,128,128]{2,1,0:T(8,128)(2,1)S(1)}, u32[]{:S(2)}, u32[]{:S(2)}) %collective-permute-start.8) | collective-permute-done | bytes 131104 | tf_op jit(solution)/shard_map/ppermute | solution.py:192
  33.5 1.3 %collective-permute-done.9 = bf16[4,128,128]{2,1,0:T(8,128)(2,1)S(1)} collective-permute-done((bf16[4,128,128]{2,1,0:T(8,128)(2,1)S(1)}, bf16[4,128,128]{2,1,0:T(8,128)(2,1)S(1)}, u32[]{:S(2)}, u32[]{:S(2)}) %collective-permute-start.9) | collective-permute-done | bytes 131104 | tf_op jit(solution)/shard_map/ppermute | solution.py:192
  34.9 0.7 %convert_add_fusion = f32[4,128,128]{2,1,0:T(8,128)} fusion(f32[4,128,128]{2,1,0:T(8,128)S(1)} %convert_add_fusion.1, bf16[4,128,128]{2,1,0:T(8,128)(2,1)S(1)} %collective-permute-done.9), kind=kLoop, calls=%fused_computation | loop fusion | flops 131072 | bytes 655360 | tf_op jit(solution)/shard_map/add | solution.py:225
  (7 shorter events, 0.2 us)
Async XLA Ops:
  0.7 9.6 %collective-permute-start.2 = (f32[4,32]{1,0:T(4,128)S(1)}, f32[4,32]{1,0:T(4,128)S(1)}, u32[]{:S(2)}, u32[]{:S(2)}) collective-permute-start(f32[4,32]{1,0:T(4,128)S(1)} %select_bitcast_fusion), channel_id=1, source_target_pairs={{0,12},{4,8},{8,4},{12,0},{1,13},{5,9},{9,5},{13,1},{2,14},{6,10},... | collective-permute-start | bytes 1544 | tf_op jit(solution)/shard_map/ppermute | solution.py:192
  5.8 4.5 %collective-permute-start.1 = (f32[4,32]{1,0:T(4,128)S(1)}, f32[4,32]{1,0:T(4,128)S(1)}, u32[]{:S(2)}, u32[]{:S(2)}) collective-permute-start(f32[4,32]{1,0:T(4,128)S(1)} %select_bitcast_fusion), channel_id=1, source_target_pairs={{0,8},{4,12},{8,0},{12,4},{1,9},{5,13},{9,1},{13,5},{2,10},{6,14},... | collective-permute-start | bytes 1544 | tf_op jit(solution)/shard_map/ppermute | solution.py:192
  5.8 4.5 %collective-permute-start = (f32[4,32]{1,0:T(4,128)S(1)}, f32[4,32]{1,0:T(4,128)S(1)}, u32[]{:S(2)}, u32[]{:S(2)}) collective-permute-start(f32[4,32]{1,0:T(4,128)S(1)} %select_bitcast_fusion), channel_id=1, source_target_pairs={{0,4},{4,0},{8,12},{12,8},{1,5},{5,1},{9,13},{13,9},{2,6},{6,2},{1... | collective-permute-start | bytes 1544 | tf_op jit(solution)/shard_map/ppermute | solution.py:192
  14.4 5.0 %collective-permute-start.3 = (bf16[4,128,128]{2,1,0:T(8,128)(2,1)S(1)}, bf16[4,128,128]{2,1,0:T(8,128)(2,1)S(1)}, u32[]{:S(2)}, u32[]{:S(2)}) collective-permute-start(bf16[4,128,128]{2,1,0:T(8,128)(2,1)S(1)} %get-tuple-element.27), channel_id=1, source_target_pairs={{0,2},{2,0},{1,3},{3,1},{4,6},{6,4},{5,7},{7,5},{8,10},{10,8},{9,1... | collective-permute-start | bytes 393224 | tf_op jit(solution)/shard_map/ppermute | solution.py:192
  19.5 5.4 %collective-permute-start.4 = (bf16[4,128,128]{2,1,0:T(8,128)(2,1)S(1)}, bf16[4,128,128]{2,1,0:T(8,128)(2,1)S(1)}, u32[]{:S(2)}, u32[]{:S(2)}) collective-permute-start(bf16[4,128,128]{2,1,0:T(8,128)(2,1)S(1)} %get-tuple-element.37), channel_id=1, source_target_pairs={{0,2},{2,0},{1,3},{3,1},{4,6},{6,4},{5,7},{7,5},{8,10},{10,8},{9,1... | collective-permute-start | bytes 393224 | tf_op jit(solution)/shard_map/ppermute | solution.py:192
  20.7 11.3 %collective-permute-start.7 = (bf16[4,128,128]{2,1,0:T(8,128)(2,1)S(1)}, bf16[4,128,128]{2,1,0:T(8,128)(2,1)S(1)}, u32[]{:S(2)}, u32[]{:S(2)}) collective-permute-start(bf16[4,128,128]{2,1,0:T(8,128)(2,1)S(1)} %add_convert_fusion.2), channel_id=1, source_target_pairs={{0,12},{4,8},{8,4},{12,0},{1,13},{5,9},{9,5},{13,1},{2,14},{6,10},... | collective-permute-start | bytes 393224 | tf_op jit(solution)/shard_map/ppermute | solution.py:192
  24.3 5.0 %collective-permute-start.6 = (bf16[4,128,128]{2,1,0:T(8,128)(2,1)S(1)}, bf16[4,128,128]{2,1,0:T(8,128)(2,1)S(1)}, u32[]{:S(2)}, u32[]{:S(2)}) collective-permute-start(bf16[4,128,128]{2,1,0:T(8,128)(2,1)S(1)} %get-tuple-element.42), channel_id=1, source_target_pairs={{0,2},{2,0},{1,3},{3,1},{4,6},{6,4},{5,7},{7,5},{8,10},{10,8},{9,1... | collective-permute-start | bytes 393224 | tf_op jit(solution)/shard_map/ppermute | solution.py:192
  24.9 8.6 %collective-permute-start.8 = (bf16[4,128,128]{2,1,0:T(8,128)(2,1)S(1)}, bf16[4,128,128]{2,1,0:T(8,128)(2,1)S(1)}, u32[]{:S(2)}, u32[]{:S(2)}) collective-permute-start(bf16[4,128,128]{2,1,0:T(8,128)(2,1)S(1)} %add_convert_fusion.1), channel_id=1, source_target_pairs={{0,8},{4,12},{8,0},{12,4},{1,9},{5,13},{9,1},{13,5},{2,10},{6,14},... | collective-permute-start | bytes 393224 | tf_op jit(solution)/shard_map/ppermute | solution.py:192
  27.0 5.0 %collective-permute-start.5 = (bf16[4,128,128]{2,1,0:T(8,128)(2,1)S(1)}, bf16[4,128,128]{2,1,0:T(8,128)(2,1)S(1)}, u32[]{:S(2)}, u32[]{:S(2)}) collective-permute-start(bf16[4,128,128]{2,1,0:T(8,128)(2,1)S(1)} %get-tuple-element.39), channel_id=1, source_target_pairs={{0,2},{2,0},{1,3},{3,1},{4,6},{6,4},{5,7},{7,5},{8,10},{10,8},{9,1... | collective-permute-start | bytes 393224 | tf_op jit(solution)/shard_map/ppermute | solution.py:192
  29.4 5.5 %collective-permute-start.9 = (bf16[4,128,128]{2,1,0:T(8,128)(2,1)S(1)}, bf16[4,128,128]{2,1,0:T(8,128)(2,1)S(1)}, u32[]{:S(2)}, u32[]{:S(2)}) collective-permute-start(bf16[4,128,128]{2,1,0:T(8,128)(2,1)S(1)} %add_convert_fusion), channel_id=1, source_target_pairs={{0,4},{4,0},{8,12},{12,8},{1,5},{5,1},{9,13},{13,9},{2,6},{6,2},{1... | collective-permute-start | bytes 393224 | tf_op jit(solution)/shard_map/ppermute | solution.py:192

commit v25 on v14

--- a/solution.py
+++ b/solution.py
@@ -18,7 +18,8 @@
     return lax.rem(value + size, size)
 
 
-def mix_kernel(split, wave_ref, left_ref, right_ref, mixed_ref, held_ref, wave, left, sems):
+def mix_kernel(split, wave_ref, left_ref, right_ref, mixed_ref, held_ref, *refs):
+    *zeros, wave, left, sems = refs
     sec_dev = wave.shape[0]
     terms, rows, width = left.shape
     chunks = terms // MIX_TERMS
@@ -48,6 +49,8 @@
         right_copies = [pltpu.make_async_copy(right_ref, held_ref, sems.at[1])]
     for copy in right_copies:
         copy.start()
+    for ref in zeros:
+        ref[...] = jnp.zeros_like(ref)
     wave_copy.wait()
 
     @pl.loop(0, chunks)
@@ -63,17 +66,19 @@
         copy.wait()
 
 
-def mix(wavefunction, left_ops, right_ops, split):
+def mix(wavefunction, left_ops, right_ops, targets, split):
     k_dev, rows, width = left_ops.shape
     sec_dev = wavefunction.shape[0]
+    zeros = [pltpu.VMEM((targets, rows, width // 2), jnp.float32)] * (2 if split else 0)
     return pl.pallas_call(
         functools.partial(mix_kernel, split),
         out_shape=[
             pltpu.VMEM((k_dev, sec_dev, rows, width), jnp.bfloat16),
             pltpu.VMEM(right_ops.shape, jnp.bfloat16),
-        ],
+        ]
+        + zeros,
         in_specs=[pl.BlockSpec(memory_space=pltpu.HBM)] * 3,
-        out_specs=[pl.BlockSpec(memory_space=pltpu.VMEM)] * 2,
+        out_specs=[pl.BlockSpec(memory_space=pltpu.VMEM)] * (2 + len(zeros)),
         scratch_shapes=[
             pltpu.VMEM(wavefunction.shape, jnp.bfloat16),
             pltpu.VMEM(left_ops.shape, jnp.bfloat16),
@@ -110,19 +115,15 @@
                 wanted &= reaches(shift_ref[k], groups[0], sec_dev, targets)
         return count + jnp.where(wanted, 1, 0)
 
-    count = lax.fori_loop(0, terms, pick, 0)
+    count = lax.fori_loop(0, terms, pick, 0, unroll=8)
     for i in range(SUM_TERMS):
         picked[count + i] = 0
 
     if stage is None:
         sums = refs[:1]
-    elif stage == 0:
-        sums, outs = refs[:2], refs[2:-1]
+        sums[0][...] = jnp.zeros_like(sums[0])
     else:
         sums, outs = refs[2:4], refs[4:-1]
-    if not stage:
-        for total in sums:
-            total[...] = jnp.zeros_like(total)
 
     @pl.loop(0, lax.div(count + SUM_TERMS - 1, SUM_TERMS))
     def _(step):
@@ -199,13 +200,15 @@
     devices = lax.axis_size("sector")
     live = jnp.where(coupled.T > 0, site_coef.T, 0.0)
     split = lax.axis_size("op") == 2 and devices == 4
-    mixed, held = mix(wavefunction, left_ops, right_ops, split)
+    mixed, held, *sums = mix(
+        wavefunction, left_ops, right_ops, sec_dev * devices, split
+    )
 
     if split:
         coefs = [live] + [shift_by(live, "sector", -g) for g in range(1, devices)]
         coef = jnp.concatenate(coefs, axis=0)
         order = ((2,), (1, 3, 0))
-        *sums, mine_2, theirs_2 = summed(sector_shift, coef, mixed, held, order, 0)
+        *sums, mine_2, theirs_2 = summed(sector_shift, coef, mixed, held, order, 0, sums)
         crossed_2 = shift_by(theirs_2, "op", 1)
         _, _, mine_1, theirs_1, mine_3, theirs_3, mine_0, theirs_0 = summed(
             sector_shift, after(coef, theirs_2), mixed, held, order, 1, sums

time: 35.3 us -> 35.3 us (level); the launches traced: 35.2 us -> 34.8 us
  waiting for transfers between devices: 7.95 us -> 7.23 us
  starting transfers between devices: 14.5 us -> 15.2 us
  Pallas kernels: 11 us -> 10.6 us
    ppermute x10, starting transfers between devices: 14.5 us -> 15.2 us  [shift_by(): lax.ppermute(value, axis, [(i, (i + distance) % size) for i in range(size)])]
    ppermute x10, waiting for transfers between devices: 7.95 us -> 7.23 us  [shift_by(): lax.ppermute(value, axis, [(i, (i + distance) % size) for i in range(size)])]
    pallas_call x2, Pallas kernels: 7.09 us -> 6.66 us  [summed(): pl.pallas_call(functools.partial(sum_kernel, order, stage), out_shape=out...]
where the time goes in v25:
time: 35.3 us; the launch traced here: 34.8 us
  starting transfers between devices  15.2 us (43%)
  Pallas kernels  10.6 us (30%)
  waiting for transfers between devices  7.23 us (20%)
  other arithmetic  1.64 us (5%)
    ppermute x10, starting transfers between devices, shift_by(): lax.ppermute(value, axis, [(i, (i + distance) % size) for i in range(size)])  15.2 us
    ppermute x10, waiting for transfers between devices, shift_by(): lax.ppermute(value, axis, [(i, (i + distance) % size) for i in range(size)])  7.23 us
    pallas_call x2, Pallas kernels, summed(): pl.pallas_call(functools.partial(sum_kernel, order, stage), out_shape=out...  6.66 us
    pallas_call x1, Pallas kernels, mix(): pl.pallas_call(functools.partial(mix_kernel, split), out_shape=[pltpu.VME...  3.95 us
    add x3, other arithmetic, per_device(): sigma = lax.optimization_barrier(sigma) + other.astype(jnp.float32)  0.78 us
  transfers between devices with their start and end apart: 10, of which 5 were waited for; matrix products, arithmetic and copies ran while one was open for 0% of the time, Pallas kernels for 22%

profile of v25, /device:TPU:0, one launch (start us, length us, event | category | flops | bytes accessed | tf_op | source)
XLA Modules:
  0.0 34.8 jit_solution(3041932445602043301)
XLA Ops:
  0.0 0.7 %select_bitcast_fusion = f32[4,32]{1,0:T(4,128)S(1)} fusion(f32[32,4]{0,1:T(4,128)} %param.9, s32[32,4]{0,1:T(4,128)} %param.10), kind=kLoop, calls=%fused_computation.8 | loop fusion | flops 256 | bytes 1536 | tf_op jit(solution)/shard_map/jit(_where)/select_n | solution.py:201
  0.7 3.0 %collective-permute-start.2 = (f32[4,32]{1,0:T(4,128)S(1)}, f32[4,32]{1,0:T(4,128)S(1)}, u32[]{:S(2)}, u32[]{:S(2)}) collective-permute-start(f32[4,32]{1,0:T(4,128)S(1)} %select_bitcast_fusion), channel_id=1, source_target_pairs={{0,4},{4,8},{8,12},{12,0},{1,5},{5,9},{9,13},{13,1},{2,6},{6,10},{... | collective-permute-start | bytes 1544 | tf_op jit(solution)/shard_map/ppermute | solution.py:191
  3.7 2.6 %collective-permute-start.1 = (f32[4,32]{1,0:T(4,128)S(1)}, f32[4,32]{1,0:T(4,128)S(1)}, u32[]{:S(2)}, u32[]{:S(2)}) collective-permute-start(f32[4,32]{1,0:T(4,128)S(1)} %select_bitcast_fusion), channel_id=1, source_target_pairs={{0,8},{4,12},{8,0},{12,4},{1,9},{5,13},{9,1},{13,5},{2,10},{6,14},... | collective-permute-start | bytes 1544 | tf_op jit(solution)/shard_map/ppermute | solution.py:191
  6.3 1.3 %collective-permute-start = (f32[4,32]{1,0:T(4,128)S(1)}, f32[4,32]{1,0:T(4,128)S(1)}, u32[]{:S(2)}, u32[]{:S(2)}) collective-permute-start(f32[4,32]{1,0:T(4,128)S(1)} %select_bitcast_fusion), channel_id=1, source_target_pairs={{0,12},{4,0},{8,4},{12,8},{1,13},{5,1},{9,5},{13,9},{2,14},{6,2},{... | collective-permute-start | bytes 1544 | tf_op jit(solution)/shard_map/ppermute | solution.py:191
  7.7 4.0 %shard_map.64 = (bf16[32,4,128,256]{3,2,1,0:T(8,128)(2,1)S(1)}, bf16[32,256,256]{2,1,0:T(8,128)(2,1)S(1)}, f32[16,128,128]{2,1,0:T(8,128)S(1)}, f32[16,128,128]{2,1,0:T(8,128)S(1)}) custom-call(bf16[4,256,256]{2,1,0:T(8,128)(2,1)} %wave_ref.1, bf16[32,128,256]{2,1,0:T(8,128)(2,1)} %left_ref.1, bf16[32,256,256]{2,1,0:T(8,128)(2,1)} %right_ref.1), custom_call_target="tpu_custom_call" | custom-call | flops 2147483648 | bytes 6291456 | tf_op jit(solution)/shard_map/pallas_call | solution.py:73
  11.6 0.0 collective-permute-done.2
  11.6 0.0 collective-permute-done.1
  11.6 0.0 collective-permute-done
  11.7 3.0 %shard_map.65 = (f32[16,128,128]{2,1,0:T(8,128)S(1)}, f32[16,128,128]{2,1,0:T(8,128)S(1)}, f32[4,128,128]{2,1,0:T(8,128)S(1)}, bf16[4,128,128]{2,1,0:T(8,128)(2,1)S(1)}) custom-call(s32[32]{0:T(128)} %shift_ref.3, f32[16,32]{1,0:T(8,128)S(1)} %pad_maximum_fusion.coef_ref, ...), custom_call_target="tpu_custom_call", output_to_operand_aliasing={{0}: (4, {}), {1}: (5, {})} | custom-call | flops 1073741824 | bytes 6291456 | tf_op jit(solution)/shard_map/pallas_call | solution.py:168
  14.7 1.6 %collective-permute-start.3 = (bf16[4,128,128]{2,1,0:T(8,128)(2,1)S(1)}, bf16[4,128,128]{2,1,0:T(8,128)(2,1)S(1)}, u32[]{:S(2)}, u32[]{:S(2)}) collective-permute-start(bf16[4,128,128]{2,1,0:T(8,128)(2,1)S(1)} %get-tuple-element.31), channel_id=1, source_target_pairs={{0,2},{2,0},{1,3},{3,1},{4,6},{6,4},{5,7},{7,5},{8,10},{10,8},{9,1... | collective-permute-start | bytes 393224 | tf_op jit(solution)/shard_map/ppermute | solution.py:191
  16.3 3.6 %shard_map.66 = (f32[16,128,128]{2,1,0:T(8,128)S(1)}, f32[16,128,128]{2,1,0:T(8,128)S(1)}, f32[4,128,128]{2,1,0:T(8,128)S(1)}, bf16[4,128,128]{2,1,0:T(8,128)(2,...) custom-call(s32[32]{0:T(128)} %shift_ref.3, ...), custom_call_target="tpu_custom_call", output_to_operand_aliasing={{0}: (4, {}), {1}: (5, {})} | custom-call | flops 1073741824 | bytes 6291456 | tf_op jit(solution)/shard_map/pallas_call | solution.py:168
  19.9 0.0 collective-permute-done.3
  20.0 1.4 %collective-permute-start.4 = (bf16[4,128,128]{2,1,0:T(8,128)(2,1)S(1)}, bf16[4,128,128]{2,1,0:T(8,128)(2,1)S(1)}, u32[]{:S(2)}, u32[]{:S(2)}) collective-permute-start(bf16[4,128,128]{2,1,0:T(8,128)(2,1)S(1)} %get-tuple-element.41), channel_id=1, source_target_pairs={{0,2},{2,0},{1,3},{3,1},{4,6},{6,4},{5,7},{7,5},{8,10},{10,8},{9,1... | collective-permute-start | bytes 393224 | tf_op jit(solution)/shard_map/ppermute | solution.py:191
  21.3 0.3 collective-permute-start.7
  21.7 0.7 %collective-permute-start.6 = (bf16[4,128,128]{2,1,0:T(8,128)(2,1)S(1)}, bf16[4,128,128]{2,1,0:T(8,128)(2,1)S(1)}, u32[]{:S(2)}, u32[]{:S(2)}) collective-permute-start(bf16[4,128,128]{2,1,0:T(8,128)(2,1)S(1)} %get-tuple-element.46), channel_id=1, source_target_pairs={{0,2},{2,0},{1,3},{3,1},{4,6},{6,4},{5,7},{7,5},{8,10},{10,8},{9,1... | collective-permute-start | bytes 393224 | tf_op jit(solution)/shard_map/ppermute | solution.py:191
  22.4 3.2 %collective-permute-done.4 = bf16[4,128,128]{2,1,0:T(8,128)(2,1)S(1)} collective-permute-done((bf16[4,128,128]{2,1,0:T(8,128)(2,1)S(1)}, bf16[4,128,128]{2,1,0:T(8,128)(2,1)S(1)}, u32[]{:S(2)}, u32[]{:S(2)}) %collective-permute-start.4) | collective-permute-done | bytes 131104 | tf_op jit(solution)/shard_map/ppermute | solution.py:191
  25.6 0.9 %collective-permute-start.8 = (bf16[4,128,128]{2,1,0:T(8,128)(2,1)S(1)}, bf16[4,128,128]{2,1,0:T(8,128)(2,1)S(1)}, u32[]{:S(2)}, u32[]{:S(2)}) collective-permute-start(bf16[4,128,128]{2,1,0:T(8,128)(2,1)S(1)} %add_convert_fusion.1), channel_id=1, source_target_pairs={{0,4},{4,8},{8,12},{12,0},{1,5},{5,9},{9,13},{13,1},{2,6},{6,10},{... | collective-permute-start | bytes 393224 | tf_op jit(solution)/shard_map/ppermute | solution.py:191
  26.5 1.2 %collective-permute-start.5 = (bf16[4,128,128]{2,1,0:T(8,128)(2,1)S(1)}, bf16[4,128,128]{2,1,0:T(8,128)(2,1)S(1)}, u32[]{:S(2)}, u32[]{:S(2)}) collective-permute-start(bf16[4,128,128]{2,1,0:T(8,128)(2,1)S(1)} %get-tuple-element.43), channel_id=1, source_target_pairs={{0,2},{2,0},{1,3},{3,1},{4,6},{6,4},{5,7},{7,5},{8,10},{10,8},{9,1... | collective-permute-start | bytes 393224 | tf_op jit(solution)/shard_map/ppermute | solution.py:191
  27.6 0.6 %collective-permute-done.6 = bf16[4,128,128]{2,1,0:T(8,128)(2,1)S(1)} collective-permute-done((bf16[4,128,128]{2,1,0:T(8,128)(2,1)S(1)}, bf16[4,128,128]{2,1,0:T(8,128)(2,1)S(1)}, u32[]{:S(2)}, u32[]{:S(2)}) %collective-permute-start.6) | collective-permute-done | bytes 131104 | tf_op jit(solution)/shard_map/ppermute | solution.py:191
  28.2 2.3 %collective-permute-start.9 = (bf16[4,128,128]{2,1,0:T(8,128)(2,1)S(1)}, bf16[4,128,128]{2,1,0:T(8,128)(2,1)S(1)}, u32[]{:S(2)}, u32[]{:S(2)}) collective-permute-start(bf16[4,128,128]{2,1,0:T(8,128)(2,1)S(1)} %add_convert_fusion), channel_id=1, source_target_pairs={{0,12},{4,0},{8,4},{12,8},{1,13},{5,1},{9,5},{13,9},{2,14},{6,2},{... | collective-permute-start | bytes 393224 | tf_op jit(solution)/shard_map/ppermute | solution.py:191
  30.5 0.9 %collective-permute-done.5 = bf16[4,128,128]{2,1,0:T(8,128)(2,1)S(1)} collective-permute-done((bf16[4,128,128]{2,1,0:T(8,128)(2,1)S(1)}, bf16[4,128,128]{2,1,0:T(8,128)(2,1)S(1)}, u32[]{:S(2)}, u32[]{:S(2)}) %collective-permute-start.5) | collective-permute-done | bytes 131104 | tf_op jit(solution)/shard_map/ppermute | solution.py:191
  31.5 1.2 %collective-permute-done.7 = bf16[4,128,128]{2,1,0:T(8,128)(2,1)S(1)} collective-permute-done((bf16[4,128,128]{2,1,0:T(8,128)(2,1)S(1)}, bf16[4,128,128]{2,1,0:T(8,128)(2,1)S(1)}, u32[]{:S(2)}, u32[]{:S(2)}) %collective-permute-start.7) | collective-permute-done | bytes 131104 | tf_op jit(solution)/shard_map/ppermute | solution.py:191
  32.7 0.0 collective-permute-done.8
  32.7 1.4 %collective-permute-done.9 = bf16[4,128,128]{2,1,0:T(8,128)(2,1)S(1)} collective-permute-done((bf16[4,128,128]{2,1,0:T(8,128)(2,1)S(1)}, bf16[4,128,128]{2,1,0:T(8,128)(2,1)S(1)}, u32[]{:S(2)}, u32[]{:S(2)}) %collective-permute-start.9) | collective-permute-done | bytes 131104 | tf_op jit(solution)/shard_map/ppermute | solution.py:191
  34.1 0.7 %convert_add_fusion = f32[4,128,128]{2,1,0:T(8,128)} fusion(f32[4,128,128]{2,1,0:T(8,128)S(1)} %convert_add_fusion.1, bf16[4,128,128]{2,1,0:T(8,128)(2,1)S(1)} %collective-permute-done.9), kind=kLoop, calls=%fused_computation | loop fusion | flops 131072 | bytes 655360 | tf_op jit(solution)/shard_map/add | solution.py:227
  (7 shorter events, 0.2 us)
Async XLA Ops:
  0.7 10.9 %collective-permute-start.2 = (f32[4,32]{1,0:T(4,128)S(1)}, f32[4,32]{1,0:T(4,128)S(1)}, u32[]{:S(2)}, u32[]{:S(2)}) collective-permute-start(f32[4,32]{1,0:T(4,128)S(1)} %select_bitcast_fusion), channel_id=1, source_target_pairs={{0,4},{4,8},{8,12},{12,0},{1,5},{5,9},{9,13},{13,1},{2,6},{6,10},{... | collective-permute-start | bytes 1544 | tf_op jit(solution)/shard_map/ppermute | solution.py:191
  3.7 7.9 %collective-permute-start.1 = (f32[4,32]{1,0:T(4,128)S(1)}, f32[4,32]{1,0:T(4,128)S(1)}, u32[]{:S(2)}, u32[]{:S(2)}) collective-permute-start(f32[4,32]{1,0:T(4,128)S(1)} %select_bitcast_fusion), channel_id=1, source_target_pairs={{0,8},{4,12},{8,0},{12,4},{1,9},{5,13},{9,1},{13,5},{2,10},{6,14},... | collective-permute-start | bytes 1544 | tf_op jit(solution)/shard_map/ppermute | solution.py:191
  6.3 5.3 %collective-permute-start = (f32[4,32]{1,0:T(4,128)S(1)}, f32[4,32]{1,0:T(4,128)S(1)}, u32[]{:S(2)}, u32[]{:S(2)}) collective-permute-start(f32[4,32]{1,0:T(4,128)S(1)} %select_bitcast_fusion), channel_id=1, source_target_pairs={{0,12},{4,0},{8,4},{12,8},{1,13},{5,1},{9,5},{13,9},{2,14},{6,2},{... | collective-permute-start | bytes 1544 | tf_op jit(solution)/shard_map/ppermute | solution.py:191
  14.7 5.2 %collective-permute-start.3 = (bf16[4,128,128]{2,1,0:T(8,128)(2,1)S(1)}, bf16[4,128,128]{2,1,0:T(8,128)(2,1)S(1)}, u32[]{:S(2)}, u32[]{:S(2)}) collective-permute-start(bf16[4,128,128]{2,1,0:T(8,128)(2,1)S(1)} %get-tuple-element.31), channel_id=1, source_target_pairs={{0,2},{2,0},{1,3},{3,1},{4,6},{6,4},{5,7},{7,5},{8,10},{10,8},{9,1... | collective-permute-start | bytes 393224 | tf_op jit(solution)/shard_map/ppermute | solution.py:191
  20.0 5.6 %collective-permute-start.4 = (bf16[4,128,128]{2,1,0:T(8,128)(2,1)S(1)}, bf16[4,128,128]{2,1,0:T(8,128)(2,1)S(1)}, u32[]{:S(2)}, u32[]{:S(2)}) collective-permute-start(bf16[4,128,128]{2,1,0:T(8,128)(2,1)S(1)} %get-tuple-element.41), channel_id=1, source_target_pairs={{0,2},{2,0},{1,3},{3,1},{4,6},{6,4},{5,7},{7,5},{8,10},{10,8},{9,1... | collective-permute-start | bytes 393224 | tf_op jit(solution)/shard_map/ppermute | solution.py:191
  21.3 11.3 %collective-permute-start.7 = (bf16[4,128,128]{2,1,0:T(8,128)(2,1)S(1)}, bf16[4,128,128]{2,1,0:T(8,128)(2,1)S(1)}, u32[]{:S(2)}, u32[]{:S(2)}) collective-permute-start(bf16[4,128,128]{2,1,0:T(8,128)(2,1)S(1)} %add_convert_fusion.2), channel_id=1, source_target_pairs={{0,8},{4,12},{8,0},{12,4},{1,9},{5,13},{9,1},{13,5},{2,10},{6,14},... | collective-permute-start | bytes 393224 | tf_op jit(solution)/shard_map/ppermute | solution.py:191
  21.7 6.5 %collective-permute-start.6 = (bf16[4,128,128]{2,1,0:T(8,128)(2,1)S(1)}, bf16[4,128,128]{2,1,0:T(8,128)(2,1)S(1)}, u32[]{:S(2)}, u32[]{:S(2)}) collective-permute-start(bf16[4,128,128]{2,1,0:T(8,128)(2,1)S(1)} %get-tuple-element.46), channel_id=1, source_target_pairs={{0,2},{2,0},{1,3},{3,1},{4,6},{6,4},{5,7},{7,5},{8,10},{10,8},{9,1... | collective-permute-start | bytes 393224 | tf_op jit(solution)/shard_map/ppermute | solution.py:191
  25.6 7.1 %collective-permute-start.8 = (bf16[4,128,128]{2,1,0:T(8,128)(2,1)S(1)}, bf16[4,128,128]{2,1,0:T(8,128)(2,1)S(1)}, u32[]{:S(2)}, u32[]{:S(2)}) collective-permute-start(bf16[4,128,128]{2,1,0:T(8,128)(2,1)S(1)} %add_convert_fusion.1), channel_id=1, source_target_pairs={{0,4},{4,8},{8,12},{12,0},{1,5},{5,9},{9,13},{13,1},{2,6},{6,10},{... | collective-permute-start | bytes 393224 | tf_op jit(solution)/shard_map/ppermute | solution.py:191
  26.5 5.0 %collective-permute-start.5 = (bf16[4,128,128]{2,1,0:T(8,128)(2,1)S(1)}, bf16[4,128,128]{2,1,0:T(8,128)(2,1)S(1)}, u32[]{:S(2)}, u32[]{:S(2)}) collective-permute-start(bf16[4,128,128]{2,1,0:T(8,128)(2,1)S(1)} %get-tuple-element.43), channel_id=1, source_target_pairs={{0,2},{2,0},{1,3},{3,1},{4,6},{6,4},{5,7},{7,5},{8,10},{10,8},{9,1... | collective-permute-start | bytes 393224 | tf_op jit(solution)/shard_map/ppermute | solution.py:191
  28.2 5.8 %collective-permute-start.9 = (bf16[4,128,128]{2,1,0:T(8,128)(2,1)S(1)}, bf16[4,128,128]{2,1,0:T(8,128)(2,1)S(1)}, u32[]{:S(2)}, u32[]{:S(2)}) collective-permute-start(bf16[4,128,128]{2,1,0:T(8,128)(2,1)S(1)} %add_convert_fusion), channel_id=1, source_target_pairs={{0,12},{4,0},{8,4},{12,8},{1,13},{5,1},{9,5},{13,9},{2,14},{6,2},{... | collective-permute-start | bytes 393224 | tf_op jit(solution)/shard_map/ppermute | solution.py:191

commit v26 on v25

--- a/solution.py
+++ b/solution.py
@@ -18,18 +18,20 @@
     return lax.rem(value + size, size)
 
 
-def mix_kernel(split, wave_ref, left_ref, right_ref, mixed_ref, held_ref, *refs):
-    *zeros, wave, left, sems = refs
+def mix_kernel(split, shift_ref, wave_ref, left_ref, right_ref, mixed_ref, held_ref, row_ref, *refs):
+    *zeros, shifts, wave, left, sems = refs
     sec_dev = wave.shape[0]
     terms, rows, width = left.shape
     chunks = terms // MIX_TERMS
 
     def left_copy(c):
         part = pl.ds(c * MIX_TERMS, MIX_TERMS)
-        return pltpu.make_async_copy(left_ref.at[part], left.at[part], sems.at[3 + c])
+        return pltpu.make_async_copy(left_ref.at[part], left.at[part], sems.at[4 + c])
 
     wave_copy = pltpu.make_async_copy(wave_ref, wave, sems.at[0])
     wave_copy.start()
+    shift_copy = pltpu.make_async_copy(shift_ref, shifts, sems.at[3])
+    shift_copy.start()
     for c in range(chunks):
         left_copy(c).start()
     if split:
@@ -51,6 +53,8 @@
         copy.start()
     for ref in zeros:
         ref[...] = jnp.zeros_like(ref)
+    shift_copy.wait()
+    row_ref[...] = shifts[...].astype(jnp.float32)
     wave_copy.wait()
 
     @pl.loop(0, chunks)
@@ -66,7 +70,7 @@
         copy.wait()
 
 
-def mix(wavefunction, left_ops, right_ops, targets, split):
+def mix(shift, wavefunction, left_ops, right_ops, targets, split):
     k_dev, rows, width = left_ops.shape
     sec_dev = wavefunction.shape[0]
     zeros = [pltpu.VMEM((targets, rows, width // 2), jnp.float32)] * (2 if split else 0)
@@ -75,14 +79,16 @@
         out_shape=[
             pltpu.VMEM((k_dev, sec_dev, rows, width), jnp.bfloat16),
             pltpu.VMEM(right_ops.shape, jnp.bfloat16),
+            pltpu.VMEM(shift.shape, jnp.float32),
         ]
         + zeros,
-        in_specs=[pl.BlockSpec(memory_space=pltpu.HBM)] * 3,
-        out_specs=[pl.BlockSpec(memory_space=pltpu.VMEM)] * (2 + len(zeros)),
+        in_specs=[pl.BlockSpec(memory_space=pltpu.HBM)] * 4,
+        out_specs=[pl.BlockSpec(memory_space=pltpu.VMEM)] * (3 + len(zeros)),
         scratch_shapes=[
+            pltpu.VMEM(shift.shape, jnp.int32),
             pltpu.VMEM(wavefunction.shape, jnp.bfloat16),
             pltpu.VMEM(left_ops.shape, jnp.bfloat16),
-            pltpu.SemaphoreType.DMA((3 + k_dev // MIX_TERMS,)),
+            pltpu.SemaphoreType.DMA((4 + k_dev // MIX_TERMS,)),
         ],
         compiler_params=pltpu.CompilerParams(vmem_limit_bytes=24 * MIB),
         cost_estimate=pl.CostEstimate(
@@ -90,29 +96,37 @@
             bytes_accessed=2 * (left_ops.size + right_ops.size),
             transcendentals=0,
         ),
-    )(*(pltpu.with_memory_space_constraint(x, pltpu.HBM) for x in (wavefunction, left_ops, right_ops)))
+    )(
+        *(
+            pltpu.with_memory_space_constraint(x, pltpu.HBM)
+            for x in (shift, wavefunction, left_ops, right_ops)
+        )
+    )
 
 
 def reaches(shift, group, sec_dev, targets):
     return wrapped(-shift - group * sec_dev + sec_dev - 1, targets) < 2 * sec_dev - 1
 
 
-def sum_kernel(order, stage, shift_ref, coef_ref, mixed_ref, held_ref, *refs):
+def sum_kernel(order, stage, table_ref, mixed_ref, held_ref, *refs):
     terms, sec_dev, rows, width = mixed_ref.shape
-    targets = coef_ref.shape[0]
+    targets = table_ref.shape[0] - 1
     half = width // 2
     picked = refs[-1]
+
+    def shift_of(k):
+        return table_ref[targets, k].astype(jnp.int32)
 
     def pick(k, count):
         picked[count] = k
         if stage is None:
             return count + 1
-        wanted = True
+        wanted, shift = True, shift_of(k)
         for at, groups in enumerate(order[: stage + 1]):
             if at < stage:
-                wanted &= ~reaches(shift_ref[k], groups[0], sec_dev, targets)
+                wanted &= ~reaches(shift, groups[0], sec_dev, targets)
             elif at < len(order) - 1:
-                wanted &= reaches(shift_ref[k], groups[0], sec_dev, targets)
+                wanted &= reaches(shift, groups[0], sec_dev, targets)
         return count + jnp.where(wanted, 1, 0)
 
     count = lax.fori_loop(0, terms, pick, 0, unroll=8)
@@ -130,6 +144,7 @@
         for t in range(SUM_TERMS):
             at = step * SUM_TERMS + t
             k = picked[at]
+            shift = shift_of(k)
             product = lax.dot_general(
                 mixed_ref[k].reshape(sec_dev * rows, width),
                 held_ref[k],
@@ -137,8 +152,8 @@
                 preferred_element_type=jnp.float32,
             )
             for s in range(sec_dev):
-                target = wrapped(s - shift_ref[k], targets)
-                weight = jnp.where(at < count, coef_ref[target, k], 0.0)
+                target = wrapped(s - shift, targets)
+                weight = jnp.where(at < count, table_ref[target, k], 0.0)
                 scaled = weight * product[s * rows : (s + 1) * rows]
                 if stage is None:
                     sums[0][target] += scaled
@@ -153,9 +168,9 @@
             outs[2 * at + 1][...] = sums[1][part].astype(jnp.bfloat16)
 
 
-def summed(shift, coef, mixed, held, order, stage, sums=()):
+def summed(table, mixed, held, order, stage, sums=()):
     k_dev, sec_dev, rows, width = mixed.shape
-    targets = coef.shape[0]
+    targets = table.shape[0] - 1
     columns = width if stage is None else width // 2
     whole = pltpu.VMEM((targets, rows, columns), jnp.float32)
     out_shape = [whole]
@@ -168,10 +183,10 @@
     return pl.pallas_call(
         functools.partial(sum_kernel, order, stage),
         out_shape=out_shape,
-        in_specs=[pl.BlockSpec(memory_space=pltpu.SMEM)] * 2
+        in_specs=[pl.BlockSpec(memory_space=pltpu.SMEM)]
         + [pl.BlockSpec(memory_space=pltpu.VMEM)] * len(in_vmem),
         out_specs=[pl.BlockSpec(memory_space=pltpu.VMEM)] * len(out_shape),
-        input_output_aliases={4 + i: i for i in range(len(sums))},
+        input_output_aliases={3 + i: i for i in range(len(sums))},
         scratch_shapes=[pltpu.SMEM((k_dev + SUM_TERMS,), jnp.int32)],
         compiler_params=pltpu.CompilerParams(vmem_limit_bytes=24 * MIB),
         cost_estimate=pl.CostEstimate(
@@ -179,11 +194,7 @@
             bytes_accessed=mixed.size + held.size,
             transcendentals=0,
         ),
-    )(
-        pltpu.with_memory_space_constraint(shift, pltpu.HBM),
-        coef,
-        *(pltpu.with_memory_space_constraint(x, pltpu.VMEM) for x in in_vmem),
-    )
+    )(table, *(pltpu.with_memory_space_constraint(x, pltpu.VMEM) for x in in_vmem))
 
 
 def shift_by(value, axis, distance):
@@ -200,18 +211,18 @@
     devices = lax.axis_size("sector")
     live = jnp.where(coupled.T > 0, site_coef.T, 0.0)
     split = lax.axis_size("op") == 2 and devices == 4
-    mixed, held, *sums = mix(
-        wavefunction, left_ops, right_ops, sec_dev * devices, split
+    mixed, held, row, *sums = mix(
+        sector_shift[None], wavefunction, left_ops, right_ops, sec_dev * devices, split
     )
 
     if split:
         coefs = [live] + [shift_by(live, "sector", -g) for g in range(1, devices)]
-        coef = jnp.concatenate(coefs, axis=0)
+        table = jnp.concatenate(coefs + [row], axis=0)
         order = ((2,), (1, 3, 0))
-        *sums, mine_2, theirs_2 = summed(sector_shift, coef, mixed, held, order, 0, sums)
+        *sums, mine_2, theirs_2 = summed(table, mixed, held, order, 0, sums)
         crossed_2 = shift_by(theirs_2, "op", 1)
         _, _, mine_1, theirs_1, mine_3, theirs_3, mine_0, theirs_0 = summed(
-            sector_shift, after(coef, theirs_2), mixed, held, order, 1, sums
+            after(table, theirs_2), mixed, held, order, 1, sums
         )
         both_2 = (mine_2 + after(crossed_2, mine_1).astype(jnp.float32)).astype(jnp.bfloat16)
         arrived_2 = shift_by(both_2, "sector", 2)
@@ -229,7 +240,7 @@
 
     first = lax.axis_index("sector") * sec_dev
     coef = jnp.roll(lax.all_gather(live, "sector", axis=0, tiled=True), -first, axis=0)
-    (total,) = summed(sector_shift, coef, mixed, held, (), None)
+    (total,) = summed(jnp.concatenate([coef, row], axis=0), mixed, held, (), None)
     total = jnp.roll(total, first, axis=0)
     total = lax.psum_scatter(total, "op", scatter_dimension=2, tiled=True)
     return lax.psum_scatter(total, "sector", scatter_dimension=0, tiled=True)

time: 35.3 us -> 46.2 us (1.31)
  local copies, waits for them, and re-layouts: 0 us -> 10.8 us
  waiting for transfers between devices: 7.23 us -> 8.01 us
  starting transfers between devices: 15.2 us -> 14.7 us
    unnamed x0 -> x8, local copies, waits for them, and re-layouts: none -> 10.8 us
    ppermute x10, waiting for transfers between devices: 7.23 us -> 8.01 us  [shift_by(): lax.ppermute(value, axis, [(i, (i + distance) % size) for i in range(size)])]
    ppermute x10, starting transfers between devices: 15.2 us -> 14.7 us  [shift_by(): lax.ppermute(value, axis, [(i, (i + distance) % size) for i in range(size)])]
  transfers between devices with their start and end apart: 10 -> 10, of which waited for: 5 -> 5; matrix products, arithmetic and copies ran while one was open for 0% -> 0% of each run, Pallas kernels for 22% -> 18%
where the time goes in v26:
time: 46.2 us; the launch traced here: 46 us
  starting transfers between devices  14.7 us (32%)
  local copies, waits for them, and re-layouts  10.8 us (23%)
  Pallas kernels  10.7 us (23%)
  waiting for transfers between devices  8.01 us (17%)
  other arithmetic  1.63 us (4%)
    ppermute x10, starting transfers between devices, shift_by(): lax.ppermute(value, axis, [(i, (i + distance) % size) for i in range(size)])  14.7 us
    unnamed x8, local copies, waits for them, and re-layouts  10.8 us
    ppermute x10, waiting for transfers between devices, shift_by(): lax.ppermute(value, axis, [(i, (i + distance) % size) for i in range(size)])  8.01 us
    pallas_call x2, Pallas kernels, summed(): pl.pallas_call(functools.partial(sum_kernel, order, stage), out_shape=out...  6.77 us
    pallas_call x1, Pallas kernels, mix(): pl.pallas_call(functools.partial(mix_kernel, split), out_shape=[pltpu.VME...  3.98 us
  transfers between devices with their start and end apart: 10, of which 5 were waited for; matrix products, arithmetic and copies ran while one was open for 0% of the time, Pallas kernels for 18%

profile of v26, /device:TPU:0, one launch (start us, length us, event | category | flops | bytes accessed | tf_op | source)
XLA Modules:
  0.0 46.0 jit_solution(10591911761001315821)
XLA Ops:
  0.0 0.7 %select_bitcast_fusion = f32[4,32]{1,0:T(4,128)S(1)} fusion(f32[32,4]{0,1:T(4,128)} %param.9, s32[32,4]{0,1:T(4,128)} %param.10), kind=kLoop, calls=%fused_computation.7 | loop fusion | flops 256 | bytes 1536 | tf_op jit(solution)/shard_map/jit(_where)/select_n | solution.py:212
  0.7 3.0 %collective-permute-start.2 = (f32[4,32]{1,0:T(4,128)S(1)}, f32[4,32]{1,0:T(4,128)S(1)}, u32[]{:S(2)}, u32[]{:S(2)}) collective-permute-start(f32[4,32]{1,0:T(4,128)S(1)} %select_bitcast_fusion), channel_id=1, source_target_pairs={{0,4},{4,8},{8,12},{12,0},{1,5},{5,9},{9,13},{13,1},{2,6},{6,10},{... | collective-permute-start | bytes 1544 | tf_op jit(solution)/shard_map/ppermute | solution.py:202
  3.7 2.6 %collective-permute-start.1 = (f32[4,32]{1,0:T(4,128)S(1)}, f32[4,32]{1,0:T(4,128)S(1)}, u32[]{:S(2)}, u32[]{:S(2)}) collective-permute-start(f32[4,32]{1,0:T(4,128)S(1)} %select_bitcast_fusion), channel_id=1, source_target_pairs={{0,8},{4,12},{8,0},{12,4},{1,9},{5,13},{9,1},{13,5},{2,10},{6,14},... | collective-permute-start | bytes 1544 | tf_op jit(solution)/shard_map/ppermute | solution.py:202
  6.3 1.3 %collective-permute-start = (f32[4,32]{1,0:T(4,128)S(1)}, f32[4,32]{1,0:T(4,128)S(1)}, u32[]{:S(2)}, u32[]{:S(2)}) collective-permute-start(f32[4,32]{1,0:T(4,128)S(1)} %select_bitcast_fusion), channel_id=1, source_target_pairs={{0,12},{4,0},{8,4},{12,8},{1,13},{5,1},{9,5},{13,9},{2,14},{6,2},{... | collective-permute-start | bytes 1544 | tf_op jit(solution)/shard_map/ppermute | solution.py:202
  7.7 4.0 %shard_map.64 = (bf16[32,4,128,256]{3,2,1,0:T(8,128)(2,1)S(1)}, bf16[32,256,256]{2,1,0:T(8,128)(2,1)S(1)}, f32[1,32]{1,0:T(1,128)S(1)}, f32[16,128,128]{2,1,0:T(8,128)S(1)}, f32[16,128,128]{2,1,0:T(8,128)S(1)}) custom-call(s32[1,32]{1,0:T(1,128)} %bitcast.3, bf16[4,256,256]{2,1,0:T(8,128)(2,1)} %wave_ref.1, bf16[32,128,256]{2,1,0:T(8,128)(2,1)} %left_ref.1, ...), custom_call_target="tpu_custom_call" | custom-call | flops 2147483648 | bytes 6291456 | tf_op jit(solution)/shard_map/pallas_call | solution.py:77
  11.7 0.0 copy-start
  11.7 3.2 %copy-done = bf16[32,4,128,256]{3,2,1,0:T(8,128)(2,1)} copy-done((bf16[32,4,128,256]{3,2,1,0:T(8,128)(2,1)}, bf16[32,4,128,256]{3,2,1,0:T(8,128)(2,1)S(1)}, u32[]{:S(2)}) %copy-start) | copy-done | bytes 8388632
  14.9 0.0 copy-start.2
  14.9 2.0 %copy-done.2 = bf16[32,256,256]{2,1,0:T(8,128)(2,1)} copy-done((bf16[32,256,256]{2,1,0:T(8,128)(2,1)}, bf16[32,256,256]{2,1,0:T(8,128)(2,1)S(1)}, u32[]{:S(2)}) %copy-start.2) | copy-done | bytes 4194328
  16.9 0.0 collective-permute-done.2
  16.9 0.0 collective-permute-done.1
  16.9 0.0 collective-permute-done
  16.9 0.1 concatenate.3.table_ref
  16.9 3.4 %copy-done.1 = bf16[32,4,128,256]{3,2,1,0:T(8,128)(2,1)S(1)} copy-done((bf16[32,4,128,256]{3,2,1,0:T(8,128)(2,1)S(1)}, bf16[32,4,128,256]{3,2,1,0:T(8,128)(2,1)}, u32[]{:S(2)}) %copy-start.1) | copy-done | bytes 8388632
  20.3 2.2 %copy-done.3 = bf16[32,256,256]{2,1,0:T(8,128)(2,1)S(1)} copy-done((bf16[32,256,256]{2,1,0:T(8,128)(2,1)S(1)}, bf16[32,256,256]{2,1,0:T(8,128)(2,1)}, u32[]{:S(2)}) %copy-start.3) | copy-done | bytes 4194328
  22.5 2.6 %shard_map.65 = (f32[16,128,128]{2,1,0:T(8,128)S(1)}, f32[16,128,128]{2,1,0:T(8,128)S(1)}, f32[4,128,128]{2,1,0:T(8,128)S(1)}, bf16[4,128,128]{2,1,0:T(8,128)(2,1)S(1)}) custom-call(f32[17,32]{1,0:T(8,128)S(1)} %concatenate.3.table_ref, bf16[32,4,128,256]{3,2,1,0:T(8,128)(2,1)S(1)} %copy-done.1, ...), custom_call_target="tpu_custom_call", output_to_operand_aliasing={{0}: (3, {}), {1}: (4, {})} | custom-call | flops 1073741824 | bytes 6291456 | tf_op jit(solution)/shard_map/pallas_call | solution.py:183
  25.1 2.1 %collective-permute-start.3 = (bf16[4,128,128]{2,1,0:T(8,128)(2,1)S(1)}, bf16[4,128,128]{2,1,0:T(8,128)(2,1)S(1)}, u32[]{:S(2)}, u32[]{:S(2)}) collective-permute-start(bf16[4,128,128]{2,1,0:T(8,128)(2,1)S(1)} %get-tuple-element.33), channel_id=1, source_target_pairs={{0,2},{2,0},{1,3},{3,1},{4,6},{6,4},{5,7},{7,5},{8,10},{10,8},{9,1... | collective-permute-start | bytes 393224 | tf_op jit(solution)/shard_map/ppermute | solution.py:202
  27.1 4.2 %shard_map.66 = (f32[16,128,128]{2,1,0:T(8,128)S(1)}, f32[16,128,128]{2,1,0:T(8,128)S(1)}, f32[4,128,128]{2,1,0:T(8,128)S(1)}, bf16[4,128,128]{2,1,0:T(8,128)(2,...) custom-call(f32[17,32]{1,0:T(8,128)S(1)} %concatenate.3.table_ref, ...), custom_call_target="tpu_custom_call", output_to_operand_aliasing={{0}: (3, {}), {1}: (4, {})} | custom-call | flops 1073741824 | bytes 6291456 | tf_op jit(solution)/shard_map/pallas_call | solution.py:183
  31.4 0.0 collective-permute-done.3
  31.4 0.8 %collective-permute-start.4 = (bf16[4,128,128]{2,1,0:T(8,128)(2,1)S(1)}, bf16[4,128,128]{2,1,0:T(8,128)(2,1)S(1)}, u32[]{:S(2)}, u32[]{:S(2)}) collective-permute-start(bf16[4,128,128]{2,1,0:T(8,128)(2,1)S(1)} %get-tuple-element.43), channel_id=1, source_target_pairs={{0,2},{2,0},{1,3},{3,1},{4,6},{6,4},{5,7},{7,5},{8,10},{10,8},{9,1... | collective-permute-start | bytes 393224 | tf_op jit(solution)/shard_map/ppermute | solution.py:202
  32.2 0.3 collective-permute-start.7
  32.6 1.3 %collective-permute-start.6 = (bf16[4,128,128]{2,1,0:T(8,128)(2,1)S(1)}, bf16[4,128,128]{2,1,0:T(8,128)(2,1)S(1)}, u32[]{:S(2)}, u32[]{:S(2)}) collective-permute-start(bf16[4,128,128]{2,1,0:T(8,128)(2,1)S(1)} %get-tuple-element.48), channel_id=1, source_target_pairs={{0,2},{2,0},{1,3},{3,1},{4,6},{6,4},{5,7},{7,5},{8,10},{10,8},{9,1... | collective-permute-start | bytes 393224 | tf_op jit(solution)/shard_map/ppermute | solution.py:202
  33.8 3.2 %collective-permute-done.4 = bf16[4,128,128]{2,1,0:T(8,128)(2,1)S(1)} collective-permute-done((bf16[4,128,128]{2,1,0:T(8,128)(2,1)S(1)}, bf16[4,128,128]{2,1,0:T(8,128)(2,1)S(1)}, u32[]{:S(2)}, u32[]{:S(2)}) %collective-permute-start.4) | collective-permute-done | bytes 131104 | tf_op jit(solution)/shard_map/ppermute | solution.py:202
  37.0 0.9 %collective-permute-start.8 = (bf16[4,128,128]{2,1,0:T(8,128)(2,1)S(1)}, bf16[4,128,128]{2,1,0:T(8,128)(2,1)S(1)}, u32[]{:S(2)}, u32[]{:S(2)}) collective-permute-start(bf16[4,128,128]{2,1,0:T(8,128)(2,1)S(1)} %add_convert_fusion.1), channel_id=1, source_target_pairs={{0,4},{4,8},{8,12},{12,0},{1,5},{5,9},{9,13},{13,1},{2,6},{6,10},{... | collective-permute-start | bytes 393224 | tf_op jit(solution)/shard_map/ppermute | solution.py:202
  37.9 0.5 %collective-permute-start.5 = (bf16[4,128,128]{2,1,0:T(8,128)(2,1)S(1)}, bf16[4,128,128]{2,1,0:T(8,128)(2,1)S(1)}, u32[]{:S(2)}, u32[]{:S(2)}) collective-permute-start(bf16[4,128,128]{2,1,0:T(8,128)(2,1)S(1)} %get-tuple-element.45), channel_id=1, source_target_pairs={{0,2},{2,0},{1,3},{3,1},{4,6},{6,4},{5,7},{7,5},{8,10},{10,8},{9,1... | collective-permute-start | bytes 393224 | tf_op jit(solution)/shard_map/ppermute | solution.py:202
  38.5 1.2 %collective-permute-done.6 = bf16[4,128,128]{2,1,0:T(8,128)(2,1)S(1)} collective-permute-done((bf16[4,128,128]{2,1,0:T(8,128)(2,1)S(1)}, bf16[4,128,128]{2,1,0:T(8,128)(2,1)S(1)}, u32[]{:S(2)}, u32[]{:S(2)}) %collective-permute-start.6) | collective-permute-done | bytes 131104 | tf_op jit(solution)/shard_map/ppermute | solution.py:202
  39.7 1.8 %collective-permute-start.9 = (bf16[4,128,128]{2,1,0:T(8,128)(2,1)S(1)}, bf16[4,128,128]{2,1,0:T(8,128)(2,1)S(1)}, u32[]{:S(2)}, u32[]{:S(2)}) collective-permute-start(bf16[4,128,128]{2,1,0:T(8,128)(2,1)S(1)} %add_convert_fusion), channel_id=1, source_target_pairs={{0,12},{4,0},{8,4},{12,8},{1,13},{5,1},{9,5},{13,9},{2,14},{6,2},{... | collective-permute-start | bytes 393224 | tf_op jit(solution)/shard_map/ppermute | solution.py:202
  41.5 1.4 %collective-permute-done.5 = bf16[4,128,128]{2,1,0:T(8,128)(2,1)S(1)} collective-permute-done((bf16[4,128,128]{2,1,0:T(8,128)(2,1)S(1)}, bf16[4,128,128]{2,1,0:T(8,128)(2,1)S(1)}, u32[]{:S(2)}, u32[]{:S(2)}) %collective-permute-start.5) | collective-permute-done | bytes 131104 | tf_op jit(solution)/shard_map/ppermute | solution.py:202
  42.9 0.0 collective-permute-done.7
  43.0 0.9 %collective-permute-done.8 = bf16[4,128,128]{2,1,0:T(8,128)(2,1)S(1)} collective-permute-done((bf16[4,128,128]{2,1,0:T(8,128)(2,1)S(1)}, bf16[4,128,128]{2,1,0:T(8,128)(2,1)S(1)}, u32[]{:S(2)}, u32[]{:S(2)}) %collective-permute-start.8) | collective-permute-done | bytes 131104 | tf_op jit(solution)/shard_map/ppermute | solution.py:202
  43.9 1.3 %collective-permute-done.9 = bf16[4,128,128]{2,1,0:T(8,128)(2,1)S(1)} collective-permute-done((bf16[4,128,128]{2,1,0:T(8,128)(2,1)S(1)}, bf16[4,128,128]{2,1,0:T(8,128)(2,1)S(1)}, u32[]{:S(2)}, u32[]{:S(2)}) %collective-permute-start.9) | collective-permute-done | bytes 131104 | tf_op jit(solution)/shard_map/ppermute | solution.py:202
  45.3 0.7 %convert_add_fusion = f32[4,128,128]{2,1,0:T(8,128)} fusion(f32[4,128,128]{2,1,0:T(8,128)S(1)} %convert_add_fusion.1, bf16[4,128,128]{2,1,0:T(8,128)(2,1)S(1)} %collective-permute-done.9), kind=kLoop, calls=%fused_computation | loop fusion | flops 131072 | bytes 655360 | tf_op jit(solution)/shard_map/add | solution.py:238
  (8 shorter events, 0.2 us)
Async XLA Ops:
  0.7 16.2 %collective-permute-start.2 = (f32[4,32]{1,0:T(4,128)S(1)}, f32[4,32]{1,0:T(4,128)S(1)}, u32[]{:S(2)}, u32[]{:S(2)}) collective-permute-start(f32[4,32]{1,0:T(4,128)S(1)} %select_bitcast_fusion), channel_id=1, source_target_pairs={{0,4},{4,8},{8,12},{12,0},{1,5},{5,9},{9,13},{13,1},{2,6},{6,10},{... | collective-permute-start | bytes 1544 | tf_op jit(solution)/shard_map/ppermute | solution.py:202
  3.7 13.1 %collective-permute-start.1 = (f32[4,32]{1,0:T(4,128)S(1)}, f32[4,32]{1,0:T(4,128)S(1)}, u32[]{:S(2)}, u32[]{:S(2)}) collective-permute-start(f32[4,32]{1,0:T(4,128)S(1)} %select_bitcast_fusion), channel_id=1, source_target_pairs={{0,8},{4,12},{8,0},{12,4},{1,9},{5,13},{9,1},{13,5},{2,10},{6,14},... | collective-permute-start | bytes 1544 | tf_op jit(solution)/shard_map/ppermute | solution.py:202
  6.3 10.6 %collective-permute-start = (f32[4,32]{1,0:T(4,128)S(1)}, f32[4,32]{1,0:T(4,128)S(1)}, u32[]{:S(2)}, u32[]{:S(2)}) collective-permute-start(f32[4,32]{1,0:T(4,128)S(1)} %select_bitcast_fusion), channel_id=1, source_target_pairs={{0,12},{4,0},{8,4},{12,8},{1,13},{5,1},{9,5},{13,9},{2,14},{6,2},{... | collective-permute-start | bytes 1544 | tf_op jit(solution)/shard_map/ppermute | solution.py:202
  11.7 3.2 %copy-start = (bf16[32,4,128,256]{3,2,1,0:T(8,128)(2,1)}, bf16[32,4,128,256]{3,2,1,0:T(8,128)(2,1)S(1)}, u32[]{:S(2)}) copy-start(bf16[32,4,128,256]{3,2,1,0:T(8,128)(2,1)S(1)} %get-tuple-element.29.mixed_ref) | copy-start | bytes 25165828
  14.9 2.0 %copy-start.2 = (bf16[32,256,256]{2,1,0:T(8,128)(2,1)}, bf16[32,256,256]{2,1,0:T(8,128)(2,1)S(1)}, u32[]{:S(2)}) copy-start(bf16[32,256,256]{2,1,0:T(8,128)(2,1)S(1)} %get-tuple-element.30.held_ref) | copy-start | bytes 12582916
  16.9 3.4 %copy-start.1 = (bf16[32,4,128,256]{3,2,1,0:T(8,128)(2,1)S(1)}, bf16[32,4,128,256]{3,2,1,0:T(8,128)(2,1)}, u32[]{:S(2)}) copy-start(bf16[32,4,128,256]{3,2,1,0:T(8,128)(2,1)} %copy-done) | copy-start | bytes 25165828
  20.3 2.2 %copy-start.3 = (bf16[32,256,256]{2,1,0:T(8,128)(2,1)S(1)}, bf16[32,256,256]{2,1,0:T(8,128)(2,1)}, u32[]{:S(2)}) copy-start(bf16[32,256,256]{2,1,0:T(8,128)(2,1)} %copy-done.2) | copy-start | bytes 12582916
  25.1 6.3 %collective-permute-start.3 = (bf16[4,128,128]{2,1,0:T(8,128)(2,1)S(1)}, bf16[4,128,128]{2,1,0:T(8,128)(2,1)S(1)}, u32[]{:S(2)}, u32[]{:S(2)}) collective-permute-start(bf16[4,128,128]{2,1,0:T(8,128)(2,1)S(1)} %get-tuple-element.33), channel_id=1, source_target_pairs={{0,2},{2,0},{1,3},{3,1},{4,6},{6,4},{5,7},{7,5},{8,10},{10,8},{9,1... | collective-permute-start | bytes 393224 | tf_op jit(solution)/shard_map/ppermute | solution.py:202
  31.4 5.6 %collective-permute-start.4 = (bf16[4,128,128]{2,1,0:T(8,128)(2,1)S(1)}, bf16[4,128,128]{2,1,0:T(8,128)(2,1)S(1)}, u32[]{:S(2)}, u32[]{:S(2)}) collective-permute-start(bf16[4,128,128]{2,1,0:T(8,128)(2,1)S(1)} %get-tuple-element.43), channel_id=1, source_target_pairs={{0,2},{2,0},{1,3},{3,1},{4,6},{6,4},{5,7},{7,5},{8,10},{10,8},{9,1... | collective-permute-start | bytes 393224 | tf_op jit(solution)/shard_map/ppermute | solution.py:202
  32.2 10.7 %collective-permute-start.7 = (bf16[4,128,128]{2,1,0:T(8,128)(2,1)S(1)}, bf16[4,128,128]{2,1,0:T(8,128)(2,1)S(1)}, u32[]{:S(2)}, u32[]{:S(2)}) collective-permute-start(bf16[4,128,128]{2,1,0:T(8,128)(2,1)S(1)} %add_convert_fusion.2), channel_id=1, source_target_pairs={{0,8},{4,12},{8,0},{12,4},{1,9},{5,13},{9,1},{13,5},{2,10},{6,14},... | collective-permute-start | bytes 393224 | tf_op jit(solution)/shard_map/ppermute | solution.py:202
  32.6 7.1 %collective-permute-start.6 = (bf16[4,128,128]{2,1,0:T(8,128)(2,1)S(1)}, bf16[4,128,128]{2,1,0:T(8,128)(2,1)S(1)}, u32[]{:S(2)}, u32[]{:S(2)}) collective-permute-start(bf16[4,128,128]{2,1,0:T(8,128)(2,1)S(1)} %get-tuple-element.48), channel_id=1, source_target_pairs={{0,2},{2,0},{1,3},{3,1},{4,6},{6,4},{5,7},{7,5},{8,10},{10,8},{9,1... | collective-permute-start | bytes 393224 | tf_op jit(solution)/shard_map/ppermute | solution.py:202
  37.0 6.9 %collective-permute-start.8 = (bf16[4,128,128]{2,1,0:T(8,128)(2,1)S(1)}, bf16[4,128,128]{2,1,0:T(8,128)(2,1)S(1)}, u32[]{:S(2)}, u32[]{:S(2)}) collective-permute-start(bf16[4,128,128]{2,1,0:T(8,128)(2,1)S(1)} %add_convert_fusion.1), channel_id=1, source_target_pairs={{0,4},{4,8},{8,12},{12,0},{1,5},{5,9},{9,13},{13,1},{2,6},{6,10},{... | collective-permute-start | bytes 393224 | tf_op jit(solution)/shard_map/ppermute | solution.py:202
  37.9 5.0 %collective-permute-start.5 = (bf16[4,128,128]{2,1,0:T(8,128)(2,1)S(1)}, bf16[4,128,128]{2,1,0:T(8,128)(2,1)S(1)}, u32[]{:S(2)}, u32[]{:S(2)}) collective-permute-start(bf16[4,128,128]{2,1,0:T(8,128)(2,1)S(1)} %get-tuple-element.45), channel_id=1, source_target_pairs={{0,2},{2,0},{1,3},{3,1},{4,6},{6,4},{5,7},{7,5},{8,10},{10,8},{9,1... | collective-permute-start | bytes 393224 | tf_op jit(solution)/shard_map/ppermute | solution.py:202
  39.7 5.6 %collective-permute-start.9 = (bf16[4,128,128]{2,1,0:T(8,128)(2,1)S(1)}, bf16[4,128,128]{2,1,0:T(8,128)(2,1)S(1)}, u32[]{:S(2)}, u32[]{:S(2)}) collective-permute-start(bf16[4,128,128]{2,1,0:T(8,128)(2,1)S(1)} %add_convert_fusion), channel_id=1, source_target_pairs={{0,12},{4,0},{8,4},{12,8},{1,13},{5,1},{9,5},{13,9},{2,14},{6,2},{... | collective-permute-start | bytes 393224 | tf_op jit(solution)/shard_map/ppermute | solution.py:202

commit v27 on v25

--- a/solution.py
+++ b/solution.py
@@ -127,19 +127,25 @@
 
     @pl.loop(0, lax.div(count + SUM_TERMS - 1, SUM_TERMS))
     def _(step):
-        for t in range(SUM_TERMS):
-            at = step * SUM_TERMS + t
-            k = picked[at]
+        ks = [picked[step * SUM_TERMS + t] for t in range(SUM_TERMS)]
+        shifts = [shift_ref[k] for k in ks]
+        places = [[wrapped(s - shift, targets) for s in range(sec_dev)] for shift in shifts]
+        weights = [
+            [
+                jnp.where(step * SUM_TERMS + t < count, coef_ref[target, ks[t]], 0.0)
+                for target in places[t]
+            ]
+            for t in range(SUM_TERMS)
+        ]
+        for t, k in enumerate(ks):
             product = lax.dot_general(
                 mixed_ref[k].reshape(sec_dev * rows, width),
                 held_ref[k],
                 (((1,), (1,)), ((), ())),
                 preferred_element_type=jnp.float32,
             )
-            for s in range(sec_dev):
-                target = wrapped(s - shift_ref[k], targets)
-                weight = jnp.where(at < count, coef_ref[target, k], 0.0)
-                scaled = weight * product[s * rows : (s + 1) * rows]
+            for s, target in enumerate(places[t]):
+                scaled = weights[t][s] * product[s * rows : (s + 1) * rows]
                 if stage is None:
                     sums[0][target] += scaled
                 else:

time: 35.3 us -> 35.3 us (level); the launches traced: 34.8 us -> 35.4 us
  starting transfers between devices: 15.2 us -> 15.8 us
    ppermute x10, starting transfers between devices: 15.2 us -> 15.8 us  [shift_by(): lax.ppermute(value, axis, [(i, (i + distance) % size) for i in range(size)])]
  transfers between devices with their start and end apart: 10 -> 10, of which waited for: 5 -> 5; matrix products, arithmetic and copies ran while one was open for 0% -> 0% of each run, Pallas kernels for 22% -> 21%
where the time goes in v27:
time: 35.3 us; the launch traced here: 35.4 us
  starting transfers between devices  15.8 us (45%)
  Pallas kernels  10.6 us (30%)
  waiting for transfers between devices  7.24 us (21%)
  other arithmetic  1.64 us (5%)
    ppermute x10, starting transfers between devices, shift_by(): lax.ppermute(value, axis, [(i, (i + distance) % size) for i in range(size)])  15.8 us
    ppermute x10, waiting for transfers between devices, shift_by(): lax.ppermute(value, axis, [(i, (i + distance) % size) for i in range(size)])  7.24 us
    pallas_call x2, Pallas kernels, summed(): pl.pallas_call(functools.partial(sum_kernel, order, stage), out_shape=out...  6.69 us
    pallas_call x1, Pallas kernels, mix(): pl.pallas_call(functools.partial(mix_kernel, split), out_shape=[pltpu.VME...  3.95 us
    add x3, other arithmetic, per_device(): sigma = lax.optimization_barrier(sigma) + other.astype(jnp.float32)  0.78 us
  transfers between devices with their start and end apart: 10, of which 5 were waited for; matrix products, arithmetic and copies ran while one was open for 0% of the time, Pallas kernels for 21%

profile of v27, /device:TPU:0, one launch (start us, length us, event | category | flops | bytes accessed | tf_op | source)
XLA Modules:
  0.0 35.4 jit_solution(4521525370192885754)
XLA Ops:
  0.0 0.7 %select_bitcast_fusion = f32[4,32]{1,0:T(4,128)S(1)} fusion(f32[32,4]{0,1:T(4,128)} %param.9, s32[32,4]{0,1:T(4,128)} %param.10), kind=kLoop, calls=%fused_computation.8 | loop fusion | flops 256 | bytes 1536 | tf_op jit(solution)/shard_map/jit(_where)/select_n | solution.py:207
  0.7 3.0 %collective-permute-start.2 = (f32[4,32]{1,0:T(4,128)S(1)}, f32[4,32]{1,0:T(4,128)S(1)}, u32[]{:S(2)}, u32[]{:S(2)}) collective-permute-start(f32[4,32]{1,0:T(4,128)S(1)} %select_bitcast_fusion), channel_id=1, source_target_pairs={{0,4},{4,8},{8,12},{12,0},{1,5},{5,9},{9,13},{13,1},{2,6},{6,10},{... | collective-permute-start | bytes 1544 | tf_op jit(solution)/shard_map/ppermute | solution.py:197
  3.7 2.6 %collective-permute-start.1 = (f32[4,32]{1,0:T(4,128)S(1)}, f32[4,32]{1,0:T(4,128)S(1)}, u32[]{:S(2)}, u32[]{:S(2)}) collective-permute-start(f32[4,32]{1,0:T(4,128)S(1)} %select_bitcast_fusion), channel_id=1, source_target_pairs={{0,8},{4,12},{8,0},{12,4},{1,9},{5,13},{9,1},{13,5},{2,10},{6,14},... | collective-permute-start | bytes 1544 | tf_op jit(solution)/shard_map/ppermute | solution.py:197
  6.3 1.3 %collective-permute-start = (f32[4,32]{1,0:T(4,128)S(1)}, f32[4,32]{1,0:T(4,128)S(1)}, u32[]{:S(2)}, u32[]{:S(2)}) collective-permute-start(f32[4,32]{1,0:T(4,128)S(1)} %select_bitcast_fusion), channel_id=1, source_target_pairs={{0,12},{4,0},{8,4},{12,8},{1,13},{5,1},{9,5},{13,9},{2,14},{6,2},{... | collective-permute-start | bytes 1544 | tf_op jit(solution)/shard_map/ppermute | solution.py:197
  7.7 4.0 %shard_map.64 = (bf16[32,4,128,256]{3,2,1,0:T(8,128)(2,1)S(1)}, bf16[32,256,256]{2,1,0:T(8,128)(2,1)S(1)}, f32[16,128,128]{2,1,0:T(8,128)S(1)}, f32[16,128,128]{2,1,0:T(8,128)S(1)}) custom-call(bf16[4,256,256]{2,1,0:T(8,128)(2,1)} %wave_ref.1, bf16[32,128,256]{2,1,0:T(8,128)(2,1)} %left_ref.1, bf16[32,256,256]{2,1,0:T(8,128)(2,1)} %right_ref.1), custom_call_target="tpu_custom_call" | custom-call | flops 2147483648 | bytes 6291456 | tf_op jit(solution)/shard_map/pallas_call | solution.py:73
  11.6 0.0 collective-permute-done.2
  11.6 0.0 collective-permute-done.1
  11.6 0.0 collective-permute-done
  11.7 3.0 %shard_map.65 = (f32[16,128,128]{2,1,0:T(8,128)S(1)}, f32[16,128,128]{2,1,0:T(8,128)S(1)}, f32[4,128,128]{2,1,0:T(8,128)S(1)}, bf16[4,128,128]{2,1,0:T(8,128)(2,1)S(1)}) custom-call(s32[32]{0:T(128)} %shift_ref.3, f32[16,32]{1,0:T(8,128)S(1)} %pad_maximum_fusion.coef_ref, ...), custom_call_target="tpu_custom_call", output_to_operand_aliasing={{0}: (4, {}), {1}: (5, {})} | custom-call | flops 1073741824 | bytes 6291456 | tf_op jit(solution)/shard_map/pallas_call | solution.py:174
  14.7 2.1 %collective-permute-start.3 = (bf16[4,128,128]{2,1,0:T(8,128)(2,1)S(1)}, bf16[4,128,128]{2,1,0:T(8,128)(2,1)S(1)}, u32[]{:S(2)}, u32[]{:S(2)}) collective-permute-start(bf16[4,128,128]{2,1,0:T(8,128)(2,1)S(1)} %get-tuple-element.31), channel_id=1, source_target_pairs={{0,2},{2,0},{1,3},{3,1},{4,6},{6,4},{5,7},{7,5},{8,10},{10,8},{9,1... | collective-permute-start | bytes 393224 | tf_op jit(solution)/shard_map/ppermute | solution.py:197
  16.8 3.7 %shard_map.66 = (f32[16,128,128]{2,1,0:T(8,128)S(1)}, f32[16,128,128]{2,1,0:T(8,128)S(1)}, f32[4,128,128]{2,1,0:T(8,128)S(1)}, bf16[4,128,128]{2,1,0:T(8,128)(2,...) custom-call(s32[32]{0:T(128)} %shift_ref.3, ...), custom_call_target="tpu_custom_call", output_to_operand_aliasing={{0}: (4, {}), {1}: (5, {})} | custom-call | flops 1073741824 | bytes 6291456 | tf_op jit(solution)/shard_map/pallas_call | solution.py:174
  20.5 0.0 collective-permute-done.3
  20.5 1.4 %collective-permute-start.4 = (bf16[4,128,128]{2,1,0:T(8,128)(2,1)S(1)}, bf16[4,128,128]{2,1,0:T(8,128)(2,1)S(1)}, u32[]{:S(2)}, u32[]{:S(2)}) collective-permute-start(bf16[4,128,128]{2,1,0:T(8,128)(2,1)S(1)} %get-tuple-element.41), channel_id=1, source_target_pairs={{0,2},{2,0},{1,3},{3,1},{4,6},{6,4},{5,7},{7,5},{8,10},{10,8},{9,1... | collective-permute-start | bytes 393224 | tf_op jit(solution)/shard_map/ppermute | solution.py:197
  21.9 0.3 collective-permute-start.7
  22.2 0.7 %collective-permute-start.6 = (bf16[4,128,128]{2,1,0:T(8,128)(2,1)S(1)}, bf16[4,128,128]{2,1,0:T(8,128)(2,1)S(1)}, u32[]{:S(2)}, u32[]{:S(2)}) collective-permute-start(bf16[4,128,128]{2,1,0:T(8,128)(2,1)S(1)} %get-tuple-element.46), channel_id=1, source_target_pairs={{0,2},{2,0},{1,3},{3,1},{4,6},{6,4},{5,7},{7,5},{8,10},{10,8},{9,1... | collective-permute-start | bytes 393224 | tf_op jit(solution)/shard_map/ppermute | solution.py:197
  22.9 3.2 %collective-permute-done.4 = bf16[4,128,128]{2,1,0:T(8,128)(2,1)S(1)} collective-permute-done((bf16[4,128,128]{2,1,0:T(8,128)(2,1)S(1)}, bf16[4,128,128]{2,1,0:T(8,128)(2,1)S(1)}, u32[]{:S(2)}, u32[]{:S(2)}) %collective-permute-start.4) | collective-permute-done | bytes 131104 | tf_op jit(solution)/shard_map/ppermute | solution.py:197
  26.2 0.9 %collective-permute-start.8 = (bf16[4,128,128]{2,1,0:T(8,128)(2,1)S(1)}, bf16[4,128,128]{2,1,0:T(8,128)(2,1)S(1)}, u32[]{:S(2)}, u32[]{:S(2)}) collective-permute-start(bf16[4,128,128]{2,1,0:T(8,128)(2,1)S(1)} %add_convert_fusion.1), channel_id=1, source_target_pairs={{0,4},{4,8},{8,12},{12,0},{1,5},{5,9},{9,13},{13,1},{2,6},{6,10},{... | collective-permute-start | bytes 393224 | tf_op jit(solution)/shard_map/ppermute | solution.py:197
  27.0 1.1 %collective-permute-start.5 = (bf16[4,128,128]{2,1,0:T(8,128)(2,1)S(1)}, bf16[4,128,128]{2,1,0:T(8,128)(2,1)S(1)}, u32[]{:S(2)}, u32[]{:S(2)}) collective-permute-start(bf16[4,128,128]{2,1,0:T(8,128)(2,1)S(1)} %get-tuple-element.43), channel_id=1, source_target_pairs={{0,2},{2,0},{1,3},{3,1},{4,6},{6,4},{5,7},{7,5},{8,10},{10,8},{9,1... | collective-permute-start | bytes 393224 | tf_op jit(solution)/shard_map/ppermute | solution.py:197
  28.2 0.6 %collective-permute-done.6 = bf16[4,128,128]{2,1,0:T(8,128)(2,1)S(1)} collective-permute-done((bf16[4,128,128]{2,1,0:T(8,128)(2,1)S(1)}, bf16[4,128,128]{2,1,0:T(8,128)(2,1)S(1)}, u32[]{:S(2)}, u32[]{:S(2)}) %collective-permute-start.6) | collective-permute-done | bytes 131104 | tf_op jit(solution)/shard_map/ppermute | solution.py:197
  28.8 2.3 %collective-permute-start.9 = (bf16[4,128,128]{2,1,0:T(8,128)(2,1)S(1)}, bf16[4,128,128]{2,1,0:T(8,128)(2,1)S(1)}, u32[]{:S(2)}, u32[]{:S(2)}) collective-permute-start(bf16[4,128,128]{2,1,0:T(8,128)(2,1)S(1)} %add_convert_fusion), channel_id=1, source_target_pairs={{0,12},{4,0},{8,4},{12,8},{1,13},{5,1},{9,5},{13,9},{2,14},{6,2},{... | collective-permute-start | bytes 393224 | tf_op jit(solution)/shard_map/ppermute | solution.py:197
  31.1 0.9 %collective-permute-done.5 = bf16[4,128,128]{2,1,0:T(8,128)(2,1)S(1)} collective-permute-done((bf16[4,128,128]{2,1,0:T(8,128)(2,1)S(1)}, bf16[4,128,128]{2,1,0:T(8,128)(2,1)S(1)}, u32[]{:S(2)}, u32[]{:S(2)}) %collective-permute-start.5) | collective-permute-done | bytes 131104 | tf_op jit(solution)/shard_map/ppermute | solution.py:197
  32.0 1.2 %collective-permute-done.7 = bf16[4,128,128]{2,1,0:T(8,128)(2,1)S(1)} collective-permute-done((bf16[4,128,128]{2,1,0:T(8,128)(2,1)S(1)}, bf16[4,128,128]{2,1,0:T(8,128)(2,1)S(1)}, u32[]{:S(2)}, u32[]{:S(2)}) %collective-permute-start.7) | collective-permute-done | bytes 131104 | tf_op jit(solution)/shard_map/ppermute | solution.py:197
  33.2 0.0 collective-permute-done.8
  33.3 1.4 %collective-permute-done.9 = bf16[4,128,128]{2,1,0:T(8,128)(2,1)S(1)} collective-permute-done((bf16[4,128,128]{2,1,0:T(8,128)(2,1)S(1)}, bf16[4,128,128]{2,1,0:T(8,128)(2,1)S(1)}, u32[]{:S(2)}, u32[]{:S(2)}) %collective-permute-start.9) | collective-permute-done | bytes 131104 | tf_op jit(solution)/shard_map/ppermute | solution.py:197
  34.7 0.7 %convert_add_fusion = f32[4,128,128]{2,1,0:T(8,128)} fusion(f32[4,128,128]{2,1,0:T(8,128)S(1)} %convert_add_fusion.1, bf16[4,128,128]{2,1,0:T(8,128)(2,1)S(1)} %collective-permute-done.9), kind=kLoop, calls=%fused_computation | loop fusion | flops 131072 | bytes 655360 | tf_op jit(solution)/shard_map/add | solution.py:233
  (7 shorter events, 0.2 us)
Async XLA Ops:
  0.7 10.9 %collective-permute-start.2 = (f32[4,32]{1,0:T(4,128)S(1)}, f32[4,32]{1,0:T(4,128)S(1)}, u32[]{:S(2)}, u32[]{:S(2)}) collective-permute-start(f32[4,32]{1,0:T(4,128)S(1)} %select_bitcast_fusion), channel_id=1, source_target_pairs={{0,4},{4,8},{8,12},{12,0},{1,5},{5,9},{9,13},{13,1},{2,6},{6,10},{... | collective-permute-start | bytes 1544 | tf_op jit(solution)/shard_map/ppermute | solution.py:197
  3.7 7.9 %collective-permute-start.1 = (f32[4,32]{1,0:T(4,128)S(1)}, f32[4,32]{1,0:T(4,128)S(1)}, u32[]{:S(2)}, u32[]{:S(2)}) collective-permute-start(f32[4,32]{1,0:T(4,128)S(1)} %select_bitcast_fusion), channel_id=1, source_target_pairs={{0,8},{4,12},{8,0},{12,4},{1,9},{5,13},{9,1},{13,5},{2,10},{6,14},... | collective-permute-start | bytes 1544 | tf_op jit(solution)/shard_map/ppermute | solution.py:197
  6.3 5.3 %collective-permute-start = (f32[4,32]{1,0:T(4,128)S(1)}, f32[4,32]{1,0:T(4,128)S(1)}, u32[]{:S(2)}, u32[]{:S(2)}) collective-permute-start(f32[4,32]{1,0:T(4,128)S(1)} %select_bitcast_fusion), channel_id=1, source_target_pairs={{0,12},{4,0},{8,4},{12,8},{1,13},{5,1},{9,5},{13,9},{2,14},{6,2},{... | collective-permute-start | bytes 1544 | tf_op jit(solution)/shard_map/ppermute | solution.py:197
  14.7 5.8 %collective-permute-start.3 = (bf16[4,128,128]{2,1,0:T(8,128)(2,1)S(1)}, bf16[4,128,128]{2,1,0:T(8,128)(2,1)S(1)}, u32[]{:S(2)}, u32[]{:S(2)}) collective-permute-start(bf16[4,128,128]{2,1,0:T(8,128)(2,1)S(1)} %get-tuple-element.31), channel_id=1, source_target_pairs={{0,2},{2,0},{1,3},{3,1},{4,6},{6,4},{5,7},{7,5},{8,10},{10,8},{9,1... | collective-permute-start | bytes 393224 | tf_op jit(solution)/shard_map/ppermute | solution.py:197
  20.5 5.6 %collective-permute-start.4 = (bf16[4,128,128]{2,1,0:T(8,128)(2,1)S(1)}, bf16[4,128,128]{2,1,0:T(8,128)(2,1)S(1)}, u32[]{:S(2)}, u32[]{:S(2)}) collective-permute-start(bf16[4,128,128]{2,1,0:T(8,128)(2,1)S(1)} %get-tuple-element.41), channel_id=1, source_target_pairs={{0,2},{2,0},{1,3},{3,1},{4,6},{6,4},{5,7},{7,5},{8,10},{10,8},{9,1... | collective-permute-start | bytes 393224 | tf_op jit(solution)/shard_map/ppermute | solution.py:197
  21.9 11.3 %collective-permute-start.7 = (bf16[4,128,128]{2,1,0:T(8,128)(2,1)S(1)}, bf16[4,128,128]{2,1,0:T(8,128)(2,1)S(1)}, u32[]{:S(2)}, u32[]{:S(2)}) collective-permute-start(bf16[4,128,128]{2,1,0:T(8,128)(2,1)S(1)} %add_convert_fusion.2), channel_id=1, source_target_pairs={{0,8},{4,12},{8,0},{12,4},{1,9},{5,13},{9,1},{13,5},{2,10},{6,14},... | collective-permute-start | bytes 393224 | tf_op jit(solution)/shard_map/ppermute | solution.py:197
  22.2 6.5 %collective-permute-start.6 = (bf16[4,128,128]{2,1,0:T(8,128)(2,1)S(1)}, bf16[4,128,128]{2,1,0:T(8,128)(2,1)S(1)}, u32[]{:S(2)}, u32[]{:S(2)}) collective-permute-start(bf16[4,128,128]{2,1,0:T(8,128)(2,1)S(1)} %get-tuple-element.46), channel_id=1, source_target_pairs={{0,2},{2,0},{1,3},{3,1},{4,6},{6,4},{5,7},{7,5},{8,10},{10,8},{9,1... | collective-permute-start | bytes 393224 | tf_op jit(solution)/shard_map/ppermute | solution.py:197
  26.2 7.1 %collective-permute-start.8 = (bf16[4,128,128]{2,1,0:T(8,128)(2,1)S(1)}, bf16[4,128,128]{2,1,0:T(8,128)(2,1)S(1)}, u32[]{:S(2)}, u32[]{:S(2)}) collective-permute-start(bf16[4,128,128]{2,1,0:T(8,128)(2,1)S(1)} %add_convert_fusion.1), channel_id=1, source_target_pairs={{0,4},{4,8},{8,12},{12,0},{1,5},{5,9},{9,13},{13,1},{2,6},{6,10},{... | collective-permute-start | bytes 393224 | tf_op jit(solution)/shard_map/ppermute | solution.py:197
  27.0 5.0 %collective-permute-start.5 = (bf16[4,128,128]{2,1,0:T(8,128)(2,1)S(1)}, bf16[4,128,128]{2,1,0:T(8,128)(2,1)S(1)}, u32[]{:S(2)}, u32[]{:S(2)}) collective-permute-start(bf16[4,128,128]{2,1,0:T(8,128)(2,1)S(1)} %get-tuple-element.43), channel_id=1, source_target_pairs={{0,2},{2,0},{1,3},{3,1},{4,6},{6,4},{5,7},{7,5},{8,10},{10,8},{9,1... | collective-permute-start | bytes 393224 | tf_op jit(solution)/shard_map/ppermute | solution.py:197
  28.8 5.8 %collective-permute-start.9 = (bf16[4,128,128]{2,1,0:T(8,128)(2,1)S(1)}, bf16[4,128,128]{2,1,0:T(8,128)(2,1)S(1)}, u32[]{:S(2)}, u32[]{:S(2)}) collective-permute-start(bf16[4,128,128]{2,1,0:T(8,128)(2,1)S(1)} %add_convert_fusion), channel_id=1, source_target_pairs={{0,12},{4,0},{8,4},{12,8},{1,13},{5,1},{9,5},{13,9},{2,14},{6,2},{... | collective-permute-start | bytes 393224 | tf_op jit(solution)/shard_map/ppermute | solution.py:197
